TPU v7x, 128 devices: a whole 4x4x4 slice. The times are simulated.
128 devices in a mesh: lat: 16 (over z, x_lo, core), lon: 8 (over x_hi, y).
Axes of the slice: x: 4 (x_hi: 2, x_lo: 2; x = x_hi * 2 + x_lo), y: 4, z: 4, core: 2. Of those that a mesh axis runs over, the one named last changes fastest.
Arguments:
- increments: float32 [48, 768, 3072], P(None, 'lat', 'lon'), may hold values from -6 to 6
- lengths: float32 [48, 3], replicated, may hold values from 0.6 to 40, as said below
- weights: float32 [48, 3], replicated, may hold values from 0.3 to 1
Outputs:
- control: float32 [48, 768, 3072], P(None, 'lat', 'lon')
Inputs may be any that keep to these rules, and one draw needn't show every extreme that they name: Column 0 of lengths lies in 0.6 to 1.5, column 1 in 4 to 10, column 2 in 16 to 40 grid cells.
All inputs are finite; a program needn't handle non-finite values.
Results may differ from a plain program's by a relative error of at most 0.0001.
Values sent between devices are 32-bit elements; how exact they have to be, the bound alone decides.
No kernel may reach another device: no remote copies, remote signals or barrier semaphores. Data moves between devices by JAX's collectives and lax.ppermute only.
A program may use at most 192 MiB of HBM per device.

v0:
```python
import jax
import jax.numpy as jnp
from jax import lax
from jax.sharding import PartitionSpec as P

LEVELS = 8
SCALES = 3
BLOCK = 256


precise_mode = lax.Precision.HIGHEST


def with_halo(block, sides, width, periodic):
    for axis, dim in sides:
        count = lax.axis_size(axis)
        forward = [(i, i + 1) for i in range(count - 1)]
        if periodic:
            forward.append((count - 1, 0))
        backward = [(target, source) for source, target in forward]
        low = lax.ppermute(
            lax.slice_in_dim(block, block.shape[dim] - width, None, axis=dim), axis, forward
        )
        high = lax.ppermute(lax.slice_in_dim(block, 0, width, axis=dim), axis, backward)
        block = jnp.concatenate([low, block, high], axis=dim)
    return block


def line_tables(decay_rate, block_width, block_count):
    offsets = jnp.arange(block_width, dtype=jnp.float32)
    offset_gap = offsets[:, None] - offsets[None, :]
    inside = offset_gap >= 0
    rate_grid = decay_rate[..., None, None]
    leakage = -jnp.expm1(-rate_grid)
    lower_matrix = jnp.where(
        inside, leakage * jnp.exp(-rate_grid * jnp.where(inside, offset_gap, 0.0)), 0.0
    )
    block_steps = jnp.arange(block_count, dtype=jnp.float32)
    block_gap = block_steps[:, None] - block_steps[None, :]
    block_inside = block_gap >= 0
    carry_matrix = jnp.where(
        block_inside,
        jnp.exp(-rate_grid * block_width * jnp.where(block_inside, block_gap, 0.0)),
        0.0,
    )
    rise_powers = jnp.exp(-decay_rate[..., None] * (offsets + 1.0))
    fall_powers = jnp.exp(-decay_rate[..., None] * (block_width - offsets))
    return (lower_matrix, carry_matrix, rise_powers, fall_powers)


def filter_last(stack, decay_rate, block_width):
    fields, across, length = stack.shape
    block_count = length // block_width
    lower_matrix, carry_matrix, rise_powers, fall_powers = line_tables(
        decay_rate, block_width, block_count
    )
    blocks = stack.reshape(fields, across, block_count, block_width)
    block_local = jnp.einsum("fij,fakj->faki", lower_matrix, blocks, precision=precise_mode)
    block_ends = jnp.einsum(
        "fkm,fam->fak", carry_matrix, block_local[..., block_width - 1], precision=precise_mode
    )
    before = jnp.concatenate([jnp.zeros_like(block_ends[..., :1]), block_ends[..., :-1]], axis=2)
    forward_pass = block_local + before[..., None] * rise_powers[:, None, None, :]
    block_local = jnp.einsum("fji,fakj->faki", lower_matrix, forward_pass, precision=precise_mode)
    block_starts = jnp.einsum(
        "fmk,fam->fak", carry_matrix, block_local[..., 0], precision=precise_mode
    )
    following = jnp.concatenate(
        [block_starts[..., 1:], jnp.zeros_like(block_starts[..., :1])], axis=2
    )
    backward_pass = block_local + following[..., None] * fall_powers[:, None, None, :]
    return backward_pass.reshape(fields, across, length)


def filter_mid(stack, decay_rate, block_width):
    fields, length, across = stack.shape
    block_count = length // block_width
    lower_matrix, carry_matrix, rise_powers, fall_powers = line_tables(
        decay_rate, block_width, block_count
    )
    blocks = stack.reshape(fields, block_count, block_width, across)
    block_local = jnp.einsum("fij,fkja->fkia", lower_matrix, blocks, precision=precise_mode)
    block_ends = jnp.einsum(
        "fkm,fma->fka", carry_matrix, block_local[:, :, block_width - 1, :], precision=precise_mode
    )
    before = jnp.concatenate([jnp.zeros_like(block_ends[:, :1]), block_ends[:, :-1]], axis=1)
    forward_pass = block_local + before[:, :, None, :] * rise_powers[:, None, :, None]
    block_local = jnp.einsum("fji,fkja->fkia", lower_matrix, forward_pass, precision=precise_mode)
    block_starts = jnp.einsum(
        "fmk,fma->fka", carry_matrix, block_local[:, :, 0, :], precision=precise_mode
    )
    following = jnp.concatenate([block_starts[:, 1:], jnp.zeros_like(block_starts[:, :1])], axis=1)
    backward_pass = block_local + following[:, :, None, :] * fall_powers[:, None, :, None]
    return backward_pass.reshape(fields, length, across)


def shards(increments, lengths, weights):
    decay_rate = 1.0 / lengths
    decay = jnp.exp(-decay_rate)
    leakage = -jnp.expm1(-decay_rate)
    coefficient = weights * (1.0 + decay) ** 3 / (leakage * (1.0 + decay * decay))
    wind_fields = increments[: 2 * LEVELS]
    north_padded = with_halo(wind_fields, (("lat", 1),), 1, False)
    east_padded = with_halo(wind_fields, (("lon", 2),), 1, True)
    row_change = 0.5 * (north_padded[:, 2:, :] - north_padded[:, :-2, :])
    column_change = 0.5 * (east_padded[:, :, 2:] - east_padded[:, :, :-2])
    stream = row_change[:LEVELS] - column_change[LEVELS:]
    potential = -column_change[:LEVELS] - row_change[LEVELS:]
    adjoint = jnp.concatenate([stream, potential, increments[2 * LEVELS :]], axis=0)
    row_lines = lax.all_to_all(adjoint, "lon", split_axis=0, concat_axis=2, tiled=True)
    group_size = row_lines.shape[0]
    group_start = lax.axis_index("lon") * group_size
    group_rates = lax.dynamic_slice_in_dim(decay_rate, group_start, group_size, 0)
    group_coef = lax.dynamic_slice_in_dim(coefficient, group_start, group_size, 0)
    filtered = jnp.stack(
        [
            filter_last(row_lines, group_rates[:, scale_index], BLOCK)
            for scale_index in range(SCALES)
        ]
    )
    column_lines = lax.all_to_all(filtered, "lat", split_axis=3, concat_axis=2, tiled=True)
    summed = jnp.zeros(column_lines.shape[1:], jnp.float32)
    for scale_index in range(SCALES):
        second = filter_mid(column_lines[scale_index], group_rates[:, scale_index], BLOCK)
        summed = summed + group_coef[:, scale_index][:, None, None] * second
    returned = lax.all_to_all(summed, "lat", split_axis=1, concat_axis=2, tiled=True)
    control = lax.all_to_all(returned, "lon", split_axis=2, concat_axis=0, tiled=True)
    return control


def solution(mesh):
    in_specs = (P(None, "lat", "lon"), P(), P())
    out_specs = P(None, "lat", "lon")
    return jax.shard_map(shards, mesh=mesh, in_specs=in_specs, out_specs=out_specs, check_vma=False)
```

profile of v0, /device:TPU:1, one launch (start us, length us, event | category | flops | bytes accessed | tf_op | source)
XLA Modules:
  0.0 831.1 jit_solution(3273385985263019577)
XLA Ops:
  1.1 3.3 collective-permute-start
  4.4 3.1 collective-permute-start.1
  8.8 5.2 collective-permute-start.2
  14.0 8.9 %collective-permute-done.2 = f32[16,48,1]{2,1,0:T(8,128)S(1)} collective-permute-done((f32[16,48,1]{2,1,0:T(8,128)S(1)}, f32[16,48,1]{2,1,0:T(8,128)S(1)}, u32[]{:S(2)}, u32[]{:S(2)}) %collective-permute-start.2) | collective-permute-done | bytes 3104 | tf_op jit(solution)/shard_map/ppermute | solution.py:24
  23.0 5.6 collective-permute-done.3
  31.8 4.6 all-to-all-start
  37.0 41.1 %all-to-all-done = f32[48,48,384]{2,1,0:T(8,128)} async-done(((f32[48,48,384]{2,1,0:T(8,128)}), f32[48,48,384]{2,1,0:T(8,128)}, u32[]{:S(2)}, u32[]{:S(2)}) %all-to-all-start) | async-done | bytes 3538976 | tf_op jit(solution)/shard_map/all_to_all | solution.py:110
  78.0 5.8 copy.141
  83.9 5.0 reshape.464
  88.9 8.0 fusion.31
  98.3 3.9 fusion.15
  103.5 4.3 copy.66
  107.7 5.0 stack_reshape.9
  112.7 7.8 fusion.29
  121.8 3.9 fusion.12
  127.0 4.3 copy.69
  131.2 5.0 stack_reshape.10
  136.2 8.0 fusion.27
  145.5 3.9 fusion.9
  150.7 4.2 copy.72
  154.9 5.0 stack_reshape.11
  159.9 9.4 %pad_maximum_fusion = f32[3,6,48,3072]{3,2,1,0:T(8,128)} fusion(f32[1,6,48,3072]{3,2,1,0:T(8,128)} %stack_reshape.11, f32[1,6,48,3072]{3,2,1,0:T(8,128)} %stack_reshape.10, f32[1,6,48,3072]{3,2,1,0:T(8,128)} %stack_reshape.9), kind=kLoop, calls=%fused_computation | loop fusion | flops 5308416 | bytes 21233664 | tf_op jit(solution)/shard_map/stack | solution.py:115
  169.3 22.9 %copy.73 = f32[3,6,48,3072]{2,1,0,3:T(8,128)} copy(f32[3,6,48,3072]{3,2,1,0:T(8,128)} %pad_maximum_fusion) | data formatting | bytes 21233664 | tf_op jit(solution)/shard_map/stack | solution.py:115
  192.2 31.1 %reshape.477 = f32[16,1,165888]{2,1,0:T(1,128)} reshape(f32[3072,3,6,48]{3,2,1,0:T(8,128)} %bitcast.117) | data formatting | bytes 21233664
  223.3 6.8 all-to-all-start.1
  230.3 118.2 %all-to-all-done.1 = f32[16,1,165888]{2,1,0:T(1,128)} async-done(((f32[16,1,165888]{2,1,0:T(1,128)}), f32[16,1,165888]{2,1,0:T(1,128)}, u32[]{:S(2)}, u32[]{:S(2)}) %all-to-all-start.1) | async-done | bytes 10616864 | tf_op jit(solution)/shard_map/all_to_all | solution.py:121
  349.0 114.3 %reduce.12 = f32[16,165888]{1,0:T(8,128)} reduce(f32[16,1,165888]{2,1,0:T(1,128)} %all-to-all-done.1, f32[]{:T(128)} %broadcast.365), dimensions={1}, to_apply=%all_to_all.51.reduce_sub_computation | reduce | bytes 21233668 | tf_op jit(solution)/shard_map/all_to_all | solution.py:121
  463.3 40.1 %reshape.478 = f32[3072,3,6,48]{3,2,1,0:T(8,128)} reshape(f32[16,165888]{1,0:T(8,128)} %reduce.12) | data formatting | bytes 21233664
  503.4 29.1 %copy.74 = f32[3,6,48,16,192]{4,2,3,1,0:T(8,128)} copy(f32[3,6,48,16,192]{2,1,0,4,3:T(8,128)} %bitcast.118) | data formatting | bytes 21233664 | tf_op jit(solution)/shard_map/all_to_all | solution.py:121
  532.5 10.7 %fusion.171 = (f32[1,6,16,48,192]{4,3,2,1,0:T(8,128)}, f32[1,6,16,48,192]{4,3,2,1,0:T(8,128)}, f32[1,6,16,48,192]{4,3,2,1,0:T(8,128)}) fusion(f32[3,6,16,48,192]{4,3,2,1,0:T(8,128)} %bitcast.119), kind=kLoop, calls=%fused_computation.227 | loop fusion | bytes 21233664 | tf_op jit(solution)/shard_map/slice | solution.py:124
  543.1 9.6 %convolution_bitcast_fusion.2 = f32[6,3,256,192]{2,3,1,0:T(8,128)S(1)} fusion(f32[6,3,256,192]{3,2,1,0:T(8,128)} %bitcast.125, f32[256,256]{1,0:T(8,128)S(1)} %fusion.121, f32[6]{0:T(128)S(1)} %get-tuple-element.33, f32[6]{0:T(128)S(1)} %get-tuple-element.32, pred[256,256]{1,0:T(8,128)(4,1)S(1)} %fusion.122), kind=kOutput, calls=%fused_computation.33 | convolution fusion | flops 2719088640 | bytes 7405616 | tf_op jit(solution)/shard_map/fij,fkja->fkia/dot_general | solution.py:82
  556.2 5.9 fusion.18
  565.2 2.5 add_bitcast_fusion.2
  567.8 2.2 copy.119
  569.9 9.7 %convolution_bitcast_fusion.1 = f32[6,3,256,192]{2,3,1,0:T(8,128)S(1)} fusion(f32[6,3,256,192]{3,2,1,0:T(8,128)} %bitcast.124, f32[6]{0:T(128)S(1)} %get-tuple-element.35, f32[6]{0:T(128)S(1)} %get-tuple-element.30, f32[256,256]{1,0:T(8,128)S(1)} %fusion.121, pred[256,256]{1,0:T(8,128)(4,1)S(1)} %fusion.122), kind=kOutput, calls=%fused_computation.32 | convolution fusion | flops 2719088640 | bytes 7405616 | tf_op jit(solution)/shard_map/fij,fkja->fkia/dot_general | solution.py:82
  583.2 5.9 fusion.21
  592.2 2.5 add_bitcast_fusion.1
  596.8 9.8 %convolution_bitcast_fusion = f32[6,3,256,192]{2,3,1,0:T(8,128)S(1)} fusion(f32[6,3,256,192]{3,2,1,0:T(8,128)} %bitcast.123, f32[6]{0:T(128)S(1)} %get-tuple-element.34, f32[6]{0:T(128)S(1)} %get-tuple-element.28, f32[256,256]{1,0:T(8,128)S(1)} %fusion.121, pred[256,256]{1,0:T(8,128)(4,1)S(1)} %fusion.122), kind=kOutput, calls=%fused_computation.31 | convolution fusion | flops 2719088640 | bytes 7405616 | tf_op jit(solution)/shard_map/fij,fkja->fkia/dot_general | solution.py:82
  610.1 5.9 fusion.24
  619.1 2.5 add_bitcast_fusion
  625.5 4.1 copy.96
  629.5 77.3 %all_to_all.66 = f32[6,768,192]{2,0,1:T(8,128)} all-to-all(f32[6,768,192]{2,0,1:T(8,128)} %copy.96), channel_id=1, replica_groups=mesh['lat'=16,'lon'=8] {'lat'}, dimensions={1} | all-to-all | bytes 7077888 | tf_op jit(solution)/shard_map/all_to_all | solution.py:126
  706.8 10.4 %copy.115 = f32[6,48,16,192]{1,0,3,2:T(8,128)} copy(f32[6,48,16,192]{3,0,1,2:T(8,128)} %bitcast.122) | data formatting | bytes 7077888 | tf_op jit(solution)/shard_map/all_to_all | solution.py:126
  717.2 12.8 %reshape.479 = f32[8,1,110592]{2,1,0:T(1,128)} reshape(f32[3072,6,48]{2,1,0:T(8,128)} %bitcast.120) | data formatting | bytes 7077888
  730.0 46.9 %all_to_all.67 = f32[8,1,110592]{2,1,0:T(1,128)S(1)} all-to-all(f32[8,1,110592]{2,1,0:T(1,128)} %reshape.479), channel_id=1, replica_groups=mesh['lat'=16,'lon'=8] {'lon'}, dimensions={0} | all-to-all | bytes 7077888 | tf_op jit(solution)/shard_map/all_to_all | solution.py:127
  776.8 31.2 %reduce.13 = f32[8,110592]{1,0:T(8,128)} reduce(f32[8,1,110592]{2,1,0:T(1,128)S(1)} %all_to_all.67, f32[]{:T(128)} %broadcast.365), dimensions={1}, to_apply=%all_to_all.58.reduce_sub_computation | reduce | bytes 7077892 | tf_op jit(solution)/shard_map/all_to_all | solution.py:127
  808.0 14.1 %reshape.480 = f32[3072,6,48]{2,1,0:T(8,128)} reshape(f32[8,110592]{1,0:T(8,128)} %reduce.13) | data formatting | bytes 7077888
  822.1 8.6 %copy.101 = f32[8,6,48,384]{3,2,1,0:T(8,128)} copy(f32[8,6,48,384]{2,1,3,0:T(8,128)} %bitcast.121) | data formatting | bytes 7077888 | tf_op jit(solution)/shard_map/all_to_all | solution.py:127
  (96 shorter events, 39.7 us)
Async XLA Ops:
  1.1 27.5 %collective-permute-start = (f32[16,1,384]{2,1,0:T(1,128)S(1)}, f32[16,1,384]{2,1,0:T(1,128)S(1)}, u32[]{:S(2)}, u32[]{:S(2)}) collective-permute-start(f32[16,1,384]{2,1,0:T(1,128)S(1)} %get-tuple-element.10), channel_id=1, source_target_pairs={{8,0},{16,8},{24,16},{32,24},{40,32},{48,40},{56,48},{64,56},{72,6... | collective-permute-start | bytes 73736 | tf_op jit(solution)/shard_map/ppermute | solution.py:24
  4.4 24.2 %collective-permute-start.1 = (f32[16,1,384]{2,1,0:T(1,128)S(1)}, f32[16,1,384]{2,1,0:T(1,128)S(1)}, u32[]{:S(2)}, u32[]{:S(2)}) collective-permute-start(f32[16,1,384]{2,1,0:T(1,128)S(1)} %get-tuple-element.11), channel_id=1, source_target_pairs={{0,8},{8,16},{16,24},{24,32},{32,40},{40,48},{48,56},{56,64},{64,7... | collective-permute-start | bytes 73736 | tf_op jit(solution)/shard_map/ppermute | solution.py:21
  8.8 14.2 %collective-permute-start.2 = (f32[16,48,1]{2,1,0:T(8,128)S(1)}, f32[16,48,1]{2,1,0:T(8,128)S(1)}, u32[]{:S(2)}, u32[]{:S(2)}) collective-permute-start(f32[16,48,1]{2,1,0:T(8,128)S(1)} %get-tuple-element.8), channel_id=1, source_target_pairs={{1,0},{2,1},{3,2},{4,3},{5,4},{6,5},{7,6},{0,7},{9,8},{10,9},{11,1... | collective-permute-start | bytes 9224 | tf_op jit(solution)/shard_map/ppermute | solution.py:24
  14.0 14.6 %slice-start = ((f32[48,48,384]{2,1,0:T(8,128)}), f32[16,48,384]{2,1,0:T(8,128)S(1)}, s32[]{:S(2)}) async-start(f32[48,48,384]{2,1,0:T(8,128)} %param.3), calls=%async_computation.4 | async-start | bytes 2359296 | tf_op jit(solution)/shard_map/slice | solution.py:102
  14.0 14.6 %collective-permute-start.3 = (f32[16,48,1]{2,1,0:T(8,128)S(1)}, f32[16,48,1]{2,1,0:T(8,128)S(1)}, u32[]{:S(2)}, u32[]{:S(2)}) collective-permute-start(f32[16,48,1]{2,1,0:T(8,128)S(1)} %get-tuple-element.9), channel_id=1, source_target_pairs={{0,1},{1,2},{2,3},{3,4},{4,5},{5,6},{6,7},{7,0},{8,9},{9,10},{10,1... | collective-permute-start | bytes 9224 | tf_op jit(solution)/shard_map/ppermute | solution.py:21
  14.0 15.7 %slice-start.1 = ((f32[48,48,384]{2,1,0:T(8,128)}), f32[32,48,384]{2,1,0:T(8,128)S(1)}, s32[]{:S(2)}) async-start(f32[48,48,384]{2,1,0:T(8,128)} %param.3), calls=%async_computation.5 | async-start | bytes 4718592 | tf_op jit(solution)/shard_map/slice | solution.py:109
  31.8 4.7 copy-start.8
  31.8 4.7 copy-start.9
  31.8 46.3 %all-to-all-start = ((f32[48,48,384]{2,1,0:T(8,128)}), f32[48,48,384]{2,1,0:T(8,128)}, u32[]{:S(2)}, u32[]{:S(2)}) async-start(f32[48,48,384]{2,1,0:T(8,128)} %pad_maximum_fusion.1), calls=%async_computation | async-start | bytes 7077888 | tf_op jit(solution)/shard_map/all_to_all | solution.py:110
  223.3 125.1 %all-to-all-start.1 = ((f32[16,1,165888]{2,1,0:T(1,128)}), f32[16,1,165888]{2,1,0:T(1,128)}, u32[]{:S(2)}, u32[]{:S(2)}) async-start(f32[16,1,165888]{2,1,0:T(1,128)} %reshape.477), calls=%async_computation.1 | async-start | bytes 21233664 | tf_op jit(solution)/shard_map/all_to_all | solution.py:121
  552.7 1.8 copy-start.4
  562.2 1.8 copy-start.1
  579.7 1.8 copy-start.5
  589.1 1.8 copy-start.2
  606.6 1.8 copy-start.3
  616.0 1.8 copy-start
  621.6 2.0 copy-start.6
  621.6 3.1 copy-start.7
where the time goes:
time: 842 us; the launch traced here: 831 us
  local copies, waits for them, and re-layouts  256 us (30%)
  waiting for transfers between devices  174 us (21%)
  other arithmetic  169 us (20%)
  blocking collectives  124 us (15%)
  matrix products  85 us (10%)
  starting transfers between devices  23.1 us (3%)
    all_to_all x1, waiting for transfers between devices, shards(): lax.all_to_all(filtered, 'lat', split_axis=3, concat_axis=2, tiled=True)  118 us
    all_to_all x1, other arithmetic, shards(): lax.all_to_all(filtered, 'lat', split_axis=3, concat_axis=2, tiled=True)  114 us
    unnamed x24, local copies, waits for them, and re-layouts  112 us
    all_to_all x1, blocking collectives, shards(): lax.all_to_all(summed, 'lat', split_axis=1, concat_axis=2, tiled=True)  77.3 us
    all_to_all x1, blocking collectives, shards(): lax.all_to_all(returned, 'lon', split_axis=2, concat_axis=0, tiled=True)  46.9 us
    all_to_all x1, waiting for transfers between devices, shards(): lax.all_to_all(adjoint, 'lon', split_axis=0, concat_axis=2, tiled=True)  41.1 us
    another operation x4, local copies, waits for them, and re-layouts, shards(): jnp.stack([filter_last(row_lines, group_rates[:, scale_index], BLOCK) for...  37.8 us
    all_to_all x1, other arithmetic, shards(): lax.all_to_all(returned, 'lon', split_axis=2, concat_axis=0, tiled=True)  31.2 us
  transfers between devices with their start and end apart: 6, of which 4 were waited for; matrix products, arithmetic and copies ran while one was open for 0% of the time, Pallas kernels for 0%

commit v1 on v0

v1 whole, which is shorter than its diff:
```python
import functools

import jax
import jax.numpy as jnp
from jax import lax
from jax.experimental import pallas as pl
from jax.experimental.pallas import tpu as pltpu
from jax.sharding import PartitionSpec as P

LEVELS = 8
SCALES = 3
WINDS = 16
FIELDS = 48
ROWS = 48
COLS = 384
GROUP = 8
GROUPS = FIELDS // GROUP
NLAT = 16
NLON = 8
LANES = 128
PARTS = COLS // LANES
HALF = FIELDS // 2
HALF_ROWS = SCALES * HALF
F32 = jnp.float32
BF16 = jnp.bfloat16

VMEM = pl.BlockSpec(memory_space=pltpu.VMEM)
SMEM = pl.BlockSpec(memory_space=pltpu.SMEM)
BIG = 48 * 1024 * 1024


def params(**kw):
    return pltpu.CompilerParams(vmem_limit_bytes=BIG, **kw)


def iota(shape, dim):
    return lax.broadcasted_iota(jnp.int32, shape, dim)


def fiota(shape, dim):
    return iota(shape, dim).astype(F32)


def split(value):
    high = value.astype(BF16)
    return high, (value - high.astype(F32)).astype(BF16)


def mm(a, b):
    return jnp.dot(a, b, preferred_element_type=F32)


def lane_fields(shape):
    lane = iota(shape, 1)
    virtual = lane & 31
    wind_field = ((virtual >> 4) << 3) + (virtual & 7)
    return lane, lane >> 5, virtual, wind_field, virtual + WINDS


def lane_rates(lengths):
    rate = 1.0 / lengths
    shape = (FIELDS, LANES)
    lane, scale, _, wind_field, rest_field = lane_fields(shape)
    value = jnp.where(scale == 0, rate[:, 0:1], jnp.where(scale == 1, rate[:, 1:2], rate[:, 2:3]))
    field = iota(shape, 0)
    pick = lambda which: jnp.sum(jnp.where(field == which, value, 0.0), axis=0, keepdims=True)
    used = lane[:1] < 96
    return jnp.where(used, pick(wind_field), 1.0), jnp.where(used, pick(rest_field), 1.0)


def lane_kinds(shape):
    _, _, virtual, _, _ = lane_fields(shape)
    second = virtual >= 16
    north = (virtual & 15) >= 8
    zonal = second != north
    sign = jnp.where(second | north, -1.0, 1.0).astype(F32)
    return zonal, sign


def row_sums_kernel(where_ref, len_ref, x_ref, sums_ref, edge_ref, high_ref, low_ref):
    group = pl.program_id(0)
    lon = where_ref[1]

    @pl.when(group == 0)
    def _():
        rate0, rate1 = lane_rates(len_ref[...])
        column = fiota((COLS, LANES), 0)
        for tile, rate in enumerate((rate0, rate1)):
            for side, steps in enumerate((COLS - 1 - column, column)):
                high, low = split(jnp.exp(-rate * steps))
                high_ref[tile, :, side * LANES:(side + 1) * LANES] = high
                low_ref[tile, :, side * LANES:(side + 1) * LANES] = low
        sums_ref[...] = jnp.zeros_like(sums_ref)
        edge_ref[...] = jnp.zeros_like(edge_ref)

    x = x_ref[...].reshape(GROUP * ROWS, COLS)
    xh, xl = split(x)
    tile = jnp.where(group < 2, 0, 1)
    wh = high_ref[tile]
    wl = low_ref[tile]
    res = mm(xh, wh) + mm(xl, wh) + mm(xh, wl)
    lane = iota((ROWS, LANES), 1)
    virtual = lane & 31

    @pl.when(group < 2)
    def _():
        left, right = sums_ref[:, 0:128], sums_ref[:, 128:256]
        first, last = edge_ref[:, 0:128], edge_ref[:, 128:256]
        for i in range(GROUP):
            mine = (virtual & 15) == group * GROUP + i
            rows = slice(i * ROWS, (i + 1) * ROWS)
            left = jnp.where(mine, res[rows, 0:128], left)
            right = jnp.where(mine, res[rows, 128:256], right)
            first = jnp.where(mine, x[rows, 0:1], first)
            last = jnp.where(mine, x[rows, COLS - 1:COLS], last)
        sums_ref[:, 0:128] = left
        sums_ref[:, 128:256] = right
        sums_ref[:, 256:384] = jnp.where(lon == 0, first, jnp.where(lon == NLON - 1, last, 0.0))
        edge_ref[:, 0:128] = first
        edge_ref[:, 128:256] = last

    @pl.when(group >= 2)
    def _():
        left, right = sums_ref[:, 384:512], sums_ref[:, 512:640]
        for i in range(GROUP):
            mine = virtual == (group - 2) * GROUP + i
            rows = slice(i * ROWS, (i + 1) * ROWS)
            left = jnp.where(mine, res[rows, 0:128], left)
            right = jnp.where(mine, res[rows, 128:256], right)
        sums_ref[:, 384:512] = left
        sums_ref[:, 512:640] = right


def row_sums(where, lengths, x):
    return pl.pallas_call(
        row_sums_kernel,
        grid=(GROUPS,),
        in_specs=[SMEM, pl.BlockSpec((FIELDS, SCALES), lambda g: (0, 0)),
                  pl.BlockSpec((GROUP, ROWS, COLS), lambda g: (g, 0, 0))],
        out_specs=[pl.BlockSpec((ROWS, 640), lambda g: (0, 0)), pl.BlockSpec((ROWS, 256), lambda g: (0, 0))],
        out_shape=[jax.ShapeDtypeStruct((ROWS, 640), F32), jax.ShapeDtypeStruct((ROWS, 256), F32)],
        scratch_shapes=[pltpu.VMEM((2, COLS, 256), BF16), pltpu.VMEM((2, COLS, 256), BF16)],
        compiler_params=params(),
        name="row_sums",
    )(where, lengths, x)


def zonal_difference(x):
    shape = x.shape
    axis = len(shape) - 1
    column = iota(shape, axis)
    ahead = jnp.where(column == COLS - 1, 0.0, pltpu.roll(x, COLS - 1, axis))
    behind = jnp.where(column == 0, 0.0, pltpu.roll(x, 1, axis))
    return 0.5 * (ahead - behind)


def local_sums_kernel(where_ref, len_ref, x1_ref, x2_ref, out_ref, acc_ref):
    group = pl.program_id(0)
    top = where_ref[0] == 0
    rate = 1.0 / len_ref[...]
    row_rate = jnp.concatenate([rate[:, s:s + 1] for _ in range(2) for s in range(SCALES)], axis=0)
    shape = (2 * SCALES * GROUP, ROWS)
    out_row = iota(shape, 0)
    member = out_row & 7
    left_side = out_row < SCALES * GROUP
    row = fiota(shape, 1)
    plain = jnp.exp(-row_rate * jnp.where(left_side, ROWS - 1 - row, row))

    def weighted(matrix, x, i):
        mh, ml = split(jnp.where(member == i, matrix, 0.0))
        xh, xl = split(x)
        return mm(mh, xh) + mm(mh, xl) + mm(ml, xh)

    @pl.when(group < 2)
    def _():
        decay = jnp.exp(-row_rate)
        gain = 0.5 * (1.0 - decay * decay) / decay
        start = jnp.where(top & (row == 0.0), 0.5 * jnp.exp(-row_rate * ROWS), 0.0)
        slope = jnp.where(left_side, -gain * plain - start, gain * plain)
        second_sign = jnp.where(group == 0, 1.0, -1.0)
        acc = jnp.zeros((2 * SCALES * GROUP, COLS), F32)
        for i in range(GROUP):
            acc += weighted(plain, -zonal_difference(x2_ref[i]), i)
            acc += weighted(slope, second_sign * x1_ref[i], i)
        acc_ref[...] = acc

    @pl.when(group >= 2)
    def _():
        acc = jnp.zeros((2 * SCALES * GROUP, COLS), F32)
        for i in range(GROUP):
            acc += weighted(plain, x1_ref[i], i)
        acc_ref[...] = acc

    acc = acc_ref[...]
    column = iota(acc.shape, 1)
    forward, backward = acc, acc
    factor = jnp.exp(-row_rate)
    step = 1
    while step < COLS:
        forward = forward + factor * jnp.where(column >= step, pltpu.roll(forward, step, 1), 0.0)
        backward = backward + factor * jnp.where(column < COLS - step, pltpu.roll(backward, COLS - step, 1), 0.0)
        factor = factor * factor
        step *= 2
    acc = forward + backward - acc
    for side in range(2):
        for s in range(SCALES):
            k = side * SCALES + s
            out_ref[0, side, s, 0] = acc[k * GROUP:(k + 1) * GROUP]


def other_wind(g):
    return jnp.where(g < 2, 1 - g, 0)


def local_sums(where, lengths, x):
    out = pl.pallas_call(
        local_sums_kernel,
        grid=(GROUPS,),
        in_specs=[SMEM, pl.BlockSpec((GROUP, SCALES), lambda g: (g, 0)),
                  pl.BlockSpec((GROUP, ROWS, COLS), lambda g: (g, 0, 0)),
                  pl.BlockSpec((GROUP, ROWS, COLS), lambda g: (other_wind(g), 0, 0))],
        out_specs=pl.BlockSpec((1, 2, SCALES, 1, GROUP, COLS), lambda g: (g // 3, 0, 0, g % 3, 0, 0)),
        out_shape=jax.ShapeDtypeStruct((2, 2, SCALES, 3, GROUP, COLS), F32),
        scratch_shapes=[pltpu.VMEM((2 * SCALES * GROUP, COLS), F32)],
        compiler_params=params(),
        name="local_sums",
    )(where, lengths, x, x)
    return out.reshape(2, 2 * HALF_ROWS, COLS)


def lon_merge_kernel(where_ref, len_ref, own_ref, g1_ref, g2_ref, g3_ref, part_ref, mine_ref):
    y = where_ref[1] & 3
    yf = y.astype(F32)
    rates = lane_rates(len_ref[...])
    got = (g1_ref, g2_ref, g3_ref)
    for tile in range(2):
        step = lambda n: jnp.exp(-rates[tile] * (COLS * n))
        base = tile * 384
        lanes_l = slice(base, base + 128)
        lanes_r = slice(base + 128, base + 256)
        left_total = step(3.0 - yf) * own_ref[:, lanes_l]
        right_total = step(yf) * own_ref[:, lanes_r]
        left = jnp.zeros((ROWS, LANES), F32)
        right = jnp.zeros((ROWS, LANES), F32)
        for d, ref in zip((1, 2, 3), got):
            below = y >= d
            lg, rg = ref[:, lanes_l], ref[:, lanes_r]
            left = left + jnp.where(below, step(d - 1.0), 0.0) * lg
            right = right + jnp.where(below, 0.0, step(3.0 - d)) * rg
            other = jnp.where(below, yf - d, yf - d + 4.0)
            left_total = left_total + step(3.0 - other) * lg
            right_total = right_total + step(other) * rg
        part_ref[:, tile * 256:tile * 256 + 128] = left
        part_ref[:, tile * 256 + 128:tile * 256 + 256] = right
        mine_ref[:, lanes_l] = left_total
        mine_ref[:, lanes_r] = right_total
    edge = slice(256, 384)
    mine_ref[:, edge] = own_ref[:, edge] + g1_ref[:, edge] + g2_ref[:, edge] + g3_ref[:, edge]


def lon_merge(where, lengths, own, got):
    return pl.pallas_call(
        lon_merge_kernel,
        in_specs=[SMEM] + [VMEM] * 5,
        out_specs=[VMEM, VMEM],
        out_shape=[jax.ShapeDtypeStruct((ROWS, 512), F32), jax.ShapeDtypeStruct((ROWS, 640), F32)],
        compiler_params=params(),
        name="lon_merge",
    )(where, lengths, own, *got)


def column_sums_kernel(where_ref, len_ref, part_ref, mine_ref, theirs_ref, edge_ref, local_ref,
                       carry_ref, keep_ref, send_ref):
    lat, lon = where_ref[0], where_ref[1]
    y = lon & 3
    yf = y.astype(F32)
    high = lon >= 4
    highf = jnp.where(high, 1.0, 0.0)
    lowf = 1.0 - highf
    lonf = lon.astype(F32)
    top = lat == 0
    rates = lane_rates(len_ref[...])
    zonal, sign = lane_kinds((1, LANES))
    row = fiota((ROWS, LANES), 0)
    weights = []
    for tile in range(2):
        rate = rates[tile]
        step = lambda n: jnp.exp(-rate * (COLS * n))
        decay = jnp.exp(-rate)
        base = tile * 384
        lanes_l = slice(base, base + 128)
        lanes_r = slice(base + 128, base + 256)
        left = part_ref[:, tile * 256:tile * 256 + 128] + (highf * step(yf)) * theirs_ref[:, lanes_l]
        right = part_ref[:, tile * 256 + 128:tile * 256 + 256] + (lowf * step(3.0 - yf)) * theirs_ref[:, lanes_r]
        whole = ((highf + lowf * step(4.0)) * mine_ref[:, lanes_l]
                 + (lowf + highf * step(4.0)) * theirs_ref[:, lanes_l])
        end = step(7.0 - lonf)
        weight_l = jnp.exp(-rate * (ROWS - 1 - row))
        weight_r = jnp.exp(-rate * row)
        carry_l = left
        carry_r = right - (end * decay) * whole
        if tile == 0:
            v0 = lowf * mine_ref[:, 256:384] + highf * theirs_ref[:, 256:384]
            vn = highf * mine_ref[:, 256:384] + lowf * theirs_ref[:, 256:384]
            gain = 0.5 * (1.0 - decay * decay) / decay
            initial = -0.5 * (v0 + vn / decay)
            zonal_l = step(lonf) * initial - gain * left + 0.5 * edge_ref[:, 0:128]
            zonal_r = (gain * right - 0.5 * edge_ref[:, 128:256]
                       + end * (gain * v0 - decay * (step(8.0) * initial - gain * whole)))
            carry_l = sign * jnp.where(zonal, zonal_l, carry_l)
            carry_r = sign * jnp.where(zonal, zonal_r, carry_r)
            start = jnp.where(top & (row == 0.0), 0.5 * jnp.exp(-rate * ROWS), 0.0)
            weight_l = jnp.where(zonal, weight_l, -gain * weight_l - start)
            weight_r = jnp.where(zonal, weight_r, gain * weight_r)
        carry_ref[:, tile * 256:tile * 256 + 128] = carry_l
        carry_ref[:, tile * 256 + 128:tile * 256 + 256] = carry_r
        fold = lambda w, c: jnp.sum(w * c, axis=0, keepdims=True)
        weights.append(((fold(weight_l, carry_l), fold(weight_l, carry_r)),
                        (fold(weight_r, carry_l), fold(weight_r, carry_r))))
    shape = (HALF_ROWS, LANES)
    lane, lane_scale, _, wind_field, rest_field = lane_fields(shape)
    out_row = iota(shape, 0)
    scale = jnp.where(out_row < HALF, 0, jnp.where(out_row < 2 * HALF, 1, 2))
    core = lat & 1
    column = fiota((HALF_ROWS, COLS), 1)
    for ref, half in ((send_ref, 1 - core), (keep_ref, core)):
        field = out_row - scale * HALF + half * HALF
        same = lane_scale == scale
        wind = same & (wind_field == field)
        rest = same & (rest_field == field)
        lengths = len_ref[pl.ds(pl.multiple_of(half * HALF, 8), HALF), :]
        rate = 1.0 / lengths
        rate = jnp.concatenate([rate[:, s:s + 1] for s in range(SCALES)], axis=0)
        fall = jnp.exp(-rate * (column + 1.0))
        rise = jnp.exp(-rate * (COLS - column))
        for side in range(2):
            pick = lambda k: jnp.sum(
                jnp.where(wind, weights[0][side][k], 0.0) + jnp.where(rest, weights[1][side][k], 0.0),
                axis=1, keepdims=True)
            rows = slice(side * HALF_ROWS, (side + 1) * HALF_ROWS)
            ref[rows, :] = local_ref[half, rows, :] + pick(0) * fall + pick(1) * rise


def column_sums(where, lengths, part, mine, theirs, edge, local):
    half = jax.ShapeDtypeStruct((2 * HALF_ROWS, COLS), F32)
    return pl.pallas_call(
        column_sums_kernel,
        in_specs=[SMEM] + [VMEM] * 6,
        out_specs=[VMEM] * 3,
        out_shape=[jax.ShapeDtypeStruct((ROWS, 512), F32), half, half],
        compiler_params=params(),
        name="column_sums",
    )(where, lengths, part, mine, theirs, edge, local)


def half_rates(where_ref, len_ref):
    core = where_ref[0] & 1
    rate = 1.0 / len_ref[pl.ds(pl.multiple_of(core * HALF, 8), HALF), :]
    return jnp.concatenate([rate[:, s:s + 1] for s in range(SCALES)], axis=0)


LEFT = slice(0, HALF_ROWS)
RIGHT = slice(HALF_ROWS, 2 * HALF_ROWS)


def chip_merge_kernel(where_ref, len_ref, keep_ref, got_ref, chip_ref):
    rate = half_rates(where_ref, len_ref)
    odd = (where_ref[0] & 1) == 1
    step = jnp.exp(-rate * ROWS)
    one = jnp.ones_like(step)
    mine_l, got_l = jnp.where(odd, one, step), jnp.where(odd, step, one)
    chip_ref[LEFT, :] = mine_l * keep_ref[LEFT, :] + got_l * got_ref[LEFT, :]
    chip_ref[RIGHT, :] = got_l * keep_ref[RIGHT, :] + mine_l * got_ref[RIGHT, :]


def chip_merge(where, lengths, keep, got):
    return pl.pallas_call(
        chip_merge_kernel,
        in_specs=[SMEM] + [VMEM] * 3,
        out_specs=VMEM,
        out_shape=jax.ShapeDtypeStruct((2 * HALF_ROWS, COLS), F32),
        compiler_params=params(),
        name="chip_merge",
    )(where, lengths, keep, got)


def quad_merge_kernel(where_ref, len_ref, chip_ref, pair_ref, left_ref, s1_ref, s2_ref, s3_ref):
    rate = half_rates(where_ref, len_ref)
    z = where_ref[0] >> 2
    zf = z.astype(F32)
    odd = ((where_ref[0] >> 1) & 1) == 1
    step = jnp.exp(-rate * (2 * ROWS))
    one = jnp.ones_like(step)
    mine_l, got_l = jnp.where(odd, one, step), jnp.where(odd, step, one)
    left = mine_l * chip_ref[LEFT, :] + got_l * pair_ref[LEFT, :]
    right = got_l * chip_ref[RIGHT, :] + mine_l * pair_ref[RIGHT, :]
    image = jnp.exp(-rate * (1.0 + 4 * ROWS * jnp.maximum(7.0 - 2.0 * zf, 1.0)))
    back = right - image * left
    left_ref[...] = left
    for d, ref in ((1, s1_ref), (2, s2_ref), (3, s3_ref)):
        ref[...] = jnp.where(z + d <= 3, left, back)


def quad_merge(where, lengths, chip, pair):
    one = jax.ShapeDtypeStruct((HALF_ROWS, COLS), F32)
    return pl.pallas_call(
        quad_merge_kernel,
        in_specs=[SMEM] + [VMEM] * 3,
        out_specs=[VMEM] * 4,
        out_shape=[one] * 4,
        compiler_params=params(),
        name="quad_merge",
    )(where, lengths, chip, pair)


def lat_carry_kernel(where_ref, len_ref, keep_ref, got_ref, pair_ref, left_ref, g1_ref, g2_ref, g3_ref,
                     own_ref, send_ref):
    rate = half_rates(where_ref, len_ref)
    lat = where_ref[0]
    z = lat >> 2
    zf = z.astype(F32)
    quad = lambda n: jnp.exp(-rate * (4 * ROWS * n))
    left = jnp.zeros((HALF_ROWS, COLS), F32)
    right = jnp.zeros((HALF_ROWS, COLS), F32)
    whole = quad(3.0 - zf) * left_ref[...]
    for d, ref in ((1, g1_ref), (2, g2_ref), (3, g3_ref)):
        below = z >= d
        g = ref[...]
        left = left + jnp.where(below, quad(d - 1.0), 0.0) * g
        right = right + jnp.where(below, 0.0, quad(3.0 - d)) * g
        whole = whole + jnp.where(below, quad(3.0 - zf + d), 0.0) * g
    right = right - (quad(3.0 - zf) * jnp.exp(-rate)) * whole
    odd_chip = ((lat >> 1) & 1) == 1
    pair = jnp.exp(-rate * (2 * ROWS))
    zero = jnp.zeros_like(pair)
    one = jnp.ones_like(pair)
    left = jnp.where(odd_chip, pair, one) * left + jnp.where(odd_chip, one, zero) * pair_ref[LEFT, :]
    right = jnp.where(odd_chip, one, pair) * right + jnp.where(odd_chip, zero, one) * pair_ref[RIGHT, :]
    odd = (lat & 1) == 1
    device = jnp.exp(-rate * ROWS)
    low_left = jnp.where(odd, got_ref[LEFT, :], keep_ref[LEFT, :])
    high_right = jnp.where(odd, keep_ref[RIGHT, :], got_ref[RIGHT, :])
    high_l = low_left + device * left
    low_r = high_right + device * right
    own_ref[LEFT, :] = jnp.where(odd, high_l, left)
    own_ref[RIGHT, :] = jnp.where(odd, right, low_r)
    send_ref[LEFT, :] = jnp.where(odd, left, high_l)
    send_ref[RIGHT, :] = jnp.where(odd, low_r, right)


def lat_carry(where, lengths, keep, got, pair, left, gs):
    half = jax.ShapeDtypeStruct((2 * HALF_ROWS, COLS), F32)
    return pl.pallas_call(
        lat_carry_kernel,
        in_specs=[SMEM] + [VMEM] * 8,
        out_specs=[VMEM] * 2,
        out_shape=[half, half],
        compiler_params=params(),
        name="lat_carry",
    )(where, lengths, keep, got, pair, left, *gs)


def scale_weights(lengths, weights):
    rate = 1.0 / lengths
    decay = jnp.exp(-rate)
    leak = 1.0 - decay
    cube = (1.0 + decay) * (1.0 + decay) * (1.0 + decay)
    coefficient = weights * cube / (leak * (1.0 + decay * decay))
    kappa = leak / (1.0 + decay)
    return rate, coefficient * kappa * kappa


def local_filter_kernel(where_ref, len_ref, weight_ref, carry_ref, x1_ref, x2_ref, out_ref):
    group = pl.program_id(0)
    top = where_ref[0] == 0
    shape = (SCALES * ROWS, LANES)
    r48 = iota(shape, 0)
    scale_of = jnp.where(r48 < ROWS, 0, jnp.where(r48 < 2 * ROWS, 1, 2))
    row = (r48 - scale_of * ROWS).astype(F32)
    lane = iota(shape, 1)
    source = jnp.where(lane >= ROWS, lane - ROWS, lane).astype(F32)
    used = lane < 2 * ROWS
    gap = jnp.abs(row - source)
    gap_low = jnp.abs(source - 1.0 - row)
    gap_high = jnp.abs(source + 1.0 - row)
    first = source == 0.0
    spread = jnp.abs(fiota((LANES, LANES), 0) - fiota((LANES, LANES), 1))
    column = fiota((1, LANES), 1)
    small_lane = iota((ROWS, LANES), 1)
    tag = small_lane & 31
    zeros = jnp.zeros((32, COLS + LANES), BF16)
    corner = jnp.zeros((LANES, LANES), BF16)

    def carry_tile(tile, virtual):
        left = carry_ref[:, tile * 256:tile * 256 + 128]
        right = carry_ref[:, tile * 256 + 128:tile * 256 + 256]
        left = pltpu.roll(left, (LANES - virtual) & (LANES - 1), 1)
        right = pltpu.roll(right, (LANES + 1 - virtual) & (LANES - 1), 1)
        return jnp.where(tag == 0, left, jnp.where(tag == 1, right, 0.0))

    def column_pass(matrix, x, carry):
        mh, ml = split(jnp.where(used, matrix, 0.0))
        lhs = jnp.concatenate([mh, ml[:, :ROWS]], axis=1)
        xh, xl = split(jnp.concatenate([x, carry], axis=1))
        rhs = jnp.concatenate([xh, xl, zeros, xh], axis=0)
        return mm(lhs, rhs)

    def one(i, wind):
        rate, weight = scale_weights(len_ref[pl.ds(i, 1), :], weight_ref[pl.ds(i, 1), :])
        by_row = lambda v: jnp.concatenate([jnp.broadcast_to(v[:, s:s + 1], (ROWS, 1)) for s in range(SCALES)], axis=0)
        rate_row, weight_row = by_row(rate), by_row(weight)
        plain = weight_row * jnp.exp(-rate_row * gap)
        if wind:
            slope = jnp.exp(-rate_row * gap_low) - jnp.exp(-rate_row * gap_high)
            slope = slope - jnp.where(top & first, jnp.exp(-rate_row * (row + 1.0)), 0.0)
            slope = (0.5 * weight_row) * slope
            second_sign = jnp.where(group == 0, 1.0, -1.0)
            meridional = jnp.where(group == 0, i, 24 + i)
            zonal = jnp.where(group == 0, 8 + i, 16 + i)
            w = column_pass(plain, -zonal_difference(x2_ref[i]), carry_tile(0, zonal))
            w = w + column_pass(slope, second_sign * x1_ref[i], carry_tile(0, meridional))
        else:
            w = column_pass(plain, x1_ref[i], carry_tile(1, (group - 2) * GROUP + i))
        parts = [None] * PARTS
        for s in range(SCALES):
            rate_s = rate[:, s:s + 1]
            rows = slice(s * ROWS, (s + 1) * ROWS)
            stack = jnp.concatenate([w[rows, b * LANES:(b + 1) * LANES] for b in range(PARTS)], axis=0)
            wh, wl = split(stack)
            th, tl = split(jnp.exp(-rate_s * spread))
            lhs = jnp.concatenate([wh, wl], axis=1)
            rhs = jnp.concatenate([jnp.concatenate([th, tl], axis=1), jnp.concatenate([th, corner], axis=1)], axis=0)
            out = mm(lhs, rhs)
            out = out[:, :LANES] + out[:, LANES:]
            left, right = out[:, LANES - 1:LANES], out[:, 0:1]
            carry = w[rows, COLS:]
            c0l, c2r = carry[:, 32 * s:32 * s + 1], carry[:, 32 * s + 1:32 * s + 2]
            jump = jnp.exp(-rate_s * LANES)
            c1l = left[0:ROWS] + jump * c0l
            c2l = left[ROWS:2 * ROWS] + jump * c1l
            c1r = right[2 * ROWS:] + jump * c2r
            c0r = right[ROWS:2 * ROWS] + jump * c1r
            fall = jnp.exp(-rate_s * (column + 1.0))
            rise = jnp.exp(-rate_s * (LANES - column))
            for b, (cl, cr) in enumerate(((c0l, c0r), (c1l, c1r), (c2l, c2r))):
                term = out[b * ROWS:(b + 1) * ROWS] + cl * fall + cr * rise
                parts[b] = term if s == 0 else parts[b] + term
        for b in range(PARTS):
            out_ref[i, :, b * LANES:(b + 1) * LANES] = parts[b]

    @pl.when(group < 2)
    def _():
        for i in range(GROUP):
            one(i, True)

    @pl.when(group >= 2)
    def _():
        for i in range(GROUP):
            one(i, False)


def local_filter(where, lengths, weights, carry, x):
    return pl.pallas_call(
        local_filter_kernel,
        grid=(GROUPS,),
        in_specs=[SMEM, pl.BlockSpec((GROUP, SCALES), lambda g: (g, 0)),
                  pl.BlockSpec((GROUP, SCALES), lambda g: (g, 0)),
                  pl.BlockSpec((ROWS, 512), lambda g: (0, 0)),
                  pl.BlockSpec((GROUP, ROWS, COLS), lambda g: (g, 0, 0)),
                  pl.BlockSpec((GROUP, ROWS, COLS), lambda g: (other_wind(g), 0, 0))],
        out_specs=pl.BlockSpec((GROUP, ROWS, COLS), lambda g: (g, 0, 0)),
        out_shape=jax.ShapeDtypeStruct((FIELDS, ROWS, COLS), F32),
        compiler_params=params(),
        name="local_filter",
    )(where, lengths, weights, carry, x, x)


def finish_kernel(where_ref, len_ref, weight_ref, z_ref, own_ref, got_ref, out_ref):
    group = pl.program_id(0)
    core = where_ref[0] & 1
    mine = jnp.where(group < 3, 0, 1) == core
    rate, weight = scale_weights(len_ref[...], weight_ref[...])
    row = fiota((ROWS, 1), 0)
    carry = jnp.where(mine, own_ref[...], got_ref[...])
    for i in range(GROUP):
        total = z_ref[i]
        for s in range(SCALES):
            r, w = rate[i:i + 1, s:s + 1], weight[i:i + 1, s:s + 1]
            up = w * jnp.exp(-r * (row + 1.0))
            down = w * jnp.exp(-r * (ROWS - row))
            total = total + up * carry[0, s, 0, i:i + 1] + down * carry[1, s, 0, i:i + 1]
        out_ref[i] = total


def finish(where, lengths, weights, z, own, got):
    shaped = lambda t: t.reshape(2, SCALES, 3, GROUP, COLS)
    carry_spec = pl.BlockSpec((2, SCALES, 1, GROUP, COLS), lambda g: (0, 0, g % 3, 0, 0))
    return pl.pallas_call(
        finish_kernel,
        grid=(GROUPS,),
        in_specs=[SMEM, pl.BlockSpec((GROUP, SCALES), lambda g: (g, 0)),
                  pl.BlockSpec((GROUP, SCALES), lambda g: (g, 0)),
                  pl.BlockSpec((GROUP, ROWS, COLS), lambda g: (g, 0, 0)), carry_spec, carry_spec],
        out_specs=pl.BlockSpec((GROUP, ROWS, COLS), lambda g: (g, 0, 0)),
        out_shape=jax.ShapeDtypeStruct((FIELDS, ROWS, COLS), F32),
        compiler_params=params(),
        name="finish",
    )(where, lengths, weights, z, shaped(own), shaped(got))


def shards(x, lengths, weights):
    where = jnp.stack([lax.axis_index("lat"), lax.axis_index("lon")]).astype(jnp.int32)
    sums, edge = row_sums(where, lengths, x)
    got = []
    for d in (1, 2, 3):
        perm = [(h * 4 + i, h * 4 + (i + d) % 4) for h in range(2) for i in range(4)]
        got.append(lax.ppermute(sums, "lon", perm))
    local = local_sums(where, lengths, x)
    part, mine = lon_merge(where, lengths, sums, got)
    theirs = lax.ppermute(mine, "lon", [(i, i ^ 4) for i in range(NLON)])
    carry, keep, send = column_sums(where, lengths, part, mine, theirs, edge, local)
    core_pairs = [(i, i ^ 1) for i in range(NLAT)]
    got_core = lax.ppermute(send, "lat", core_pairs)
    chip = chip_merge(where, lengths, keep, got_core)
    pair = lax.ppermute(chip, "lat", [(i, i ^ 2) for i in range(NLAT)])
    left, *sends = quad_merge(where, lengths, chip, pair)
    gs = [lax.ppermute(t, "lat", [(i, (i + 4 * d) % NLAT) for i in range(NLAT)]) for d, t in zip((1, 2, 3), sends)]
    z = local_filter(where, lengths, weights, carry, x)
    own, other = lat_carry(where, lengths, keep, got_core, pair, left, gs)
    got_carry = lax.ppermute(other, "lat", core_pairs)
    return finish(where, lengths, weights, z, own, got_carry)


def solution(mesh):
    in_specs = (P(None, "lat", "lon"), P(), P())
    out_specs = P(None, "lat", "lon")
    return jax.shard_map(shards, mesh=mesh, in_specs=in_specs, out_specs=out_specs, check_vma=False)
```

time: 842 us -> 127 us (0.15); the launches traced: 831 us -> 126 us
  local copies, waits for them, and re-layouts: 256 us -> 4.95 us
  other arithmetic: 169 us -> 0.07 us
  waiting for transfers between devices: 174 us -> 19.3 us
  blocking collectives: 124 us -> 0 us
  matrix products: 85 us -> 0 us
  Pallas kernels: 0 us -> 84.9 us
    all_to_all x2 -> x0, waiting for transfers between devices: 159 us -> none  [the longest x1 118 us: shards(): lax.all_to_all(filtered, 'lat', split_axis=3, concat_axis=2, tiled=True)]
    all_to_all x2 -> x0, other arithmetic: 145 us -> none  [the longest x1 114 us: shards(): lax.all_to_all(filtered, 'lat', split_axis=3, concat_axis=2, tiled=True)]
    all_to_all x2 -> x0, blocking collectives: 124 us -> none  [the longest x1 77.3 us: shards(): lax.all_to_all(summed, 'lat', split_axis=1, concat_axis=2, tiled=True)]
    unnamed x24 -> x12, local copies, waits for them, and re-layouts: 112 us -> 4.95 us
    dot_general x24 -> x0, matrix products: 85 us -> none  [the longest x3 29.1 us: filter_mid(): jnp.einsum('fij,fkja->fkia', lower_matrix, blocks, precision=precise_mode)]
    pallas_call x0 -> x9, Pallas kernels: none -> 84.9 us  [the longest x1 62.7 us: local_filter(): pl.pallas_call(local_filter_kernel, grid=(GROUPS,), in_specs=[SMEM, pl.Bl...]
    all_to_all x5 -> x0, local copies, waits for them, and re-layouts: 54.4 us -> none  [the longest x2 29.6 us: shards(): lax.all_to_all(filtered, 'lat', split_axis=3, concat_axis=2, tiled=True)]
    another operation x4 -> x0, local copies, waits for them, and re-layouts: 37.8 us -> none  [shards(): jnp.stack([filter_last(row_lines, group_rates[:, scale_index], BLOCK) for...]
  transfers between devices with their start and end apart: 6 -> 10, of which waited for: 4 -> 8; matrix products, arithmetic and copies ran while one was open for 0% -> 0% of each run, Pallas kernels for 0% -> 57%
where the time goes in v1:
time: 127 us; the launch traced here: 126 us
  Pallas kernels  84.9 us (67%)
  waiting for transfers between devices  19.3 us (15%)
  starting transfers between devices  17 us (13%)
  local copies, waits for them, and re-layouts  4.95 us (4%)
    pallas_call x1, Pallas kernels, local_filter(): pl.pallas_call(local_filter_kernel, grid=(GROUPS,), in_specs=[SMEM, pl.Bl...  62.7 us
    pallas_call x1, Pallas kernels, local_sums(): pl.pallas_call(local_sums_kernel, grid=(GROUPS,), in_specs=[SMEM, pl.Bloc...  9 us
    ppermute x3, waiting for transfers between devices, shards(): got.append(lax.ppermute(sums, 'lon', perm))  8.14 us
    ppermute x1, waiting for transfers between devices, shards(): pair = lax.ppermute(chip, 'lat', [(i, i ^ 2) for i in range(NLAT)])  6.33 us
    ppermute x3, starting transfers between devices, shards(): lax.ppermute(t, 'lat', [(i, (i + 4 * d) % NLAT) for i in range(NLAT)])  5.74 us
    pallas_call x1, Pallas kernels, finish(): pl.pallas_call(finish_kernel, grid=(GROUPS,), in_specs=[SMEM, pl.BlockSpe...  5 us
    unnamed x12, local copies, waits for them, and re-layouts  4.95 us
    ppermute x3, starting transfers between devices, shards(): got.append(lax.ppermute(sums, 'lon', perm))  4.67 us
  transfers between devices with their start and end apart: 10, of which 8 were waited for; matrix products, arithmetic and copies ran while one was open for 0% of the time, Pallas kernels for 57%

profile of v1, /device:TPU:1, one launch (start us, length us, event | category | flops | bytes accessed | tf_op | source)
XLA Modules:
  0.0 126.3 jit_solution(252452888585471637)
XLA Ops:
  0.0 1.4 %copy.13.len_ref = f32[48,3]{1,0:T(8,128)} copy(f32[48,3]{0,1:T(4,128)} %param.4) | data formatting | bytes 1152 | tf_op args[1]
  1.4 0.1 pad_add_fusion.where_ref
  1.4 0.0 copy-start
  1.5 2.0 %copy-done = f32[48,48,384]{2,1,0:T(8,128)S(1)} copy-done((f32[48,48,384]{2,1,0:T(8,128)S(1)}, f32[48,48,384]{2,1,0:T(8,128)}, u32[]{:S(2)}) %copy-start) | copy-done | bytes 3538968
  3.5 0.0 copy-start.2
  3.5 0.7 copy-done.2
  4.2 0.0 copy-start.1
  4.2 4.3 %row_sums.1 = (f32[48,640]{1,0:T(8,128)S(1)}, f32[48,256]{1,0:T(8,128)S(1)}) custom-call(s32[2]{0:T(128)S(1)} %pad_add_fusion.where_ref, f32[48,3]{1,0:T(8,128)S(1)} %copy-done.2, f32[48,48,384]{2,1,0:T(8,128)S(1)} %copy-done), custom_call_target="tpu_custom_call" | custom-call | tf_op jit(solution)/shard_map/row_sums/pallas_call | solution.py:135
  8.5 3.6 %collective-permute-start.2 = (f32[48,640]{1,0:T(8,128)S(1)}, f32[48,640]{1,0:T(8,128)S(1)}, u32[]{:S(2)}, u32[]{:S(2)}) collective-permute-start(f32[48,640]{1,0:T(8,128)S(1)} %get-tuple-element.18.own_ref), channel_id=1, source_target_pairs={{0,3},{1,0},{2,1},{3,2},{4,7},{5,4},{6,5},{7,6},{8,11},{9,8},{10,9... | collective-permute-start | bytes 368648 | tf_op jit(solution)/shard_map/ppermute | solution.py:617
  12.1 0.3 collective-permute-start.1
  12.5 0.7 collective-permute-start
  13.1 3.6 %collective-permute-done.2.g3_ref = f32[48,640]{1,0:T(8,128)S(1)} collective-permute-done((f32[48,640]{1,0:T(8,128)S(1)}, f32[48,640]{1,0:T(8,128)S(1)}, u32[]{:S(2)}, u32[]{:S(2)}) %collective-permute-start.2) | collective-permute-done | bytes 122912 | tf_op jit(solution)/shard_map/ppermute | solution.py:617
  16.7 0.7 collective-permute-done.1.g2_ref
  17.4 3.8 %collective-permute-done.g1_ref = f32[48,640]{1,0:T(8,128)S(1)} collective-permute-done((f32[48,640]{1,0:T(8,128)S(1)}, f32[48,640]{1,0:T(8,128)S(1)}, u32[]{:S(2)}, u32[]{:S(2)}) %collective-permute-start) | collective-permute-done | bytes 122912 | tf_op jit(solution)/shard_map/ppermute | solution.py:617
  21.3 0.7 lon_merge.1
  22.0 0.0 copy-start.4
  22.0 2.8 %collective-permute-start.3 = (f32[48,640]{1,0:T(8,128)S(1)}, f32[48,640]{1,0:T(8,128)S(1)}, u32[]{:S(2)}, u32[]{:S(2)}) collective-permute-start(f32[48,640]{1,0:T(8,128)S(1)} %get-tuple-element.20.mine_ref), channel_id=1, source_target_pairs={{0,4},{1,5},{2,6},{3,7},{4,0},{5,1},{6,2},{7,3},{8,12},{9,13},{10,... | collective-permute-start | bytes 368648 | tf_op jit(solution)/shard_map/ppermute | solution.py:620
  24.8 0.0 copy-done.1
  24.8 9.0 %local_sums.1 = f32[2,2,3,3,8,384]{5,4,3,2,1,0:T(8,128)S(1)} custom-call(s32[2]{0:T(128)S(1)} %pad_add_fusion.where_ref, f32[48,3]{1,0:T(8,128)S(1)} %copy-done.2, f32[48,48,384]{2,1,0:T(8,128)S(1)} %copy-done.1, f32[48,48,384]{2,1,0:T(8,128)S(1)} %copy-done.1), custom_call_target="tpu_custom_call" | custom-call | tf_op jit(solution)/shard_map/local_sums/pallas_call | solution.py:216
  33.8 0.0 collective-permute-done.3.theirs_ref
  33.9 0.9 column_sums.1
  34.8 1.1 collective-permute-start.4
  35.9 1.1 collective-permute-done.4.got_ref
  37.0 0.7 chip_merge.1.chip_ref
  37.7 0.4 collective-permute-start.5
  38.1 6.3 %collective-permute-done.5.pair_ref = f32[144,384]{1,0:T(8,128)S(1)} collective-permute-done((f32[144,384]{1,0:T(8,128)S(1)}, f32[144,384]{1,0:T(8,128)S(1)}, u32[]{:S(2)}, u32[]{:S(2)}) %collective-permute-start.5) | collective-permute-done | bytes 221216 | tf_op jit(solution)/shard_map/ppermute | solution.py:625
  44.4 0.7 quad_merge.1
  45.1 1.7 %collective-permute-start.6 = (f32[72,384]{1,0:T(8,128)S(1)}, f32[72,384]{1,0:T(8,128)S(1)}, u32[]{:S(2)}, u32[]{:S(2)}) collective-permute-start(f32[72,384]{1,0:T(8,128)S(1)} %get-tuple-element.26), channel_id=1, source_target_pairs={{0,32},{8,40},{16,48},{24,56},{32,64},{40,72},{48,80},{56,88},{64,... | collective-permute-start | bytes 331784 | tf_op jit(solution)/shard_map/ppermute | solution.py:627
  46.8 3.3 %collective-permute-start.7 = (f32[72,384]{1,0:T(8,128)S(1)}, f32[72,384]{1,0:T(8,128)S(1)}, u32[]{:S(2)}, u32[]{:S(2)}) collective-permute-start(f32[72,384]{1,0:T(8,128)S(1)} %get-tuple-element.27), channel_id=1, source_target_pairs={{0,64},{8,72},{16,80},{24,88},{32,96},{40,104},{48,112},{56,120},{... | collective-permute-start | bytes 331784 | tf_op jit(solution)/shard_map/ppermute | solution.py:627
  50.2 0.7 collective-permute-start.8
  50.9 0.2 collective-permute-done.6.g1_ref
  51.1 3.0 %collective-permute-done.7.g2_ref = f32[72,384]{1,0:T(8,128)S(1)} collective-permute-done((f32[72,384]{1,0:T(8,128)S(1)}, f32[72,384]{1,0:T(8,128)S(1)}, u32[]{:S(2)}, u32[]{:S(2)}) %collective-permute-start.7) | collective-permute-done | bytes 110624 | tf_op jit(solution)/shard_map/ppermute | solution.py:627
  54.1 0.5 collective-permute-done.8.g3_ref
  54.6 0.9 lat_carry.1
  55.5 2.3 %collective-permute-start.9 = (f32[144,384]{1,0:T(8,128)S(1)}, f32[144,384]{1,0:T(8,128)S(1)}, u32[]{:S(2)}, u32[]{:S(2)}) collective-permute-start(f32[144,384]{1,0:T(8,128)S(1)} %get-tuple-element.30), channel_id=1, source_target_pairs={{0,8},{8,0},{16,24},{24,16},{32,40},{40,32},{48,56},{56,48},{64,72... | collective-permute-start | bytes 663560 | tf_op jit(solution)/shard_map/ppermute | solution.py:630
  57.8 0.0 copy-done.4
  57.8 0.1 copy.14.weight_ref
  57.9 0.0 copy-start.3
  57.9 0.7 copy-done.3
  58.6 62.7 %local_filter.1.z_ref = f32[48,48,384]{2,1,0:T(8,128)S(1)} custom-call(s32[2]{0:T(128)S(1)} %pad_add_fusion.where_ref, f32[48,3]{1,0:T(8,128)S(1)} %copy-done.3, f32[48,3]{1,0:T(8,128)S(1)} %copy.14.weight_ref, f32[48,512]{1,0:T(8,128)S(1)} %get-tuple-element.22.carry_ref, f32[48,48,384]{2,1,0:T(8,128)} %x2_ref.3, f32[48,48,384]{2,1,0:T(8,128)} %x2_ref.3), custom_call_target="tpu_custom_call" | custom-call | tf_op jit(solution)/shard_map/local_filter/pallas_call | solution.py:563
  121.3 0.0 collective-permute-done.9
  121.3 5.0 %finish.1 = f32[48,48,384]{2,1,0:T(8,128)} custom-call(s32[2]{0:T(128)S(1)} %pad_add_fusion.where_ref, f32[48,3]{1,0:T(8,128)S(1)} %copy-done.3, f32[48,3]{1,0:T(8,128)S(1)} %copy.14.weight_ref, f32[48,48,384]{2,1,0:T(8,128)S(1)} %local_filter.1.z_ref, f32[2,3,3,8,384]{4,3,2,1,0:T(8,128)S(1)} %bitcast.6, f32[2,3,3,8,384]{4,3,2,1,0:T(8,128)S(1)} %bitcast.7), custom_call_target="tpu_custom_call" | custom-call | tf_op jit(solution)/shard_map/finish/pallas_call | solution.py:598
Async XLA Ops:
  1.4 2.0 %copy-start = (f32[48,48,384]{2,1,0:T(8,128)S(1)}, f32[48,48,384]{2,1,0:T(8,128)}, u32[]{:S(2)}) copy-start(f32[48,48,384]{2,1,0:T(8,128)} %x2_ref.3) | copy-start | bytes 10616836
  3.5 0.7 copy-start.2
  4.2 20.6 %copy-start.1 = (f32[48,48,384]{2,1,0:T(8,128)S(1)}, f32[48,48,384]{2,1,0:T(8,128)}, u32[]{:S(2)}) copy-start(f32[48,48,384]{2,1,0:T(8,128)} %x2_ref.3) | copy-start | bytes 10616836
  8.5 8.2 %collective-permute-start.2 = (f32[48,640]{1,0:T(8,128)S(1)}, f32[48,640]{1,0:T(8,128)S(1)}, u32[]{:S(2)}, u32[]{:S(2)}) collective-permute-start(f32[48,640]{1,0:T(8,128)S(1)} %get-tuple-element.18.own_ref), channel_id=1, source_target_pairs={{0,3},{1,0},{2,1},{3,2},{4,7},{5,4},{6,5},{7,6},{8,11},{9,8},{10,9... | collective-permute-start | bytes 368648 | tf_op jit(solution)/shard_map/ppermute | solution.py:617
  12.1 5.3 %collective-permute-start.1 = (f32[48,640]{1,0:T(8,128)S(1)}, f32[48,640]{1,0:T(8,128)S(1)}, u32[]{:S(2)}, u32[]{:S(2)}) collective-permute-start(f32[48,640]{1,0:T(8,128)S(1)} %get-tuple-element.18.own_ref), channel_id=1, source_target_pairs={{0,2},{1,3},{2,0},{3,1},{4,6},{5,7},{6,4},{7,5},{8,10},{9,11},{10,... | collective-permute-start | bytes 368648 | tf_op jit(solution)/shard_map/ppermute | solution.py:617
  12.5 8.8 %collective-permute-start = (f32[48,640]{1,0:T(8,128)S(1)}, f32[48,640]{1,0:T(8,128)S(1)}, u32[]{:S(2)}, u32[]{:S(2)}) collective-permute-start(f32[48,640]{1,0:T(8,128)S(1)} %get-tuple-element.18.own_ref), channel_id=1, source_target_pairs={{0,1},{1,2},{2,3},{3,0},{4,5},{5,6},{6,7},{7,4},{8,9},{9,10},{10,1... | collective-permute-start | bytes 368648 | tf_op jit(solution)/shard_map/ppermute | solution.py:617
  22.0 35.8 %copy-start.4 = (f32[48,3]{0,1:T(4,128)S(1)}, f32[48,3]{0,1:T(4,128)}, u32[]{:S(2)}) copy-start(f32[48,3]{0,1:T(4,128)} %param.5) | copy-start | bytes 1732
  22.0 11.8 %collective-permute-start.3 = (f32[48,640]{1,0:T(8,128)S(1)}, f32[48,640]{1,0:T(8,128)S(1)}, u32[]{:S(2)}, u32[]{:S(2)}) collective-permute-start(f32[48,640]{1,0:T(8,128)S(1)} %get-tuple-element.20.mine_ref), channel_id=1, source_target_pairs={{0,4},{1,5},{2,6},{3,7},{4,0},{5,1},{6,2},{7,3},{8,12},{9,13},{10,... | collective-permute-start | bytes 368648 | tf_op jit(solution)/shard_map/ppermute | solution.py:620
  34.8 2.2 %collective-permute-start.4 = (f32[144,384]{1,0:T(8,128)S(1)}, f32[144,384]{1,0:T(8,128)S(1)}, u32[]{:S(2)}, u32[]{:S(2)}) collective-permute-start(f32[144,384]{1,0:T(8,128)S(1)} %get-tuple-element.24), channel_id=1, source_target_pairs={{0,8},{8,0},{16,24},{24,16},{32,40},{40,32},{48,56},{56,48},{64,72... | collective-permute-start | bytes 663560 | tf_op jit(solution)/shard_map/ppermute | solution.py:623
  37.7 6.7 %collective-permute-start.5 = (f32[144,384]{1,0:T(8,128)S(1)}, f32[144,384]{1,0:T(8,128)S(1)}, u32[]{:S(2)}, u32[]{:S(2)}) collective-permute-start(f32[144,384]{1,0:T(8,128)S(1)} %chip_merge.1.chip_ref), channel_id=1, source_target_pairs={{0,16},{8,24},{16,0},{24,8},{32,48},{40,56},{48,32},{56,40},{64,80... | collective-permute-start | bytes 663560 | tf_op jit(solution)/shard_map/ppermute | solution.py:625
  45.1 6.0 %collective-permute-start.6 = (f32[72,384]{1,0:T(8,128)S(1)}, f32[72,384]{1,0:T(8,128)S(1)}, u32[]{:S(2)}, u32[]{:S(2)}) collective-permute-start(f32[72,384]{1,0:T(8,128)S(1)} %get-tuple-element.26), channel_id=1, source_target_pairs={{0,32},{8,40},{16,48},{24,56},{32,64},{40,72},{48,80},{56,88},{64,... | collective-permute-start | bytes 331784 | tf_op jit(solution)/shard_map/ppermute | solution.py:627
  46.8 7.3 %collective-permute-start.7 = (f32[72,384]{1,0:T(8,128)S(1)}, f32[72,384]{1,0:T(8,128)S(1)}, u32[]{:S(2)}, u32[]{:S(2)}) collective-permute-start(f32[72,384]{1,0:T(8,128)S(1)} %get-tuple-element.27), channel_id=1, source_target_pairs={{0,64},{8,72},{16,80},{24,88},{32,96},{40,104},{48,112},{56,120},{... | collective-permute-start | bytes 331784 | tf_op jit(solution)/shard_map/ppermute | solution.py:627
  50.2 4.5 %collective-permute-start.8 = (f32[72,384]{1,0:T(8,128)S(1)}, f32[72,384]{1,0:T(8,128)S(1)}, u32[]{:S(2)}, u32[]{:S(2)}) collective-permute-start(f32[72,384]{1,0:T(8,128)S(1)} %get-tuple-element.28), channel_id=1, source_target_pairs={{0,96},{8,104},{16,112},{24,120},{32,0},{40,8},{48,16},{56,24},{64... | collective-permute-start | bytes 331784 | tf_op jit(solution)/shard_map/ppermute | solution.py:627
  55.5 65.8 %collective-permute-start.9 = (f32[144,384]{1,0:T(8,128)S(1)}, f32[144,384]{1,0:T(8,128)S(1)}, u32[]{:S(2)}, u32[]{:S(2)}) collective-permute-start(f32[144,384]{1,0:T(8,128)S(1)} %get-tuple-element.30), channel_id=1, source_target_pairs={{0,8},{8,0},{16,24},{24,16},{32,40},{40,32},{48,56},{56,48},{64,72... | collective-permute-start | bytes 663560 | tf_op jit(solution)/shard_map/ppermute | solution.py:630
  57.9 0.7 copy-start.3

commit v2 on v1

v2 whole, which is shorter than its diff:
```python
import functools

import jax
import jax.numpy as jnp
from jax import lax
from jax.experimental import pallas as pl
from jax.experimental.pallas import tpu as pltpu
from jax.sharding import PartitionSpec as P

LEVELS = 8
SCALES = 3
WINDS = 16
FIELDS = 48
ROWS = 48
COLS = 384
GROUP = 8
GROUPS = FIELDS // GROUP
NLAT = 16
NLON = 8
LANES = 128
PARTS = COLS // LANES
HALF = FIELDS // 2
HALF_ROWS = SCALES * HALF
F32 = jnp.float32
BF16 = jnp.bfloat16

VMEM = pl.BlockSpec(memory_space=pltpu.VMEM)
SMEM = pl.BlockSpec(memory_space=pltpu.SMEM)
BIG = 48 * 1024 * 1024
WHOLE = 61 * 1024 * 1024


def params(**kw):
    return pltpu.CompilerParams(vmem_limit_bytes=BIG, **kw)


def iota(shape, dim):
    return lax.broadcasted_iota(jnp.int32, shape, dim)


def fiota(shape, dim):
    return iota(shape, dim).astype(F32)


def split(value):
    high = value.astype(BF16)
    return high, (value - high.astype(F32)).astype(BF16)


def mm(a, b):
    return jnp.dot(a, b, preferred_element_type=F32)


def lane_fields(shape):
    lane = iota(shape, 1)
    virtual = lane & 31
    wind_field = ((virtual >> 4) << 3) + (virtual & 7)
    return lane, lane >> 5, virtual, wind_field, virtual + WINDS


def exact(a, b, dims):
    return lax.dot_general(a, b, (dims, ((), ())), precision=lax.Precision.HIGHEST, preferred_element_type=F32)


def lane_rates(rate):
    shape = (FIELDS, LANES)
    _, _, _, wind_field, rest_field = lane_fields(shape)
    field = iota(shape, 0)
    lane = iota((1, LANES), 1)

    def pick(which):
        every = exact(rate, jnp.where(field == which, 1.0, 0.0).astype(F32), ((1,), (0,)))
        value = jnp.where(lane < 32, every[0:1], jnp.where(lane < 64, every[1:2], every[2:3]))
        return jnp.where(lane < 96, value, 1.0)

    return pick(wind_field), pick(rest_field)


def scale_weights(rate, weights):
    decay = jnp.exp(-rate)
    leak = 1.0 - decay
    cube = (1.0 + decay) * (1.0 + decay) * (1.0 + decay)
    coefficient = weights * cube / (leak * (1.0 + decay * decay))
    kappa = leak / (1.0 + decay)
    return coefficient * kappa * kappa


def lane_kinds(shape):
    _, _, virtual, _, _ = lane_fields(shape)
    second = virtual >= 16
    north = (virtual & 15) >= 8
    zonal = second != north
    sign = jnp.where(second | north, -1.0, 1.0).astype(F32)
    return zonal, sign


def row_sums_kernel(where_ref, len_ref, weight_ref, x_ref, sums_ref, edge_ref, table_ref, lanes_ref, w_ref, buf_ref, sem):
    lon = where_ref[1]
    copies = [pltpu.make_async_copy(x_ref.at[pl.ds(g * GROUP, GROUP)], buf_ref.at[g], sem.at[g]) for g in range(GROUPS)]
    for copy in copies:
        copy.start()
    rate = 1.0 / len_ref[...]
    pair = lane_rates(rate)
    lanes_ref[...] = jnp.concatenate([pair[0], pair[1], jnp.ones((6, LANES), F32)], axis=0)
    column = fiota((COLS, LANES), 0)
    for tile, rates in enumerate(pair):
        for side, steps in enumerate((COLS - 1 - column, column)):
            high, low = split(jnp.exp(-rates * steps))
            lanes = slice(side * LANES, (side + 1) * LANES)
            w_ref[tile, 0:COLS, lanes] = high
            w_ref[tile, COLS:2 * COLS, lanes] = high
            w_ref[tile, 2 * COLS:, lanes] = low
    both = jnp.concatenate([rate, scale_weights(rate, weight_ref[...]), jnp.ones((2, FIELDS), F32)], axis=0)
    eye = jnp.where(iota((8, LANES), 0) == iota((8, LANES), 1), 1.0, 0.0).astype(F32)
    table_ref[...] = exact(both, eye, ((0,), (0,)))
    virtual = iota((ROWS, LANES), 1) & 31
    zero = jnp.zeros((ROWS, LANES), F32)
    left, right, first, last = zero, zero, zero, zero
    for g in range(GROUPS):
        copies[g].wait()
        x = buf_ref[g].reshape(GROUP * ROWS, COLS)
        xh, xl = split(x)
        res = mm(jnp.concatenate([xh, xl, xh], axis=1), w_ref[0 if g < 2 else 1])
        if g == 2:
            left, right = zero, zero
        for i in range(GROUP):
            rows = slice(i * ROWS, (i + 1) * ROWS)
            mine = (virtual & 15) == g * GROUP + i if g < 2 else virtual == (g - 2) * GROUP + i
            left = jnp.where(mine, res[rows, 0:128], left)
            right = jnp.where(mine, res[rows, 128:256], right)
            if g < 2:
                first = jnp.where(mine, x[rows, 0:1], first)
                last = jnp.where(mine, x[rows, COLS - 1:COLS], last)
        if g == 1:
            sums_ref[:, 0:128] = left
            sums_ref[:, 128:256] = right
            sums_ref[:, 256:384] = jnp.where(lon == 0, first, jnp.where(lon == NLON - 1, last, 0.0))
            edge_ref[:, 0:128] = first
            edge_ref[:, 128:256] = last
    sums_ref[:, 384:512] = left
    sums_ref[:, 512:640] = right


HBM = pl.BlockSpec(memory_space=pltpu.HBM)
ANY = pl.BlockSpec(memory_space=pl.ANY)


def row_sums(where, lengths, weights, x):
    return pl.pallas_call(
        row_sums_kernel,
        in_specs=[SMEM, VMEM, VMEM, HBM],
        out_specs=[VMEM] * 4,
        out_shape=[jax.ShapeDtypeStruct((ROWS, 640), F32), jax.ShapeDtypeStruct((ROWS, 256), F32),
                   jax.ShapeDtypeStruct((FIELDS, LANES), F32), jax.ShapeDtypeStruct((8, LANES), F32)],
        scratch_shapes=[pltpu.VMEM((2, 3 * COLS, 256), BF16), pltpu.VMEM((GROUPS, GROUP, ROWS, COLS), F32),
                        pltpu.SemaphoreType.DMA((GROUPS,))],
        compiler_params=pltpu.CompilerParams(vmem_limit_bytes=WHOLE),
        name="row_sums",
    )(where, lengths, weights, x)


def zonal_difference(x):
    shape = x.shape
    axis = len(shape) - 1
    column = iota(shape, axis)
    ahead = jnp.where(column == COLS - 1, 0.0, pltpu.roll(x, COLS - 1, axis))
    behind = jnp.where(column == 0, 0.0, pltpu.roll(x, 1, axis))
    return 0.5 * (ahead - behind)


def local_sums_kernel(where_ref, table_ref, x_ref, out_ref):
    top = where_ref[0] == 0
    count = 2 * SCALES * GROUP
    shape = (count, LANES)
    out_row = iota(shape, 0)
    member = out_row & 7
    left_side = out_row < SCALES * GROUP
    lane = iota(shape, 1)
    source = jnp.where(lane >= ROWS, lane - ROWS, lane).astype(F32)
    used = lane < 2 * ROWS
    steps = jnp.where(left_side, ROWS - 1 - source, source)
    zeros = jnp.zeros((32, COLS), BF16)

    def weighted(matrix, x, i):
        mh, ml = split(jnp.where(used & (member == i), matrix, 0.0))
        xh, xl = split(x)
        return mm(jnp.concatenate([mh, ml[:, :ROWS]], axis=1), jnp.concatenate([xh, xl, zeros, xh], axis=0))

    def group_sums(group, wind):
        rate = table_ref[group * GROUP:(group + 1) * GROUP, :]
        row_rate = jnp.concatenate([rate[:, s:s + 1] for _ in range(2) for s in range(SCALES)], axis=0)
        wide = jnp.broadcast_to(row_rate, shape)
        plain = jnp.exp(-wide * steps)
        acc = jnp.zeros((count, COLS), F32)
        if wind:
            decay = jnp.exp(-wide)
            gain = 0.5 * (1.0 - decay * decay) / decay
            start = jnp.where(top & (source == 0.0), 0.5 * jnp.exp(-wide * ROWS), 0.0)
            slope = jnp.where(left_side, -gain * plain - start, gain * plain)
            second_sign = jnp.where(group == 0, 1.0, -1.0)
            for i in range(GROUP):
                acc += weighted(plain, -zonal_difference(x_ref[(1 - group) * GROUP + i]), i)
                acc += weighted(slope, second_sign * x_ref[group * GROUP + i], i)
        else:
            for i in range(GROUP):
                acc += weighted(plain, x_ref[group * GROUP + i], i)
        return acc, row_rate

    made = [group_sums(group, group < 2) for group in range(GROUPS)]
    acc = jnp.concatenate([m[0] for m in made], axis=0)
    factor = jnp.concatenate([jnp.broadcast_to(jnp.exp(-m[1]), (count, LANES)) for m in made], axis=0)
    factor = jnp.concatenate([factor] * PARTS, axis=1)
    column = iota(acc.shape, 1)
    forward, backward = acc, acc
    step = 1
    while step < COLS:
        forward = forward + factor * jnp.where(column >= step, pltpu.roll(forward, step, 1), 0.0)
        backward = backward + factor * jnp.where(column < COLS - step, pltpu.roll(backward, COLS - step, 1), 0.0)
        factor = factor * factor
        step *= 2
    acc = forward + backward - acc
    for group in range(GROUPS):
        for side in range(2):
            for s in range(SCALES):
                k = group * count + (side * SCALES + s) * GROUP
                out_ref[group // 3, side, s, group % 3] = acc[k:k + GROUP]


def local_sums(where, table, x):
    out = pl.pallas_call(
        local_sums_kernel,
        in_specs=[SMEM, VMEM, VMEM],
        out_specs=VMEM,
        out_shape=jax.ShapeDtypeStruct((2, 2, SCALES, 3, GROUP, COLS), F32),
        compiler_params=params(),
        name="local_sums",
    )(where, table, x)
    return out.reshape(2, 2 * HALF_ROWS, COLS)


def lon_merge_kernel(where_ref, lanes_ref, own_ref, g1_ref, g2_ref, g3_ref, _, part_ref, mine_ref):
    y = where_ref[1] & 3
    yf = y.astype(F32)
    rates = (lanes_ref[0:1, :], lanes_ref[1:2, :])
    got = (g1_ref, g2_ref, g3_ref)
    for tile in range(2):
        step = lambda n: jnp.exp(-rates[tile] * (COLS * n))
        base = tile * 384
        lanes_l = slice(base, base + 128)
        lanes_r = slice(base + 128, base + 256)
        left_total = step(3.0 - yf) * own_ref[:, lanes_l]
        right_total = step(yf) * own_ref[:, lanes_r]
        left = jnp.zeros((ROWS, LANES), F32)
        right = jnp.zeros((ROWS, LANES), F32)
        for d, ref in zip((1, 2, 3), got):
            below = y >= d
            lg, rg = ref[:, lanes_l], ref[:, lanes_r]
            left = left + jnp.where(below, step(d - 1.0), 0.0) * lg
            right = right + jnp.where(below, 0.0, step(3.0 - d)) * rg
            other = jnp.where(below, yf - d, yf - d + 4.0)
            left_total = left_total + step(3.0 - other) * lg
            right_total = right_total + step(other) * rg
        part_ref[:, tile * 256:tile * 256 + 128] = left
        part_ref[:, tile * 256 + 128:tile * 256 + 256] = right
        mine_ref[:, lanes_l] = left_total
        mine_ref[:, lanes_r] = right_total
    edge = slice(256, 384)
    mine_ref[:, edge] = own_ref[:, edge] + g1_ref[:, edge] + g2_ref[:, edge] + g3_ref[:, edge]


def lon_merge(where, lanes, own, got, after):
    return pl.pallas_call(
        lon_merge_kernel,
        in_specs=[SMEM] + [VMEM] * 5 + [ANY],
        out_specs=[VMEM, VMEM],
        out_shape=[jax.ShapeDtypeStruct((ROWS, 512), F32), jax.ShapeDtypeStruct((ROWS, 640), F32)],
        compiler_params=params(),
        name="lon_merge",
    )(where, lanes, own, *got, after)


def column_sums_kernel(where_ref, table_ref, lanes_ref, part_ref, mine_ref, theirs_ref, edge_ref, local_ref,
                       carry_ref, keep_ref, send_ref):
    lat, lon = where_ref[0], where_ref[1]
    y = lon & 3
    yf = y.astype(F32)
    high = lon >= 4
    highf = jnp.where(high, 1.0, 0.0)
    lowf = 1.0 - highf
    lonf = lon.astype(F32)
    top = lat == 0
    rates = (lanes_ref[0:1, :], lanes_ref[1:2, :])
    zonal, sign = lane_kinds((1, LANES))
    row = fiota((ROWS, LANES), 0)
    weights = []
    for tile in range(2):
        rate = rates[tile]
        step = lambda n: jnp.exp(-rate * (COLS * n))
        decay = jnp.exp(-rate)
        base = tile * 384
        lanes_l = slice(base, base + 128)
        lanes_r = slice(base + 128, base + 256)
        left = part_ref[:, tile * 256:tile * 256 + 128] + (highf * step(yf)) * theirs_ref[:, lanes_l]
        right = part_ref[:, tile * 256 + 128:tile * 256 + 256] + (lowf * step(3.0 - yf)) * theirs_ref[:, lanes_r]
        whole = ((highf + lowf * step(4.0)) * mine_ref[:, lanes_l]
                 + (lowf + highf * step(4.0)) * theirs_ref[:, lanes_l])
        end = step(7.0 - lonf)
        weight_l = jnp.exp(-rate * (ROWS - 1 - row))
        weight_r = jnp.exp(-rate * row)
        carry_l = left
        carry_r = right - (end * decay) * whole
        if tile == 0:
            v0 = lowf * mine_ref[:, 256:384] + highf * theirs_ref[:, 256:384]
            vn = highf * mine_ref[:, 256:384] + lowf * theirs_ref[:, 256:384]
            gain = 0.5 * (1.0 - decay * decay) / decay
            initial = -0.5 * (v0 + vn / decay)
            zonal_l = step(lonf) * initial - gain * left + 0.5 * edge_ref[:, 0:128]
            zonal_r = (gain * right - 0.5 * edge_ref[:, 128:256]
                       + end * (gain * v0 - decay * (step(8.0) * initial - gain * whole)))
            carry_l = sign * jnp.where(zonal, zonal_l, carry_l)
            carry_r = sign * jnp.where(zonal, zonal_r, carry_r)
            start = jnp.where(top & (row == 0.0), 0.5 * jnp.exp(-rate * ROWS), 0.0)
            weight_l = jnp.where(zonal, weight_l, -gain * weight_l - start)
            weight_r = jnp.where(zonal, weight_r, gain * weight_r)
        carry_ref[:, tile * 256:tile * 256 + 128] = carry_l
        carry_ref[:, tile * 256 + 128:tile * 256 + 256] = carry_r
        fold = lambda w, c: jnp.sum(w * c, axis=0, keepdims=True)
        weights.append(((fold(weight_l, carry_l), fold(weight_l, carry_r)),
                        (fold(weight_r, carry_l), fold(weight_r, carry_r))))
    shape = (HALF_ROWS, LANES)
    lane, lane_scale, _, wind_field, rest_field = lane_fields(shape)
    out_row = iota(shape, 0)
    scale = jnp.where(out_row < HALF, 0, jnp.where(out_row < 2 * HALF, 1, 2))
    core = lat & 1
    column = fiota((HALF_ROWS, COLS), 1)
    for ref, half in ((send_ref, 1 - core), (keep_ref, core)):
        field = out_row - scale * HALF + half * HALF
        same = lane_scale == scale
        wind = same & (wind_field == field)
        rest = same & (rest_field == field)
        rate = table_ref[pl.ds(pl.multiple_of(half * HALF, 8), HALF), :]
        rate = jnp.concatenate([rate[:, s:s + 1] for s in range(SCALES)], axis=0)
        fall = jnp.exp(-rate * (column + 1.0))
        rise = jnp.exp(-rate * (COLS - column))
        for side in range(2):
            pick = lambda k: jnp.sum(
                jnp.where(wind, weights[0][side][k], 0.0) + jnp.where(rest, weights[1][side][k], 0.0),
                axis=1, keepdims=True)
            rows = slice(side * HALF_ROWS, (side + 1) * HALF_ROWS)
            ref[rows, :] = local_ref[half, rows, :] + pick(0) * fall + pick(1) * rise


def column_sums(where, table, lanes, part, mine, theirs, edge, local):
    half = jax.ShapeDtypeStruct((2 * HALF_ROWS, COLS), F32)
    return pl.pallas_call(
        column_sums_kernel,
        in_specs=[SMEM] + [VMEM] * 7,
        out_specs=[VMEM] * 3,
        out_shape=[jax.ShapeDtypeStruct((ROWS, 512), F32), half, half],
        compiler_params=params(),
        name="column_sums",
    )(where, table, lanes, part, mine, theirs, edge, local)


def half_rates(where_ref, table_ref):
    core = where_ref[0] & 1
    rate = table_ref[pl.ds(pl.multiple_of(core * HALF, 8), HALF), :]
    return jnp.concatenate([rate[:, s:s + 1] for s in range(SCALES)], axis=0)


LEFT = slice(0, HALF_ROWS)
RIGHT = slice(HALF_ROWS, 2 * HALF_ROWS)


def chip_merge_kernel(where_ref, table_ref, keep_ref, got_ref, chip_ref):
    rate = half_rates(where_ref, table_ref)
    odd = (where_ref[0] & 1) == 1
    step = jnp.exp(-rate * ROWS)
    one = jnp.ones_like(step)
    mine_l, got_l = jnp.where(odd, one, step), jnp.where(odd, step, one)
    chip_ref[LEFT, :] = mine_l * keep_ref[LEFT, :] + got_l * got_ref[LEFT, :]
    chip_ref[RIGHT, :] = got_l * keep_ref[RIGHT, :] + mine_l * got_ref[RIGHT, :]


def chip_merge(where, table, keep, got):
    return pl.pallas_call(
        chip_merge_kernel,
        in_specs=[SMEM] + [VMEM] * 3,
        out_specs=VMEM,
        out_shape=jax.ShapeDtypeStruct((2 * HALF_ROWS, COLS), F32),
        compiler_params=params(),
        name="chip_merge",
    )(where, table, keep, got)


def quad_merge_kernel(where_ref, table_ref, chip_ref, pair_ref, _, left_ref, s1_ref, s2_ref, s3_ref):
    rate = half_rates(where_ref, table_ref)
    z = where_ref[0] >> 2
    zf = z.astype(F32)
    odd = ((where_ref[0] >> 1) & 1) == 1
    step = jnp.exp(-rate * (2 * ROWS))
    one = jnp.ones_like(step)
    mine_l, got_l = jnp.where(odd, one, step), jnp.where(odd, step, one)
    left = mine_l * chip_ref[LEFT, :] + got_l * pair_ref[LEFT, :]
    right = got_l * chip_ref[RIGHT, :] + mine_l * pair_ref[RIGHT, :]
    image = jnp.exp(-rate * (1.0 + 4 * ROWS * jnp.maximum(7.0 - 2.0 * zf, 1.0)))
    back = right - image * left
    left_ref[...] = left
    for d, ref in ((1, s1_ref), (2, s2_ref), (3, s3_ref)):
        ref[...] = jnp.where(z + d <= 3, left, back)


def quad_merge(where, table, chip, pair, after):
    one = jax.ShapeDtypeStruct((HALF_ROWS, COLS), F32)
    return pl.pallas_call(
        quad_merge_kernel,
        in_specs=[SMEM] + [VMEM] * 3 + [ANY],
        out_specs=[VMEM] * 4,
        out_shape=[one] * 4,
        compiler_params=params(),
        name="quad_merge",
    )(where, table, chip, pair, after)


def lat_carry_kernel(where_ref, table_ref, keep_ref, got_ref, pair_ref, left_ref, g1_ref, g2_ref, g3_ref, _,
                     own_ref, send_ref):
    rate = half_rates(where_ref, table_ref)
    lat = where_ref[0]
    z = lat >> 2
    zf = z.astype(F32)
    quad = lambda n: jnp.exp(-rate * (4 * ROWS * n))
    left = jnp.zeros((HALF_ROWS, COLS), F32)
    right = jnp.zeros((HALF_ROWS, COLS), F32)
    whole = quad(3.0 - zf) * left_ref[...]
    for d, ref in ((1, g1_ref), (2, g2_ref), (3, g3_ref)):
        below = z >= d
        g = ref[...]
        left = left + jnp.where(below, quad(d - 1.0), 0.0) * g
        right = right + jnp.where(below, 0.0, quad(3.0 - d)) * g
        whole = whole + jnp.where(below, quad(3.0 - zf + d), 0.0) * g
    right = right - (quad(3.0 - zf) * jnp.exp(-rate)) * whole
    odd_chip = ((lat >> 1) & 1) == 1
    pair = jnp.exp(-rate * (2 * ROWS))
    zero = jnp.zeros_like(pair)
    one = jnp.ones_like(pair)
    left = jnp.where(odd_chip, pair, one) * left + jnp.where(odd_chip, one, zero) * pair_ref[LEFT, :]
    right = jnp.where(odd_chip, one, pair) * right + jnp.where(odd_chip, zero, one) * pair_ref[RIGHT, :]
    odd = (lat & 1) == 1
    device = jnp.exp(-rate * ROWS)
    low_left = jnp.where(odd, got_ref[LEFT, :], keep_ref[LEFT, :])
    high_right = jnp.where(odd, keep_ref[RIGHT, :], got_ref[RIGHT, :])
    high_l = low_left + device * left
    low_r = high_right + device * right
    own_ref[LEFT, :] = jnp.where(odd, high_l, left)
    own_ref[RIGHT, :] = jnp.where(odd, right, low_r)
    send_ref[LEFT, :] = jnp.where(odd, left, high_l)
    send_ref[RIGHT, :] = jnp.where(odd, low_r, right)


def lat_carry(where, table, keep, got, pair, left, gs, after):
    half = jax.ShapeDtypeStruct((2 * HALF_ROWS, COLS), F32)
    return pl.pallas_call(
        lat_carry_kernel,
        in_specs=[SMEM] + [VMEM] * 8 + [ANY],
        out_specs=[VMEM] * 2,
        out_shape=[half, half],
        compiler_params=params(),
        name="lat_carry",
    )(where, table, keep, got, pair, left, *gs, after)


def local_filter_kernel(starts, where_ref, table_ref, carry_ref, x_ref, out_ref):
    top = where_ref[0] == 0
    shape = (ROWS, LANES)
    row = fiota(shape, 0)
    lane = iota(shape, 1)
    source = jnp.where(lane >= ROWS, lane - ROWS, lane).astype(F32)
    used = lane < 2 * ROWS
    gap = jnp.abs(row - source)
    gap_low = jnp.abs(source - 1.0 - row)
    gap_high = jnp.abs(source + 1.0 - row)
    first = source == 0.0
    spread = jnp.abs(fiota((LANES, LANES), 0) - fiota((LANES, LANES), 1))
    tag = lane & 31
    zeros = jnp.zeros((32, COLS + LANES), BF16)
    corner = jnp.zeros((LANES, LANES), BF16)
    left_lane = (lane == LANES - 1) | (lane == 1) | (lane == 3)
    lane_scale = lambda v: jnp.where((v == LANES - 1) | (v == 0), 0, jnp.where(v <= 2, 1, 2))
    row_scale = lane_scale(lane[:1])
    base = iota((8, LANES), 0)
    column = fiota((8, LANES), 1)

    def carry_tile(tile, virtual):
        left = carry_ref[:, tile * 256:tile * 256 + 128]
        right = carry_ref[:, tile * 256 + 128:tile * 256 + 256]
        left = pltpu.roll(left, (LANES - virtual) % LANES, 1)
        right = pltpu.roll(right, (LANES + 1 - virtual) % LANES, 1)
        return jnp.where(tag == 0, left, jnp.where(tag == 1, right, 0.0))

    def column_pass(matrices, x, carry):
        parts = [split(jnp.where(used, m, 0.0)) for m in matrices]
        lhs = jnp.concatenate([jnp.concatenate([mh, ml[:, :ROWS]], axis=1) for mh, ml in parts], axis=0)
        xh, xl = split(jnp.concatenate([x, carry], axis=1))
        rhs = jnp.concatenate([xh, xl, zeros, xh], axis=0)
        return mm(lhs, rhs)

    def column_stage(f, wind):
        facts = table_ref[pl.ds(f, 1), :]
        rates = [facts[:, s:s + 1] for s in range(SCALES)]
        gains = [facts[:, SCALES + s:SCALES + s + 1] for s in range(SCALES)]
        plain = [gains[s] * jnp.exp(-rates[s] * gap) for s in range(SCALES)]
        if wind:
            slopes = []
            for s in range(SCALES):
                slope = jnp.exp(-rates[s] * gap_low) - jnp.exp(-rates[s] * gap_high)
                slope = slope - jnp.where(top & first, jnp.exp(-rates[s] * (row + 1.0)), 0.0)
                slopes.append((0.5 * gains[s]) * slope)
            stream = f < GROUP
            second_sign = 1.0 if stream else -1.0
            meridional = f if stream else f + 16
            zonal = f + 8
            pair = f + 8 if stream else f - 8
            w = column_pass(plain, -zonal_difference(x_ref[pair]), carry_tile(0, zonal))
            w = w + column_pass(slopes, second_sign * x_ref[f], carry_tile(0, meridional))
        else:
            w = column_pass(plain, x_ref[f], carry_tile(1, f - WINDS))
        return rates, w

    def row_stage(rates, w):
        outs = []
        for s in range(SCALES):
            rows = slice(s * ROWS, (s + 1) * ROWS)
            stack = jnp.concatenate([w[rows, b * LANES:(b + 1) * LANES] for b in range(PARTS)], axis=0)
            wh, wl = split(stack)
            th, tl = split(jnp.exp(-rates[s] * spread))
            lhs = jnp.concatenate([wh, wl], axis=1)
            rhs = jnp.concatenate([jnp.concatenate([th, tl], axis=1), jnp.concatenate([th, corner], axis=1)], axis=0)
            out = mm(lhs, rhs)
            outs.append(out[:, :LANES] + out[:, LANES:])
        return outs

    def carry_stage(rates, w, outs):
        for s in range(SCALES):
            rows = slice(s * ROWS, (s + 1) * ROWS)
            moved = pltpu.roll(w[rows, COLS:], (LANES - 30 * s - 1) % LANES, 1)
            turned = outs[s] if s == 0 else pltpu.roll(outs[s], 2 * s, 1)
            here = row_scale == s
            outer = moved if s == 0 else jnp.where(here, moved, outer)
            sums = turned if s == 0 else jnp.where(here, turned, sums)
        rate_row = jnp.where(row_scale == 0, rates[0], jnp.where(row_scale == 1, rates[1], rates[2]))
        jump = jnp.exp(-rate_row * LANES)
        block = [sums[b * ROWS:(b + 1) * ROWS] for b in range(PARTS)]
        from_left = [outer]
        for b in range(PARTS - 1):
            from_left.append(block[b] + jump * from_left[-1])
        from_right = [outer]
        for b in range(PARTS - 1, 0, -1):
            from_right.append(block[b] + jump * from_right[-1])
        carries = [jnp.where(left_lane, from_left[b], from_right[PARTS - 1 - b]) for b in range(PARTS)]
        ch, cl = split(jnp.concatenate(carries, axis=0))
        low_rate = jnp.where(base == 0, rates[0], jnp.where(base <= 2, rates[1], rates[2]))
        low_left = (base == 1) | (base == 3)
        low = jnp.where(base <= 4, jnp.exp(-low_rate * jnp.where(low_left, column + 1.0, LANES - column)), 0.0)
        high = jnp.where(base == 7, jnp.exp(-rates[0] * (column + 1.0)), 0.0)
        pad = jnp.zeros((8, LANES), F32)
        lh, ll = split(jnp.concatenate([low, pad], axis=0))
        hh, hl = split(jnp.concatenate([pad, high], axis=0))
        gap_rows = jnp.zeros((96, LANES), BF16)
        bh = jnp.concatenate([lh, gap_rows, hh], axis=0)
        bl = jnp.concatenate([ll, gap_rows, hl], axis=0)
        rhs = jnp.concatenate([jnp.concatenate([bh, bl], axis=1), jnp.concatenate([bh, corner], axis=1)], axis=0)
        return jnp.concatenate([ch, cl], axis=1), rhs

    for start in starts:
        wind = start < WINDS
        fields = [start + i for i in range(GROUP)]
        columns = [column_stage(f, wind) for f in fields]
        outs = [row_stage(*c) for c in columns]
        ranks = [carry_stage(*c, o) for c, o in zip(columns, outs)]
        for f, o, (lhs, rhs) in zip(fields, outs, ranks):
            out = mm(lhs, rhs)
            total = (o[0] + o[1]) + (o[2] + out[:, :LANES]) + out[:, LANES:]
            for b in range(PARTS):
                out_ref[f - starts[0], :, b * LANES:(b + 1) * LANES] = total[b * ROWS:(b + 1) * ROWS]


def local_filter(where, table, carry, x, first, count, before, through=None):
    starts = tuple(range(first, first + count, GROUP))
    operands = [where, table, carry, x, before]
    in_specs = [SMEM] + [VMEM] * 3 + [ANY]
    out_specs = [VMEM]
    out_shape = [jax.ShapeDtypeStruct((count, ROWS, COLS), F32)]
    aliases = {}
    if through is not None:
        operands.append(through)
        in_specs.append(ANY)
        out_specs.append(ANY)
        out_shape.append(jax.ShapeDtypeStruct(through.shape, through.dtype))
        aliases = {5: 1}

    def body(*refs):
        local_filter_kernel(starts, *refs[:4], refs[len(in_specs)])

    return pl.pallas_call(
        body,
        in_specs=in_specs,
        out_specs=out_specs,
        out_shape=out_shape,
        input_output_aliases=aliases,
        compiler_params=params(),
        cost_estimate=pl.CostEstimate(flops=count * 400_000_000, bytes_accessed=count * 150_000, transcendentals=0),
        name="local_filter",
    )(*operands)


def finish_kernel(bounds, where_ref, table_ref, own_ref, got_ref, *refs):
    z_refs, (out_ref, buf_ref, sem) = refs[:len(bounds)], refs[len(bounds):]
    core = where_ref[0] & 1
    row = fiota((8, LANES), 0)
    up_steps, down_steps = row + 1.0, 8.0 - row
    copies = []
    for group in range(GROUPS):
        mine = core == group // 3
        part = group % 3
        k = max(i for i, b in enumerate(bounds) if b <= group * GROUP)
        tables = [jnp.where(mine, own_ref[side, s, part], got_ref[side, s, part]) for side in range(2) for s in range(SCALES)]
        for i in range(GROUP):
            f = group * GROUP + i
            facts = table_ref[f:f + 1, :]
            ups = []
            for s in range(SCALES):
                r = jnp.broadcast_to(facts[:, s:s + 1], (8, LANES))
                w = jnp.broadcast_to(facts[:, SCALES + s:SCALES + s + 1], (8, LANES))
                jump = jnp.exp(-8.0 * r)
                up, down = [w * jnp.exp(-r * up_steps)], [w * jnp.exp(-r * down_steps)]
                for _ in range(ROWS // 8 - 1):
                    up.append(up[-1] * jump)
                    down.insert(0, down[0] * jump)
                ups.append((jnp.concatenate(up, axis=0), jnp.concatenate(down, axis=0)))
            for b in range(PARTS):
                lanes = slice(b * LANES, (b + 1) * LANES)
                total = z_refs[k][f - bounds[k], :, lanes]
                for s in range(SCALES):
                    total = total + ups[s][0] * tables[s][i:i + 1, lanes] + ups[s][1] * tables[SCALES + s][i:i + 1, lanes]
                buf_ref[group, i, :, lanes] = total
        copy = pltpu.make_async_copy(buf_ref.at[group], out_ref.at[pl.ds(group * GROUP, GROUP)], sem.at[group])
        copy.start()
        copies.append(copy)
    for copy in copies:
        copy.wait()


def finish(where, table, own, got, parts):
    shaped = lambda t: t.reshape(2, SCALES, 3, GROUP, COLS)
    bounds = [sum(p.shape[0] for p in parts[:i]) for i in range(len(parts))]
    return pl.pallas_call(
        functools.partial(finish_kernel, bounds),
        in_specs=[SMEM] + [VMEM] * (3 + len(parts)),
        out_specs=HBM,
        out_shape=jax.ShapeDtypeStruct((FIELDS, ROWS, COLS), F32),
        scratch_shapes=[pltpu.VMEM((GROUPS, GROUP, ROWS, COLS), F32), pltpu.SemaphoreType.DMA((GROUPS,))],
        compiler_params=params(),
        name="finish",
    )(where, table, shaped(own), shaped(got), *parts)


def shards(x, lengths, weights):
    where = jnp.stack([lax.axis_index("lat"), lax.axis_index("lon")]).astype(jnp.int32)
    sums, edge, table, lanes = row_sums(where, lengths.T, weights.T, x)
    got = []
    for d in (1, 2, 3):
        perm = [(h * 4 + i, h * 4 + (i + d) % 4) for h in range(2) for i in range(4)]
        got.append(lax.ppermute(sums, "lon", perm))
    local = local_sums(where, table, x)
    part, mine = lon_merge(where, lanes, sums, got, local)
    theirs = lax.ppermute(mine, "lon", [(i, i ^ 4) for i in range(NLON)])
    carry, keep, send = column_sums(where, table, lanes, part, mine, theirs, edge, local)
    core_pairs = [(i, i ^ 1) for i in range(NLAT)]
    got_core = lax.ppermute(send, "lat", core_pairs)
    chip = chip_merge(where, table, keep, got_core)
    pair = lax.ppermute(chip, "lat", [(i, i ^ 2) for i in range(NLAT)])
    (z0,) = local_filter(where, table, carry, x, 0, 16, chip)
    left, s1, s2, s3 = quad_merge(where, table, chip, pair, z0)
    quad = lambda t, d: lax.ppermute(t, "lat", [(i, (i + 4 * d) % NLAT) for i in range(NLAT)])
    g1 = quad(s1, 1)
    z1, s2 = local_filter(where, table, carry, x, 16, 16, left, s2)
    g2 = quad(s2, 2)
    z2, s3 = local_filter(where, table, carry, x, 32, 8, z1, s3)
    g3 = quad(s3, 3)
    (z3,) = local_filter(where, table, carry, x, 40, 8, z2)
    own, other = lat_carry(where, table, keep, got_core, pair, left, (g1, g2, g3), z3)
    got_carry = lax.ppermute(other, "lat", core_pairs)
    return finish(where, table, own, got_carry, (z0, z1, z2, z3))


def solution(mesh):
    in_specs = (P(None, "lat", "lon"), P(), P())
    out_specs = P(None, "lat", "lon")
    return jax.shard_map(shards, mesh=mesh, in_specs=in_specs, out_specs=out_specs, check_vma=False)
```

time: 127 us -> 61.5 us (0.48)
  Pallas kernels: 84.9 us -> 30.3 us
  waiting for transfers between devices: 19.3 us -> 7.9 us
  starting transfers between devices: 17 us -> 19.5 us
  local copies, waits for them, and re-layouts: 4.95 us -> 2.76 us
    pallas_call x8 -> x11, Pallas kernels: 84.2 us -> 29.5 us  [the longest x4 12.1 us: local_filter(): pl.pallas_call(body, in_specs=in_specs, out_specs=out_specs, out_shape=ou...]
    ppermute x3, waiting for transfers between devices: 8.14 us -> 1.28 us  [shards(): got.append(lax.ppermute(sums, 'lon', perm))]
    ppermute x1, waiting for transfers between devices: 6.33 us -> 0.6 us  [shards(): pair = lax.ppermute(chip, 'lat', [(i, i ^ 2) for i in range(NLAT)])]
    ppermute x1, waiting for transfers between devices: 0.01 us -> 2.93 us  [shards(): theirs = lax.ppermute(mine, 'lon', [(i, i ^ 4) for i in range(NLON)])]
    ppermute x3, waiting for transfers between devices: 3.74 us -> 0.88 us  [shards(): lax.ppermute(t, 'lat', [(i, (i + 4 * d) % NLAT) for i in range(NLAT)])]
    unnamed x12 -> x14, local copies, waits for them, and re-layouts: 4.95 us -> 2.76 us
  transfers between devices with their start and end apart: 10 -> 10, of which waited for: 8 -> 6; matrix products, arithmetic and copies ran while one was open for 0% -> 0% of each run, Pallas kernels for 57% -> 27%
where the time goes in v2:
time: 61.5 us; the launch traced here: 61.3 us
  Pallas kernels  30.3 us (49%)
  starting transfers between devices  19.5 us (32%)
  waiting for transfers between devices  7.9 us (13%)
  local copies, waits for them, and re-layouts  2.76 us (4%)
    pallas_call x4, Pallas kernels, local_filter(): pl.pallas_call(body, in_specs=in_specs, out_specs=out_specs, out_shape=ou...  12.1 us
    pallas_call x1, Pallas kernels, row_sums(): pl.pallas_call(row_sums_kernel, in_specs=[SMEM, VMEM, VMEM, HBM], out_spe...  6.43 us
    ppermute x3, starting transfers between devices, shards(): lax.ppermute(t, 'lat', [(i, (i + 4 * d) % NLAT) for i in range(NLAT)])  5.89 us
    ppermute x3, starting transfers between devices, shards(): got.append(lax.ppermute(sums, 'lon', perm))  4.67 us
    pallas_call x1, Pallas kernels, local_sums(): pl.pallas_call(local_sums_kernel, in_specs=[SMEM, VMEM, VMEM], out_specs=...  4.29 us
    pallas_call x1, Pallas kernels, finish(): pl.pallas_call(functools.partial(finish_kernel, bounds), in_specs=[SMEM]...  3.58 us
    ppermute x1, starting transfers between devices, shards(): got_carry = lax.ppermute(other, 'lat', core_pairs)  2.97 us
    ppermute x1, waiting for transfers between devices, shards(): theirs = lax.ppermute(mine, 'lon', [(i, i ^ 4) for i in range(NLON)])  2.93 us
  transfers between devices with their start and end apart: 10, of which 6 were waited for; matrix products, arithmetic and copies ran while one was open for 0% of the time, Pallas kernels for 27%

profile of v2, /device:TPU:1, one launch (start us, length us, event | category | flops | bytes accessed | tf_op | source)
XLA Modules:
  0.0 61.3 jit_solution(4848842059138016168)
XLA Ops:
  0.0 0.6 pad_add_fusion.where_ref.refs_0_
  0.6 0.0 copy-start.5
  0.6 6.4 %row_sums.1 = (f32[48,640]{1,0:T(8,128)}, f32[48,256]{1,0:T(8,128)}, f32[48,128]{1,0:T(8,128)}, f32[8,128]{1,0:T(8,128)}) custom-call(s32[2]{0:T(128)} %pad_add_fusion.where_ref.refs_0_, f32[3,48]{1,0:T(4,128)} %bitcast.11, f32[3,48]{1,0:T(4,128)} %bitcast.12, f32[48,48,384]{2,1,0:T(8,128)} %refs_3_.7), custom_call_target="tpu_custom_call" | custom-call | tf_op jit(solution)/shard_map/row_sums/pallas_call | solution.py:149
  7.0 3.6 %collective-permute-start.2 = (f32[48,640]{1,0:T(8,128)}, f32[48,640]{1,0:T(8,128)S(1)}, u32[]{:S(2)}, u32[]{:S(2)}) collective-permute-start(f32[48,640]{1,0:T(8,128)} %get-tuple-element.26.own_ref), channel_id=1, source_target_pairs={{0,3},{1,0},{2,1},{3,2},{4,7},{5,4},{6,5},{7,6},{8,11},{9,8},{10,9... | collective-permute-start | bytes 368648 | tf_op jit(solution)/shard_map/ppermute | solution.py:673
  10.7 0.3 collective-permute-start.1
  11.0 0.7 %collective-permute-start = (f32[48,640]{1,0:T(8,128)}, f32[48,640]{1,0:T(8,128)S(1)}, u32[]{:S(2)}, u32[]{:S(2)}) collective-permute-start(f32[48,640]{1,0:T(8,128)} %get-tuple-element.26.own_ref), channel_id=1, source_target_pairs={{0,1},{1,2},{2,3},{3,0},{4,5},{5,6},{6,7},{7,4},{8,9},{9,10},{10,1... | collective-permute-start | bytes 368648 | tf_op jit(solution)/shard_map/ppermute | solution.py:673
  11.7 0.0 copy-done.5
  11.7 0.0 copy-start
  11.7 2.0 %copy-done = f32[48,48,384]{2,1,0:T(8,128)S(1)} copy-done((f32[48,48,384]{2,1,0:T(8,128)S(1)}, f32[48,48,384]{2,1,0:T(8,128)}, u32[]{:S(2)}) %copy-start) | copy-done | bytes 3538968
  13.7 0.0 copy-start.2
  13.7 0.7 %copy-done.2 = f32[48,128]{1,0:T(8,128)S(1)} copy-done((f32[48,128]{1,0:T(8,128)S(1)}, f32[48,128]{1,0:T(8,128)}, u32[]{:S(2)}) %copy-start.2) | copy-done | bytes 24600
  14.5 0.0 copy-start.3
  14.5 0.0 copy-start.6
  14.5 0.0 copy-start.4
  14.5 0.0 copy-start.1
  14.5 4.3 %local_sums.1 = f32[2,2,3,3,8,384]{5,4,3,2,1,0:T(8,128)S(1)} custom-call(s32[2]{0:T(128)S(1)} %copy-done.5, f32[48,128]{1,0:T(8,128)S(1)} %copy-done.2, f32[48,48,384]{2,1,0:T(8,128)S(1)} %copy-done), custom_call_target="tpu_custom_call" | custom-call | tf_op jit(solution)/shard_map/local_sums/pallas_call | solution.py:230
  18.8 0.0 collective-permute-done.2.g3_ref
  18.8 0.0 collective-permute-done.1.g2_ref
  18.8 1.3 %collective-permute-done.g1_ref = f32[48,640]{1,0:T(8,128)S(1)} collective-permute-done((f32[48,640]{1,0:T(8,128)}, f32[48,640]{1,0:T(8,128)S(1)}, u32[]{:S(2)}, u32[]{:S(2)}) %collective-permute-start) | collective-permute-done | bytes 122912 | tf_op jit(solution)/shard_map/ppermute | solution.py:673
  20.1 0.0 copy-done.3
  20.1 0.0 copy-done.6
  20.1 0.6 %lon_merge.1 = (f32[48,512]{1,0:T(8,128)S(1)}, f32[48,640]{1,0:T(8,128)S(1)}) custom-call(s32[2]{0:T(128)S(1)} %copy-done.5, f32[8,128]{1,0:T(8,128)S(1)} %copy-done.6, f32[48,640]{1,0:T(8,128)S(1)} %copy-done.3, f32[48,640]{1,0:T(8,128)S(1)} %collective-permute-done.g1_ref, f32[48,640]{1,0:T(8,128)S(1)} %collective-permute-done.1.g2_ref, ...), custom_call_target="tpu_custom_call" | custom-call | tf_op jit(solution)/shard_map/lon_merge/pallas_call | solution.py:272
  20.7 2.8 %collective-permute-start.3 = (f32[48,640]{1,0:T(8,128)S(1)}, f32[48,640]{1,0:T(8,128)S(1)}, u32[]{:S(2)}, u32[]{:S(2)}) collective-permute-start(f32[48,640]{1,0:T(8,128)S(1)} %get-tuple-element.28.mine_ref), channel_id=1, source_target_pairs={{0,4},{1,5},{2,6},{3,7},{4,0},{5,1},{6,2},{7,3},{8,12},{9,13},{10,... | collective-permute-start | bytes 368648 | tf_op jit(solution)/shard_map/ppermute | solution.py:676
  23.5 2.9 %collective-permute-done.3.theirs_ref = f32[48,640]{1,0:T(8,128)S(1)} collective-permute-done((f32[48,640]{1,0:T(8,128)S(1)}, f32[48,640]{1,0:T(8,128)S(1)}, u32[]{:S(2)}, u32[]{:S(2)}) %collective-permute-start.3) | collective-permute-done | bytes 122912 | tf_op jit(solution)/shard_map/ppermute | solution.py:676
  26.5 0.0 copy-done.4
  26.5 0.9 %column_sums.1 = (f32[48,512]{1,0:T(8,128)S(1)}, f32[144,384]{1,0:T(8,128)S(1)}, f32[144,384]{1,0:T(8,128)S(1)}) custom-call(s32[2]{0:T(128)S(1)} %copy-done.5, f32[48,128]{1,0:T(8,128)S(1)} %copy-done.2, f32[8,128]{1,0:T(8,128)S(1)} %copy-done.6, f32[48,512]{1,0:T(8,128)S(1)} %get-tuple-element.27.part_ref, f32[48,640]{1,0:T(8,128)S(1)} %get-tuple-element.28.mine_ref, ...), custom_call_target="tpu_custom_call" | custom-call | tf_op jit(solution)/shard_map/column_sums/pallas_call | solution.py:355
  27.4 1.6 %collective-permute-start.4 = (f32[144,384]{1,0:T(8,128)S(1)}, f32[144,384]{1,0:T(8,128)S(1)}, u32[]{:S(2)}, u32[]{:S(2)}) collective-permute-start(f32[144,384]{1,0:T(8,128)S(1)} %get-tuple-element.31), channel_id=1, source_target_pairs={{0,8},{8,0},{16,24},{24,16},{32,40},{40,32},{48,56},{56,48},{64,72... | collective-permute-start | bytes 663560 | tf_op jit(solution)/shard_map/ppermute | solution.py:679
  29.0 1.1 %collective-permute-done.4.got_ref = f32[144,384]{1,0:T(8,128)S(1)} collective-permute-done((f32[144,384]{1,0:T(8,128)S(1)}, f32[144,384]{1,0:T(8,128)S(1)}, u32[]{:S(2)}, u32[]{:S(2)}) %collective-permute-start.4) | collective-permute-done | bytes 221216 | tf_op jit(solution)/shard_map/ppermute | solution.py:679
  30.1 0.7 %chip_merge.1.refs_4_.chip_ref = f32[144,384]{1,0:T(8,128)S(1)} custom-call(s32[2]{0:T(128)S(1)} %copy-done.5, f32[48,128]{1,0:T(8,128)S(1)} %copy-done.2, f32[144,384]{1,0:T(8,128)S(1)} %get-tuple-element.30.keep_ref, f32[144,384]{1,0:T(8,128)S(1)} %collective-permute-done.4.got_ref), custom_call_target="tpu_custom_call" | custom-call | tf_op jit(solution)/shard_map/chip_merge/pallas_call | solution.py:386
  30.9 1.5 %collective-permute-start.5 = (f32[144,384]{1,0:T(8,128)S(1)}, f32[144,384]{1,0:T(8,128)S(1)}, u32[]{:S(2)}, u32[]{:S(2)}) collective-permute-start(f32[144,384]{1,0:T(8,128)S(1)} %chip_merge.1.refs_4_.chip_ref), channel_id=1, source_target_pairs={{0,16},{8,24},{16,0},{24,8},{32,48},{40,56},{48,32},{56,40},{64,80... | collective-permute-start | bytes 663560 | tf_op jit(solution)/shard_map/ppermute | solution.py:681
  32.3 0.0 copy-done.1
  32.3 4.8 %local_filter.4._.refs_0_ = f32[16,48,384]{2,1,0:T(8,128)S(1)} custom-call(s32[2]{0:T(128)S(1)} %copy-done.5, f32[48,128]{1,0:T(8,128)S(1)} %copy-done.2, f32[48,512]{1,0:T(8,128)S(1)} %get-tuple-element.32.refs_2_, f32[48,48,384]{2,1,0:T(8,128)S(1)} %copy-done.1, f32[144,384]{1,0:T(8,128)S(1)} %chip_merge.1.refs_4_.chip_ref), custom_call_target="tpu_custom_call" | custom-call | flops 6400000000 | bytes 2400000 | tf_op jit(solution)/shard_map/local_filter/pallas_call | solution.py:604
  37.2 0.6 collective-permute-done.5.pair_ref
  37.8 0.7 %quad_merge.1 = (f32[72,384]{1,0:T(8,128)S(1)}, f32[72,384]{1,0:T(8,128)S(1)}, f32[72,384]{1,0:T(8,128)S(1)}, f32[72,384]{1,0:T(8,128)S(1)}) custom-call(s32[2]{0:T(128)S(1)} %copy-done.5, f32[48,128]{1,0:T(8,128)S(1)} %copy-done.2, f32[144,384]{1,0:T(8,128)S(1)} %chip_merge.1.refs_4_.chip_ref, f32[144,384]{1,0:T(8,128)S(1)} %collective-permute-done.5.pair_ref, ...), custom_call_target="tpu_custom_call" | custom-call | tf_op jit(solution)/shard_map/quad_merge/pallas_call | solution.py:415
  38.5 1.7 %collective-permute-start.6 = (f32[72,384]{1,0:T(8,128)S(1)}, f32[72,384]{1,0:T(8,128)S(1)}, u32[]{:S(2)}, u32[]{:S(2)}) collective-permute-start(f32[72,384]{1,0:T(8,128)S(1)} %get-tuple-element.34), channel_id=1, source_target_pairs={{0,32},{8,40},{16,48},{24,56},{32,64},{40,72},{48,80},{56,88},{64,... | collective-permute-start | bytes 331784 | tf_op jit(solution)/shard_map/ppermute | solution.py:684
  40.2 3.3 %local_filter.5 = (f32[16,48,384]{2,1,0:T(8,128)S(1)}, f32[72,384]{1,0:T(8,128)S(1)}) custom-call(s32[2]{0:T(128)S(1)} %copy-done.5, f32[48,128]{1,0:T(8,128)S(1)} %copy-done.2, f32[48,512]{1,0:T(8,128)S(1)} %get-tuple-element.32.refs_2_, f32[48,48,384]{2,1,0:T(8,128)S(1)} %copy-done.1, ...), custom_call_target="tpu_custom_call", output_to_operand_aliasing={{1}: (5, {})} | custom-call | flops 6400000000 | bytes 2400000 | tf_op jit(solution)/shard_map/local_filter/pallas_call | solution.py:604
  43.5 3.4 %collective-permute-start.7 = (f32[72,384]{1,0:T(8,128)S(1)}, f32[72,384]{1,0:T(8,128)S(1)}, u32[]{:S(2)}, u32[]{:S(2)}) collective-permute-start(f32[72,384]{1,0:T(8,128)S(1)} %get-tuple-element.36), channel_id=1, source_target_pairs={{0,64},{8,72},{16,80},{24,88},{32,96},{40,104},{48,112},{56,120},{... | collective-permute-start | bytes 331784 | tf_op jit(solution)/shard_map/ppermute | solution.py:684
  46.9 2.0 %local_filter.6 = (f32[8,48,384]{2,1,0:T(8,128)S(1)}, f32[72,384]{1,0:T(8,128)S(1)}) custom-call(s32[2]{0:T(128)S(1)} %copy-done.5, f32[48,128]{1,0:T(8,128)S(1)} %copy-done.2, f32[48,512]{1,0:T(8,128)S(1)} %get-tuple-element.32.refs_2_, f32[48,48,384]{2,1,0:T(8,128)S(1)} %copy-done.1, ...), custom_call_target="tpu_custom_call", output_to_operand_aliasing={{1}: (5, {})} | custom-call | flops 3200000000 | bytes 1200000 | tf_op jit(solution)/shard_map/local_filter/pallas_call | solution.py:604
  48.9 0.8 %collective-permute-start.8 = (f32[72,384]{1,0:T(8,128)S(1)}, f32[72,384]{1,0:T(8,128)S(1)}, u32[]{:S(2)}, u32[]{:S(2)}) collective-permute-start(f32[72,384]{1,0:T(8,128)S(1)} %get-tuple-element.39), channel_id=1, source_target_pairs={{0,96},{8,104},{16,112},{24,120},{32,0},{40,8},{48,16},{56,24},{64... | collective-permute-start | bytes 331784 | tf_op jit(solution)/shard_map/ppermute | solution.py:684
  49.7 2.0 %local_filter.7._.refs_3_ = f32[8,48,384]{2,1,0:T(8,128)S(1)} custom-call(s32[2]{0:T(128)S(1)} %copy-done.5, f32[48,128]{1,0:T(8,128)S(1)} %copy-done.2, f32[48,512]{1,0:T(8,128)S(1)} %get-tuple-element.32.refs_2_, f32[48,48,384]{2,1,0:T(8,128)S(1)} %copy-done.1, f32[8,48,384]{2,1,0:T(8,128)S(1)} %get-tuple-element.40.refs_4_.refs_2_), custom_call_target="tpu_custom_call" | custom-call | flops 3200000000 | bytes 1200000 | tf_op jit(solution)/shard_map/local_filter/pallas_call | solution.py:604
  51.7 0.0 collective-permute-done.6.g1_ref
  51.7 0.0 collective-permute-done.7.g2_ref
  51.7 0.9 %collective-permute-done.8.g3_ref = f32[72,384]{1,0:T(8,128)S(1)} collective-permute-done((f32[72,384]{1,0:T(8,128)S(1)}, f32[72,384]{1,0:T(8,128)S(1)}, u32[]{:S(2)}, u32[]{:S(2)}) %collective-permute-start.8) | collective-permute-done | bytes 110624 | tf_op jit(solution)/shard_map/ppermute | solution.py:684
  52.6 0.9 %lat_carry.1 = (f32[144,384]{1,0:T(8,128)S(1)}, f32[144,384]{1,0:T(8,128)S(1)}) custom-call(s32[2]{0:T(128)S(1)} %copy-done.5, f32[48,128]{1,0:T(8,128)S(1)} %copy-done.2, f32[144,384]{1,0:T(8,128)S(1)} %get-tuple-element.30.keep_ref, f32[144,384]{1,0:T(8,128)S(1)} %collective-permute-done.4.got_ref, f32[144,384]{1,0:T(8,128)S(1)} %collective-permute-done.5.pair_ref, ...), custom_call_target="tpu_custom_call" | custom-call | tf_op jit(solution)/shard_map/lat_carry/pallas_call | solution.py:462
  53.5 3.0 %collective-permute-start.9 = (f32[144,384]{1,0:T(8,128)S(1)}, f32[144,384]{1,0:T(8,128)S(1)}, u32[]{:S(2)}, u32[]{:S(2)}) collective-permute-start(f32[144,384]{1,0:T(8,128)S(1)} %get-tuple-element.42), channel_id=1, source_target_pairs={{0,8},{8,0},{16,24},{24,16},{32,40},{40,32},{48,56},{56,48},{64,72... | collective-permute-start | bytes 663560 | tf_op jit(solution)/shard_map/ppermute | solution.py:692
  56.4 1.1 %collective-permute-done.9 = f32[144,384]{1,0:T(8,128)S(1)} collective-permute-done((f32[144,384]{1,0:T(8,128)S(1)}, f32[144,384]{1,0:T(8,128)S(1)}, u32[]{:S(2)}, u32[]{:S(2)}) %collective-permute-start.9) | collective-permute-done | bytes 221216 | tf_op jit(solution)/shard_map/ppermute | solution.py:692
  57.5 3.6 %finish.1 = f32[48,48,384]{2,1,0:T(8,128)} custom-call(s32[2]{0:T(128)S(1)} %copy-done.5, f32[48,128]{1,0:T(8,128)S(1)} %copy-done.2, f32[2,3,3,8,384]{4,3,2,1,0:T(8,128)S(1)} %bitcast.9, f32[2,3,3,8,384]{4,3,2,1,0:T(8,128)S(1)} %bitcast.10, f32[16,48,384]{2,1,0:T(8,128)S(1)} %local_filter.4._.refs_0_, f32[16,48,384]{2,1,0:T(8,128)S(1)} %get-tuple-element.37.refs_4_.refs_1_, ...), custom_call_target="tpu_custom_call" | custom-call | tf_op jit(solution)/shard_map/finish/pallas_call | solution.py:656
Async XLA Ops:
  0.6 11.1 %copy-start.5 = (s32[2]{0:T(128)S(1)}, s32[2]{0:T(128)}, u32[]{:S(2)}) copy-start(s32[2]{0:T(128)} %pad_add_fusion.where_ref.refs_0_) | copy-start | bytes 28
  7.0 11.7 %collective-permute-start.2 = (f32[48,640]{1,0:T(8,128)}, f32[48,640]{1,0:T(8,128)S(1)}, u32[]{:S(2)}, u32[]{:S(2)}) collective-permute-start(f32[48,640]{1,0:T(8,128)} %get-tuple-element.26.own_ref), channel_id=1, source_target_pairs={{0,3},{1,0},{2,1},{3,2},{4,7},{5,4},{6,5},{7,6},{8,11},{9,8},{10,9... | collective-permute-start | bytes 368648 | tf_op jit(solution)/shard_map/ppermute | solution.py:673
  10.7 8.1 %collective-permute-start.1 = (f32[48,640]{1,0:T(8,128)}, f32[48,640]{1,0:T(8,128)S(1)}, u32[]{:S(2)}, u32[]{:S(2)}) collective-permute-start(f32[48,640]{1,0:T(8,128)} %get-tuple-element.26.own_ref), channel_id=1, source_target_pairs={{0,2},{1,3},{2,0},{3,1},{4,6},{5,7},{6,4},{7,5},{8,10},{9,11},{10,... | collective-permute-start | bytes 368648 | tf_op jit(solution)/shard_map/ppermute | solution.py:673
  11.0 9.0 %collective-permute-start = (f32[48,640]{1,0:T(8,128)}, f32[48,640]{1,0:T(8,128)S(1)}, u32[]{:S(2)}, u32[]{:S(2)}) collective-permute-start(f32[48,640]{1,0:T(8,128)} %get-tuple-element.26.own_ref), channel_id=1, source_target_pairs={{0,1},{1,2},{2,3},{3,0},{4,5},{5,6},{6,7},{7,4},{8,9},{9,10},{10,1... | collective-permute-start | bytes 368648 | tf_op jit(solution)/shard_map/ppermute | solution.py:673
  11.7 2.0 %copy-start = (f32[48,48,384]{2,1,0:T(8,128)S(1)}, f32[48,48,384]{2,1,0:T(8,128)}, u32[]{:S(2)}) copy-start(f32[48,48,384]{2,1,0:T(8,128)} %refs_3_.7) | copy-start | bytes 10616836
  13.7 0.7 %copy-start.2 = (f32[48,128]{1,0:T(8,128)S(1)}, f32[48,128]{1,0:T(8,128)}, u32[]{:S(2)}) copy-start(f32[48,128]{1,0:T(8,128)} %get-tuple-element.24.table_ref.refs_1_) | copy-start | bytes 73732
  14.5 5.6 %copy-start.3 = (f32[48,640]{1,0:T(8,128)S(1)}, f32[48,640]{1,0:T(8,128)}, u32[]{:S(2)}) copy-start(f32[48,640]{1,0:T(8,128)} %get-tuple-element.26.own_ref) | copy-start | bytes 368644
  14.5 5.6 %copy-start.6 = (f32[8,128]{1,0:T(8,128)S(1)}, f32[8,128]{1,0:T(8,128)}, u32[]{:S(2)}) copy-start(f32[8,128]{1,0:T(8,128)} %get-tuple-element.25.lanes_ref) | copy-start | bytes 12292
  14.5 12.0 %copy-start.4 = (f32[48,256]{1,0:T(8,128)S(1)}, f32[48,256]{1,0:T(8,128)}, u32[]{:S(2)}) copy-start(f32[48,256]{1,0:T(8,128)} %get-tuple-element.29.edge_ref) | copy-start | bytes 147460
  14.5 17.9 %copy-start.1 = (f32[48,48,384]{2,1,0:T(8,128)S(1)}, f32[48,48,384]{2,1,0:T(8,128)}, u32[]{:S(2)}) copy-start(f32[48,48,384]{2,1,0:T(8,128)} %refs_3_.7) | copy-start | bytes 10616836
  20.7 5.8 %collective-permute-start.3 = (f32[48,640]{1,0:T(8,128)S(1)}, f32[48,640]{1,0:T(8,128)S(1)}, u32[]{:S(2)}, u32[]{:S(2)}) collective-permute-start(f32[48,640]{1,0:T(8,128)S(1)} %get-tuple-element.28.mine_ref), channel_id=1, source_target_pairs={{0,4},{1,5},{2,6},{3,7},{4,0},{5,1},{6,2},{7,3},{8,12},{9,13},{10,... | collective-permute-start | bytes 368648 | tf_op jit(solution)/shard_map/ppermute | solution.py:676
  27.4 2.8 %collective-permute-start.4 = (f32[144,384]{1,0:T(8,128)S(1)}, f32[144,384]{1,0:T(8,128)S(1)}, u32[]{:S(2)}, u32[]{:S(2)}) collective-permute-start(f32[144,384]{1,0:T(8,128)S(1)} %get-tuple-element.31), channel_id=1, source_target_pairs={{0,8},{8,0},{16,24},{24,16},{32,40},{40,32},{48,56},{56,48},{64,72... | collective-permute-start | bytes 663560 | tf_op jit(solution)/shard_map/ppermute | solution.py:679
  30.9 6.9 %collective-permute-start.5 = (f32[144,384]{1,0:T(8,128)S(1)}, f32[144,384]{1,0:T(8,128)S(1)}, u32[]{:S(2)}, u32[]{:S(2)}) collective-permute-start(f32[144,384]{1,0:T(8,128)S(1)} %chip_merge.1.refs_4_.chip_ref), channel_id=1, source_target_pairs={{0,16},{8,24},{16,0},{24,8},{32,48},{40,56},{48,32},{56,40},{64,80... | collective-permute-start | bytes 663560 | tf_op jit(solution)/shard_map/ppermute | solution.py:681
  38.5 13.2 %collective-permute-start.6 = (f32[72,384]{1,0:T(8,128)S(1)}, f32[72,384]{1,0:T(8,128)S(1)}, u32[]{:S(2)}, u32[]{:S(2)}) collective-permute-start(f32[72,384]{1,0:T(8,128)S(1)} %get-tuple-element.34), channel_id=1, source_target_pairs={{0,32},{8,40},{16,48},{24,56},{32,64},{40,72},{48,80},{56,88},{64,... | collective-permute-start | bytes 331784 | tf_op jit(solution)/shard_map/ppermute | solution.py:684
  43.5 8.2 %collective-permute-start.7 = (f32[72,384]{1,0:T(8,128)S(1)}, f32[72,384]{1,0:T(8,128)S(1)}, u32[]{:S(2)}, u32[]{:S(2)}) collective-permute-start(f32[72,384]{1,0:T(8,128)S(1)} %get-tuple-element.36), channel_id=1, source_target_pairs={{0,64},{8,72},{16,80},{24,88},{32,96},{40,104},{48,112},{56,120},{... | collective-permute-start | bytes 331784 | tf_op jit(solution)/shard_map/ppermute | solution.py:684
  48.9 3.7 %collective-permute-start.8 = (f32[72,384]{1,0:T(8,128)S(1)}, f32[72,384]{1,0:T(8,128)S(1)}, u32[]{:S(2)}, u32[]{:S(2)}) collective-permute-start(f32[72,384]{1,0:T(8,128)S(1)} %get-tuple-element.39), channel_id=1, source_target_pairs={{0,96},{8,104},{16,112},{24,120},{32,0},{40,8},{48,16},{56,24},{64... | collective-permute-start | bytes 331784 | tf_op jit(solution)/shard_map/ppermute | solution.py:684
  53.5 4.1 %collective-permute-start.9 = (f32[144,384]{1,0:T(8,128)S(1)}, f32[144,384]{1,0:T(8,128)S(1)}, u32[]{:S(2)}, u32[]{:S(2)}) collective-permute-start(f32[144,384]{1,0:T(8,128)S(1)} %get-tuple-element.42), channel_id=1, source_target_pairs={{0,8},{8,0},{16,24},{24,16},{32,40},{40,32},{48,56},{56,48},{64,72... | collective-permute-start | bytes 663560 | tf_op jit(solution)/shard_map/ppermute | solution.py:692

commit v3 on v2

--- a/solution.py
+++ b/solution.py
@@ -27,7 +27,6 @@
 VMEM = pl.BlockSpec(memory_space=pltpu.VMEM)
 SMEM = pl.BlockSpec(memory_space=pltpu.SMEM)
 BIG = 48 * 1024 * 1024
-WHOLE = 61 * 1024 * 1024
 
 
 def params(**kw):
@@ -71,7 +70,7 @@
     def pick(which):
         every = exact(rate, jnp.where(field == which, 1.0, 0.0).astype(F32), ((1,), (0,)))
         value = jnp.where(lane < 32, every[0:1], jnp.where(lane < 64, every[1:2], every[2:3]))
-        return jnp.where(lane < 96, value, 1.0)
+        return jnp.where(lane < 96, value, 0.0)
 
     return pick(wind_field), pick(rest_field)
 
@@ -94,11 +93,7 @@
     return zonal, sign
 
 
-def row_sums_kernel(where_ref, len_ref, weight_ref, x_ref, sums_ref, edge_ref, table_ref, lanes_ref, w_ref, buf_ref, sem):
-    lon = where_ref[1]
-    copies = [pltpu.make_async_copy(x_ref.at[pl.ds(g * GROUP, GROUP)], buf_ref.at[g], sem.at[g]) for g in range(GROUPS)]
-    for copy in copies:
-        copy.start()
+def tables_kernel(len_ref, weight_ref, table_ref, lanes_ref, w_ref):
     rate = 1.0 / len_ref[...]
     pair = lane_rates(rate)
     lanes_ref[...] = jnp.concatenate([pair[0], pair[1], jnp.ones((6, LANES), F32)], axis=0)
@@ -113,12 +108,28 @@
     both = jnp.concatenate([rate, scale_weights(rate, weight_ref[...]), jnp.ones((2, FIELDS), F32)], axis=0)
     eye = jnp.where(iota((8, LANES), 0) == iota((8, LANES), 1), 1.0, 0.0).astype(F32)
     table_ref[...] = exact(both, eye, ((0,), (0,)))
-    virtual = iota((ROWS, LANES), 1) & 31
+
+
+def tables(lengths, weights):
+    return pl.pallas_call(
+        tables_kernel,
+        in_specs=[VMEM] * 2,
+        out_specs=[VMEM] * 3,
+        out_shape=[jax.ShapeDtypeStruct((FIELDS, LANES), F32), jax.ShapeDtypeStruct((8, LANES), F32),
+                   jax.ShapeDtypeStruct((2, 3 * COLS, 256), BF16)],
+        compiler_params=params(),
+        name="tables",
+    )(lengths, weights)
+
+
+def row_sums_kernel(where_ref, w_ref, x_ref, sums_ref, edge_ref):
+    lon = where_ref[1]
+    lane = iota((ROWS, LANES), 1)
+    virtual = lane & 31
     zero = jnp.zeros((ROWS, LANES), F32)
     left, right, first, last = zero, zero, zero, zero
     for g in range(GROUPS):
-        copies[g].wait()
-        x = buf_ref[g].reshape(GROUP * ROWS, COLS)
+        x = x_ref[g * GROUP:(g + 1) * GROUP].reshape(GROUP * ROWS, COLS)
         xh, xl = split(x)
         res = mm(jnp.concatenate([xh, xl, xh], axis=1), w_ref[0 if g < 2 else 1])
         if g == 2:
@@ -132,31 +143,28 @@
                 first = jnp.where(mine, x[rows, 0:1], first)
                 last = jnp.where(mine, x[rows, COLS - 1:COLS], last)
         if g == 1:
-            sums_ref[:, 0:128] = left
+            edge = jnp.where(lon == 0, first, jnp.where(lon == NLON - 1, last, 0.0))
+            sums_ref[:, 0:128] = jnp.where(lane >= 96, edge, left)
             sums_ref[:, 128:256] = right
-            sums_ref[:, 256:384] = jnp.where(lon == 0, first, jnp.where(lon == NLON - 1, last, 0.0))
             edge_ref[:, 0:128] = first
             edge_ref[:, 128:256] = last
-    sums_ref[:, 384:512] = left
-    sums_ref[:, 512:640] = right
+    sums_ref[:, 256:384] = left
+    sums_ref[:, 384:512] = right
 
 
 HBM = pl.BlockSpec(memory_space=pltpu.HBM)
 ANY = pl.BlockSpec(memory_space=pl.ANY)
 
 
-def row_sums(where, lengths, weights, x):
+def row_sums(where, w, x):
     return pl.pallas_call(
         row_sums_kernel,
-        in_specs=[SMEM, VMEM, VMEM, HBM],
-        out_specs=[VMEM] * 4,
-        out_shape=[jax.ShapeDtypeStruct((ROWS, 640), F32), jax.ShapeDtypeStruct((ROWS, 256), F32),
-                   jax.ShapeDtypeStruct((FIELDS, LANES), F32), jax.ShapeDtypeStruct((8, LANES), F32)],
-        scratch_shapes=[pltpu.VMEM((2, 3 * COLS, 256), BF16), pltpu.VMEM((GROUPS, GROUP, ROWS, COLS), F32),
-                        pltpu.SemaphoreType.DMA((GROUPS,))],
-        compiler_params=pltpu.CompilerParams(vmem_limit_bytes=WHOLE),
+        in_specs=[SMEM, VMEM, VMEM],
+        out_specs=[VMEM] * 2,
+        out_shape=[jax.ShapeDtypeStruct((ROWS, 512), F32), jax.ShapeDtypeStruct((ROWS, 256), F32)],
+        compiler_params=params(),
         name="row_sums",
-    )(where, lengths, weights, x)
+    )(where, w, x)
 
 
 def zonal_difference(x):
@@ -168,7 +176,7 @@
     return 0.5 * (ahead - behind)
 
 
-def local_sums_kernel(where_ref, table_ref, x_ref, out_ref):
+def local_sums_kernel(where_ref, table_ref, x_ref, _, out_ref):
     top = where_ref[0] == 0
     count = 2 * SCALES * GROUP
     shape = (count, LANES)
@@ -226,46 +234,54 @@
                 out_ref[group // 3, side, s, group % 3] = acc[k:k + GROUP]
 
 
-def local_sums(where, table, x):
+def local_sums(where, table, x, before):
     out = pl.pallas_call(
         local_sums_kernel,
-        in_specs=[SMEM, VMEM, VMEM],
+        in_specs=[SMEM, VMEM, VMEM, ANY],
         out_specs=VMEM,
         out_shape=jax.ShapeDtypeStruct((2, 2, SCALES, 3, GROUP, COLS), F32),
         compiler_params=params(),
+        cost_estimate=pl.CostEstimate(flops=6_000_000_000, bytes_accessed=4_000_000, transcendentals=0),
         name="local_sums",
-    )(where, table, x)
+    )(where, table, x, before)
     return out.reshape(2, 2 * HALF_ROWS, COLS)
 
 
-def lon_merge_kernel(where_ref, lanes_ref, own_ref, g1_ref, g2_ref, g3_ref, _, part_ref, mine_ref):
+def lon_merge_kernel(where_ref, lanes_ref, own_ref, g1_ref, g2_ref, g3_ref, _, part_ref, send_ref):
     y = where_ref[1] & 3
+    high = where_ref[1] >= 4
     yf = y.astype(F32)
-    rates = (lanes_ref[0:1, :], lanes_ref[1:2, :])
-    got = (g1_ref, g2_ref, g3_ref)
+    zonal, _ = lane_kinds((1, LANES))
+    lane = iota((1, LANES), 1)
     for tile in range(2):
-        step = lambda n: jnp.exp(-rates[tile] * (COLS * n))
-        base = tile * 384
+        rate = lanes_ref[tile:tile + 1, :]
+        step = lambda n: jnp.exp(-rate * (COLS * n))
+        base = tile * 256
         lanes_l = slice(base, base + 128)
         lanes_r = slice(base + 128, base + 256)
         left_total = step(3.0 - yf) * own_ref[:, lanes_l]
         right_total = step(yf) * own_ref[:, lanes_r]
         left = jnp.zeros((ROWS, LANES), F32)
         right = jnp.zeros((ROWS, LANES), F32)
-        for d, ref in zip((1, 2, 3), got):
-            below = y >= d
+        for d, ref in ((1, g1_ref), (2, g2_ref), (3, g3_ref)):
+            other = y ^ d
+            of = other.astype(F32)
+            below = other < y
             lg, rg = ref[:, lanes_l], ref[:, lanes_r]
-            left = left + jnp.where(below, step(d - 1.0), 0.0) * lg
-            right = right + jnp.where(below, 0.0, step(3.0 - d)) * rg
-            other = jnp.where(below, yf - d, yf - d + 4.0)
-            left_total = left_total + step(3.0 - other) * lg
-            right_total = right_total + step(other) * rg
-        part_ref[:, tile * 256:tile * 256 + 128] = left
-        part_ref[:, tile * 256 + 128:tile * 256 + 256] = right
-        mine_ref[:, lanes_l] = left_total
-        mine_ref[:, lanes_r] = right_total
-    edge = slice(256, 384)
-    mine_ref[:, edge] = own_ref[:, edge] + g1_ref[:, edge] + g2_ref[:, edge] + g3_ref[:, edge]
+            gap = jnp.abs(yf - of) - 1.0
+            left = left + jnp.where(below, step(gap), 0.0) * lg
+            right = right + jnp.where(below, 0.0, step(gap)) * rg
+            left_total = left_total + step(3.0 - of) * lg
+            right_total = right_total + step(of) * rg
+        part_ref[:, lanes_l] = left
+        part_ref[:, lanes_r] = right
+        part_ref[:, 512 + tile * 128:640 + tile * 128] = left_total
+        image = jnp.exp(-rate * (4.0 * COLS + 1.0))
+        if tile == 0:
+            image = jnp.where(zonal, -image, image)
+            image = jnp.where(lane >= 96, -1.0, image)
+            right_total = jnp.where(lane >= 96, 0.0, right_total)
+        send_ref[:, tile * 128:tile * 128 + 128] = jnp.where(high, right_total - image * left_total, left_total)
 
 
 def lon_merge(where, lanes, own, got, after):
@@ -273,13 +289,21 @@
         lon_merge_kernel,
         in_specs=[SMEM] + [VMEM] * 5 + [ANY],
         out_specs=[VMEM, VMEM],
-        out_shape=[jax.ShapeDtypeStruct((ROWS, 512), F32), jax.ShapeDtypeStruct((ROWS, 640), F32)],
+        out_shape=[jax.ShapeDtypeStruct((ROWS, 768), F32), jax.ShapeDtypeStruct((ROWS, 256), F32)],
         compiler_params=params(),
         name="lon_merge",
     )(where, lanes, own, *got, after)
 
 
-def column_sums_kernel(where_ref, table_ref, lanes_ref, part_ref, mine_ref, theirs_ref, edge_ref, local_ref,
+def spread_edges(tile):
+    lane = iota(tile.shape, 1)
+    out = tile
+    for k in range(6):
+        out = jnp.where((lane >> 4) == k, pltpu.roll(tile, (k * 16 + 32) % LANES, 1), out)
+    return out
+
+
+def column_sums_kernel(where_ref, table_ref, lanes_ref, part_ref, theirs_ref, edge_ref, local_ref,
                        carry_ref, keep_ref, send_ref):
     lat, lon = where_ref[0], where_ref[1]
     y = lon & 3
@@ -297,21 +321,19 @@
         rate = rates[tile]
         step = lambda n: jnp.exp(-rate * (COLS * n))
         decay = jnp.exp(-rate)
-        base = tile * 384
-        lanes_l = slice(base, base + 128)
-        lanes_r = slice(base + 128, base + 256)
-        left = part_ref[:, tile * 256:tile * 256 + 128] + (highf * step(yf)) * theirs_ref[:, lanes_l]
-        right = part_ref[:, tile * 256 + 128:tile * 256 + 256] + (lowf * step(3.0 - yf)) * theirs_ref[:, lanes_r]
-        whole = ((highf + lowf * step(4.0)) * mine_ref[:, lanes_l]
-                 + (lowf + highf * step(4.0)) * theirs_ref[:, lanes_l])
+        theirs = theirs_ref[:, tile * 128:tile * 128 + 128]
+        half = part_ref[:, 512 + tile * 128:640 + tile * 128]
+        left = part_ref[:, tile * 256:tile * 256 + 128] + (highf * step(yf)) * theirs
+        right = part_ref[:, tile * 256 + 128:tile * 256 + 256] + (lowf * step(3.0 - yf)) * theirs
+        whole = (highf + lowf * step(4.0)) * half + (highf * step(4.0)) * theirs
         end = step(7.0 - lonf)
         weight_l = jnp.exp(-rate * (ROWS - 1 - row))
         weight_r = jnp.exp(-rate * row)
         carry_l = left
         carry_r = right - (end * decay) * whole
         if tile == 0:
-            v0 = lowf * mine_ref[:, 256:384] + highf * theirs_ref[:, 256:384]
-            vn = highf * mine_ref[:, 256:384] + lowf * theirs_ref[:, 256:384]
+            v0 = spread_edges(lowf * half + highf * theirs)
+            vn = spread_edges(highf * half + lowf * theirs)
             gain = 0.5 * (1.0 - decay * decay) / decay
             initial = -0.5 * (v0 + vn / decay)
             zonal_l = step(lonf) * initial - gain * left + 0.5 * edge_ref[:, 0:128]
@@ -350,16 +372,16 @@
             ref[rows, :] = local_ref[half, rows, :] + pick(0) * fall + pick(1) * rise
 
 
-def column_sums(where, table, lanes, part, mine, theirs, edge, local):
+def column_sums(where, table, lanes, part, theirs, edge, local):
     half = jax.ShapeDtypeStruct((2 * HALF_ROWS, COLS), F32)
     return pl.pallas_call(
         column_sums_kernel,
-        in_specs=[SMEM] + [VMEM] * 7,
+        in_specs=[SMEM] + [VMEM] * 6,
         out_specs=[VMEM] * 3,
         out_shape=[jax.ShapeDtypeStruct((ROWS, 512), F32), half, half],
         compiler_params=params(),
         name="column_sums",
-    )(where, table, lanes, part, mine, theirs, edge, local)
+    )(where, table, lanes, part, theirs, edge, local)
 
 
 def half_rates(where_ref, table_ref):
@@ -407,7 +429,7 @@
     back = right - image * left
     left_ref[...] = left
     for d, ref in ((1, s1_ref), (2, s2_ref), (3, s3_ref)):
-        ref[...] = jnp.where(z + d <= 3, left, back)
+        ref[...] = jnp.where((z ^ d) > z, left, back)
 
 
 def quad_merge(where, table, chip, pair, after):
@@ -433,11 +455,14 @@
     right = jnp.zeros((HALF_ROWS, COLS), F32)
     whole = quad(3.0 - zf) * left_ref[...]
     for d, ref in ((1, g1_ref), (2, g2_ref), (3, g3_ref)):
-        below = z >= d
+        other = z ^ d
+        of = other.astype(F32)
+        below = other < z
+        gap = quad(jnp.abs(zf - of) - 1.0)
         g = ref[...]
-        left = left + jnp.where(below, quad(d - 1.0), 0.0) * g
-        right = right + jnp.where(below, 0.0, quad(3.0 - d)) * g
-        whole = whole + jnp.where(below, quad(3.0 - zf + d), 0.0) * g
+        left = left + jnp.where(below, gap, 0.0) * g
+        right = right + jnp.where(below, 0.0, gap) * g
+        whole = whole + jnp.where(below, quad(3.0 - of), 0.0) * g
     right = right - (quad(3.0 - zf) * jnp.exp(-rate)) * whole
     odd_chip = ((lat >> 1) & 1) == 1
     pair = jnp.exp(-rate * (2 * ROWS))
@@ -469,7 +494,7 @@
     )(where, table, keep, got, pair, left, *gs, after)
 
 
-def local_filter_kernel(starts, where_ref, table_ref, carry_ref, x_ref, out_ref):
+def local_filter_kernel(starts, use_x, use_carry, where_ref, table_ref, carry_ref, x_ref, base_ref, out_ref):
     top = where_ref[0] == 0
     shape = (ROWS, LANES)
     row = fiota(shape, 0)
@@ -482,13 +507,12 @@
     first = source == 0.0
     spread = jnp.abs(fiota((LANES, LANES), 0) - fiota((LANES, LANES), 1))
     tag = lane & 31
-    zeros = jnp.zeros((32, COLS + LANES), BF16)
     corner = jnp.zeros((LANES, LANES), BF16)
-    left_lane = (lane == LANES - 1) | (lane == 1) | (lane == 3)
-    lane_scale = lambda v: jnp.where((v == LANES - 1) | (v == 0), 0, jnp.where(v <= 2, 1, 2))
-    row_scale = lane_scale(lane[:1])
+    left_lane = (lane & 1) == 0
+    row_scale = jnp.minimum(lane[:1] >> 1, 2)
     base = iota((8, LANES), 0)
     column = fiota((8, LANES), 1)
+    tall_lane = iota((PARTS * ROWS, LANES), 1)
 
     def carry_tile(tile, virtual):
         left = carry_ref[:, tile * 256:tile * 256 + 128]
@@ -500,8 +524,10 @@
     def column_pass(matrices, x, carry):
         parts = [split(jnp.where(used, m, 0.0)) for m in matrices]
         lhs = jnp.concatenate([jnp.concatenate([mh, ml[:, :ROWS]], axis=1) for mh, ml in parts], axis=0)
-        xh, xl = split(jnp.concatenate([x, carry], axis=1))
-        rhs = jnp.concatenate([xh, xl, zeros, xh], axis=0)
+        wide = [t for t in (x, carry) if t is not None]
+        wide = wide[0] if len(wide) == 1 else jnp.concatenate(wide, axis=1)
+        xh, xl = split(wide)
+        rhs = jnp.concatenate([xh, xl, jnp.zeros((32, wide.shape[1]), BF16), xh], axis=0)
         return mm(lhs, rhs)
 
     def column_stage(f, wind):
@@ -523,7 +549,7 @@
             w = column_pass(plain, -zonal_difference(x_ref[pair]), carry_tile(0, zonal))
             w = w + column_pass(slopes, second_sign * x_ref[f], carry_tile(0, meridional))
         else:
-            w = column_pass(plain, x_ref[f], carry_tile(1, f - WINDS))
+            w = column_pass(plain, x_ref[f] if use_x else None, carry_tile(1, f - WINDS) if use_carry else None)
         return rates, w
 
     def row_stage(rates, w):
@@ -540,93 +566,94 @@
         return outs
 
     def carry_stage(rates, w, outs):
+        sums, outer = None, jnp.zeros((ROWS, LANES), F32)
         for s in range(SCALES):
-            rows = slice(s * ROWS, (s + 1) * ROWS)
-            moved = pltpu.roll(w[rows, COLS:], (LANES - 30 * s - 1) % LANES, 1)
-            turned = outs[s] if s == 0 else pltpu.roll(outs[s], 2 * s, 1)
             here = row_scale == s
-            outer = moved if s == 0 else jnp.where(here, moved, outer)
-            sums = turned if s == 0 else jnp.where(here, turned, sums)
+            if use_carry:
+                moved = w[s * ROWS:(s + 1) * ROWS, w.shape[1] - LANES:]
+                moved = moved if s == 0 else pltpu.roll(moved, LANES - 30 * s, 1)
+                outer = jnp.where(here, moved, outer)
+            if use_x:
+                turned = pltpu.roll(outs[s], 2 * s + 1, 1)
+                sums = turned if s == 0 else jnp.where(here, turned, sums)
         rate_row = jnp.where(row_scale == 0, rates[0], jnp.where(row_scale == 1, rates[1], rates[2]))
         jump = jnp.exp(-rate_row * LANES)
-        block = [sums[b * ROWS:(b + 1) * ROWS] for b in range(PARTS)]
-        from_left = [outer]
+        from_left, from_right = [outer], [outer]
         for b in range(PARTS - 1):
-            from_left.append(block[b] + jump * from_left[-1])
-        from_right = [outer]
-        for b in range(PARTS - 1, 0, -1):
-            from_right.append(block[b] + jump * from_right[-1])
+            ahead, behind = jump * from_left[-1], jump * from_right[-1]
+            if use_x:
+                ahead = ahead + sums[b * ROWS:(b + 1) * ROWS]
+                behind = behind + sums[(PARTS - 1 - b) * ROWS:(PARTS - b) * ROWS]
+            from_left.append(ahead)
+            from_right.append(behind)
         carries = [jnp.where(left_lane, from_left[b], from_right[PARTS - 1 - b]) for b in range(PARTS)]
-        ch, cl = split(jnp.concatenate(carries, axis=0))
-        low_rate = jnp.where(base == 0, rates[0], jnp.where(base <= 2, rates[1], rates[2]))
-        low_left = (base == 1) | (base == 3)
-        low = jnp.where(base <= 4, jnp.exp(-low_rate * jnp.where(low_left, column + 1.0, LANES - column)), 0.0)
-        high = jnp.where(base == 7, jnp.exp(-rates[0] * (column + 1.0)), 0.0)
-        pad = jnp.zeros((8, LANES), F32)
-        lh, ll = split(jnp.concatenate([low, pad], axis=0))
-        hh, hl = split(jnp.concatenate([pad, high], axis=0))
-        gap_rows = jnp.zeros((96, LANES), BF16)
-        bh = jnp.concatenate([lh, gap_rows, hh], axis=0)
-        bl = jnp.concatenate([ll, gap_rows, hl], axis=0)
-        rhs = jnp.concatenate([jnp.concatenate([bh, bl], axis=1), jnp.concatenate([bh, corner], axis=1)], axis=0)
-        return jnp.concatenate([ch, cl], axis=1), rhs
+        carries = jnp.where(tall_lane < 6, jnp.concatenate(carries, axis=0), 0.0)
+        ch = carries.astype(BF16).astype(F32)
+        lhs = (ch + pltpu.roll(carries - ch, 8, 1)).astype(BF16)[:, :16]
+        base_rate = jnp.where(base < 2, rates[0], jnp.where(base < 4, rates[1], rates[2]))
+        powers = jnp.exp(-base_rate * jnp.where((base & 1) == 0, column + 1.0, LANES - column))
+        powers = jnp.where(base < 6, powers, 0.0)
+        ph = powers.astype(BF16).astype(F32)
+        rhs = jnp.concatenate([jnp.concatenate([ph, powers - ph], axis=1),
+                               jnp.concatenate([ph, jnp.zeros((8, LANES), F32)], axis=1)], axis=0)
+        return lhs, rhs.astype(BF16)
 
     for start in starts:
         wind = start < WINDS
         fields = [start + i for i in range(GROUP)]
         columns = [column_stage(f, wind) for f in fields]
-        outs = [row_stage(*c) for c in columns]
+        outs = [row_stage(*c) if use_x else None for c in columns]
         ranks = [carry_stage(*c, o) for c, o in zip(columns, outs)]
         for f, o, (lhs, rhs) in zip(fields, outs, ranks):
             out = mm(lhs, rhs)
-            total = (o[0] + o[1]) + (o[2] + out[:, :LANES]) + out[:, LANES:]
+            total = out[:, :LANES] + out[:, LANES:]
+            if use_x:
+                total = (o[0] + o[1]) + (o[2] + total)
             for b in range(PARTS):
-                out_ref[f - starts[0], :, b * LANES:(b + 1) * LANES] = total[b * ROWS:(b + 1) * ROWS]
-
-
-def local_filter(where, table, carry, x, first, count, before, through=None):
+                lanes = slice(b * LANES, (b + 1) * LANES)
+                part = total[b * ROWS:(b + 1) * ROWS]
+                if base_ref is not None:
+                    part = part + base_ref[f - starts[0], :, lanes]
+                out_ref[f - starts[0], :, lanes] = part
+
+
+def local_filter(where, table, carry, x, first, count, before, base=None):
     starts = tuple(range(first, first + count, GROUP))
-    operands = [where, table, carry, x, before]
-    in_specs = [SMEM] + [VMEM] * 3 + [ANY]
-    out_specs = [VMEM]
-    out_shape = [jax.ShapeDtypeStruct((count, ROWS, COLS), F32)]
-    aliases = {}
-    if through is not None:
-        operands.append(through)
-        in_specs.append(ANY)
-        out_specs.append(ANY)
-        out_shape.append(jax.ShapeDtypeStruct(through.shape, through.dtype))
-        aliases = {5: 1}
+    use_x, use_carry = base is None, carry is not None
+    names = ["where", "table"] + ["carry"] * use_carry + ["x"] * use_x + ["base"] * (base is not None) + ["before"]
+    arrays = {"where": where, "table": table, "carry": carry, "x": x, "base": base, "before": before}
+    specs = {"where": SMEM, "before": ANY}
 
     def body(*refs):
-        local_filter_kernel(starts, *refs[:4], refs[len(in_specs)])
+        by_name = dict(zip(names, refs))
+        local_filter_kernel(starts, use_x, use_carry, by_name["where"], by_name["table"], by_name.get("carry"),
+                            by_name.get("x"), by_name.get("base"), refs[len(names)])
 
     return pl.pallas_call(
         body,
-        in_specs=in_specs,
-        out_specs=out_specs,
-        out_shape=out_shape,
-        input_output_aliases=aliases,
-        compiler_params=params(),
-        cost_estimate=pl.CostEstimate(flops=count * 400_000_000, bytes_accessed=count * 150_000, transcendentals=0),
+        in_specs=[specs.get(n, VMEM) for n in names],
+        out_specs=VMEM,
+        out_shape=jax.ShapeDtypeStruct((count, ROWS, COLS), F32),
+        compiler_params=params(),
+        cost_estimate=pl.CostEstimate(flops=count * 300_000_000, bytes_accessed=count * 150_000, transcendentals=0),
         name="local_filter",
-    )(*operands)
-
-
-def finish_kernel(bounds, where_ref, table_ref, own_ref, got_ref, *refs):
-    z_refs, (out_ref, buf_ref, sem) = refs[:len(bounds)], refs[len(bounds):]
+    )(*[arrays[n] for n in names])
+
+
+def finish_kernel(own_half, where_ref, table_ref, carry_ref, z0_ref, z1_ref, z2_ref, *refs):
+    out_ref, buf_ref, sem = refs[-3:]
     core = where_ref[0] & 1
+    half = core if own_half else 1 - core
+    z_refs = (z0_ref, z0_ref, z1_ref, z1_ref, z2_ref, z2_ref)
     row = fiota((8, LANES), 0)
     up_steps, down_steps = row + 1.0, 8.0 - row
     copies = []
-    for group in range(GROUPS):
-        mine = core == group // 3
-        part = group % 3
-        k = max(i for i, b in enumerate(bounds) if b <= group * GROUP)
-        tables = [jnp.where(mine, own_ref[side, s, part], got_ref[side, s, part]) for side in range(2) for s in range(SCALES)]
+    for part in range(3):
+        tables = [carry_ref[side, s, part] for side in range(2) for s in range(SCALES)]
+        start = pl.multiple_of((half * 3 + part) * GROUP, GROUP)
+        group_facts = table_ref[pl.ds(start, GROUP), :]
         for i in range(GROUP):
-            f = group * GROUP + i
-            facts = table_ref[f:f + 1, :]
+            facts = group_facts[i:i + 1, :]
             ups = []
             for s in range(SCALES):
                 r = jnp.broadcast_to(facts[:, s:s + 1], (8, LANES))
@@ -639,58 +666,65 @@
                 ups.append((jnp.concatenate(up, axis=0), jnp.concatenate(down, axis=0)))
             for b in range(PARTS):
                 lanes = slice(b * LANES, (b + 1) * LANES)
-                total = z_refs[k][f - bounds[k], :, lanes]
+                total = jnp.where(half == 0, z_refs[part][part % 2 * GROUP + i, :, lanes],
+                                  z_refs[3 + part][(3 + part) % 2 * GROUP + i, :, lanes])
                 for s in range(SCALES):
                     total = total + ups[s][0] * tables[s][i:i + 1, lanes] + ups[s][1] * tables[SCALES + s][i:i + 1, lanes]
-                buf_ref[group, i, :, lanes] = total
-        copy = pltpu.make_async_copy(buf_ref.at[group], out_ref.at[pl.ds(group * GROUP, GROUP)], sem.at[group])
+                buf_ref[part, i, :, lanes] = total
+        copy = pltpu.make_async_copy(buf_ref.at[part], out_ref.at[pl.ds(start, GROUP)], sem.at[part])
         copy.start()
         copies.append(copy)
     for copy in copies:
         copy.wait()
 
 
-def finish(where, table, own, got, parts):
-    shaped = lambda t: t.reshape(2, SCALES, 3, GROUP, COLS)
-    bounds = [sum(p.shape[0] for p in parts[:i]) for i in range(len(parts))]
-    return pl.pallas_call(
-        functools.partial(finish_kernel, bounds),
-        in_specs=[SMEM] + [VMEM] * (3 + len(parts)),
+def finish(own_half, where, table, carry, parts, out=None):
+    operands = [where, table, carry.reshape(2, SCALES, 3, GROUP, COLS), *parts]
+    in_specs = [SMEM] + [VMEM] * 5
+    aliases = {}
+    if out is not None:
+        operands.append(out)
+        in_specs.append(HBM)
+        aliases = {6: 0}
+    return pl.pallas_call(
+        functools.partial(finish_kernel, own_half),
+        in_specs=in_specs,
         out_specs=HBM,
         out_shape=jax.ShapeDtypeStruct((FIELDS, ROWS, COLS), F32),
-        scratch_shapes=[pltpu.VMEM((GROUPS, GROUP, ROWS, COLS), F32), pltpu.SemaphoreType.DMA((GROUPS,))],
-        compiler_params=params(),
+        scratch_shapes=[pltpu.VMEM((3, GROUP, ROWS, COLS), F32), pltpu.SemaphoreType.DMA((3,))],
+        input_output_aliases=aliases,
+        compiler_params=params(),
+        cost_estimate=pl.CostEstimate(flops=1_000_000_000, bytes_accessed=4_000_000, transcendentals=0),
         name="finish",
-    )(where, table, shaped(own), shaped(got), *parts)
+    )(*operands)
+
+
+def partner(axis, count, bit):
+    return functools.partial(lax.ppermute, axis_name=axis, perm=[(i, i ^ bit) for i in range(count)])
 
 
 def shards(x, lengths, weights):
     where = jnp.stack([lax.axis_index("lat"), lax.axis_index("lon")]).astype(jnp.int32)
-    sums, edge, table, lanes = row_sums(where, lengths.T, weights.T, x)
-    got = []
-    for d in (1, 2, 3):
-        perm = [(h * 4 + i, h * 4 + (i + d) % 4) for h in range(2) for i in range(4)]
-        got.append(lax.ppermute(sums, "lon", perm))
-    local = local_sums(where, table, x)
-    part, mine = lon_merge(where, lanes, sums, got, local)
-    theirs = lax.ppermute(mine, "lon", [(i, i ^ 4) for i in range(NLON)])
-    carry, keep, send = column_sums(where, table, lanes, part, mine, theirs, edge, local)
-    core_pairs = [(i, i ^ 1) for i in range(NLAT)]
-    got_core = lax.ppermute(send, "lat", core_pairs)
+    table, lanes, w = tables(lengths.T, weights.T)
+    sums, edge = row_sums(where, w, x)
+    got = [partner("lon", NLON, d)(sums) for d in (1, 2, 3)]
+    early = local_filter(where, table, None, x, 32, 16, sums)
+    part, half = lon_merge(where, lanes, sums, got, early)
+    theirs = partner("lon", NLON, 4)(half)
+    local = local_sums(where, table, x, part)
+    carry, keep, send = column_sums(where, table, lanes, part, theirs, edge, local)
+    got_core = partner("lat", NLAT, 1)(send)
     chip = chip_merge(where, table, keep, got_core)
-    pair = lax.ppermute(chip, "lat", [(i, i ^ 2) for i in range(NLAT)])
-    (z0,) = local_filter(where, table, carry, x, 0, 16, chip)
-    left, s1, s2, s3 = quad_merge(where, table, chip, pair, z0)
-    quad = lambda t, d: lax.ppermute(t, "lat", [(i, (i + 4 * d) % NLAT) for i in range(NLAT)])
-    g1 = quad(s1, 1)
-    z1, s2 = local_filter(where, table, carry, x, 16, 16, left, s2)
-    g2 = quad(s2, 2)
-    z2, s3 = local_filter(where, table, carry, x, 32, 8, z1, s3)
-    g3 = quad(s3, 3)
-    (z3,) = local_filter(where, table, carry, x, 40, 8, z2)
-    own, other = lat_carry(where, table, keep, got_core, pair, left, (g1, g2, g3), z3)
-    got_carry = lax.ppermute(other, "lat", core_pairs)
-    return finish(where, table, own, got_carry, (z0, z1, z2, z3))
+    pair = partner("lat", NLAT, 2)(chip)
+    z0 = local_filter(where, table, carry, x, 0, 16, chip)
+    left, *sends = quad_merge(where, table, chip, pair, z0)
+    gs = [partner("lat", NLAT, 4 * d)(t) for d, t in zip((1, 2, 3), sends)]
+    z1 = local_filter(where, table, carry, x, 16, 16, left)
+    z2 = local_filter(where, table, carry, x, 32, 16, z1, early)
+    own, other = lat_carry(where, table, keep, got_core, pair, left, gs, z2)
+    got_carry = partner("lat", NLAT, 1)(other)
+    out = finish(True, where, table, own, (z0, z1, z2))
+    return finish(False, where, table, got_carry, (z0, z1, z2), out)
 
 
 def solution(mesh):

time: 61.5 us -> 56 us (0.911)
  waiting for transfers between devices: 7.9 us -> 3.73 us
  starting transfers between devices: 19.5 us -> 17.5 us
    ppermute x10, waiting for transfers between devices: 7.9 us -> 3.73 us  [the longest x1 1.13 us: shards(): pair = partner('lat', NLAT, 2)(chip)]
    ppermute x10, starting transfers between devices: 19.5 us -> 17.5 us  [the longest x3 5.01 us: shards(): gs = [partner('lat', NLAT, 4 * d)(t) for d, t in zip((1, 2, 3), sends)]]
    unnamed x14 -> x8, local copies, waits for them, and re-layouts: 2.76 us -> 3.36 us
    pallas_call x8 -> x10, Pallas kernels: 27.3 us -> 27.9 us  [the longest x4 14.7 us: local_filter(): pl.pallas_call(body, in_specs=[specs.get(n, VMEM) for n in names], out_sp...]
  transfers between devices with their start and end apart: 10 -> 10, of which waited for: 6 -> 4; matrix products, arithmetic and copies ran while one was open for 0% -> 0% of each run, Pallas kernels for 27% -> 39%
where the time goes in v3:
time: 56 us; the launch traced here: 55.8 us
  Pallas kernels  30.8 us (55%)
  starting transfers between devices  17.5 us (31%)
  waiting for transfers between devices  3.73 us (7%)
  local copies, waits for them, and re-layouts  3.36 us (6%)
    pallas_call x4, Pallas kernels, local_filter(): pl.pallas_call(body, in_specs=[specs.get(n, VMEM) for n in names], out_sp...  14.7 us
    pallas_call x2, Pallas kernels, finish(): pl.pallas_call(functools.partial(finish_kernel, own_half), in_specs=in_sp...  5.22 us
    ppermute x3, starting transfers between devices, shards(): gs = [partner('lat', NLAT, 4 * d)(t) for d, t in zip((1, 2, 3), sends)]  5.01 us
    ppermute x3, starting transfers between devices, shards(): got = [partner('lon', NLON, d)(sums) for d in (1, 2, 3)]  4.31 us
    pallas_call x1, Pallas kernels, local_sums(): pl.pallas_call(local_sums_kernel, in_specs=[SMEM, VMEM, VMEM, ANY], out_s...  4.29 us
    unnamed x8, local copies, waits for them, and re-layouts  3.36 us
    ppermute x1, starting transfers between devices, shards(): got_core = partner('lat', NLAT, 1)(send)  3.16 us
    ppermute x1, starting transfers between devices, shards(): theirs = partner('lon', NLON, 4)(half)  2.82 us
  transfers between devices with their start and end apart: 10, of which 4 were waited for; matrix products, arithmetic and copies ran while one was open for 0% of the time, Pallas kernels for 39%

profile of v3, /device:TPU:1, one launch (start us, length us, event | category | flops | bytes accessed | tf_op | source)
XLA Modules:
  0.0 55.8 jit_solution(3774398327468690098)
XLA Ops:
  0.0 0.1 pad_add_fusion.where_ref.refs_0_
  0.1 0.0 copy-start.2
  0.1 0.7 %copy-done.2 = f32[48,3]{0,1:T(4,128)S(1)} copy-done((f32[48,3]{0,1:T(4,128)S(1)}, f32[48,3]{0,1:T(4,128)}, u32[]{:S(2)}) %copy-start.2) | copy-done | bytes 600
  0.8 0.0 copy-start.3
  0.8 0.7 %copy-done.3 = f32[48,3]{0,1:T(4,128)S(1)} copy-done((f32[48,3]{0,1:T(4,128)S(1)}, f32[48,3]{0,1:T(4,128)}, u32[]{:S(2)}) %copy-start.3) | copy-done | bytes 600
  1.4 0.4 tables.1
  1.9 0.0 copy-start
  1.9 2.0 %copy-done = f32[48,48,384]{2,1,0:T(8,128)S(1)} copy-done((f32[48,48,384]{2,1,0:T(8,128)S(1)}, f32[48,48,384]{2,1,0:T(8,128)}, u32[]{:S(2)}) %copy-start) | copy-done | bytes 3538968
  3.9 0.0 copy-start.1
  3.9 2.3 %row_sums.1 = (f32[48,512]{1,0:T(8,128)S(1)}, f32[48,256]{1,0:T(8,128)S(1)}) custom-call(s32[2]{0:T(128)S(1)} %pad_add_fusion.where_ref.refs_0_, bf16[2,1152,256]{2,1,0:T(8,128)(2,1)S(1)} %get-tuple-element.23.w_ref, f32[48,48,384]{2,1,0:T(8,128)S(1)} %copy-done), custom_call_target="tpu_custom_call" | custom-call | tf_op jit(solution)/shard_map/row_sums/pallas_call | solution.py:160
  6.2 3.6 %collective-permute-start.2 = (f32[48,512]{1,0:T(8,128)S(1)}, f32[48,512]{1,0:T(8,128)S(1)}, u32[]{:S(2)}, u32[]{:S(2)}) collective-permute-start(f32[48,512]{1,0:T(8,128)S(1)} %get-tuple-element.24.refs_3_.own_ref), channel_id=1, source_target_pairs={{0,3},{1,2},{2,1},{3,0},{4,7},{5,6},{6,5},{7,4},{8,11},{9,10},{10,... | collective-permute-start | bytes 294920 | tf_op jit(solution)/shard_map/ppermute | solution.py:710
  9.8 0.3 collective-permute-start.1
  10.2 0.3 collective-permute-start
  10.5 0.0 copy-done.1
  10.5 3.6 %local_filter.4._.refs_3_ = f32[16,48,384]{2,1,0:T(8,128)S(1)} custom-call(s32[2]{0:T(128)S(1)} %pad_add_fusion.where_ref.refs_0_, f32[48,128]{1,0:T(8,128)S(1)} %get-tuple-element.21.refs_1_.table_ref, f32[48,48,384]{2,1,0:T(8,128)S(1)} %copy-done.1, f32[48,512]{1,0:T(8,128)S(1)} %get-tuple-element.24.refs_3_.own_ref), custom_call_target="tpu_custom_call" | custom-call | flops 4800000000 | bytes 2400000 | tf_op jit(solution)/shard_map/local_filter/pallas_call | solution.py:632
  14.1 0.0 collective-permute-done.2.g3_ref
  14.2 0.6 %collective-permute-done.1.g2_ref = f32[48,512]{1,0:T(8,128)S(1)} collective-permute-done((f32[48,512]{1,0:T(8,128)S(1)}, f32[48,512]{1,0:T(8,128)S(1)}, u32[]{:S(2)}, u32[]{:S(2)}) %collective-permute-start.1) | collective-permute-done | bytes 98336 | tf_op jit(solution)/shard_map/ppermute | solution.py:710
  14.8 0.0 collective-permute-done.g1_ref
  14.8 0.6 %lon_merge.1 = (f32[48,768]{1,0:T(8,128)S(1)}, f32[48,256]{1,0:T(8,128)S(1)}) custom-call(s32[2]{0:T(128)S(1)} %pad_add_fusion.where_ref.refs_0_, f32[8,128]{1,0:T(8,128)S(1)} %get-tuple-element.22.lanes_ref, f32[48,512]{1,0:T(8,128)S(1)} %get-tuple-element.24.refs_3_.own_ref, f32[48,512]{1,0:T(8,128)S(1)} %collective-permute-done.g1_ref, ...), custom_call_target="tpu_custom_call" | custom-call | tf_op jit(solution)/shard_map/lon_merge/pallas_call | solution.py:288
  15.4 2.8 %collective-permute-start.3 = (f32[48,256]{1,0:T(8,128)S(1)}, f32[48,256]{1,0:T(8,128)S(1)}, u32[]{:S(2)}, u32[]{:S(2)}) collective-permute-start(f32[48,256]{1,0:T(8,128)S(1)} %get-tuple-element.26), channel_id=1, source_target_pairs={{0,4},{1,5},{2,6},{3,7},{4,0},{5,1},{6,2},{7,3},{8,12},{9,13},{10,... | collective-permute-start | bytes 147464 | tf_op jit(solution)/shard_map/ppermute | solution.py:713
  18.2 4.3 %local_sums.1 = f32[2,2,3,3,8,384]{5,4,3,2,1,0:T(8,128)S(1)} custom-call(s32[2]{0:T(128)S(1)} %pad_add_fusion.where_ref.refs_0_, f32[48,128]{1,0:T(8,128)S(1)} %get-tuple-element.21.refs_1_.table_ref, f32[48,48,384]{2,1,0:T(8,128)S(1)} %copy-done.1, f32[48,768]{1,0:T(8,128)S(1)} %get-tuple-element.25._.part_ref), custom_call_target="tpu_custom_call" | custom-call | flops 6000000000 | bytes 4000000 | tf_op jit(solution)/shard_map/local_sums/pallas_call | solution.py:238
  22.5 0.0 collective-permute-done.3.theirs_ref
  22.6 1.0 %column_sums.1 = (f32[48,512]{1,0:T(8,128)S(1)}, f32[144,384]{1,0:T(8,128)S(1)}, f32[144,384]{1,0:T(8,128)S(1)}) custom-call(s32[2]{0:T(128)S(1)} %pad_add_fusion.where_ref.refs_0_, f32[48,128]{1,0:T(8,128)S(1)} %get-tuple-element.21.refs_1_.table_ref, f32[8,128]{1,0:T(8,128)S(1)} %get-tuple-element.22.lanes_ref, ...), custom_call_target="tpu_custom_call" | custom-call | tf_op jit(solution)/shard_map/column_sums/pallas_call | solution.py:377
  23.5 3.2 %collective-permute-start.4 = (f32[144,384]{1,0:T(8,128)S(1)}, f32[144,384]{1,0:T(8,128)S(1)}, u32[]{:S(2)}, u32[]{:S(2)}) collective-permute-start(f32[144,384]{1,0:T(8,128)S(1)} %get-tuple-element.29), channel_id=1, source_target_pairs={{0,8},{8,0},{16,24},{24,16},{32,40},{40,32},{48,56},{56,48},{64,72... | collective-permute-start | bytes 663560 | tf_op jit(solution)/shard_map/ppermute | solution.py:716
  26.7 1.1 %collective-permute-done.4.got_ref = f32[144,384]{1,0:T(8,128)S(1)} collective-permute-done((f32[144,384]{1,0:T(8,128)S(1)}, f32[144,384]{1,0:T(8,128)S(1)}, u32[]{:S(2)}, u32[]{:S(2)}) %collective-permute-start.4) | collective-permute-done | bytes 221216 | tf_op jit(solution)/shard_map/ppermute | solution.py:716
  27.8 0.7 %chip_merge.1.refs_4_.chip_ref = f32[144,384]{1,0:T(8,128)S(1)} custom-call(s32[2]{0:T(128)S(1)} %pad_add_fusion.where_ref.refs_0_, f32[48,128]{1,0:T(8,128)S(1)} %get-tuple-element.21.refs_1_.table_ref, f32[144,384]{1,0:T(8,128)S(1)} %get-tuple-element.28.keep_ref, f32[144,384]{1,0:T(8,128)S(1)} %collective-permute-done.4.got_ref), custom_call_target="tpu_custom_call" | custom-call | tf_op jit(solution)/shard_map/chip_merge/pallas_call | solution.py:408
  28.5 0.6 %collective-permute-start.5 = (f32[144,384]{1,0:T(8,128)S(1)}, f32[144,384]{1,0:T(8,128)S(1)}, u32[]{:S(2)}, u32[]{:S(2)}) collective-permute-start(f32[144,384]{1,0:T(8,128)S(1)} %chip_merge.1.refs_4_.chip_ref), channel_id=1, source_target_pairs={{0,16},{8,24},{16,0},{24,8},{32,48},{40,56},{48,32},{56,40},{64,80... | collective-permute-start | bytes 663560 | tf_op jit(solution)/shard_map/ppermute | solution.py:718
  29.1 5.2 %local_filter.5._.z0_ref = f32[16,48,384]{2,1,0:T(8,128)S(1)} custom-call(s32[2]{0:T(128)S(1)} %pad_add_fusion.where_ref.refs_0_, f32[48,128]{1,0:T(8,128)S(1)} %get-tuple-element.21.refs_1_.table_ref, f32[48,512]{1,0:T(8,128)S(1)} %get-tuple-element.30.refs_2_, f32[48,48,384]{2,1,0:T(8,128)S(1)} %copy-done.1, f32[144,384]{1,0:T(8,128)S(1)} %chip_merge.1.refs_4_.chip_ref), custom_call_target="tpu_custom_call" | custom-call | flops 4800000000 | bytes 2400000 | tf_op jit(solution)/shard_map/local_filter/pallas_call | solution.py:632
  34.3 1.1 %collective-permute-done.5.pair_ref = f32[144,384]{1,0:T(8,128)S(1)} collective-permute-done((f32[144,384]{1,0:T(8,128)S(1)}, f32[144,384]{1,0:T(8,128)S(1)}, u32[]{:S(2)}, u32[]{:S(2)}) %collective-permute-start.5) | collective-permute-done | bytes 221216 | tf_op jit(solution)/shard_map/ppermute | solution.py:718
  35.4 0.7 %quad_merge.1 = (f32[72,384]{1,0:T(8,128)S(1)}, f32[72,384]{1,0:T(8,128)S(1)}, f32[72,384]{1,0:T(8,128)S(1)}, f32[72,384]{1,0:T(8,128)S(1)}) custom-call(s32[2]{0:T(128)S(1)} %pad_add_fusion.where_ref.refs_0_, f32[48,128]{1,0:T(8,128)S(1)} %get-tuple-element.21.refs_1_.table_ref, f32[144,384]{1,0:T(8,128)S(1)} %chip_merge.1.refs_4_.chip_ref, ...), custom_call_target="tpu_custom_call" | custom-call | tf_op jit(solution)/shard_map/quad_merge/pallas_call | solution.py:437
  36.2 1.7 %collective-permute-start.6 = (f32[72,384]{1,0:T(8,128)S(1)}, f32[72,384]{1,0:T(8,128)S(1)}, u32[]{:S(2)}, u32[]{:S(2)}) collective-permute-start(f32[72,384]{1,0:T(8,128)S(1)} %get-tuple-element.32), channel_id=1, source_target_pairs={{0,32},{8,40},{16,48},{24,56},{32,0},{40,8},{48,16},{56,24},{64,96... | collective-permute-start | bytes 331784 | tf_op jit(solution)/shard_map/ppermute | solution.py:721
  37.9 3.3 %collective-permute-start.7 = (f32[72,384]{1,0:T(8,128)S(1)}, f32[72,384]{1,0:T(8,128)S(1)}, u32[]{:S(2)}, u32[]{:S(2)}) collective-permute-start(f32[72,384]{1,0:T(8,128)S(1)} %get-tuple-element.33), channel_id=1, source_target_pairs={{0,64},{8,72},{16,80},{24,88},{32,96},{40,104},{48,112},{56,120},{... | collective-permute-start | bytes 331784 | tf_op jit(solution)/shard_map/ppermute | solution.py:721
  41.2 0.0 collective-permute-start.8
  41.2 3.8 %local_filter.6.refs_4_.z1_ref = f32[16,48,384]{2,1,0:T(8,128)S(1)} custom-call(s32[2]{0:T(128)S(1)} %pad_add_fusion.where_ref.refs_0_, f32[48,128]{1,0:T(8,128)S(1)} %get-tuple-element.21.refs_1_.table_ref, f32[48,512]{1,0:T(8,128)S(1)} %get-tuple-element.30.refs_2_, f32[48,48,384]{2,1,0:T(8,128)S(1)} %copy-done.1, ...), custom_call_target="tpu_custom_call" | custom-call | flops 4800000000 | bytes 2400000 | tf_op jit(solution)/shard_map/local_filter/pallas_call | solution.py:632
  45.0 2.1 %local_filter.7._.z2_ref = f32[16,48,384]{2,1,0:T(8,128)S(1)} custom-call(s32[2]{0:T(128)S(1)} %pad_add_fusion.where_ref.refs_0_, f32[48,128]{1,0:T(8,128)S(1)} %get-tuple-element.21.refs_1_.table_ref, f32[48,512]{1,0:T(8,128)S(1)} %get-tuple-element.30.refs_2_, f32[16,48,384]{2,1,0:T(8,128)S(1)} %local_filter.4._.refs_3_, ...), custom_call_target="tpu_custom_call" | custom-call | flops 4800000000 | bytes 2400000 | tf_op jit(solution)/shard_map/local_filter/pallas_call | solution.py:632
  47.0 0.0 collective-permute-done.6.g1_ref
  47.0 0.0 collective-permute-done.7.g2_ref
  47.0 0.8 %collective-permute-done.8.g3_ref = f32[72,384]{1,0:T(8,128)S(1)} collective-permute-done((f32[72,384]{1,0:T(8,128)S(1)}, f32[72,384]{1,0:T(8,128)S(1)}, u32[]{:S(2)}, u32[]{:S(2)}) %collective-permute-start.8) | collective-permute-done | bytes 110624 | tf_op jit(solution)/shard_map/ppermute | solution.py:721
  47.9 0.9 %lat_carry.1 = (f32[144,384]{1,0:T(8,128)S(1)}, f32[144,384]{1,0:T(8,128)S(1)}) custom-call(s32[2]{0:T(128)S(1)} %pad_add_fusion.where_ref.refs_0_, f32[48,128]{1,0:T(8,128)S(1)} %get-tuple-element.21.refs_1_.table_ref, f32[144,384]{1,0:T(8,128)S(1)} %get-tuple-element.28.keep_ref, f32[144,384]{1,0:T(8,128)S(1)} %collective-permute-done.4.got_ref, ...), custom_call_target="tpu_custom_call" | custom-call | tf_op jit(solution)/shard_map/lat_carry/pallas_call | solution.py:487
  48.7 1.6 %collective-permute-start.9 = (f32[144,384]{1,0:T(8,128)S(1)}, f32[144,384]{1,0:T(8,128)S(1)}, u32[]{:S(2)}, u32[]{:S(2)}) collective-permute-start(f32[144,384]{1,0:T(8,128)S(1)} %get-tuple-element.35), channel_id=1, source_target_pairs={{0,8},{8,0},{16,24},{24,16},{32,40},{40,32},{48,56},{56,48},{64,72... | collective-permute-start | bytes 663560 | tf_op jit(solution)/shard_map/ppermute | solution.py:725
  50.4 2.6 %finish.2.refs_0_ = f32[48,48,384]{2,1,0:T(8,128)} custom-call(s32[2]{0:T(128)S(1)} %pad_add_fusion.where_ref.refs_0_, f32[48,128]{1,0:T(8,128)S(1)} %get-tuple-element.21.refs_1_.table_ref, f32[2,3,3,8,384]{4,3,2,1,0:T(8,128)S(1)} %bitcast.8, f32[16,48,384]{2,1,0:T(8,128)S(1)} %local_filter.5._.z0_ref, f32[16,48,384]{2,1,0:T(8,128)S(1)} %local_filter.6.refs_4_.z1_ref, ...), custom_call_target="tpu_custom_call" | custom-call | flops 1000000000 | bytes 4000000 | tf_op jit(solution)/shard_map/finish/pallas_call | solution.py:689
  53.0 0.0 collective-permute-done.9
  53.0 2.6 %finish.3 = f32[48,48,384]{2,1,0:T(8,128)} custom-call(s32[2]{0:T(128)S(1)} %pad_add_fusion.where_ref.refs_0_, f32[48,128]{1,0:T(8,128)S(1)} %get-tuple-element.21.refs_1_.table_ref, f32[2,3,3,8,384]{4,3,2,1,0:T(8,128)S(1)} %bitcast.9, f32[16,48,384]{2,1,0:T(8,128)S(1)} %local_filter.5._.z0_ref, ...), custom_call_target="tpu_custom_call", output_to_operand_aliasing={{}: (6, {})} | custom-call | flops 1000000000 | bytes 4000000 | tf_op jit(solution)/shard_map/finish/pallas_call | solution.py:689
Async XLA Ops:
  0.1 0.7 %copy-start.2 = (f32[48,3]{0,1:T(4,128)S(1)}, f32[48,3]{0,1:T(4,128)}, u32[]{:S(2)}) copy-start(f32[48,3]{0,1:T(4,128)} %param.4) | copy-start | bytes 1732
  0.8 0.7 %copy-start.3 = (f32[48,3]{0,1:T(4,128)S(1)}, f32[48,3]{0,1:T(4,128)}, u32[]{:S(2)}) copy-start(f32[48,3]{0,1:T(4,128)} %param.5) | copy-start | bytes 1732
  1.9 2.0 %copy-start = (f32[48,48,384]{2,1,0:T(8,128)S(1)}, f32[48,48,384]{2,1,0:T(8,128)}, u32[]{:S(2)}) copy-start(f32[48,48,384]{2,1,0:T(8,128)} %refs_3_.3) | copy-start | bytes 10616836
  3.9 6.6 %copy-start.1 = (f32[48,48,384]{2,1,0:T(8,128)S(1)}, f32[48,48,384]{2,1,0:T(8,128)}, u32[]{:S(2)}) copy-start(f32[48,48,384]{2,1,0:T(8,128)} %refs_3_.3) | copy-start | bytes 10616836
  6.2 8.0 %collective-permute-start.2 = (f32[48,512]{1,0:T(8,128)S(1)}, f32[48,512]{1,0:T(8,128)S(1)}, u32[]{:S(2)}, u32[]{:S(2)}) collective-permute-start(f32[48,512]{1,0:T(8,128)S(1)} %get-tuple-element.24.refs_3_.own_ref), channel_id=1, source_target_pairs={{0,3},{1,2},{2,1},{3,0},{4,7},{5,6},{6,5},{7,4},{8,11},{9,10},{10,... | collective-permute-start | bytes 294920 | tf_op jit(solution)/shard_map/ppermute | solution.py:710
  9.8 5.0 %collective-permute-start.1 = (f32[48,512]{1,0:T(8,128)S(1)}, f32[48,512]{1,0:T(8,128)S(1)}, u32[]{:S(2)}, u32[]{:S(2)}) collective-permute-start(f32[48,512]{1,0:T(8,128)S(1)} %get-tuple-element.24.refs_3_.own_ref), channel_id=1, source_target_pairs={{0,2},{1,3},{2,0},{3,1},{4,6},{5,7},{6,4},{7,5},{8,10},{9,11},{10,... | collective-permute-start | bytes 294920 | tf_op jit(solution)/shard_map/ppermute | solution.py:710
  10.2 4.6 %collective-permute-start = (f32[48,512]{1,0:T(8,128)S(1)}, f32[48,512]{1,0:T(8,128)S(1)}, u32[]{:S(2)}, u32[]{:S(2)}) collective-permute-start(f32[48,512]{1,0:T(8,128)S(1)} %get-tuple-element.24.refs_3_.own_ref), channel_id=1, source_target_pairs={{0,1},{1,0},{2,3},{3,2},{4,5},{5,4},{6,7},{7,6},{8,9},{9,8},{10,11... | collective-permute-start | bytes 294920 | tf_op jit(solution)/shard_map/ppermute | solution.py:710
  15.4 7.1 %collective-permute-start.3 = (f32[48,256]{1,0:T(8,128)S(1)}, f32[48,256]{1,0:T(8,128)S(1)}, u32[]{:S(2)}, u32[]{:S(2)}) collective-permute-start(f32[48,256]{1,0:T(8,128)S(1)} %get-tuple-element.26), channel_id=1, source_target_pairs={{0,4},{1,5},{2,6},{3,7},{4,0},{5,1},{6,2},{7,3},{8,12},{9,13},{10,... | collective-permute-start | bytes 147464 | tf_op jit(solution)/shard_map/ppermute | solution.py:713
  23.5 4.3 %collective-permute-start.4 = (f32[144,384]{1,0:T(8,128)S(1)}, f32[144,384]{1,0:T(8,128)S(1)}, u32[]{:S(2)}, u32[]{:S(2)}) collective-permute-start(f32[144,384]{1,0:T(8,128)S(1)} %get-tuple-element.29), channel_id=1, source_target_pairs={{0,8},{8,0},{16,24},{24,16},{32,40},{40,32},{48,56},{56,48},{64,72... | collective-permute-start | bytes 663560 | tf_op jit(solution)/shard_map/ppermute | solution.py:716
  28.5 6.9 %collective-permute-start.5 = (f32[144,384]{1,0:T(8,128)S(1)}, f32[144,384]{1,0:T(8,128)S(1)}, u32[]{:S(2)}, u32[]{:S(2)}) collective-permute-start(f32[144,384]{1,0:T(8,128)S(1)} %chip_merge.1.refs_4_.chip_ref), channel_id=1, source_target_pairs={{0,16},{8,24},{16,0},{24,8},{32,48},{40,56},{48,32},{56,40},{64,80... | collective-permute-start | bytes 663560 | tf_op jit(solution)/shard_map/ppermute | solution.py:718
  36.2 10.9 %collective-permute-start.6 = (f32[72,384]{1,0:T(8,128)S(1)}, f32[72,384]{1,0:T(8,128)S(1)}, u32[]{:S(2)}, u32[]{:S(2)}) collective-permute-start(f32[72,384]{1,0:T(8,128)S(1)} %get-tuple-element.32), channel_id=1, source_target_pairs={{0,32},{8,40},{16,48},{24,56},{32,0},{40,8},{48,16},{56,24},{64,96... | collective-permute-start | bytes 331784 | tf_op jit(solution)/shard_map/ppermute | solution.py:721
  37.9 9.2 %collective-permute-start.7 = (f32[72,384]{1,0:T(8,128)S(1)}, f32[72,384]{1,0:T(8,128)S(1)}, u32[]{:S(2)}, u32[]{:S(2)}) collective-permute-start(f32[72,384]{1,0:T(8,128)S(1)} %get-tuple-element.33), channel_id=1, source_target_pairs={{0,64},{8,72},{16,80},{24,88},{32,96},{40,104},{48,112},{56,120},{... | collective-permute-start | bytes 331784 | tf_op jit(solution)/shard_map/ppermute | solution.py:721
  41.2 6.7 %collective-permute-start.8 = (f32[72,384]{1,0:T(8,128)S(1)}, f32[72,384]{1,0:T(8,128)S(1)}, u32[]{:S(2)}, u32[]{:S(2)}) collective-permute-start(f32[72,384]{1,0:T(8,128)S(1)} %get-tuple-element.34), channel_id=1, source_target_pairs={{0,96},{8,104},{16,112},{24,120},{32,64},{40,72},{48,80},{56,88},{... | collective-permute-start | bytes 331784 | tf_op jit(solution)/shard_map/ppermute | solution.py:721
  48.7 4.3 %collective-permute-start.9 = (f32[144,384]{1,0:T(8,128)S(1)}, f32[144,384]{1,0:T(8,128)S(1)}, u32[]{:S(2)}, u32[]{:S(2)}) collective-permute-start(f32[144,384]{1,0:T(8,128)S(1)} %get-tuple-element.35), channel_id=1, source_target_pairs={{0,8},{8,0},{16,24},{24,16},{32,40},{40,32},{48,56},{56,48},{64,72... | collective-permute-start | bytes 663560 | tf_op jit(solution)/shard_map/ppermute | solution.py:725

commit v4 on v3

--- a/solution.py
+++ b/solution.py
@@ -27,6 +27,7 @@
 VMEM = pl.BlockSpec(memory_space=pltpu.VMEM)
 SMEM = pl.BlockSpec(memory_space=pltpu.SMEM)
 BIG = 48 * 1024 * 1024
+WHOLE = 50 * 1024 * 1024
 
 
 def params(**kw):
@@ -93,8 +94,14 @@
     return zonal, sign
 
 
-def tables_kernel(len_ref, weight_ref, table_ref, lanes_ref, w_ref):
-    rate = 1.0 / len_ref[...]
+def row_sums_kernel(where_ref, len_ref, x_ref, sums_ref, edge_ref, table_ref, lanes_ref, held_ref, w_ref, sem):
+    lon = where_ref[1]
+    copies = []
+    for g in range(GROUPS):
+        here = pl.ds(g * GROUP, GROUP)
+        copies.append(pltpu.make_async_copy(x_ref.at[here], held_ref.at[here], sem.at[g]))
+        copies[-1].start()
+    rate = 1.0 / len_ref[0:SCALES, :]
     pair = lane_rates(rate)
     lanes_ref[...] = jnp.concatenate([pair[0], pair[1], jnp.ones((6, LANES), F32)], axis=0)
     column = fiota((COLS, LANES), 0)
@@ -105,31 +112,16 @@
             w_ref[tile, 0:COLS, lanes] = high
             w_ref[tile, COLS:2 * COLS, lanes] = high
             w_ref[tile, 2 * COLS:, lanes] = low
-    both = jnp.concatenate([rate, scale_weights(rate, weight_ref[...]), jnp.ones((2, FIELDS), F32)], axis=0)
+    both = jnp.concatenate([rate, scale_weights(rate, len_ref[SCALES:, :]), jnp.ones((2, FIELDS), F32)], axis=0)
     eye = jnp.where(iota((8, LANES), 0) == iota((8, LANES), 1), 1.0, 0.0).astype(F32)
     table_ref[...] = exact(both, eye, ((0,), (0,)))
-
-
-def tables(lengths, weights):
-    return pl.pallas_call(
-        tables_kernel,
-        in_specs=[VMEM] * 2,
-        out_specs=[VMEM] * 3,
-        out_shape=[jax.ShapeDtypeStruct((FIELDS, LANES), F32), jax.ShapeDtypeStruct((8, LANES), F32),
-                   jax.ShapeDtypeStruct((2, 3 * COLS, 256), BF16)],
-        compiler_params=params(),
-        name="tables",
-    )(lengths, weights)
-
-
-def row_sums_kernel(where_ref, w_ref, x_ref, sums_ref, edge_ref):
-    lon = where_ref[1]
     lane = iota((ROWS, LANES), 1)
     virtual = lane & 31
     zero = jnp.zeros((ROWS, LANES), F32)
     left, right, first, last = zero, zero, zero, zero
     for g in range(GROUPS):
-        x = x_ref[g * GROUP:(g + 1) * GROUP].reshape(GROUP * ROWS, COLS)
+        copies[g].wait()
+        x = held_ref[g * GROUP:(g + 1) * GROUP].reshape(GROUP * ROWS, COLS)
         xh, xl = split(x)
         res = mm(jnp.concatenate([xh, xl, xh], axis=1), w_ref[0 if g < 2 else 1])
         if g == 2:
@@ -156,15 +148,18 @@
 ANY = pl.BlockSpec(memory_space=pl.ANY)
 
 
-def row_sums(where, w, x):
+def row_sums(where, facts, x):
     return pl.pallas_call(
         row_sums_kernel,
-        in_specs=[SMEM, VMEM, VMEM],
-        out_specs=[VMEM] * 2,
-        out_shape=[jax.ShapeDtypeStruct((ROWS, 512), F32), jax.ShapeDtypeStruct((ROWS, 256), F32)],
-        compiler_params=params(),
+        in_specs=[SMEM, VMEM, HBM],
+        out_specs=[VMEM] * 5,
+        out_shape=[jax.ShapeDtypeStruct((ROWS, 512), F32), jax.ShapeDtypeStruct((ROWS, 256), F32),
+                   jax.ShapeDtypeStruct((FIELDS, LANES), F32), jax.ShapeDtypeStruct((8, LANES), F32),
+                   jax.ShapeDtypeStruct((FIELDS, ROWS, COLS), F32)],
+        scratch_shapes=[pltpu.VMEM((2, 3 * COLS, 256), BF16), pltpu.SemaphoreType.DMA((GROUPS,))],
+        compiler_params=pltpu.CompilerParams(vmem_limit_bytes=WHOLE),
         name="row_sums",
-    )(where, w, x)
+    )(where, facts, x)
 
 
 def zonal_difference(x):
@@ -384,55 +379,93 @@
     )(where, table, lanes, part, theirs, edge, local)
 
 
-def half_rates(where_ref, table_ref):
-    core = where_ref[0] & 1
-    rate = table_ref[pl.ds(pl.multiple_of(core * HALF, 8), HALF), :]
-    return jnp.concatenate([rate[:, s:s + 1] for s in range(SCALES)], axis=0)
-
-
 LEFT = slice(0, HALF_ROWS)
 RIGHT = slice(HALF_ROWS, 2 * HALF_ROWS)
-
-
-def chip_merge_kernel(where_ref, table_ref, keep_ref, got_ref, chip_ref):
-    rate = half_rates(where_ref, table_ref)
-    odd = (where_ref[0] & 1) == 1
-    step = jnp.exp(-rate * ROWS)
-    one = jnp.ones_like(step)
-    mine_l, got_l = jnp.where(odd, one, step), jnp.where(odd, step, one)
-    chip_ref[LEFT, :] = mine_l * keep_ref[LEFT, :] + got_l * got_ref[LEFT, :]
-    chip_ref[RIGHT, :] = got_l * keep_ref[RIGHT, :] + mine_l * got_ref[RIGHT, :]
-
-
-def chip_merge(where, table, keep, got):
+STEPS = 21
+
+
+def steps_kernel(where_ref, table_ref, _, out_ref):
+    lat = where_ref[0]
+    odd = (lat & 1) == 1
+    odd_chip = ((lat >> 1) & 1) == 1
+    z = lat >> 2
+    zf = z.astype(F32)
+    rate = table_ref[pl.ds(pl.multiple_of((lat & 1) * HALF, 8), HALF), :]
+    rate = jnp.concatenate([rate[:, s:s + 1] for s in range(SCALES)], axis=0)
+    rate = jnp.broadcast_to(rate, (HALF_ROWS, LANES))
+    power = lambda n: jnp.exp(-rate * n)
+    quad = lambda n: power(4.0 * ROWS * n)
+    one, zero = jnp.ones_like(rate), jnp.zeros_like(rate)
+    device, chip = power(1.0 * ROWS), power(2.0 * ROWS)
+    out = [jnp.where(odd, one, device), jnp.where(odd, device, one)]
+    out += [jnp.where(odd_chip, one, chip), jnp.where(odd_chip, chip, one)]
+    out += [power(1.0 + 4 * ROWS * jnp.maximum(7.0 - 2.0 * zf, 1.0))]
+    for d in (1, 2, 3):
+        other = z ^ d
+        of = other.astype(F32)
+        below = other < z
+        gap = quad(jnp.abs(zf - of) - 1.0)
+        out += [jnp.where(below, gap, zero), jnp.where(below, zero, gap), jnp.where(below, quad(3.0 - of), zero)]
+    out += [quad(3.0 - zf), quad(3.0 - zf) * power(1.0)]
+    out += [jnp.where(odd_chip, chip, one), jnp.where(odd_chip, one, zero)]
+    out += [jnp.where(odd_chip, one, chip), jnp.where(odd_chip, zero, one)]
+    out += [device]
+    for k, value in enumerate(out):
+        out_ref[k] = value
+
+
+def lat_steps(where, table, before):
+    return pl.pallas_call(
+        steps_kernel,
+        in_specs=[SMEM, VMEM, ANY],
+        out_specs=VMEM,
+        out_shape=jax.ShapeDtypeStruct((STEPS, HALF_ROWS, LANES), F32),
+        compiler_params=params(),
+        name="lat_steps",
+    )(where, table, before)
+
+
+def by_tile(body):
+    for b in range(PARTS):
+        body(slice(b * LANES, (b + 1) * LANES))
+
+
+def chip_merge_kernel(steps_ref, keep_ref, got_ref, chip_ref):
+    def body(lanes):
+        mine, other = steps_ref[0], steps_ref[1]
+        chip_ref[LEFT, lanes] = mine * keep_ref[LEFT, lanes] + other * got_ref[LEFT, lanes]
+        chip_ref[RIGHT, lanes] = other * keep_ref[RIGHT, lanes] + mine * got_ref[RIGHT, lanes]
+
+    by_tile(body)
+
+
+def chip_merge(steps, keep, got):
     return pl.pallas_call(
         chip_merge_kernel,
-        in_specs=[SMEM] + [VMEM] * 3,
+        in_specs=[VMEM] * 3,
         out_specs=VMEM,
         out_shape=jax.ShapeDtypeStruct((2 * HALF_ROWS, COLS), F32),
         compiler_params=params(),
         name="chip_merge",
-    )(where, table, keep, got)
-
-
-def quad_merge_kernel(where_ref, table_ref, chip_ref, pair_ref, _, left_ref, s1_ref, s2_ref, s3_ref):
-    rate = half_rates(where_ref, table_ref)
+    )(steps, keep, got)
+
+
+def quad_merge_kernel(where_ref, steps_ref, chip_ref, pair_ref, _, left_ref, s1_ref, s2_ref, s3_ref):
     z = where_ref[0] >> 2
-    zf = z.astype(F32)
-    odd = ((where_ref[0] >> 1) & 1) == 1
-    step = jnp.exp(-rate * (2 * ROWS))
-    one = jnp.ones_like(step)
-    mine_l, got_l = jnp.where(odd, one, step), jnp.where(odd, step, one)
-    left = mine_l * chip_ref[LEFT, :] + got_l * pair_ref[LEFT, :]
-    right = got_l * chip_ref[RIGHT, :] + mine_l * pair_ref[RIGHT, :]
-    image = jnp.exp(-rate * (1.0 + 4 * ROWS * jnp.maximum(7.0 - 2.0 * zf, 1.0)))
-    back = right - image * left
-    left_ref[...] = left
-    for d, ref in ((1, s1_ref), (2, s2_ref), (3, s3_ref)):
-        ref[...] = jnp.where((z ^ d) > z, left, back)
-
-
-def quad_merge(where, table, chip, pair, after):
+
+    def body(lanes):
+        mine, other, image = steps_ref[2], steps_ref[3], steps_ref[4]
+        left = mine * chip_ref[LEFT, lanes] + other * pair_ref[LEFT, lanes]
+        right = other * chip_ref[RIGHT, lanes] + mine * pair_ref[RIGHT, lanes]
+        back = right - image * left
+        left_ref[:, lanes] = left
+        for d, ref in ((1, s1_ref), (2, s2_ref), (3, s3_ref)):
+            ref[:, lanes] = jnp.where((z ^ d) > z, left, back)
+
+    by_tile(body)
+
+
+def quad_merge(where, steps, chip, pair, after):
     one = jax.ShapeDtypeStruct((HALF_ROWS, COLS), F32)
     return pl.pallas_call(
         quad_merge_kernel,
@@ -441,48 +474,36 @@
         out_shape=[one] * 4,
         compiler_params=params(),
         name="quad_merge",
-    )(where, table, chip, pair, after)
-
-
-def lat_carry_kernel(where_ref, table_ref, keep_ref, got_ref, pair_ref, left_ref, g1_ref, g2_ref, g3_ref, _,
+    )(where, steps, chip, pair, after)
+
+
+def lat_carry_kernel(where_ref, steps_ref, keep_ref, got_ref, pair_ref, left_ref, g1_ref, g2_ref, g3_ref, _,
                      own_ref, send_ref):
-    rate = half_rates(where_ref, table_ref)
-    lat = where_ref[0]
-    z = lat >> 2
-    zf = z.astype(F32)
-    quad = lambda n: jnp.exp(-rate * (4 * ROWS * n))
-    left = jnp.zeros((HALF_ROWS, COLS), F32)
-    right = jnp.zeros((HALF_ROWS, COLS), F32)
-    whole = quad(3.0 - zf) * left_ref[...]
-    for d, ref in ((1, g1_ref), (2, g2_ref), (3, g3_ref)):
-        other = z ^ d
-        of = other.astype(F32)
-        below = other < z
-        gap = quad(jnp.abs(zf - of) - 1.0)
-        g = ref[...]
-        left = left + jnp.where(below, gap, 0.0) * g
-        right = right + jnp.where(below, 0.0, gap) * g
-        whole = whole + jnp.where(below, quad(3.0 - of), 0.0) * g
-    right = right - (quad(3.0 - zf) * jnp.exp(-rate)) * whole
-    odd_chip = ((lat >> 1) & 1) == 1
-    pair = jnp.exp(-rate * (2 * ROWS))
-    zero = jnp.zeros_like(pair)
-    one = jnp.ones_like(pair)
-    left = jnp.where(odd_chip, pair, one) * left + jnp.where(odd_chip, one, zero) * pair_ref[LEFT, :]
-    right = jnp.where(odd_chip, one, pair) * right + jnp.where(odd_chip, zero, one) * pair_ref[RIGHT, :]
-    odd = (lat & 1) == 1
-    device = jnp.exp(-rate * ROWS)
-    low_left = jnp.where(odd, got_ref[LEFT, :], keep_ref[LEFT, :])
-    high_right = jnp.where(odd, keep_ref[RIGHT, :], got_ref[RIGHT, :])
-    high_l = low_left + device * left
-    low_r = high_right + device * right
-    own_ref[LEFT, :] = jnp.where(odd, high_l, left)
-    own_ref[RIGHT, :] = jnp.where(odd, right, low_r)
-    send_ref[LEFT, :] = jnp.where(odd, left, high_l)
-    send_ref[RIGHT, :] = jnp.where(odd, low_r, right)
-
-
-def lat_carry(where, table, keep, got, pair, left, gs, after):
+    odd = (where_ref[0] & 1) == 1
+
+    def body(lanes):
+        left, right, whole = 0.0, 0.0, steps_ref[14] * left_ref[:, lanes]
+        for k, ref in ((5, g1_ref), (8, g2_ref), (11, g3_ref)):
+            g = ref[:, lanes]
+            left = left + steps_ref[k] * g
+            right = right + steps_ref[k + 1] * g
+            whole = whole + steps_ref[k + 2] * g
+        right = right - steps_ref[15] * whole
+        left = steps_ref[16] * left + steps_ref[17] * pair_ref[LEFT, lanes]
+        right = steps_ref[18] * right + steps_ref[19] * pair_ref[RIGHT, lanes]
+        low_left = jnp.where(odd, got_ref[LEFT, lanes], keep_ref[LEFT, lanes])
+        high_right = jnp.where(odd, keep_ref[RIGHT, lanes], got_ref[RIGHT, lanes])
+        high_l = low_left + steps_ref[20] * left
+        low_r = high_right + steps_ref[20] * right
+        own_ref[LEFT, lanes] = jnp.where(odd, high_l, left)
+        own_ref[RIGHT, lanes] = jnp.where(odd, right, low_r)
+        send_ref[LEFT, lanes] = jnp.where(odd, left, high_l)
+        send_ref[RIGHT, lanes] = jnp.where(odd, low_r, right)
+
+    by_tile(body)
+
+
+def lat_carry(where, steps, keep, got, pair, left, gs, after):
     half = jax.ShapeDtypeStruct((2 * HALF_ROWS, COLS), F32)
     return pl.pallas_call(
         lat_carry_kernel,
@@ -491,7 +512,7 @@
         out_shape=[half, half],
         compiler_params=params(),
         name="lat_carry",
-    )(where, table, keep, got, pair, left, *gs, after)
+    )(where, steps, keep, got, pair, left, *gs, after)
 
 
 def local_filter_kernel(starts, use_x, use_carry, where_ref, table_ref, carry_ref, x_ref, base_ref, out_ref):
@@ -508,11 +529,11 @@
     spread = jnp.abs(fiota((LANES, LANES), 0) - fiota((LANES, LANES), 1))
     tag = lane & 31
     corner = jnp.zeros((LANES, LANES), BF16)
-    left_lane = (lane & 1) == 0
-    row_scale = jnp.minimum(lane[:1] >> 1, 2)
+    left_lane = (lane == LANES - 1) | (lane == 1) | (lane == 3)
+    flat = lane[:1]
+    row_scale = jnp.where((flat == LANES - 1) | (flat == 0), 0, jnp.where(flat <= 2, 1, 2))
     base = iota((8, LANES), 0)
     column = fiota((8, LANES), 1)
-    tall_lane = iota((PARTS * ROWS, LANES), 1)
 
     def carry_tile(tile, virtual):
         left = carry_ref[:, tile * 256:tile * 256 + 128]
@@ -570,11 +591,10 @@
         for s in range(SCALES):
             here = row_scale == s
             if use_carry:
-                moved = w[s * ROWS:(s + 1) * ROWS, w.shape[1] - LANES:]
-                moved = moved if s == 0 else pltpu.roll(moved, LANES - 30 * s, 1)
-                outer = jnp.where(here, moved, outer)
+                moved = pltpu.roll(w[s * ROWS:(s + 1) * ROWS, w.shape[1] - LANES:], LANES - 30 * s - 1, 1)
+                outer = moved if s == 0 else jnp.where(here, moved, outer)
             if use_x:
-                turned = pltpu.roll(outs[s], 2 * s + 1, 1)
+                turned = outs[s] if s == 0 else pltpu.roll(outs[s], 2 * s, 1)
                 sums = turned if s == 0 else jnp.where(here, turned, sums)
         rate_row = jnp.where(row_scale == 0, rates[0], jnp.where(row_scale == 1, rates[1], rates[2]))
         jump = jnp.exp(-rate_row * LANES)
@@ -587,16 +607,19 @@
             from_left.append(ahead)
             from_right.append(behind)
         carries = [jnp.where(left_lane, from_left[b], from_right[PARTS - 1 - b]) for b in range(PARTS)]
-        carries = jnp.where(tall_lane < 6, jnp.concatenate(carries, axis=0), 0.0)
-        ch = carries.astype(BF16).astype(F32)
-        lhs = (ch + pltpu.roll(carries - ch, 8, 1)).astype(BF16)[:, :16]
-        base_rate = jnp.where(base < 2, rates[0], jnp.where(base < 4, rates[1], rates[2]))
-        powers = jnp.exp(-base_rate * jnp.where((base & 1) == 0, column + 1.0, LANES - column))
-        powers = jnp.where(base < 6, powers, 0.0)
-        ph = powers.astype(BF16).astype(F32)
-        rhs = jnp.concatenate([jnp.concatenate([ph, powers - ph], axis=1),
-                               jnp.concatenate([ph, jnp.zeros((8, LANES), F32)], axis=1)], axis=0)
-        return lhs, rhs.astype(BF16)
+        ch, cl = split(jnp.concatenate(carries, axis=0))
+        low_rate = jnp.where(base == 0, rates[0], jnp.where(base <= 2, rates[1], rates[2]))
+        low_left = (base == 1) | (base == 3)
+        low = jnp.where(base <= 4, jnp.exp(-low_rate * jnp.where(low_left, column + 1.0, LANES - column)), 0.0)
+        high = jnp.where(base == 7, jnp.exp(-rates[0] * (column + 1.0)), 0.0)
+        pad = jnp.zeros((8, LANES), F32)
+        lh, ll = split(jnp.concatenate([low, pad], axis=0))
+        hh, hl = split(jnp.concatenate([pad, high], axis=0))
+        gap_rows = jnp.zeros((96, LANES), BF16)
+        bh = jnp.concatenate([lh, gap_rows, hh], axis=0)
+        bl = jnp.concatenate([ll, gap_rows, hl], axis=0)
+        rhs = jnp.concatenate([jnp.concatenate([bh, bl], axis=1), jnp.concatenate([bh, corner], axis=1)], axis=0)
+        return jnp.concatenate([ch, cl], axis=1), rhs
 
     for start in starts:
         wind = start < WINDS
@@ -640,63 +663,80 @@
     )(*[arrays[n] for n in names])
 
 
-def finish_kernel(own_half, where_ref, table_ref, carry_ref, z0_ref, z1_ref, z2_ref, *refs):
-    out_ref, buf_ref, sem = refs[-3:]
-    core = where_ref[0] & 1
-    half = core if own_half else 1 - core
-    z_refs = (z0_ref, z0_ref, z1_ref, z1_ref, z2_ref, z2_ref)
+def add_carries(half, table_ref, carry_ref, z_refs, part, store):
     row = fiota((8, LANES), 0)
     up_steps, down_steps = row + 1.0, 8.0 - row
-    copies = []
+    tables = [carry_ref[side, s, part] for side in range(2) for s in range(SCALES)]
+    start = pl.multiple_of((half * 3 + part) * GROUP, GROUP)
+    group_facts = table_ref[pl.ds(start, GROUP), :]
+    for i in range(GROUP):
+        facts = group_facts[i:i + 1, :]
+        ups = []
+        for s in range(SCALES):
+            r = jnp.broadcast_to(facts[:, s:s + 1], (8, LANES))
+            w = jnp.broadcast_to(facts[:, SCALES + s:SCALES + s + 1], (8, LANES))
+            jump = jnp.exp(-8.0 * r)
+            up, down = [w * jnp.exp(-r * up_steps)], [w * jnp.exp(-r * down_steps)]
+            for _ in range(ROWS // 8 - 1):
+                up.append(up[-1] * jump)
+                down.insert(0, down[0] * jump)
+            ups.append((jnp.concatenate(up, axis=0), jnp.concatenate(down, axis=0)))
+        for b in range(PARTS):
+            lanes = slice(b * LANES, (b + 1) * LANES)
+            total = jnp.where(half == 0, z_refs[part // 2][part % 2 * GROUP + i, :, lanes],
+                              z_refs[(3 + part) // 2][(3 + part) % 2 * GROUP + i, :, lanes])
+            for s in range(SCALES):
+                total = total + ups[s][0] * tables[s][i:i + 1, lanes] + ups[s][1] * tables[SCALES + s][i:i + 1, lanes]
+            store(i, lanes, total)
+
+
+def finish_own_kernel(where_ref, table_ref, carry_ref, z0_ref, z1_ref, z2_ref, out_ref):
     for part in range(3):
-        tables = [carry_ref[side, s, part] for side in range(2) for s in range(SCALES)]
-        start = pl.multiple_of((half * 3 + part) * GROUP, GROUP)
-        group_facts = table_ref[pl.ds(start, GROUP), :]
-        for i in range(GROUP):
-            facts = group_facts[i:i + 1, :]
-            ups = []
-            for s in range(SCALES):
-                r = jnp.broadcast_to(facts[:, s:s + 1], (8, LANES))
-                w = jnp.broadcast_to(facts[:, SCALES + s:SCALES + s + 1], (8, LANES))
-                jump = jnp.exp(-8.0 * r)
-                up, down = [w * jnp.exp(-r * up_steps)], [w * jnp.exp(-r * down_steps)]
-                for _ in range(ROWS // 8 - 1):
-                    up.append(up[-1] * jump)
-                    down.insert(0, down[0] * jump)
-                ups.append((jnp.concatenate(up, axis=0), jnp.concatenate(down, axis=0)))
-            for b in range(PARTS):
-                lanes = slice(b * LANES, (b + 1) * LANES)
-                total = jnp.where(half == 0, z_refs[part][part % 2 * GROUP + i, :, lanes],
-                                  z_refs[3 + part][(3 + part) % 2 * GROUP + i, :, lanes])
-                for s in range(SCALES):
-                    total = total + ups[s][0] * tables[s][i:i + 1, lanes] + ups[s][1] * tables[SCALES + s][i:i + 1, lanes]
-                buf_ref[part, i, :, lanes] = total
-        copy = pltpu.make_async_copy(buf_ref.at[part], out_ref.at[pl.ds(start, GROUP)], sem.at[part])
-        copy.start()
-        copies.append(copy)
+        def store(i, lanes, value):
+            out_ref[part * GROUP + i, :, lanes] = value
+
+        add_carries(where_ref[0] & 1, table_ref, carry_ref, (z0_ref, z1_ref, z2_ref), part, store)
+
+
+def finish_own(where, table, carry, parts):
+    return pl.pallas_call(
+        finish_own_kernel,
+        in_specs=[SMEM] + [VMEM] * 5,
+        out_specs=VMEM,
+        out_shape=jax.ShapeDtypeStruct((HALF, ROWS, COLS), F32),
+        compiler_params=params(),
+        cost_estimate=pl.CostEstimate(flops=1_000_000_000, bytes_accessed=2_000_000, transcendentals=0),
+        name="finish_own",
+    )(where, table, carry.reshape(2, SCALES, 3, GROUP, COLS), *parts)
+
+
+def finish_kernel(where_ref, table_ref, carry_ref, z0_ref, z1_ref, z2_ref, own_ref, out_ref, buf_ref, sem):
+    half = 1 - (where_ref[0] & 1)
+    ready = pltpu.make_async_copy(own_ref, out_ref.at[pl.ds((1 - half) * HALF, HALF)], sem.at[3])
+    ready.start()
+    copies = [ready]
+    for part in range(3):
+        def store(i, lanes, value):
+            buf_ref[part, i, :, lanes] = value
+
+        add_carries(half, table_ref, carry_ref, (z0_ref, z1_ref, z2_ref), part, store)
+        there = out_ref.at[pl.ds((half * 3 + part) * GROUP, GROUP)]
+        copies.append(pltpu.make_async_copy(buf_ref.at[part], there, sem.at[part]))
+        copies[-1].start()
     for copy in copies:
         copy.wait()
 
 
-def finish(own_half, where, table, carry, parts, out=None):
-    operands = [where, table, carry.reshape(2, SCALES, 3, GROUP, COLS), *parts]
-    in_specs = [SMEM] + [VMEM] * 5
-    aliases = {}
-    if out is not None:
-        operands.append(out)
-        in_specs.append(HBM)
-        aliases = {6: 0}
-    return pl.pallas_call(
-        functools.partial(finish_kernel, own_half),
-        in_specs=in_specs,
+def finish(where, table, carry, parts, own):
+    return pl.pallas_call(
+        finish_kernel,
+        in_specs=[SMEM] + [VMEM] * 6,
         out_specs=HBM,
         out_shape=jax.ShapeDtypeStruct((FIELDS, ROWS, COLS), F32),
-        scratch_shapes=[pltpu.VMEM((3, GROUP, ROWS, COLS), F32), pltpu.SemaphoreType.DMA((3,))],
-        input_output_aliases=aliases,
-        compiler_params=params(),
-        cost_estimate=pl.CostEstimate(flops=1_000_000_000, bytes_accessed=4_000_000, transcendentals=0),
+        scratch_shapes=[pltpu.VMEM((3, GROUP, ROWS, COLS), F32), pltpu.SemaphoreType.DMA((4,))],
+        compiler_params=params(),
         name="finish",
-    )(*operands)
+    )(where, table, carry.reshape(2, SCALES, 3, GROUP, COLS), *parts, own)
 
 
 def partner(axis, count, bit):
@@ -705,26 +745,27 @@
 
 def shards(x, lengths, weights):
     where = jnp.stack([lax.axis_index("lat"), lax.axis_index("lon")]).astype(jnp.int32)
-    table, lanes, w = tables(lengths.T, weights.T)
-    sums, edge = row_sums(where, w, x)
+    facts = jnp.concatenate([lengths.T, weights.T], axis=0)
+    sums, edge, table, lanes, held = row_sums(where, facts, x)
     got = [partner("lon", NLON, d)(sums) for d in (1, 2, 3)]
-    early = local_filter(where, table, None, x, 32, 16, sums)
+    early = local_filter(where, table, None, held, 32, 16, sums)
     part, half = lon_merge(where, lanes, sums, got, early)
     theirs = partner("lon", NLON, 4)(half)
-    local = local_sums(where, table, x, part)
+    local = local_sums(where, table, held, part)
+    steps = lat_steps(where, table, part)
     carry, keep, send = column_sums(where, table, lanes, part, theirs, edge, local)
     got_core = partner("lat", NLAT, 1)(send)
-    chip = chip_merge(where, table, keep, got_core)
+    chip = chip_merge(steps, keep, got_core)
     pair = partner("lat", NLAT, 2)(chip)
-    z0 = local_filter(where, table, carry, x, 0, 16, chip)
-    left, *sends = quad_merge(where, table, chip, pair, z0)
+    z0 = local_filter(where, table, carry, held, 0, 16, chip)
+    left, *sends = quad_merge(where, steps, chip, pair, z0)
     gs = [partner("lat", NLAT, 4 * d)(t) for d, t in zip((1, 2, 3), sends)]
-    z1 = local_filter(where, table, carry, x, 16, 16, left)
-    z2 = local_filter(where, table, carry, x, 32, 16, z1, early)
-    own, other = lat_carry(where, table, keep, got_core, pair, left, gs, z2)
+    z1 = local_filter(where, table, carry, held, 16, 16, left)
+    z2 = local_filter(where, table, carry, held, 32, 16, z1, early)
+    own, other = lat_carry(where, steps, keep, got_core, pair, left, gs, z2)
     got_carry = partner("lat", NLAT, 1)(other)
-    out = finish(True, where, table, own, (z0, z1, z2))
-    return finish(False, where, table, got_carry, (z0, z1, z2), out)
+    done = finish_own(where, table, own, (z0, z1, z2))
+    return finish(where, table, got_carry, (z0, z1, z2), done)
 
 
 def solution(mesh):

time: 56 us -> 57.7 us (1.030)
  waiting for transfers between devices: 3.73 us -> 7.75 us
  local copies, waits for them, and re-layouts: 3.36 us -> 0 us
  other arithmetic: 0.07 us -> 0.78 us
  Pallas kernels: 30.8 us -> 31.4 us
    ppermute x3, waiting for transfers between devices: 0.85 us -> 4.87 us  [shards(): gs = [partner('lat', NLAT, 4 * d)(t) for d, t in zip((1, 2, 3), sends)]]
    unnamed x8 -> x0, local copies, waits for them, and re-layouts: 3.36 us -> none
    pallas_call x5, Pallas kernels: 8.64 us -> 10.9 us  [the longest x1 5.61 us: row_sums(): pl.pallas_call(row_sums_kernel, in_specs=[SMEM, VMEM, HBM], out_specs=[VM...]
    pallas_call x4, Pallas kernels: 14.7 us -> 13.3 us  [local_filter(): pl.pallas_call(body, in_specs=[specs.get(n, VMEM) for n in names], out_sp...]
    ppermute x1, waiting for transfers between devices: 1.1 us -> 0.38 us  [shards(): got_core = partner('lat', NLAT, 1)(send)]
    concatenate x0 -> x1, other arithmetic: none -> 0.71 us  [shards(): facts = jnp.concatenate([lengths.T, weights.T], axis=0)]
  transfers between devices with their start and end apart: 10 -> 10, of which waited for: 4 -> 5; matrix products, arithmetic and copies ran while one was open for 0% -> 0% of each run, Pallas kernels for 39% -> 29%
where the time goes in v4:
time: 57.7 us; the launch traced here: 57.5 us
  Pallas kernels  31.4 us (54%)
  starting transfers between devices  17.3 us (30%)
  waiting for transfers between devices  7.75 us (13%)
  other arithmetic  0.78 us (1%)
    pallas_call x4, Pallas kernels, local_filter(): pl.pallas_call(body, in_specs=[specs.get(n, VMEM) for n in names], out_sp...  13.3 us
    pallas_call x1, Pallas kernels, row_sums(): pl.pallas_call(row_sums_kernel, in_specs=[SMEM, VMEM, HBM], out_specs=[VM...  5.61 us
    ppermute x3, starting transfers between devices, shards(): gs = [partner('lat', NLAT, 4 * d)(t) for d, t in zip((1, 2, 3), sends)]  5.02 us
    ppermute x3, waiting for transfers between devices, shards(): gs = [partner('lat', NLAT, 4 * d)(t) for d, t in zip((1, 2, 3), sends)]  4.87 us
    ppermute x3, starting transfers between devices, shards(): got = [partner('lon', NLON, d)(sums) for d in (1, 2, 3)]  4.31 us
    pallas_call x1, Pallas kernels, local_sums(): pl.pallas_call(local_sums_kernel, in_specs=[SMEM, VMEM, VMEM, ANY], out_s...  4.31 us
    ppermute x1, starting transfers between devices, shards(): got_core = partner('lat', NLAT, 1)(send)  3.15 us
    ppermute x1, starting transfers between devices, shards(): theirs = partner('lon', NLON, 4)(half)  2.82 us
  transfers between devices with their start and end apart: 10, of which 5 were waited for; matrix products, arithmetic and copies ran while one was open for 0% of the time, Pallas kernels for 29%

profile of v4, /device:TPU:1, one launch (start us, length us, event | category | flops | bytes accessed | tf_op | source)
XLA Modules:
  0.0 57.5 jit_solution(8082719842280516012)
XLA Ops:
  0.0 0.1 pad_add_fusion.where_ref.refs_0_
  0.1 0.7 %pad_maximum_fusion.len_ref = f32[6,48]{1,0:T(8,128)S(1)} fusion(f32[3,48]{1,0:T(4,128)} %bitcast.10, f32[3,48]{1,0:T(4,128)} %bitcast.11), kind=kLoop, calls=%fused_computation | loop fusion | flops 288 | bytes 2304 | tf_op jit(solution)/shard_map/concatenate | solution.py:748
  0.8 5.6 %row_sums.1 = (f32[48,512]{1,0:T(8,128)S(1)}, f32[48,256]{1,0:T(8,128)S(1)}, f32[48,128]{1,0:T(8,128)S(1)}, f32[8,128]{1,0:T(8,128)S(1)}, f32[48,48,384]{2,1,0:T(8,128)S(1)}) custom-call(s32[2]{0:T(128)S(1)} %pad_add_fusion.where_ref.refs_0_, f32[6,48]{1,0:T(8,128)S(1)} %pad_maximum_fusion.len_ref, f32[48,48,384]{2,1,0:T(8,128)} %x_ref.1), custom_call_target="tpu_custom_call" | custom-call | tf_op jit(solution)/shard_map/row_sums/pallas_call | solution.py:152
  6.4 3.6 %collective-permute-start.2 = (f32[48,512]{1,0:T(8,128)S(1)}, f32[48,512]{1,0:T(8,128)S(1)}, u32[]{:S(2)}, u32[]{:S(2)}) collective-permute-start(f32[48,512]{1,0:T(8,128)S(1)} %get-tuple-element.23.refs_3_.own_ref), channel_id=1, source_target_pairs={{0,3},{1,2},{2,1},{3,0},{4,7},{5,6},{6,5},{7,4},{8,11},{9,10},{10,... | collective-permute-start | bytes 294920 | tf_op jit(solution)/shard_map/ppermute | solution.py:750
  10.0 0.3 collective-permute-start.1
  10.4 0.3 collective-permute-start
  10.7 3.3 %local_filter.4._.refs_3_ = f32[16,48,384]{2,1,0:T(8,128)S(1)} custom-call(s32[2]{0:T(128)S(1)} %pad_add_fusion.where_ref.refs_0_, f32[48,128]{1,0:T(8,128)S(1)} %get-tuple-element.21.refs_1_.table_ref, f32[48,48,384]{2,1,0:T(8,128)S(1)} %get-tuple-element.24.refs_2_.x_ref.refs_3_, f32[48,512]{1,0:T(8,128)S(1)} %get-tuple-element.23.refs_3_.own_ref), custom_call_target="tpu_custom_call" | custom-call | flops 4800000000 | bytes 2400000 | tf_op jit(solution)/shard_map/local_filter/pallas_call | solution.py:655
  14.0 0.0 collective-permute-done.2.g3_ref
  14.0 1.0 %collective-permute-done.1.g2_ref = f32[48,512]{1,0:T(8,128)S(1)} collective-permute-done((f32[48,512]{1,0:T(8,128)S(1)}, f32[48,512]{1,0:T(8,128)S(1)}, u32[]{:S(2)}, u32[]{:S(2)}) %collective-permute-start.1) | collective-permute-done | bytes 98336 | tf_op jit(solution)/shard_map/ppermute | solution.py:750
  15.0 0.0 collective-permute-done.g1_ref
  15.0 0.6 %lon_merge.1 = (f32[48,768]{1,0:T(8,128)S(1)}, f32[48,256]{1,0:T(8,128)S(1)}) custom-call(s32[2]{0:T(128)S(1)} %pad_add_fusion.where_ref.refs_0_, f32[8,128]{1,0:T(8,128)S(1)} %get-tuple-element.22.lanes_ref, f32[48,512]{1,0:T(8,128)S(1)} %get-tuple-element.23.refs_3_.own_ref, f32[48,512]{1,0:T(8,128)S(1)} %collective-permute-done.g1_ref, ...), custom_call_target="tpu_custom_call" | custom-call | tf_op jit(solution)/shard_map/lon_merge/pallas_call | solution.py:283
  15.6 2.8 %collective-permute-start.3 = (f32[48,256]{1,0:T(8,128)S(1)}, f32[48,256]{1,0:T(8,128)S(1)}, u32[]{:S(2)}, u32[]{:S(2)}) collective-permute-start(f32[48,256]{1,0:T(8,128)S(1)} %get-tuple-element.26), channel_id=1, source_target_pairs={{0,4},{1,5},{2,6},{3,7},{4,0},{5,1},{6,2},{7,3},{8,12},{9,13},{10,... | collective-permute-start | bytes 147464 | tf_op jit(solution)/shard_map/ppermute | solution.py:753
  18.5 4.3 %local_sums.1 = f32[2,2,3,3,8,384]{5,4,3,2,1,0:T(8,128)S(1)} custom-call(s32[2]{0:T(128)S(1)} %pad_add_fusion.where_ref.refs_0_, f32[48,128]{1,0:T(8,128)S(1)} %get-tuple-element.21.refs_1_.table_ref, f32[48,48,384]{2,1,0:T(8,128)S(1)} %get-tuple-element.24.refs_2_.x_ref.refs_3_, f32[48,768]{1,0:T(8,128)S(1)} %get-tuple-element.25._.part_ref), custom_call_target="tpu_custom_call" | custom-call | flops 6000000000 | bytes 4000000 | tf_op jit(solution)/shard_map/local_sums/pallas_call | solution.py:233
  22.8 0.0 collective-permute-done.3.theirs_ref
  22.8 1.0 %column_sums.1 = (f32[48,512]{1,0:T(8,128)S(1)}, f32[144,384]{1,0:T(8,128)S(1)}, f32[144,384]{1,0:T(8,128)S(1)}) custom-call(s32[2]{0:T(128)S(1)} %pad_add_fusion.where_ref.refs_0_, f32[48,128]{1,0:T(8,128)S(1)} %get-tuple-element.21.refs_1_.table_ref, f32[8,128]{1,0:T(8,128)S(1)} %get-tuple-element.22.lanes_ref, ...), custom_call_target="tpu_custom_call" | custom-call | tf_op jit(solution)/shard_map/column_sums/pallas_call | solution.py:372
  23.8 3.2 %collective-permute-start.4 = (f32[144,384]{1,0:T(8,128)S(1)}, f32[144,384]{1,0:T(8,128)S(1)}, u32[]{:S(2)}, u32[]{:S(2)}) collective-permute-start(f32[144,384]{1,0:T(8,128)S(1)} %get-tuple-element.29), channel_id=1, source_target_pairs={{0,8},{8,0},{16,24},{24,16},{32,40},{40,32},{48,56},{56,48},{64,72... | collective-permute-start | bytes 663560 | tf_op jit(solution)/shard_map/ppermute | solution.py:757
  26.9 0.7 %lat_steps.1.steps_ref = f32[21,72,128]{2,1,0:T(8,128)S(1)} custom-call(s32[2]{0:T(128)S(1)} %pad_add_fusion.where_ref.refs_0_, f32[48,128]{1,0:T(8,128)S(1)} %get-tuple-element.21.refs_1_.table_ref, f32[48,768]{1,0:T(8,128)S(1)} %get-tuple-element.25._.part_ref), custom_call_target="tpu_custom_call" | custom-call | tf_op jit(solution)/shard_map/lat_steps/pallas_call | solution.py:418
  27.7 0.4 collective-permute-done.4.got_ref
  28.1 0.6 %collective-permute-start.5 = (f32[144,384]{1,0:T(8,128)S(1)}, f32[144,384]{1,0:T(8,128)S(1)}, u32[]{:S(2)}, u32[]{:S(2)}) collective-permute-start(f32[144,384]{1,0:T(8,128)S(1)} %chip_merge.1.refs_4_.chip_ref), channel_id=1, source_target_pairs={{0,16},{8,24},{16,0},{24,8},{32,48},{40,56},{48,32},{56,40},{64,80... | collective-permute-start | bytes 663560 | tf_op jit(solution)/shard_map/ppermute | solution.py:759
  28.7 4.8 %local_filter.5._.z0_ref = f32[16,48,384]{2,1,0:T(8,128)S(1)} custom-call(s32[2]{0:T(128)S(1)} %pad_add_fusion.where_ref.refs_0_, f32[48,128]{1,0:T(8,128)S(1)} %get-tuple-element.21.refs_1_.table_ref, f32[48,512]{1,0:T(8,128)S(1)} %get-tuple-element.30.refs_2_, f32[48,48,384]{2,1,0:T(8,128)S(1)} %get-tuple-element.24.refs_2_.x_ref.refs_3_, ...), custom_call_target="tpu_custom_call" | custom-call | flops 4800000000 | bytes 2400000 | tf_op jit(solution)/shard_map/local_filter/pallas_call | solution.py:655
  33.5 1.5 %collective-permute-done.5.pair_ref = f32[144,384]{1,0:T(8,128)S(1)} collective-permute-done((f32[144,384]{1,0:T(8,128)S(1)}, f32[144,384]{1,0:T(8,128)S(1)}, u32[]{:S(2)}, u32[]{:S(2)}) %collective-permute-start.5) | collective-permute-done | bytes 221216 | tf_op jit(solution)/shard_map/ppermute | solution.py:759
  35.0 0.6 %quad_merge.1 = (f32[72,384]{1,0:T(8,128)S(1)}, f32[72,384]{1,0:T(8,128)S(1)}, f32[72,384]{1,0:T(8,128)S(1)}, f32[72,384]{1,0:T(8,128)S(1)}) custom-call(s32[2]{0:T(128)S(1)} %pad_add_fusion.where_ref.refs_0_, f32[21,72,128]{2,1,0:T(8,128)S(1)} %lat_steps.1.steps_ref, f32[144,384]{1,0:T(8,128)S(1)} %chip_merge.1.refs_4_.chip_ref, ...), custom_call_target="tpu_custom_call" | custom-call | tf_op jit(solution)/shard_map/quad_merge/pallas_call | solution.py:470
  35.6 3.4 %local_filter.6.refs_4_.z1_ref = f32[16,48,384]{2,1,0:T(8,128)S(1)} custom-call(s32[2]{0:T(128)S(1)} %pad_add_fusion.where_ref.refs_0_, f32[48,128]{1,0:T(8,128)S(1)} %get-tuple-element.21.refs_1_.table_ref, f32[48,512]{1,0:T(8,128)S(1)} %get-tuple-element.30.refs_2_, f32[48,48,384]{2,1,0:T(8,128)S(1)} %get-tuple-element.24.refs_2_.x_ref.refs_3_, ...), custom_call_target="tpu_custom_call" | custom-call | flops 4800000000 | bytes 2400000 | tf_op jit(solution)/shard_map/local_filter/pallas_call | solution.py:655
  38.9 1.7 %collective-permute-start.6 = (f32[72,384]{1,0:T(8,128)S(1)}, f32[72,384]{1,0:T(8,128)S(1)}, u32[]{:S(2)}, u32[]{:S(2)}) collective-permute-start(f32[72,384]{1,0:T(8,128)S(1)} %get-tuple-element.32), channel_id=1, source_target_pairs={{0,32},{8,40},{16,48},{24,56},{32,0},{40,8},{48,16},{56,24},{64,96... | collective-permute-start | bytes 331784 | tf_op jit(solution)/shard_map/ppermute | solution.py:762
  40.7 3.3 %collective-permute-start.7 = (f32[72,384]{1,0:T(8,128)S(1)}, f32[72,384]{1,0:T(8,128)S(1)}, u32[]{:S(2)}, u32[]{:S(2)}) collective-permute-start(f32[72,384]{1,0:T(8,128)S(1)} %get-tuple-element.33), channel_id=1, source_target_pairs={{0,64},{8,72},{16,80},{24,88},{32,96},{40,104},{48,112},{56,120},{... | collective-permute-start | bytes 331784 | tf_op jit(solution)/shard_map/ppermute | solution.py:762
  44.0 0.0 collective-permute-start.8
  44.0 1.8 %local_filter.7._.z2_ref = f32[16,48,384]{2,1,0:T(8,128)S(1)} custom-call(s32[2]{0:T(128)S(1)} %pad_add_fusion.where_ref.refs_0_, f32[48,128]{1,0:T(8,128)S(1)} %get-tuple-element.21.refs_1_.table_ref, f32[48,512]{1,0:T(8,128)S(1)} %get-tuple-element.30.refs_2_, f32[16,48,384]{2,1,0:T(8,128)S(1)} %local_filter.4._.refs_3_, ...), custom_call_target="tpu_custom_call" | custom-call | flops 4800000000 | bytes 2400000 | tf_op jit(solution)/shard_map/local_filter/pallas_call | solution.py:655
  45.8 0.0 collective-permute-done.6.g1_ref
  45.8 2.1 %collective-permute-done.7.g2_ref = f32[72,384]{1,0:T(8,128)S(1)} collective-permute-done((f32[72,384]{1,0:T(8,128)S(1)}, f32[72,384]{1,0:T(8,128)S(1)}, u32[]{:S(2)}, u32[]{:S(2)}) %collective-permute-start.7) | collective-permute-done | bytes 110624 | tf_op jit(solution)/shard_map/ppermute | solution.py:762
  47.9 2.8 %collective-permute-done.8.g3_ref = f32[72,384]{1,0:T(8,128)S(1)} collective-permute-done((f32[72,384]{1,0:T(8,128)S(1)}, f32[72,384]{1,0:T(8,128)S(1)}, u32[]{:S(2)}, u32[]{:S(2)}) %collective-permute-start.8) | collective-permute-done | bytes 110624 | tf_op jit(solution)/shard_map/ppermute | solution.py:762
  50.7 0.8 %lat_carry.1 = (f32[144,384]{1,0:T(8,128)S(1)}, f32[144,384]{1,0:T(8,128)S(1)}) custom-call(s32[2]{0:T(128)S(1)} %pad_add_fusion.where_ref.refs_0_, f32[21,72,128]{2,1,0:T(8,128)S(1)} %lat_steps.1.steps_ref, f32[144,384]{1,0:T(8,128)S(1)} %get-tuple-element.28.keep_ref, f32[144,384]{1,0:T(8,128)S(1)} %collective-permute-done.4.got_ref, ...), custom_call_target="tpu_custom_call" | custom-call | tf_op jit(solution)/shard_map/lat_carry/pallas_call | solution.py:508
  51.4 1.4 %collective-permute-start.9 = (f32[144,384]{1,0:T(8,128)S(1)}, f32[144,384]{1,0:T(8,128)S(1)}, u32[]{:S(2)}, u32[]{:S(2)}) collective-permute-start(f32[144,384]{1,0:T(8,128)S(1)} %get-tuple-element.35), channel_id=1, source_target_pairs={{0,8},{8,0},{16,24},{24,16},{32,40},{40,32},{48,56},{56,48},{64,72... | collective-permute-start | bytes 663560 | tf_op jit(solution)/shard_map/ppermute | solution.py:766
  52.8 1.7 %finish_own.1.own_ref = f32[24,48,384]{2,1,0:T(8,128)S(1)} custom-call(s32[2]{0:T(128)S(1)} %pad_add_fusion.where_ref.refs_0_, f32[48,128]{1,0:T(8,128)S(1)} %get-tuple-element.21.refs_1_.table_ref, f32[2,3,3,8,384]{4,3,2,1,0:T(8,128)S(1)} %bitcast.9, f32[16,48,384]{2,1,0:T(8,128)S(1)} %local_filter.5._.z0_ref, ...), custom_call_target="tpu_custom_call" | custom-call | flops 1000000000 | bytes 2000000 | tf_op jit(solution)/shard_map/finish_own/pallas_call | solution.py:702
  54.5 0.0 collective-permute-done.9
  54.6 2.8 %finish.1 = f32[48,48,384]{2,1,0:T(8,128)} custom-call(s32[2]{0:T(128)S(1)} %pad_add_fusion.where_ref.refs_0_, f32[48,128]{1,0:T(8,128)S(1)} %get-tuple-element.21.refs_1_.table_ref, f32[2,3,3,8,384]{4,3,2,1,0:T(8,128)S(1)} %bitcast.8, f32[16,48,384]{2,1,0:T(8,128)S(1)} %local_filter.5._.z0_ref, f32[16,48,384]{2,1,0:T(8,128)S(1)} %local_filter.6.refs_4_.z1_ref, ...), custom_call_target="tpu_custom_call" | custom-call | tf_op jit(solution)/shard_map/finish/pallas_call | solution.py:731
  (1 shorter events, 0.0 us)
Async XLA Ops:
  6.4 7.6 %collective-permute-start.2 = (f32[48,512]{1,0:T(8,128)S(1)}, f32[48,512]{1,0:T(8,128)S(1)}, u32[]{:S(2)}, u32[]{:S(2)}) collective-permute-start(f32[48,512]{1,0:T(8,128)S(1)} %get-tuple-element.23.refs_3_.own_ref), channel_id=1, source_target_pairs={{0,3},{1,2},{2,1},{3,0},{4,7},{5,6},{6,5},{7,4},{8,11},{9,10},{10,... | collective-permute-start | bytes 294920 | tf_op jit(solution)/shard_map/ppermute | solution.py:750
  10.0 5.0 %collective-permute-start.1 = (f32[48,512]{1,0:T(8,128)S(1)}, f32[48,512]{1,0:T(8,128)S(1)}, u32[]{:S(2)}, u32[]{:S(2)}) collective-permute-start(f32[48,512]{1,0:T(8,128)S(1)} %get-tuple-element.23.refs_3_.own_ref), channel_id=1, source_target_pairs={{0,2},{1,3},{2,0},{3,1},{4,6},{5,7},{6,4},{7,5},{8,10},{9,11},{10,... | collective-permute-start | bytes 294920 | tf_op jit(solution)/shard_map/ppermute | solution.py:750
  10.4 4.6 %collective-permute-start = (f32[48,512]{1,0:T(8,128)S(1)}, f32[48,512]{1,0:T(8,128)S(1)}, u32[]{:S(2)}, u32[]{:S(2)}) collective-permute-start(f32[48,512]{1,0:T(8,128)S(1)} %get-tuple-element.23.refs_3_.own_ref), channel_id=1, source_target_pairs={{0,1},{1,0},{2,3},{3,2},{4,5},{5,4},{6,7},{7,6},{8,9},{9,8},{10,11... | collective-permute-start | bytes 294920 | tf_op jit(solution)/shard_map/ppermute | solution.py:750
  15.6 7.1 %collective-permute-start.3 = (f32[48,256]{1,0:T(8,128)S(1)}, f32[48,256]{1,0:T(8,128)S(1)}, u32[]{:S(2)}, u32[]{:S(2)}) collective-permute-start(f32[48,256]{1,0:T(8,128)S(1)} %get-tuple-element.26), channel_id=1, source_target_pairs={{0,4},{1,5},{2,6},{3,7},{4,0},{5,1},{6,2},{7,3},{8,12},{9,13},{10,... | collective-permute-start | bytes 147464 | tf_op jit(solution)/shard_map/ppermute | solution.py:753
  23.8 4.3 %collective-permute-start.4 = (f32[144,384]{1,0:T(8,128)S(1)}, f32[144,384]{1,0:T(8,128)S(1)}, u32[]{:S(2)}, u32[]{:S(2)}) collective-permute-start(f32[144,384]{1,0:T(8,128)S(1)} %get-tuple-element.29), channel_id=1, source_target_pairs={{0,8},{8,0},{16,24},{24,16},{32,40},{40,32},{48,56},{56,48},{64,72... | collective-permute-start | bytes 663560 | tf_op jit(solution)/shard_map/ppermute | solution.py:757
  28.1 6.9 %collective-permute-start.5 = (f32[144,384]{1,0:T(8,128)S(1)}, f32[144,384]{1,0:T(8,128)S(1)}, u32[]{:S(2)}, u32[]{:S(2)}) collective-permute-start(f32[144,384]{1,0:T(8,128)S(1)} %chip_merge.1.refs_4_.chip_ref), channel_id=1, source_target_pairs={{0,16},{8,24},{16,0},{24,8},{32,48},{40,56},{48,32},{56,40},{64,80... | collective-permute-start | bytes 663560 | tf_op jit(solution)/shard_map/ppermute | solution.py:759
  38.9 6.9 %collective-permute-start.6 = (f32[72,384]{1,0:T(8,128)S(1)}, f32[72,384]{1,0:T(8,128)S(1)}, u32[]{:S(2)}, u32[]{:S(2)}) collective-permute-start(f32[72,384]{1,0:T(8,128)S(1)} %get-tuple-element.32), channel_id=1, source_target_pairs={{0,32},{8,40},{16,48},{24,56},{32,0},{40,8},{48,16},{56,24},{64,96... | collective-permute-start | bytes 331784 | tf_op jit(solution)/shard_map/ppermute | solution.py:762
  40.7 7.3 %collective-permute-start.7 = (f32[72,384]{1,0:T(8,128)S(1)}, f32[72,384]{1,0:T(8,128)S(1)}, u32[]{:S(2)}, u32[]{:S(2)}) collective-permute-start(f32[72,384]{1,0:T(8,128)S(1)} %get-tuple-element.33), channel_id=1, source_target_pairs={{0,64},{8,72},{16,80},{24,88},{32,96},{40,104},{48,112},{56,120},{... | collective-permute-start | bytes 331784 | tf_op jit(solution)/shard_map/ppermute | solution.py:762
  44.0 6.7 %collective-permute-start.8 = (f32[72,384]{1,0:T(8,128)S(1)}, f32[72,384]{1,0:T(8,128)S(1)}, u32[]{:S(2)}, u32[]{:S(2)}) collective-permute-start(f32[72,384]{1,0:T(8,128)S(1)} %get-tuple-element.34), channel_id=1, source_target_pairs={{0,96},{8,104},{16,112},{24,120},{32,64},{40,72},{48,80},{56,88},{... | collective-permute-start | bytes 331784 | tf_op jit(solution)/shard_map/ppermute | solution.py:762
  51.4 3.1 %collective-permute-start.9 = (f32[144,384]{1,0:T(8,128)S(1)}, f32[144,384]{1,0:T(8,128)S(1)}, u32[]{:S(2)}, u32[]{:S(2)}) collective-permute-start(f32[144,384]{1,0:T(8,128)S(1)} %get-tuple-element.35), channel_id=1, source_target_pairs={{0,8},{8,0},{16,24},{24,16},{32,40},{40,32},{48,56},{56,48},{64,72... | collective-permute-start | bytes 663560 | tf_op jit(solution)/shard_map/ppermute | solution.py:766

commit v5 on v4

--- a/solution.py
+++ b/solution.py
@@ -97,9 +97,9 @@
 def row_sums_kernel(where_ref, len_ref, x_ref, sums_ref, edge_ref, table_ref, lanes_ref, held_ref, w_ref, sem):
     lon = where_ref[1]
     copies = []
-    for g in range(GROUPS):
-        here = pl.ds(g * GROUP, GROUP)
-        copies.append(pltpu.make_async_copy(x_ref.at[here], held_ref.at[here], sem.at[g]))
+    for k, (start, stop) in enumerate(((0, WINDS), (WINDS, FIELDS))):
+        here = pl.ds(start, stop - start)
+        copies.append(pltpu.make_async_copy(x_ref.at[here], held_ref.at[here], sem.at[k]))
         copies[-1].start()
     rate = 1.0 / len_ref[0:SCALES, :]
     pair = lane_rates(rate)
@@ -120,7 +120,8 @@
     zero = jnp.zeros((ROWS, LANES), F32)
     left, right, first, last = zero, zero, zero, zero
     for g in range(GROUPS):
-        copies[g].wait()
+        if g in (0, 2):
+            copies[g // 2].wait()
         x = held_ref[g * GROUP:(g + 1) * GROUP].reshape(GROUP * ROWS, COLS)
         xh, xl = split(x)
         res = mm(jnp.concatenate([xh, xl, xh], axis=1), w_ref[0 if g < 2 else 1])
@@ -156,7 +157,7 @@
         out_shape=[jax.ShapeDtypeStruct((ROWS, 512), F32), jax.ShapeDtypeStruct((ROWS, 256), F32),
                    jax.ShapeDtypeStruct((FIELDS, LANES), F32), jax.ShapeDtypeStruct((8, LANES), F32),
                    jax.ShapeDtypeStruct((FIELDS, ROWS, COLS), F32)],
-        scratch_shapes=[pltpu.VMEM((2, 3 * COLS, 256), BF16), pltpu.SemaphoreType.DMA((GROUPS,))],
+        scratch_shapes=[pltpu.VMEM((2, 3 * COLS, 256), BF16), pltpu.SemaphoreType.DMA((2,))],
         compiler_params=pltpu.CompilerParams(vmem_limit_bytes=WHOLE),
         name="row_sums",
     )(where, facts, x)
@@ -236,7 +237,7 @@
         out_specs=VMEM,
         out_shape=jax.ShapeDtypeStruct((2, 2, SCALES, 3, GROUP, COLS), F32),
         compiler_params=params(),
-        cost_estimate=pl.CostEstimate(flops=6_000_000_000, bytes_accessed=4_000_000, transcendentals=0),
+        cost_estimate=pl.CostEstimate(flops=600000000, bytes_accessed=4_000_000, transcendentals=0),
         name="local_sums",
     )(where, table, x, before)
     return out.reshape(2, 2 * HALF_ROWS, COLS)
@@ -658,7 +659,7 @@
         out_specs=VMEM,
         out_shape=jax.ShapeDtypeStruct((count, ROWS, COLS), F32),
         compiler_params=params(),
-        cost_estimate=pl.CostEstimate(flops=count * 300_000_000, bytes_accessed=count * 150_000, transcendentals=0),
+        cost_estimate=pl.CostEstimate(flops=int(count * 30000000), bytes_accessed=count * 150_000, transcendentals=0),
         name="local_filter",
     )(*[arrays[n] for n in names])
 

time: 57.7 us -> 52.5 us (0.910)
  waiting for transfers between devices: 7.75 us -> 4.39 us
  Pallas kernels: 31.4 us -> 29.6 us
    ppermute x3, waiting for transfers between devices: 4.87 us -> 1.51 us  [shards(): gs = [partner('lat', NLAT, 4 * d)(t) for d, t in zip((1, 2, 3), sends)]]
    pallas_call x1, Pallas kernels: 5.61 us -> 3.84 us  [row_sums(): pl.pallas_call(row_sums_kernel, in_specs=[SMEM, VMEM, HBM], out_specs=[VM...]
  transfers between devices with their start and end apart: 10 -> 10, of which waited for: 5 -> 4; matrix products, arithmetic and copies ran while one was open for 0% -> 0% of each run, Pallas kernels for 29% -> 38%
where the time goes in v5:
time: 52.5 us; the launch traced here: 52.4 us
  Pallas kernels  29.6 us (56%)
  starting transfers between devices  17.3 us (33%)
  waiting for transfers between devices  4.39 us (8%)
  other arithmetic  0.78 us (1%)
    pallas_call x4, Pallas kernels, local_filter(): pl.pallas_call(body, in_specs=[specs.get(n, VMEM) for n in names], out_sp...  13.3 us
    ppermute x3, starting transfers between devices, shards(): gs = [partner('lat', NLAT, 4 * d)(t) for d, t in zip((1, 2, 3), sends)]  5.02 us
    ppermute x3, starting transfers between devices, shards(): got = [partner('lon', NLON, d)(sums) for d in (1, 2, 3)]  4.31 us
    pallas_call x1, Pallas kernels, local_sums(): pl.pallas_call(local_sums_kernel, in_specs=[SMEM, VMEM, VMEM, ANY], out_s...  4.29 us
    pallas_call x1, Pallas kernels, row_sums(): pl.pallas_call(row_sums_kernel, in_specs=[SMEM, VMEM, HBM], out_specs=[VM...  3.84 us
    ppermute x1, starting transfers between devices, shards(): got_core = partner('lat', NLAT, 1)(send)  3.15 us
    ppermute x1, starting transfers between devices, shards(): theirs = partner('lon', NLON, 4)(half)  2.82 us
    pallas_call x1, Pallas kernels, finish(): pl.pallas_call(finish_kernel, in_specs=[SMEM] + [VMEM] * 6, out_specs=HBM...  2.81 us
  transfers between devices with their start and end apart: 10, of which 4 were waited for; matrix products, arithmetic and copies ran while one was open for 0% of the time, Pallas kernels for 38%

profile of v5, /device:TPU:1, one launch (start us, length us, event | category | flops | bytes accessed | tf_op | source)
XLA Modules:
  0.0 52.4 jit_solution(13725820923160967738)
XLA Ops:
  0.0 0.1 pad_add_fusion.where_ref.refs_0_
  0.1 0.7 %pad_maximum_fusion.len_ref = f32[6,48]{1,0:T(8,128)S(1)} fusion(f32[3,48]{1,0:T(4,128)} %bitcast.10, f32[3,48]{1,0:T(4,128)} %bitcast.11), kind=kLoop, calls=%fused_computation | loop fusion | flops 288 | bytes 2304 | tf_op jit(solution)/shard_map/concatenate | solution.py:749
  0.8 3.8 %row_sums.1 = (f32[48,512]{1,0:T(8,128)S(1)}, f32[48,256]{1,0:T(8,128)S(1)}, f32[48,128]{1,0:T(8,128)S(1)}, f32[8,128]{1,0:T(8,128)S(1)}, f32[48,48,384]{2,1,0:T(8,128)S(1)}) custom-call(s32[2]{0:T(128)S(1)} %pad_add_fusion.where_ref.refs_0_, f32[6,48]{1,0:T(8,128)S(1)} %pad_maximum_fusion.len_ref, f32[48,48,384]{2,1,0:T(8,128)} %x_ref.1), custom_call_target="tpu_custom_call" | custom-call | tf_op jit(solution)/shard_map/row_sums/pallas_call | solution.py:153
  4.6 3.6 %collective-permute-start.2 = (f32[48,512]{1,0:T(8,128)S(1)}, f32[48,512]{1,0:T(8,128)S(1)}, u32[]{:S(2)}, u32[]{:S(2)}) collective-permute-start(f32[48,512]{1,0:T(8,128)S(1)} %get-tuple-element.23.refs_3_.own_ref), channel_id=1, source_target_pairs={{0,3},{1,2},{2,1},{3,0},{4,7},{5,6},{6,5},{7,4},{8,11},{9,10},{10,... | collective-permute-start | bytes 294920 | tf_op jit(solution)/shard_map/ppermute | solution.py:751
  8.3 0.3 collective-permute-start.1
  8.6 0.3 collective-permute-start
  8.9 3.3 %local_filter.4._.refs_3_ = f32[16,48,384]{2,1,0:T(8,128)S(1)} custom-call(s32[2]{0:T(128)S(1)} %pad_add_fusion.where_ref.refs_0_, f32[48,128]{1,0:T(8,128)S(1)} %get-tuple-element.21.refs_1_.table_ref, f32[48,48,384]{2,1,0:T(8,128)S(1)} %get-tuple-element.24.refs_2_.x_ref.refs_3_, f32[48,512]{1,0:T(8,128)S(1)} %get-tuple-element.23.refs_3_.own_ref), custom_call_target="tpu_custom_call" | custom-call | flops 480000000 | bytes 2400000 | tf_op jit(solution)/shard_map/local_filter/pallas_call | solution.py:656
  12.2 0.0 collective-permute-done.2.g3_ref
  12.2 1.0 %collective-permute-done.1.g2_ref = f32[48,512]{1,0:T(8,128)S(1)} collective-permute-done((f32[48,512]{1,0:T(8,128)S(1)}, f32[48,512]{1,0:T(8,128)S(1)}, u32[]{:S(2)}, u32[]{:S(2)}) %collective-permute-start.1) | collective-permute-done | bytes 98336 | tf_op jit(solution)/shard_map/ppermute | solution.py:751
  13.2 0.0 collective-permute-done.g1_ref
  13.2 0.6 %lon_merge.1 = (f32[48,768]{1,0:T(8,128)S(1)}, f32[48,256]{1,0:T(8,128)S(1)}) custom-call(s32[2]{0:T(128)S(1)} %pad_add_fusion.where_ref.refs_0_, f32[8,128]{1,0:T(8,128)S(1)} %get-tuple-element.22.lanes_ref, f32[48,512]{1,0:T(8,128)S(1)} %get-tuple-element.23.refs_3_.own_ref, f32[48,512]{1,0:T(8,128)S(1)} %collective-permute-done.g1_ref, ...), custom_call_target="tpu_custom_call" | custom-call | tf_op jit(solution)/shard_map/lon_merge/pallas_call | solution.py:284
  13.9 2.8 %collective-permute-start.3 = (f32[48,256]{1,0:T(8,128)S(1)}, f32[48,256]{1,0:T(8,128)S(1)}, u32[]{:S(2)}, u32[]{:S(2)}) collective-permute-start(f32[48,256]{1,0:T(8,128)S(1)} %get-tuple-element.26), channel_id=1, source_target_pairs={{0,4},{1,5},{2,6},{3,7},{4,0},{5,1},{6,2},{7,3},{8,12},{9,13},{10,... | collective-permute-start | bytes 147464 | tf_op jit(solution)/shard_map/ppermute | solution.py:754
  16.7 4.3 %local_sums.1 = f32[2,2,3,3,8,384]{5,4,3,2,1,0:T(8,128)S(1)} custom-call(s32[2]{0:T(128)S(1)} %pad_add_fusion.where_ref.refs_0_, f32[48,128]{1,0:T(8,128)S(1)} %get-tuple-element.21.refs_1_.table_ref, f32[48,48,384]{2,1,0:T(8,128)S(1)} %get-tuple-element.24.refs_2_.x_ref.refs_3_, f32[48,768]{1,0:T(8,128)S(1)} %get-tuple-element.25._.part_ref), custom_call_target="tpu_custom_call" | custom-call | flops 600000000 | bytes 4000000 | tf_op jit(solution)/shard_map/local_sums/pallas_call | solution.py:234
  21.0 0.0 collective-permute-done.3.theirs_ref
  21.0 1.0 %column_sums.1 = (f32[48,512]{1,0:T(8,128)S(1)}, f32[144,384]{1,0:T(8,128)S(1)}, f32[144,384]{1,0:T(8,128)S(1)}) custom-call(s32[2]{0:T(128)S(1)} %pad_add_fusion.where_ref.refs_0_, f32[48,128]{1,0:T(8,128)S(1)} %get-tuple-element.21.refs_1_.table_ref, f32[8,128]{1,0:T(8,128)S(1)} %get-tuple-element.22.lanes_ref, ...), custom_call_target="tpu_custom_call" | custom-call | tf_op jit(solution)/shard_map/column_sums/pallas_call | solution.py:373
  22.0 3.1 %collective-permute-start.4 = (f32[144,384]{1,0:T(8,128)S(1)}, f32[144,384]{1,0:T(8,128)S(1)}, u32[]{:S(2)}, u32[]{:S(2)}) collective-permute-start(f32[144,384]{1,0:T(8,128)S(1)} %get-tuple-element.29), channel_id=1, source_target_pairs={{0,8},{8,0},{16,24},{24,16},{32,40},{40,32},{48,56},{56,48},{64,72... | collective-permute-start | bytes 663560 | tf_op jit(solution)/shard_map/ppermute | solution.py:758
  25.2 0.7 %lat_steps.1.steps_ref = f32[21,72,128]{2,1,0:T(8,128)S(1)} custom-call(s32[2]{0:T(128)S(1)} %pad_add_fusion.where_ref.refs_0_, f32[48,128]{1,0:T(8,128)S(1)} %get-tuple-element.21.refs_1_.table_ref, f32[48,768]{1,0:T(8,128)S(1)} %get-tuple-element.25._.part_ref), custom_call_target="tpu_custom_call" | custom-call | tf_op jit(solution)/shard_map/lat_steps/pallas_call | solution.py:419
  25.9 0.4 collective-permute-done.4.got_ref
  26.3 0.6 %collective-permute-start.5 = (f32[144,384]{1,0:T(8,128)S(1)}, f32[144,384]{1,0:T(8,128)S(1)}, u32[]{:S(2)}, u32[]{:S(2)}) collective-permute-start(f32[144,384]{1,0:T(8,128)S(1)} %chip_merge.1.refs_4_.chip_ref), channel_id=1, source_target_pairs={{0,16},{8,24},{16,0},{24,8},{32,48},{40,56},{48,32},{56,40},{64,80... | collective-permute-start | bytes 663560 | tf_op jit(solution)/shard_map/ppermute | solution.py:760
  26.9 4.8 %local_filter.5._.z0_ref = f32[16,48,384]{2,1,0:T(8,128)S(1)} custom-call(s32[2]{0:T(128)S(1)} %pad_add_fusion.where_ref.refs_0_, f32[48,128]{1,0:T(8,128)S(1)} %get-tuple-element.21.refs_1_.table_ref, f32[48,512]{1,0:T(8,128)S(1)} %get-tuple-element.30.refs_2_, f32[48,48,384]{2,1,0:T(8,128)S(1)} %get-tuple-element.24.refs_2_.x_ref.refs_3_, ...), custom_call_target="tpu_custom_call" | custom-call | flops 480000000 | bytes 2400000 | tf_op jit(solution)/shard_map/local_filter/pallas_call | solution.py:656
  31.7 1.5 %collective-permute-done.5.pair_ref = f32[144,384]{1,0:T(8,128)S(1)} collective-permute-done((f32[144,384]{1,0:T(8,128)S(1)}, f32[144,384]{1,0:T(8,128)S(1)}, u32[]{:S(2)}, u32[]{:S(2)}) %collective-permute-start.5) | collective-permute-done | bytes 221216 | tf_op jit(solution)/shard_map/ppermute | solution.py:760
  33.2 0.6 %quad_merge.1 = (f32[72,384]{1,0:T(8,128)S(1)}, f32[72,384]{1,0:T(8,128)S(1)}, f32[72,384]{1,0:T(8,128)S(1)}, f32[72,384]{1,0:T(8,128)S(1)}) custom-call(s32[2]{0:T(128)S(1)} %pad_add_fusion.where_ref.refs_0_, f32[21,72,128]{2,1,0:T(8,128)S(1)} %lat_steps.1.steps_ref, f32[144,384]{1,0:T(8,128)S(1)} %chip_merge.1.refs_4_.chip_ref, ...), custom_call_target="tpu_custom_call" | custom-call | tf_op jit(solution)/shard_map/quad_merge/pallas_call | solution.py:471
  33.8 1.7 %collective-permute-start.6 = (f32[72,384]{1,0:T(8,128)S(1)}, f32[72,384]{1,0:T(8,128)S(1)}, u32[]{:S(2)}, u32[]{:S(2)}) collective-permute-start(f32[72,384]{1,0:T(8,128)S(1)} %get-tuple-element.32), channel_id=1, source_target_pairs={{0,32},{8,40},{16,48},{24,56},{32,0},{40,8},{48,16},{56,24},{64,96... | collective-permute-start | bytes 331784 | tf_op jit(solution)/shard_map/ppermute | solution.py:763
  35.5 3.3 %collective-permute-start.7 = (f32[72,384]{1,0:T(8,128)S(1)}, f32[72,384]{1,0:T(8,128)S(1)}, u32[]{:S(2)}, u32[]{:S(2)}) collective-permute-start(f32[72,384]{1,0:T(8,128)S(1)} %get-tuple-element.33), channel_id=1, source_target_pairs={{0,64},{8,72},{16,80},{24,88},{32,96},{40,104},{48,112},{56,120},{... | collective-permute-start | bytes 331784 | tf_op jit(solution)/shard_map/ppermute | solution.py:763
  38.8 0.0 collective-permute-start.8
  38.8 3.3 %local_filter.6.refs_4_.z1_ref = f32[16,48,384]{2,1,0:T(8,128)S(1)} custom-call(s32[2]{0:T(128)S(1)} %pad_add_fusion.where_ref.refs_0_, f32[48,128]{1,0:T(8,128)S(1)} %get-tuple-element.21.refs_1_.table_ref, f32[48,512]{1,0:T(8,128)S(1)} %get-tuple-element.30.refs_2_, f32[48,48,384]{2,1,0:T(8,128)S(1)} %get-tuple-element.24.refs_2_.x_ref.refs_3_, ...), custom_call_target="tpu_custom_call" | custom-call | flops 480000000 | bytes 2400000 | tf_op jit(solution)/shard_map/local_filter/pallas_call | solution.py:656
  42.2 1.8 %local_filter.7._.z2_ref = f32[16,48,384]{2,1,0:T(8,128)S(1)} custom-call(s32[2]{0:T(128)S(1)} %pad_add_fusion.where_ref.refs_0_, f32[48,128]{1,0:T(8,128)S(1)} %get-tuple-element.21.refs_1_.table_ref, f32[48,512]{1,0:T(8,128)S(1)} %get-tuple-element.30.refs_2_, f32[16,48,384]{2,1,0:T(8,128)S(1)} %local_filter.4._.refs_3_, ...), custom_call_target="tpu_custom_call" | custom-call | flops 480000000 | bytes 2400000 | tf_op jit(solution)/shard_map/local_filter/pallas_call | solution.py:656
  44.0 0.0 collective-permute-done.6.g1_ref
  44.0 0.0 collective-permute-done.7.g2_ref
  44.0 1.5 %collective-permute-done.8.g3_ref = f32[72,384]{1,0:T(8,128)S(1)} collective-permute-done((f32[72,384]{1,0:T(8,128)S(1)}, f32[72,384]{1,0:T(8,128)S(1)}, u32[]{:S(2)}, u32[]{:S(2)}) %collective-permute-start.8) | collective-permute-done | bytes 110624 | tf_op jit(solution)/shard_map/ppermute | solution.py:763
  45.5 0.7 %lat_carry.1 = (f32[144,384]{1,0:T(8,128)S(1)}, f32[144,384]{1,0:T(8,128)S(1)}) custom-call(s32[2]{0:T(128)S(1)} %pad_add_fusion.where_ref.refs_0_, f32[21,72,128]{2,1,0:T(8,128)S(1)} %lat_steps.1.steps_ref, f32[144,384]{1,0:T(8,128)S(1)} %get-tuple-element.28.keep_ref, f32[144,384]{1,0:T(8,128)S(1)} %collective-permute-done.4.got_ref, ...), custom_call_target="tpu_custom_call" | custom-call | tf_op jit(solution)/shard_map/lat_carry/pallas_call | solution.py:509
  46.3 1.4 %collective-permute-start.9 = (f32[144,384]{1,0:T(8,128)S(1)}, f32[144,384]{1,0:T(8,128)S(1)}, u32[]{:S(2)}, u32[]{:S(2)}) collective-permute-start(f32[144,384]{1,0:T(8,128)S(1)} %get-tuple-element.35), channel_id=1, source_target_pairs={{0,8},{8,0},{16,24},{24,16},{32,40},{40,32},{48,56},{56,48},{64,72... | collective-permute-start | bytes 663560 | tf_op jit(solution)/shard_map/ppermute | solution.py:767
  47.7 1.7 %finish_own.1.own_ref = f32[24,48,384]{2,1,0:T(8,128)S(1)} custom-call(s32[2]{0:T(128)S(1)} %pad_add_fusion.where_ref.refs_0_, f32[48,128]{1,0:T(8,128)S(1)} %get-tuple-element.21.refs_1_.table_ref, f32[2,3,3,8,384]{4,3,2,1,0:T(8,128)S(1)} %bitcast.9, f32[16,48,384]{2,1,0:T(8,128)S(1)} %local_filter.5._.z0_ref, ...), custom_call_target="tpu_custom_call" | custom-call | flops 1000000000 | bytes 2000000 | tf_op jit(solution)/shard_map/finish_own/pallas_call | solution.py:703
  49.4 0.0 collective-permute-done.9
  49.4 2.8 %finish.1 = f32[48,48,384]{2,1,0:T(8,128)} custom-call(s32[2]{0:T(128)S(1)} %pad_add_fusion.where_ref.refs_0_, f32[48,128]{1,0:T(8,128)S(1)} %get-tuple-element.21.refs_1_.table_ref, f32[2,3,3,8,384]{4,3,2,1,0:T(8,128)S(1)} %bitcast.8, f32[16,48,384]{2,1,0:T(8,128)S(1)} %local_filter.5._.z0_ref, f32[16,48,384]{2,1,0:T(8,128)S(1)} %local_filter.6.refs_4_.z1_ref, ...), custom_call_target="tpu_custom_call" | custom-call | tf_op jit(solution)/shard_map/finish/pallas_call | solution.py:732
  (1 shorter events, 0.0 us)
Async XLA Ops:
  4.6 7.6 %collective-permute-start.2 = (f32[48,512]{1,0:T(8,128)S(1)}, f32[48,512]{1,0:T(8,128)S(1)}, u32[]{:S(2)}, u32[]{:S(2)}) collective-permute-start(f32[48,512]{1,0:T(8,128)S(1)} %get-tuple-element.23.refs_3_.own_ref), channel_id=1, source_target_pairs={{0,3},{1,2},{2,1},{3,0},{4,7},{5,6},{6,5},{7,4},{8,11},{9,10},{10,... | collective-permute-start | bytes 294920 | tf_op jit(solution)/shard_map/ppermute | solution.py:751
  8.3 5.0 %collective-permute-start.1 = (f32[48,512]{1,0:T(8,128)S(1)}, f32[48,512]{1,0:T(8,128)S(1)}, u32[]{:S(2)}, u32[]{:S(2)}) collective-permute-start(f32[48,512]{1,0:T(8,128)S(1)} %get-tuple-element.23.refs_3_.own_ref), channel_id=1, source_target_pairs={{0,2},{1,3},{2,0},{3,1},{4,6},{5,7},{6,4},{7,5},{8,10},{9,11},{10,... | collective-permute-start | bytes 294920 | tf_op jit(solution)/shard_map/ppermute | solution.py:751
  8.6 4.6 %collective-permute-start = (f32[48,512]{1,0:T(8,128)S(1)}, f32[48,512]{1,0:T(8,128)S(1)}, u32[]{:S(2)}, u32[]{:S(2)}) collective-permute-start(f32[48,512]{1,0:T(8,128)S(1)} %get-tuple-element.23.refs_3_.own_ref), channel_id=1, source_target_pairs={{0,1},{1,0},{2,3},{3,2},{4,5},{5,4},{6,7},{7,6},{8,9},{9,8},{10,11... | collective-permute-start | bytes 294920 | tf_op jit(solution)/shard_map/ppermute | solution.py:751
  13.9 7.1 %collective-permute-start.3 = (f32[48,256]{1,0:T(8,128)S(1)}, f32[48,256]{1,0:T(8,128)S(1)}, u32[]{:S(2)}, u32[]{:S(2)}) collective-permute-start(f32[48,256]{1,0:T(8,128)S(1)} %get-tuple-element.26), channel_id=1, source_target_pairs={{0,4},{1,5},{2,6},{3,7},{4,0},{5,1},{6,2},{7,3},{8,12},{9,13},{10,... | collective-permute-start | bytes 147464 | tf_op jit(solution)/shard_map/ppermute | solution.py:754
  22.0 4.3 %collective-permute-start.4 = (f32[144,384]{1,0:T(8,128)S(1)}, f32[144,384]{1,0:T(8,128)S(1)}, u32[]{:S(2)}, u32[]{:S(2)}) collective-permute-start(f32[144,384]{1,0:T(8,128)S(1)} %get-tuple-element.29), channel_id=1, source_target_pairs={{0,8},{8,0},{16,24},{24,16},{32,40},{40,32},{48,56},{56,48},{64,72... | collective-permute-start | bytes 663560 | tf_op jit(solution)/shard_map/ppermute | solution.py:758
  26.3 6.9 %collective-permute-start.5 = (f32[144,384]{1,0:T(8,128)S(1)}, f32[144,384]{1,0:T(8,128)S(1)}, u32[]{:S(2)}, u32[]{:S(2)}) collective-permute-start(f32[144,384]{1,0:T(8,128)S(1)} %chip_merge.1.refs_4_.chip_ref), channel_id=1, source_target_pairs={{0,16},{8,24},{16,0},{24,8},{32,48},{40,56},{48,32},{56,40},{64,80... | collective-permute-start | bytes 663560 | tf_op jit(solution)/shard_map/ppermute | solution.py:760
  33.8 10.2 %collective-permute-start.6 = (f32[72,384]{1,0:T(8,128)S(1)}, f32[72,384]{1,0:T(8,128)S(1)}, u32[]{:S(2)}, u32[]{:S(2)}) collective-permute-start(f32[72,384]{1,0:T(8,128)S(1)} %get-tuple-element.32), channel_id=1, source_target_pairs={{0,32},{8,40},{16,48},{24,56},{32,0},{40,8},{48,16},{56,24},{64,96... | collective-permute-start | bytes 331784 | tf_op jit(solution)/shard_map/ppermute | solution.py:763
  35.5 8.5 %collective-permute-start.7 = (f32[72,384]{1,0:T(8,128)S(1)}, f32[72,384]{1,0:T(8,128)S(1)}, u32[]{:S(2)}, u32[]{:S(2)}) collective-permute-start(f32[72,384]{1,0:T(8,128)S(1)} %get-tuple-element.33), channel_id=1, source_target_pairs={{0,64},{8,72},{16,80},{24,88},{32,96},{40,104},{48,112},{56,120},{... | collective-permute-start | bytes 331784 | tf_op jit(solution)/shard_map/ppermute | solution.py:763
  38.8 6.7 %collective-permute-start.8 = (f32[72,384]{1,0:T(8,128)S(1)}, f32[72,384]{1,0:T(8,128)S(1)}, u32[]{:S(2)}, u32[]{:S(2)}) collective-permute-start(f32[72,384]{1,0:T(8,128)S(1)} %get-tuple-element.34), channel_id=1, source_target_pairs={{0,96},{8,104},{16,112},{24,120},{32,64},{40,72},{48,80},{56,88},{... | collective-permute-start | bytes 331784 | tf_op jit(solution)/shard_map/ppermute | solution.py:763
  46.3 3.1 %collective-permute-start.9 = (f32[144,384]{1,0:T(8,128)S(1)}, f32[144,384]{1,0:T(8,128)S(1)}, u32[]{:S(2)}, u32[]{:S(2)}) collective-permute-start(f32[144,384]{1,0:T(8,128)S(1)} %get-tuple-element.35), channel_id=1, source_target_pairs={{0,8},{8,0},{16,24},{24,16},{32,40},{40,32},{48,56},{56,48},{64,72... | collective-permute-start | bytes 663560 | tf_op jit(solution)/shard_map/ppermute | solution.py:767

commit v6 on v5

--- a/solution.py
+++ b/solution.py
@@ -25,9 +25,16 @@
 BF16 = jnp.bfloat16
 
 VMEM = pl.BlockSpec(memory_space=pltpu.VMEM)
-SMEM = pl.BlockSpec(memory_space=pltpu.SMEM)
 BIG = 48 * 1024 * 1024
 WHOLE = 50 * 1024 * 1024
+
+
+def lat_index():
+    return lax.axis_index("lat")
+
+
+def lon_index():
+    return lax.axis_index("lon")
 
 
 def params(**kw):
@@ -94,8 +101,8 @@
     return zonal, sign
 
 
-def row_sums_kernel(where_ref, len_ref, x_ref, sums_ref, edge_ref, table_ref, lanes_ref, held_ref, w_ref, sem):
-    lon = where_ref[1]
+def row_sums_kernel(len_ref, x_ref, sums_ref, edge_ref, table_ref, lanes_ref, held_ref, w_ref, sem):
+    lon = lon_index()
     copies = []
     for k, (start, stop) in enumerate(((0, WINDS), (WINDS, FIELDS))):
         here = pl.ds(start, stop - start)
@@ -149,10 +156,10 @@
 ANY = pl.BlockSpec(memory_space=pl.ANY)
 
 
-def row_sums(where, facts, x):
+def row_sums(facts, x):
     return pl.pallas_call(
         row_sums_kernel,
-        in_specs=[SMEM, VMEM, HBM],
+        in_specs=[VMEM, HBM],
         out_specs=[VMEM] * 5,
         out_shape=[jax.ShapeDtypeStruct((ROWS, 512), F32), jax.ShapeDtypeStruct((ROWS, 256), F32),
                    jax.ShapeDtypeStruct((FIELDS, LANES), F32), jax.ShapeDtypeStruct((8, LANES), F32),
@@ -160,7 +167,7 @@
         scratch_shapes=[pltpu.VMEM((2, 3 * COLS, 256), BF16), pltpu.SemaphoreType.DMA((2,))],
         compiler_params=pltpu.CompilerParams(vmem_limit_bytes=WHOLE),
         name="row_sums",
-    )(where, facts, x)
+    )(facts, x)
 
 
 def zonal_difference(x):
@@ -172,8 +179,8 @@
     return 0.5 * (ahead - behind)
 
 
-def local_sums_kernel(where_ref, table_ref, x_ref, _, out_ref):
-    top = where_ref[0] == 0
+def local_sums_kernel(table_ref, x_ref, _, out_ref):
+    top = lat_index() == 0
     count = 2 * SCALES * GROUP
     shape = (count, LANES)
     out_row = iota(shape, 0)
@@ -230,22 +237,22 @@
                 out_ref[group // 3, side, s, group % 3] = acc[k:k + GROUP]
 
 
-def local_sums(where, table, x, before):
+def local_sums(table, x, before):
     out = pl.pallas_call(
         local_sums_kernel,
-        in_specs=[SMEM, VMEM, VMEM, ANY],
+        in_specs=[VMEM, VMEM, ANY],
         out_specs=VMEM,
         out_shape=jax.ShapeDtypeStruct((2, 2, SCALES, 3, GROUP, COLS), F32),
         compiler_params=params(),
         cost_estimate=pl.CostEstimate(flops=600000000, bytes_accessed=4_000_000, transcendentals=0),
         name="local_sums",
-    )(where, table, x, before)
+    )(table, x, before)
     return out.reshape(2, 2 * HALF_ROWS, COLS)
 
 
-def lon_merge_kernel(where_ref, lanes_ref, own_ref, g1_ref, g2_ref, g3_ref, _, part_ref, send_ref):
-    y = where_ref[1] & 3
-    high = where_ref[1] >= 4
+def lon_merge_kernel(lanes_ref, own_ref, g1_ref, g2_ref, g3_ref, _, part_ref, send_ref):
+    y = lon_index() & 3
+    high = lon_index() >= 4
     yf = y.astype(F32)
     zonal, _ = lane_kinds((1, LANES))
     lane = iota((1, LANES), 1)
@@ -280,15 +287,15 @@
         send_ref[:, tile * 128:tile * 128 + 128] = jnp.where(high, right_total - image * left_total, left_total)
 
 
-def lon_merge(where, lanes, own, got, after):
+def lon_merge(lanes, own, got, after):
     return pl.pallas_call(
         lon_merge_kernel,
-        in_specs=[SMEM] + [VMEM] * 5 + [ANY],
+        in_specs=[VMEM] * 5 + [ANY],
         out_specs=[VMEM, VMEM],
         out_shape=[jax.ShapeDtypeStruct((ROWS, 768), F32), jax.ShapeDtypeStruct((ROWS, 256), F32)],
         compiler_params=params(),
         name="lon_merge",
-    )(where, lanes, own, *got, after)
+    )(lanes, own, *got, after)
 
 
 def spread_edges(tile):
@@ -299,9 +306,9 @@
     return out
 
 
-def column_sums_kernel(where_ref, table_ref, lanes_ref, part_ref, theirs_ref, edge_ref, local_ref,
+def column_sums_kernel(table_ref, lanes_ref, part_ref, theirs_ref, edge_ref, local_ref,
                        carry_ref, keep_ref, send_ref):
-    lat, lon = where_ref[0], where_ref[1]
+    lat, lon = lat_index(), lon_index()
     y = lon & 3
     yf = y.astype(F32)
     high = lon >= 4
@@ -368,16 +375,16 @@
             ref[rows, :] = local_ref[half, rows, :] + pick(0) * fall + pick(1) * rise
 
 
-def column_sums(where, table, lanes, part, theirs, edge, local):
+def column_sums(table, lanes, part, theirs, edge, local):
     half = jax.ShapeDtypeStruct((2 * HALF_ROWS, COLS), F32)
     return pl.pallas_call(
         column_sums_kernel,
-        in_specs=[SMEM] + [VMEM] * 6,
+        in_specs=[VMEM] * 6,
         out_specs=[VMEM] * 3,
         out_shape=[jax.ShapeDtypeStruct((ROWS, 512), F32), half, half],
         compiler_params=params(),
         name="column_sums",
-    )(where, table, lanes, part, theirs, edge, local)
+    )(table, lanes, part, theirs, edge, local)
 
 
 LEFT = slice(0, HALF_ROWS)
@@ -385,8 +392,8 @@
 STEPS = 21
 
 
-def steps_kernel(where_ref, table_ref, _, out_ref):
-    lat = where_ref[0]
+def steps_kernel(table_ref, _, out_ref):
+    lat = lat_index()
     odd = (lat & 1) == 1
     odd_chip = ((lat >> 1) & 1) == 1
     z = lat >> 2
@@ -415,15 +422,15 @@
         out_ref[k] = value
 
 
-def lat_steps(where, table, before):
+def lat_steps(table, before):
     return pl.pallas_call(
         steps_kernel,
-        in_specs=[SMEM, VMEM, ANY],
+        in_specs=[VMEM, ANY],
         out_specs=VMEM,
         out_shape=jax.ShapeDtypeStruct((STEPS, HALF_ROWS, LANES), F32),
         compiler_params=params(),
         name="lat_steps",
-    )(where, table, before)
+    )(table, before)
 
 
 def by_tile(body):
@@ -451,8 +458,8 @@
     )(steps, keep, got)
 
 
-def quad_merge_kernel(where_ref, steps_ref, chip_ref, pair_ref, _, left_ref, s1_ref, s2_ref, s3_ref):
-    z = where_ref[0] >> 2
+def quad_merge_kernel(steps_ref, chip_ref, pair_ref, _, left_ref, s1_ref, s2_ref, s3_ref):
+    z = lat_index() >> 2
 
     def body(lanes):
         mine, other, image = steps_ref[2], steps_ref[3], steps_ref[4]
@@ -466,21 +473,21 @@
     by_tile(body)
 
 
-def quad_merge(where, steps, chip, pair, after):
+def quad_merge(steps, chip, pair, after):
     one = jax.ShapeDtypeStruct((HALF_ROWS, COLS), F32)
     return pl.pallas_call(
         quad_merge_kernel,
-        in_specs=[SMEM] + [VMEM] * 3 + [ANY],
+        in_specs=[VMEM] * 3 + [ANY],
         out_specs=[VMEM] * 4,
         out_shape=[one] * 4,
         compiler_params=params(),
         name="quad_merge",
-    )(where, steps, chip, pair, after)
-
-
-def lat_carry_kernel(where_ref, steps_ref, keep_ref, got_ref, pair_ref, left_ref, g1_ref, g2_ref, g3_ref, _,
+    )(steps, chip, pair, after)
+
+
+def lat_carry_kernel(steps_ref, keep_ref, got_ref, pair_ref, left_ref, g1_ref, g2_ref, g3_ref, _,
                      own_ref, send_ref):
-    odd = (where_ref[0] & 1) == 1
+    odd = (lat_index() & 1) == 1
 
     def body(lanes):
         left, right, whole = 0.0, 0.0, steps_ref[14] * left_ref[:, lanes]
@@ -504,20 +511,20 @@
     by_tile(body)
 
 
-def lat_carry(where, steps, keep, got, pair, left, gs, after):
+def lat_carry(steps, keep, got, pair, left, gs, after):
     half = jax.ShapeDtypeStruct((2 * HALF_ROWS, COLS), F32)
     return pl.pallas_call(
         lat_carry_kernel,
-        in_specs=[SMEM] + [VMEM] * 8 + [ANY],
+        in_specs=[VMEM] * 8 + [ANY],
         out_specs=[VMEM] * 2,
         out_shape=[half, half],
         compiler_params=params(),
         name="lat_carry",
-    )(where, steps, keep, got, pair, left, *gs, after)
-
-
-def local_filter_kernel(starts, use_x, use_carry, where_ref, table_ref, carry_ref, x_ref, base_ref, out_ref):
-    top = where_ref[0] == 0
+    )(steps, keep, got, pair, left, *gs, after)
+
+
+def local_filter_kernel(starts, use_x, use_carry, table_ref, carry_ref, x_ref, base_ref, out_ref):
+    top = lat_index() == 0
     shape = (ROWS, LANES)
     row = fiota(shape, 0)
     lane = iota(shape, 1)
@@ -641,16 +648,16 @@
                 out_ref[f - starts[0], :, lanes] = part
 
 
-def local_filter(where, table, carry, x, first, count, before, base=None):
+def local_filter(table, carry, x, first, count, before, base=None):
     starts = tuple(range(first, first + count, GROUP))
     use_x, use_carry = base is None, carry is not None
-    names = ["where", "table"] + ["carry"] * use_carry + ["x"] * use_x + ["base"] * (base is not None) + ["before"]
-    arrays = {"where": where, "table": table, "carry": carry, "x": x, "base": base, "before": before}
-    specs = {"where": SMEM, "before": ANY}
+    names = ["table"] + ["carry"] * use_carry + ["x"] * use_x + ["base"] * (base is not None) + ["before"]
+    arrays = {"table": table, "carry": carry, "x": x, "base": base, "before": before}
+    specs = {"before": ANY}
 
     def body(*refs):
         by_name = dict(zip(names, refs))
-        local_filter_kernel(starts, use_x, use_carry, by_name["where"], by_name["table"], by_name.get("carry"),
+        local_filter_kernel(starts, use_x, use_carry, by_name["table"], by_name.get("carry"),
                             by_name.get("x"), by_name.get("base"), refs[len(names)])
 
     return pl.pallas_call(
@@ -691,28 +698,28 @@
             store(i, lanes, total)
 
 
-def finish_own_kernel(where_ref, table_ref, carry_ref, z0_ref, z1_ref, z2_ref, out_ref):
+def finish_own_kernel(table_ref, carry_ref, z0_ref, z1_ref, z2_ref, out_ref):
     for part in range(3):
         def store(i, lanes, value):
             out_ref[part * GROUP + i, :, lanes] = value
 
-        add_carries(where_ref[0] & 1, table_ref, carry_ref, (z0_ref, z1_ref, z2_ref), part, store)
-
-
-def finish_own(where, table, carry, parts):
+        add_carries(lat_index() & 1, table_ref, carry_ref, (z0_ref, z1_ref, z2_ref), part, store)
+
+
+def finish_own(table, carry, parts):
     return pl.pallas_call(
         finish_own_kernel,
-        in_specs=[SMEM] + [VMEM] * 5,
+        in_specs=[VMEM] * 5,
         out_specs=VMEM,
         out_shape=jax.ShapeDtypeStruct((HALF, ROWS, COLS), F32),
         compiler_params=params(),
         cost_estimate=pl.CostEstimate(flops=1_000_000_000, bytes_accessed=2_000_000, transcendentals=0),
         name="finish_own",
-    )(where, table, carry.reshape(2, SCALES, 3, GROUP, COLS), *parts)
-
-
-def finish_kernel(where_ref, table_ref, carry_ref, z0_ref, z1_ref, z2_ref, own_ref, out_ref, buf_ref, sem):
-    half = 1 - (where_ref[0] & 1)
+    )(table, carry.reshape(2, SCALES, 3, GROUP, COLS), *parts)
+
+
+def finish_kernel(table_ref, carry_ref, z0_ref, z1_ref, z2_ref, own_ref, out_ref, buf_ref, sem):
+    half = 1 - (lat_index() & 1)
     ready = pltpu.make_async_copy(own_ref, out_ref.at[pl.ds((1 - half) * HALF, HALF)], sem.at[3])
     ready.start()
     copies = [ready]
@@ -728,16 +735,16 @@
         copy.wait()
 
 
-def finish(where, table, carry, parts, own):
+def finish(table, carry, parts, own):
     return pl.pallas_call(
         finish_kernel,
-        in_specs=[SMEM] + [VMEM] * 6,
+        in_specs=[VMEM] * 6,
         out_specs=HBM,
         out_shape=jax.ShapeDtypeStruct((FIELDS, ROWS, COLS), F32),
         scratch_shapes=[pltpu.VMEM((3, GROUP, ROWS, COLS), F32), pltpu.SemaphoreType.DMA((4,))],
         compiler_params=params(),
         name="finish",
-    )(where, table, carry.reshape(2, SCALES, 3, GROUP, COLS), *parts, own)
+    )(table, carry.reshape(2, SCALES, 3, GROUP, COLS), *parts, own)
 
 
 def partner(axis, count, bit):
@@ -745,28 +752,27 @@
 
 
 def shards(x, lengths, weights):
-    where = jnp.stack([lax.axis_index("lat"), lax.axis_index("lon")]).astype(jnp.int32)
     facts = jnp.concatenate([lengths.T, weights.T], axis=0)
-    sums, edge, table, lanes, held = row_sums(where, facts, x)
+    sums, edge, table, lanes, held = row_sums(facts, x)
     got = [partner("lon", NLON, d)(sums) for d in (1, 2, 3)]
-    early = local_filter(where, table, None, held, 32, 16, sums)
-    part, half = lon_merge(where, lanes, sums, got, early)
+    early = local_filter(table, None, held, 32, 16, sums)
+    part, half = lon_merge(lanes, sums, got, early)
     theirs = partner("lon", NLON, 4)(half)
-    local = local_sums(where, table, held, part)
-    steps = lat_steps(where, table, part)
-    carry, keep, send = column_sums(where, table, lanes, part, theirs, edge, local)
+    local = local_sums(table, held, part)
+    steps = lat_steps(table, part)
+    carry, keep, send = column_sums(table, lanes, part, theirs, edge, local)
     got_core = partner("lat", NLAT, 1)(send)
     chip = chip_merge(steps, keep, got_core)
     pair = partner("lat", NLAT, 2)(chip)
-    z0 = local_filter(where, table, carry, held, 0, 16, chip)
-    left, *sends = quad_merge(where, steps, chip, pair, z0)
+    z0 = local_filter(table, carry, held, 0, 16, chip)
+    left, *sends = quad_merge(steps, chip, pair, z0)
     gs = [partner("lat", NLAT, 4 * d)(t) for d, t in zip((1, 2, 3), sends)]
-    z1 = local_filter(where, table, carry, held, 16, 16, left)
-    z2 = local_filter(where, table, carry, held, 32, 16, z1, early)
-    own, other = lat_carry(where, steps, keep, got_core, pair, left, gs, z2)
+    z1 = local_filter(table, carry, held, 16, 16, left)
+    z2 = local_filter(table, carry, held, 32, 16, z1, early)
+    own, other = lat_carry(steps, keep, got_core, pair, left, gs, z2)
     got_carry = partner("lat", NLAT, 1)(other)
-    done = finish_own(where, table, own, (z0, z1, z2))
-    return finish(where, table, got_carry, (z0, z1, z2), done)
+    done = finish_own(table, own, (z0, z1, z2))
+    return finish(table, got_carry, (z0, z1, z2), done)
 
 
 def solution(mesh):

time: 52.5 us -> 48.2 us (0.918)
  Pallas kernels: 29.6 us -> 22.6 us
  waiting for transfers between devices: 4.39 us -> 7.12 us
    pallas_call x9, Pallas kernels: 16.3 us -> 11.5 us  [the longest x1 3.67 us: local_sums(): pl.pallas_call(local_sums_kernel, in_specs=[VMEM, VMEM, ANY], out_specs=V...]
    pallas_call x4, Pallas kernels: 13.3 us -> 11.1 us  [local_filter(): pl.pallas_call(body, in_specs=[specs.get(n, VMEM) for n in names], out_sp...]
    ppermute x3, waiting for transfers between devices: 1.51 us -> 2.56 us  [shards(): gs = [partner('lat', NLAT, 4 * d)(t) for d, t in zip((1, 2, 3), sends)]]
    ppermute x1, waiting for transfers between devices: 1.49 us -> 2.06 us  [shards(): pair = partner('lat', NLAT, 2)(chip)]
    ppermute x3, waiting for transfers between devices: 1.01 us -> 1.57 us  [shards(): got = [partner('lon', NLON, d)(sums) for d in (1, 2, 3)]]
    ppermute x1, waiting for transfers between devices: 0.38 us -> 0.92 us  [shards(): got_core = partner('lat', NLAT, 1)(send)]
  transfers between devices with their start and end apart: 10 -> 10, of which waited for: 4 -> 5; matrix products, arithmetic and copies ran while one was open for 0% -> 0% of each run, Pallas kernels for 38% -> 34%
where the time goes in v6:
time: 48.2 us; the launch traced here: 48 us
  Pallas kernels  22.6 us (47%)
  starting transfers between devices  17.3 us (36%)
  waiting for transfers between devices  7.12 us (15%)
  other arithmetic  0.71 us (1%)
    pallas_call x4, Pallas kernels, local_filter(): pl.pallas_call(body, in_specs=[specs.get(n, VMEM) for n in names], out_sp...  11.1 us
    ppermute x3, starting transfers between devices, shards(): gs = [partner('lat', NLAT, 4 * d)(t) for d, t in zip((1, 2, 3), sends)]  5.02 us
    ppermute x3, starting transfers between devices, shards(): got = [partner('lon', NLON, d)(sums) for d in (1, 2, 3)]  4.31 us
    pallas_call x1, Pallas kernels, local_sums(): pl.pallas_call(local_sums_kernel, in_specs=[VMEM, VMEM, ANY], out_specs=V...  3.67 us
    pallas_call x1, Pallas kernels, row_sums(): pl.pallas_call(row_sums_kernel, in_specs=[VMEM, HBM], out_specs=[VMEM] *...  3.33 us
    ppermute x1, starting transfers between devices, shards(): got_core = partner('lat', NLAT, 1)(send)  3.15 us
    ppermute x1, starting transfers between devices, shards(): theirs = partner('lon', NLON, 4)(half)  2.82 us
    ppermute x3, waiting for transfers between devices, shards(): gs = [partner('lat', NLAT, 4 * d)(t) for d, t in zip((1, 2, 3), sends)]  2.56 us
  transfers between devices with their start and end apart: 10, of which 5 were waited for; matrix products, arithmetic and copies ran while one was open for 0% of the time, Pallas kernels for 34%

profile of v6, /device:TPU:1, one launch (start us, length us, event | category | flops | bytes accessed | tf_op | source)
XLA Modules:
  0.0 48.0 jit_solution(5620560488854604482)
XLA Ops:
  0.0 0.7 %pad_maximum_fusion.len_ref = f32[6,48]{1,0:T(8,128)S(1)} fusion(f32[3,48]{1,0:T(4,128)} %bitcast.8, f32[3,48]{1,0:T(4,128)} %bitcast.9), kind=kLoop, calls=%fused_computation | loop fusion | flops 288 | bytes 2304 | tf_op jit(solution)/shard_map/concatenate | solution.py:755
  0.7 3.3 %row_sums.1 = (f32[48,512]{1,0:T(8,128)S(1)}, f32[48,256]{1,0:T(8,128)S(1)}, f32[48,128]{1,0:T(8,128)S(1)}, f32[8,128]{1,0:T(8,128)S(1)}, f32[48,48,384]{2,1,0:T(8,128)S(1)}) custom-call(f32[6,48]{1,0:T(8,128)S(1)} %pad_maximum_fusion.len_ref, f32[48,48,384]{2,1,0:T(8,128)} %x_ref.1), custom_call_target="tpu_custom_call" | custom-call | tf_op jit(solution)/shard_map/row_sums/pallas_call | solution.py:160
  4.0 3.6 %collective-permute-start.2 = (f32[48,512]{1,0:T(8,128)S(1)}, f32[48,512]{1,0:T(8,128)S(1)}, u32[]{:S(2)}, u32[]{:S(2)}) collective-permute-start(f32[48,512]{1,0:T(8,128)S(1)} %get-tuple-element.23.refs_2_.own_ref), channel_id=1, source_target_pairs={{0,3},{1,2},{2,1},{3,0},{4,7},{5,6},{6,5},{7,4},{8,11},{9,10},{10,... | collective-permute-start | bytes 294920 | tf_op jit(solution)/shard_map/ppermute | solution.py:757
  7.7 0.4 collective-permute-start.1
  8.0 0.3 collective-permute-start
  8.4 2.7 %local_filter.4._.refs_2_ = f32[16,48,384]{2,1,0:T(8,128)S(1)} custom-call(f32[48,128]{1,0:T(8,128)S(1)} %get-tuple-element.21.refs_0_.table_ref, f32[48,48,384]{2,1,0:T(8,128)S(1)} %get-tuple-element.24.refs_1_.x_ref.refs_2_, f32[48,512]{1,0:T(8,128)S(1)} %get-tuple-element.23.refs_2_.own_ref), custom_call_target="tpu_custom_call" | custom-call | flops 480000000 | bytes 2400000 | tf_op jit(solution)/shard_map/local_filter/pallas_call | solution.py:663
  11.1 0.4 collective-permute-done.2.g3_ref
  11.4 1.2 %collective-permute-done.1.g2_ref = f32[48,512]{1,0:T(8,128)S(1)} collective-permute-done((f32[48,512]{1,0:T(8,128)S(1)}, f32[48,512]{1,0:T(8,128)S(1)}, u32[]{:S(2)}, u32[]{:S(2)}) %collective-permute-start.1) | collective-permute-done | bytes 98336 | tf_op jit(solution)/shard_map/ppermute | solution.py:757
  12.7 0.0 collective-permute-done.g1_ref
  12.7 0.1 lon_merge.1
  12.8 2.8 %collective-permute-start.3 = (f32[48,256]{1,0:T(8,128)S(1)}, f32[48,256]{1,0:T(8,128)S(1)}, u32[]{:S(2)}, u32[]{:S(2)}) collective-permute-start(f32[48,256]{1,0:T(8,128)S(1)} %get-tuple-element.26), channel_id=1, source_target_pairs={{0,4},{1,5},{2,6},{3,7},{4,0},{5,1},{6,2},{7,3},{8,12},{9,13},{10,... | collective-permute-start | bytes 147464 | tf_op jit(solution)/shard_map/ppermute | solution.py:760
  15.6 3.7 %local_sums.1 = f32[2,2,3,3,8,384]{5,4,3,2,1,0:T(8,128)S(1)} custom-call(f32[48,128]{1,0:T(8,128)S(1)} %get-tuple-element.21.refs_0_.table_ref, f32[48,48,384]{2,1,0:T(8,128)S(1)} %get-tuple-element.24.refs_1_.x_ref.refs_2_, f32[48,768]{1,0:T(8,128)S(1)} %get-tuple-element.25._.part_ref), custom_call_target="tpu_custom_call" | custom-call | flops 600000000 | bytes 4000000 | tf_op jit(solution)/shard_map/local_sums/pallas_call | solution.py:241
  19.2 0.0 collective-permute-done.3.theirs_ref
  19.3 0.5 %column_sums.1 = (f32[48,512]{1,0:T(8,128)S(1)}, f32[144,384]{1,0:T(8,128)S(1)}, f32[144,384]{1,0:T(8,128)S(1)}) custom-call(f32[48,128]{1,0:T(8,128)S(1)} %get-tuple-element.21.refs_0_.table_ref, f32[8,128]{1,0:T(8,128)S(1)} %get-tuple-element.22.lanes_ref, f32[48,768]{1,0:T(8,128)S(1)} %get-tuple-element.25._.part_ref, ...), custom_call_target="tpu_custom_call" | custom-call | tf_op jit(solution)/shard_map/column_sums/pallas_call | solution.py:380
  19.8 3.2 %collective-permute-start.4 = (f32[144,384]{1,0:T(8,128)S(1)}, f32[144,384]{1,0:T(8,128)S(1)}, u32[]{:S(2)}, u32[]{:S(2)}) collective-permute-start(f32[144,384]{1,0:T(8,128)S(1)} %get-tuple-element.29), channel_id=1, source_target_pairs={{0,8},{8,0},{16,24},{24,16},{32,40},{40,32},{48,56},{56,48},{64,72... | collective-permute-start | bytes 663560 | tf_op jit(solution)/shard_map/ppermute | solution.py:764
  22.9 0.2 lat_steps.1.steps_ref
  23.1 0.9 %collective-permute-done.4.got_ref = f32[144,384]{1,0:T(8,128)S(1)} collective-permute-done((f32[144,384]{1,0:T(8,128)S(1)}, f32[144,384]{1,0:T(8,128)S(1)}, u32[]{:S(2)}, u32[]{:S(2)}) %collective-permute-start.4) | collective-permute-done | bytes 221216 | tf_op jit(solution)/shard_map/ppermute | solution.py:764
  24.0 0.6 %collective-permute-start.5 = (f32[144,384]{1,0:T(8,128)S(1)}, f32[144,384]{1,0:T(8,128)S(1)}, u32[]{:S(2)}, u32[]{:S(2)}) collective-permute-start(f32[144,384]{1,0:T(8,128)S(1)} %chip_merge.1.refs_3_.chip_ref), channel_id=1, source_target_pairs={{0,16},{8,24},{16,0},{24,8},{32,48},{40,56},{48,32},{56,40},{64,80... | collective-permute-start | bytes 663560 | tf_op jit(solution)/shard_map/ppermute | solution.py:766
  24.6 4.3 %local_filter.5._.z0_ref = f32[16,48,384]{2,1,0:T(8,128)S(1)} custom-call(f32[48,128]{1,0:T(8,128)S(1)} %get-tuple-element.21.refs_0_.table_ref, f32[48,512]{1,0:T(8,128)S(1)} %get-tuple-element.30.refs_1_, f32[48,48,384]{2,1,0:T(8,128)S(1)} %get-tuple-element.24.refs_1_.x_ref.refs_2_, f32[144,384]{1,0:T(8,128)S(1)} %chip_merge.1.refs_3_.chip_ref), custom_call_target="tpu_custom_call" | custom-call | flops 480000000 | bytes 2400000 | tf_op jit(solution)/shard_map/local_filter/pallas_call | solution.py:663
  28.9 2.1 %collective-permute-done.5.pair_ref = f32[144,384]{1,0:T(8,128)S(1)} collective-permute-done((f32[144,384]{1,0:T(8,128)S(1)}, f32[144,384]{1,0:T(8,128)S(1)}, u32[]{:S(2)}, u32[]{:S(2)}) %collective-permute-start.5) | collective-permute-done | bytes 221216 | tf_op jit(solution)/shard_map/ppermute | solution.py:766
  30.9 0.1 quad_merge.1
  31.0 1.7 %collective-permute-start.6 = (f32[72,384]{1,0:T(8,128)S(1)}, f32[72,384]{1,0:T(8,128)S(1)}, u32[]{:S(2)}, u32[]{:S(2)}) collective-permute-start(f32[72,384]{1,0:T(8,128)S(1)} %get-tuple-element.32), channel_id=1, source_target_pairs={{0,32},{8,40},{16,48},{24,56},{32,0},{40,8},{48,16},{56,24},{64,96... | collective-permute-start | bytes 331784 | tf_op jit(solution)/shard_map/ppermute | solution.py:769
  32.7 3.3 %collective-permute-start.7 = (f32[72,384]{1,0:T(8,128)S(1)}, f32[72,384]{1,0:T(8,128)S(1)}, u32[]{:S(2)}, u32[]{:S(2)}) collective-permute-start(f32[72,384]{1,0:T(8,128)S(1)} %get-tuple-element.33), channel_id=1, source_target_pairs={{0,64},{8,72},{16,80},{24,88},{32,96},{40,104},{48,112},{56,120},{... | collective-permute-start | bytes 331784 | tf_op jit(solution)/shard_map/ppermute | solution.py:769
  36.0 0.0 collective-permute-start.8
  36.0 2.8 %local_filter.6.refs_3_.z1_ref = f32[16,48,384]{2,1,0:T(8,128)S(1)} custom-call(f32[48,128]{1,0:T(8,128)S(1)} %get-tuple-element.21.refs_0_.table_ref, f32[48,512]{1,0:T(8,128)S(1)} %get-tuple-element.30.refs_1_, f32[48,48,384]{2,1,0:T(8,128)S(1)} %get-tuple-element.24.refs_1_.x_ref.refs_2_, f32[72,384]{1,0:T(8,128)S(1)} %get-tuple-element.31.refs_3_.left_ref), custom_call_target="tpu_custom_call" | custom-call | flops 480000000 | bytes 2400000 | tf_op jit(solution)/shard_map/local_filter/pallas_call | solution.py:663
  38.9 1.3 %local_filter.7._.z2_ref = f32[16,48,384]{2,1,0:T(8,128)S(1)} custom-call(f32[48,128]{1,0:T(8,128)S(1)} %get-tuple-element.21.refs_0_.table_ref, f32[48,512]{1,0:T(8,128)S(1)} %get-tuple-element.30.refs_1_, f32[16,48,384]{2,1,0:T(8,128)S(1)} %local_filter.4._.refs_2_, f32[16,48,384]{2,1,0:T(8,128)S(1)} %local_filter.6.refs_3_.z1_ref), custom_call_target="tpu_custom_call" | custom-call | flops 480000000 | bytes 2400000 | tf_op jit(solution)/shard_map/local_filter/pallas_call | solution.py:663
  40.2 0.0 collective-permute-done.6.g1_ref
  40.2 0.0 collective-permute-done.7.g2_ref
  40.2 2.6 %collective-permute-done.8.g3_ref = f32[72,384]{1,0:T(8,128)S(1)} collective-permute-done((f32[72,384]{1,0:T(8,128)S(1)}, f32[72,384]{1,0:T(8,128)S(1)}, u32[]{:S(2)}, u32[]{:S(2)}) %collective-permute-start.8) | collective-permute-done | bytes 110624 | tf_op jit(solution)/shard_map/ppermute | solution.py:769
  42.7 0.2 lat_carry.1
  42.9 1.4 %collective-permute-start.9 = (f32[144,384]{1,0:T(8,128)S(1)}, f32[144,384]{1,0:T(8,128)S(1)}, u32[]{:S(2)}, u32[]{:S(2)}) collective-permute-start(f32[144,384]{1,0:T(8,128)S(1)} %get-tuple-element.35), channel_id=1, source_target_pairs={{0,8},{8,0},{16,24},{24,16},{32,40},{40,32},{48,56},{56,48},{64,72... | collective-permute-start | bytes 663560 | tf_op jit(solution)/shard_map/ppermute | solution.py:773
  44.3 1.1 %finish_own.1.own_ref = f32[24,48,384]{2,1,0:T(8,128)S(1)} custom-call(f32[48,128]{1,0:T(8,128)S(1)} %get-tuple-element.21.refs_0_.table_ref, f32[2,3,3,8,384]{4,3,2,1,0:T(8,128)S(1)} %bitcast.6, f32[16,48,384]{2,1,0:T(8,128)S(1)} %local_filter.5._.z0_ref, f32[16,48,384]{2,1,0:T(8,128)S(1)} %local_filter.6.refs_3_.z1_ref, ...), custom_call_target="tpu_custom_call" | custom-call | flops 1000000000 | bytes 2000000 | tf_op jit(solution)/shard_map/finish_own/pallas_call | solution.py:710
  45.5 0.0 collective-permute-done.9
  45.5 2.4 %finish.1 = f32[48,48,384]{2,1,0:T(8,128)} custom-call(f32[48,128]{1,0:T(8,128)S(1)} %get-tuple-element.21.refs_0_.table_ref, f32[2,3,3,8,384]{4,3,2,1,0:T(8,128)S(1)} %bitcast.7, f32[16,48,384]{2,1,0:T(8,128)S(1)} %local_filter.5._.z0_ref, f32[16,48,384]{2,1,0:T(8,128)S(1)} %local_filter.6.refs_3_.z1_ref, f32[16,48,384]{2,1,0:T(8,128)S(1)} %local_filter.7._.z2_ref, ...), custom_call_target="tpu_custom_call" | custom-call | tf_op jit(solution)/shard_map/finish/pallas_call | solution.py:739
  (1 shorter events, 0.0 us)
Async XLA Ops:
  4.0 7.4 %collective-permute-start.2 = (f32[48,512]{1,0:T(8,128)S(1)}, f32[48,512]{1,0:T(8,128)S(1)}, u32[]{:S(2)}, u32[]{:S(2)}) collective-permute-start(f32[48,512]{1,0:T(8,128)S(1)} %get-tuple-element.23.refs_2_.own_ref), channel_id=1, source_target_pairs={{0,3},{1,2},{2,1},{3,0},{4,7},{5,6},{6,5},{7,4},{8,11},{9,10},{10,... | collective-permute-start | bytes 294920 | tf_op jit(solution)/shard_map/ppermute | solution.py:757
  7.7 5.0 %collective-permute-start.1 = (f32[48,512]{1,0:T(8,128)S(1)}, f32[48,512]{1,0:T(8,128)S(1)}, u32[]{:S(2)}, u32[]{:S(2)}) collective-permute-start(f32[48,512]{1,0:T(8,128)S(1)} %get-tuple-element.23.refs_2_.own_ref), channel_id=1, source_target_pairs={{0,2},{1,3},{2,0},{3,1},{4,6},{5,7},{6,4},{7,5},{8,10},{9,11},{10,... | collective-permute-start | bytes 294920 | tf_op jit(solution)/shard_map/ppermute | solution.py:757
  8.0 4.6 %collective-permute-start = (f32[48,512]{1,0:T(8,128)S(1)}, f32[48,512]{1,0:T(8,128)S(1)}, u32[]{:S(2)}, u32[]{:S(2)}) collective-permute-start(f32[48,512]{1,0:T(8,128)S(1)} %get-tuple-element.23.refs_2_.own_ref), channel_id=1, source_target_pairs={{0,1},{1,0},{2,3},{3,2},{4,5},{5,4},{6,7},{7,6},{8,9},{9,8},{10,11... | collective-permute-start | bytes 294920 | tf_op jit(solution)/shard_map/ppermute | solution.py:757
  12.8 6.5 %collective-permute-start.3 = (f32[48,256]{1,0:T(8,128)S(1)}, f32[48,256]{1,0:T(8,128)S(1)}, u32[]{:S(2)}, u32[]{:S(2)}) collective-permute-start(f32[48,256]{1,0:T(8,128)S(1)} %get-tuple-element.26), channel_id=1, source_target_pairs={{0,4},{1,5},{2,6},{3,7},{4,0},{5,1},{6,2},{7,3},{8,12},{9,13},{10,... | collective-permute-start | bytes 147464 | tf_op jit(solution)/shard_map/ppermute | solution.py:760
  19.8 4.3 %collective-permute-start.4 = (f32[144,384]{1,0:T(8,128)S(1)}, f32[144,384]{1,0:T(8,128)S(1)}, u32[]{:S(2)}, u32[]{:S(2)}) collective-permute-start(f32[144,384]{1,0:T(8,128)S(1)} %get-tuple-element.29), channel_id=1, source_target_pairs={{0,8},{8,0},{16,24},{24,16},{32,40},{40,32},{48,56},{56,48},{64,72... | collective-permute-start | bytes 663560 | tf_op jit(solution)/shard_map/ppermute | solution.py:764
  24.0 6.9 %collective-permute-start.5 = (f32[144,384]{1,0:T(8,128)S(1)}, f32[144,384]{1,0:T(8,128)S(1)}, u32[]{:S(2)}, u32[]{:S(2)}) collective-permute-start(f32[144,384]{1,0:T(8,128)S(1)} %chip_merge.1.refs_3_.chip_ref), channel_id=1, source_target_pairs={{0,16},{8,24},{16,0},{24,8},{32,48},{40,56},{48,32},{56,40},{64,80... | collective-permute-start | bytes 663560 | tf_op jit(solution)/shard_map/ppermute | solution.py:766
  31.0 9.2 %collective-permute-start.6 = (f32[72,384]{1,0:T(8,128)S(1)}, f32[72,384]{1,0:T(8,128)S(1)}, u32[]{:S(2)}, u32[]{:S(2)}) collective-permute-start(f32[72,384]{1,0:T(8,128)S(1)} %get-tuple-element.32), channel_id=1, source_target_pairs={{0,32},{8,40},{16,48},{24,56},{32,0},{40,8},{48,16},{56,24},{64,96... | collective-permute-start | bytes 331784 | tf_op jit(solution)/shard_map/ppermute | solution.py:769
  32.7 7.4 %collective-permute-start.7 = (f32[72,384]{1,0:T(8,128)S(1)}, f32[72,384]{1,0:T(8,128)S(1)}, u32[]{:S(2)}, u32[]{:S(2)}) collective-permute-start(f32[72,384]{1,0:T(8,128)S(1)} %get-tuple-element.33), channel_id=1, source_target_pairs={{0,64},{8,72},{16,80},{24,88},{32,96},{40,104},{48,112},{56,120},{... | collective-permute-start | bytes 331784 | tf_op jit(solution)/shard_map/ppermute | solution.py:769
  36.0 6.7 %collective-permute-start.8 = (f32[72,384]{1,0:T(8,128)S(1)}, f32[72,384]{1,0:T(8,128)S(1)}, u32[]{:S(2)}, u32[]{:S(2)}) collective-permute-start(f32[72,384]{1,0:T(8,128)S(1)} %get-tuple-element.34), channel_id=1, source_target_pairs={{0,96},{8,104},{16,112},{24,120},{32,64},{40,72},{48,80},{56,88},{... | collective-permute-start | bytes 331784 | tf_op jit(solution)/shard_map/ppermute | solution.py:769
  42.9 2.5 %collective-permute-start.9 = (f32[144,384]{1,0:T(8,128)S(1)}, f32[144,384]{1,0:T(8,128)S(1)}, u32[]{:S(2)}, u32[]{:S(2)}) collective-permute-start(f32[144,384]{1,0:T(8,128)S(1)} %get-tuple-element.35), channel_id=1, source_target_pairs={{0,8},{8,0},{16,24},{24,16},{32,40},{40,32},{48,56},{56,48},{64,72... | collective-permute-start | bytes 663560 | tf_op jit(solution)/shard_map/ppermute | solution.py:773

commit v7 on v6

--- a/solution.py
+++ b/solution.py
@@ -250,7 +250,7 @@
     return out.reshape(2, 2 * HALF_ROWS, COLS)
 
 
-def lon_merge_kernel(lanes_ref, own_ref, g1_ref, g2_ref, g3_ref, _, part_ref, send_ref):
+def lon_merge_kernel(lanes_ref, own_ref, g1_ref, g3_ref, g2_ref, _, part_ref, send_ref):
     y = lon_index() & 3
     high = lon_index() >= 4
     yf = y.astype(F32)
@@ -295,7 +295,7 @@
         out_shape=[jax.ShapeDtypeStruct((ROWS, 768), F32), jax.ShapeDtypeStruct((ROWS, 256), F32)],
         compiler_params=params(),
         name="lon_merge",
-    )(lanes, own, *got, after)
+    )(lanes, own, got[0], got[2], got[1], after)
 
 
 def spread_edges(tile):
@@ -485,7 +485,7 @@
     )(steps, chip, pair, after)
 
 
-def lat_carry_kernel(steps_ref, keep_ref, got_ref, pair_ref, left_ref, g1_ref, g2_ref, g3_ref, _,
+def lat_carry_kernel(steps_ref, keep_ref, got_ref, pair_ref, left_ref, g2_ref, g1_ref, g3_ref, _,
                      own_ref, send_ref):
     odd = (lat_index() & 1) == 1
 
@@ -520,7 +520,7 @@
         out_shape=[half, half],
         compiler_params=params(),
         name="lat_carry",
-    )(steps, keep, got, pair, left, *gs, after)
+    )(steps, keep, got, pair, left, gs[1], gs[0], gs[2], after)
 
 
 def local_filter_kernel(starts, use_x, use_carry, table_ref, carry_ref, x_ref, base_ref, out_ref):

time: 48.2 us -> 46.4 us (0.963)
  waiting for transfers between devices: 7.12 us -> 4.87 us
  starting transfers between devices: 17.3 us -> 17.8 us
    ppermute x3, waiting for transfers between devices: 2.56 us -> 0.71 us  [shards(): gs = [partner('lat', NLAT, 4 * d)(t) for d, t in zip((1, 2, 3), sends)]]
    ppermute x1, starting transfers between devices: 1.41 us -> 2.94 us  [shards(): got_carry = partner('lat', NLAT, 1)(other)]
    ppermute x1, starting transfers between devices: 3.15 us -> 2.46 us  [shards(): got_core = partner('lat', NLAT, 1)(send)]
    ppermute x3, starting transfers between devices: 5.02 us -> 4.42 us  [shards(): gs = [partner('lat', NLAT, 4 * d)(t) for d, t in zip((1, 2, 3), sends)]]
  transfers between devices with their start and end apart: 10 -> 10, of which waited for: 5 -> 4; matrix products, arithmetic and copies ran while one was open for 0% -> 0% of each run, Pallas kernels for 34% -> 35%
where the time goes in v7:
time: 46.4 us; the launch traced here: 46.3 us
  Pallas kernels  22.6 us (49%)
  starting transfers between devices  17.8 us (38%)
  waiting for transfers between devices  4.87 us (10%)
  other arithmetic  0.71 us (2%)
    pallas_call x4, Pallas kernels, local_filter(): pl.pallas_call(body, in_specs=[specs.get(n, VMEM) for n in names], out_sp...  11.1 us
    ppermute x3, starting transfers between devices, shards(): got = [partner('lon', NLON, d)(sums) for d in (1, 2, 3)]  4.6 us
    ppermute x3, starting transfers between devices, shards(): gs = [partner('lat', NLAT, 4 * d)(t) for d, t in zip((1, 2, 3), sends)]  4.42 us
    pallas_call x1, Pallas kernels, local_sums(): pl.pallas_call(local_sums_kernel, in_specs=[VMEM, VMEM, ANY], out_specs=V...  3.67 us
    pallas_call x1, Pallas kernels, row_sums(): pl.pallas_call(row_sums_kernel, in_specs=[VMEM, HBM], out_specs=[VMEM] *...  3.33 us
    ppermute x1, starting transfers between devices, shards(): got_carry = partner('lat', NLAT, 1)(other)  2.94 us
    ppermute x1, starting transfers between devices, shards(): theirs = partner('lon', NLON, 4)(half)  2.82 us
    ppermute x1, starting transfers between devices, shards(): got_core = partner('lat', NLAT, 1)(send)  2.46 us
  transfers between devices with their start and end apart: 10, of which 4 were waited for; matrix products, arithmetic and copies ran while one was open for 0% of the time, Pallas kernels for 35%

profile of v7, /device:TPU:1, one launch (start us, length us, event | category | flops | bytes accessed | tf_op | source)
XLA Modules:
  0.0 46.3 jit_solution(14125783041386963625)
XLA Ops:
  0.0 0.7 %pad_maximum_fusion.len_ref = f32[6,48]{1,0:T(8,128)S(1)} fusion(f32[3,48]{1,0:T(4,128)} %bitcast.8, f32[3,48]{1,0:T(4,128)} %bitcast.9), kind=kLoop, calls=%fused_computation | loop fusion | flops 288 | bytes 2304 | tf_op jit(solution)/shard_map/concatenate | solution.py:755
  0.7 3.3 %row_sums.1 = (f32[48,512]{1,0:T(8,128)S(1)}, f32[48,256]{1,0:T(8,128)S(1)}, f32[48,128]{1,0:T(8,128)S(1)}, f32[8,128]{1,0:T(8,128)S(1)}, f32[48,48,384]{2,1,0:T(8,128)S(1)}) custom-call(f32[6,48]{1,0:T(8,128)S(1)} %pad_maximum_fusion.len_ref, f32[48,48,384]{2,1,0:T(8,128)} %x_ref.1), custom_call_target="tpu_custom_call" | custom-call | tf_op jit(solution)/shard_map/row_sums/pallas_call | solution.py:160
  4.0 3.8 %collective-permute-start.2 = (f32[48,512]{1,0:T(8,128)S(1)}, f32[48,512]{1,0:T(8,128)S(1)}, u32[]{:S(2)}, u32[]{:S(2)}) collective-permute-start(f32[48,512]{1,0:T(8,128)S(1)} %get-tuple-element.23.refs_2_.own_ref), channel_id=1, source_target_pairs={{0,2},{1,3},{2,0},{3,1},{4,6},{5,7},{6,4},{7,5},{8,10},{9,11},{10,... | collective-permute-start | bytes 294920 | tf_op jit(solution)/shard_map/ppermute | solution.py:757
  7.9 0.8 %collective-permute-start.1 = (f32[48,512]{1,0:T(8,128)S(1)}, f32[48,512]{1,0:T(8,128)S(1)}, u32[]{:S(2)}, u32[]{:S(2)}) collective-permute-start(f32[48,512]{1,0:T(8,128)S(1)} %get-tuple-element.23.refs_2_.own_ref), channel_id=1, source_target_pairs={{0,3},{1,2},{2,1},{3,0},{4,7},{5,6},{6,5},{7,4},{8,11},{9,10},{10,... | collective-permute-start | bytes 294920 | tf_op jit(solution)/shard_map/ppermute | solution.py:757
  8.7 0.0 collective-permute-start
  8.7 2.7 %local_filter.4._.refs_2_ = f32[16,48,384]{2,1,0:T(8,128)S(1)} custom-call(f32[48,128]{1,0:T(8,128)S(1)} %get-tuple-element.21.refs_0_.table_ref, f32[48,48,384]{2,1,0:T(8,128)S(1)} %get-tuple-element.24.refs_1_.x_ref.refs_2_, f32[48,512]{1,0:T(8,128)S(1)} %get-tuple-element.23.refs_2_.own_ref), custom_call_target="tpu_custom_call" | custom-call | flops 480000000 | bytes 2400000 | tf_op jit(solution)/shard_map/local_filter/pallas_call | solution.py:663
  11.4 0.0 collective-permute-done.2.g2_ref
  11.4 1.2 %collective-permute-done.1.g3_ref = f32[48,512]{1,0:T(8,128)S(1)} collective-permute-done((f32[48,512]{1,0:T(8,128)S(1)}, f32[48,512]{1,0:T(8,128)S(1)}, u32[]{:S(2)}, u32[]{:S(2)}) %collective-permute-start.1) | collective-permute-done | bytes 98336 | tf_op jit(solution)/shard_map/ppermute | solution.py:757
  12.6 0.0 collective-permute-done.g1_ref
  12.6 0.1 lon_merge.1
  12.6 2.8 %collective-permute-start.3 = (f32[48,256]{1,0:T(8,128)S(1)}, f32[48,256]{1,0:T(8,128)S(1)}, u32[]{:S(2)}, u32[]{:S(2)}) collective-permute-start(f32[48,256]{1,0:T(8,128)S(1)} %get-tuple-element.26), channel_id=1, source_target_pairs={{0,4},{1,5},{2,6},{3,7},{4,0},{5,1},{6,2},{7,3},{8,12},{9,13},{10,... | collective-permute-start | bytes 147464 | tf_op jit(solution)/shard_map/ppermute | solution.py:760
  15.5 3.7 %local_sums.1 = f32[2,2,3,3,8,384]{5,4,3,2,1,0:T(8,128)S(1)} custom-call(f32[48,128]{1,0:T(8,128)S(1)} %get-tuple-element.21.refs_0_.table_ref, f32[48,48,384]{2,1,0:T(8,128)S(1)} %get-tuple-element.24.refs_1_.x_ref.refs_2_, f32[48,768]{1,0:T(8,128)S(1)} %get-tuple-element.25._.part_ref), custom_call_target="tpu_custom_call" | custom-call | flops 600000000 | bytes 4000000 | tf_op jit(solution)/shard_map/local_sums/pallas_call | solution.py:241
  19.1 0.0 collective-permute-done.3.theirs_ref
  19.2 0.5 %column_sums.1 = (f32[48,512]{1,0:T(8,128)S(1)}, f32[144,384]{1,0:T(8,128)S(1)}, f32[144,384]{1,0:T(8,128)S(1)}) custom-call(f32[48,128]{1,0:T(8,128)S(1)} %get-tuple-element.21.refs_0_.table_ref, f32[8,128]{1,0:T(8,128)S(1)} %get-tuple-element.22.lanes_ref, f32[48,768]{1,0:T(8,128)S(1)} %get-tuple-element.25._.part_ref, ...), custom_call_target="tpu_custom_call" | custom-call | tf_op jit(solution)/shard_map/column_sums/pallas_call | solution.py:380
  19.6 2.5 %collective-permute-start.4 = (f32[144,384]{1,0:T(8,128)S(1)}, f32[144,384]{1,0:T(8,128)S(1)}, u32[]{:S(2)}, u32[]{:S(2)}) collective-permute-start(f32[144,384]{1,0:T(8,128)S(1)} %get-tuple-element.29), channel_id=1, source_target_pairs={{0,8},{8,0},{16,24},{24,16},{32,40},{40,32},{48,56},{56,48},{64,72... | collective-permute-start | bytes 663560 | tf_op jit(solution)/shard_map/ppermute | solution.py:764
  22.1 0.2 lat_steps.1.steps_ref
  22.3 0.9 %collective-permute-done.4.got_ref = f32[144,384]{1,0:T(8,128)S(1)} collective-permute-done((f32[144,384]{1,0:T(8,128)S(1)}, f32[144,384]{1,0:T(8,128)S(1)}, u32[]{:S(2)}, u32[]{:S(2)}) %collective-permute-start.4) | collective-permute-done | bytes 221216 | tf_op jit(solution)/shard_map/ppermute | solution.py:764
  23.2 0.6 %collective-permute-start.5 = (f32[144,384]{1,0:T(8,128)S(1)}, f32[144,384]{1,0:T(8,128)S(1)}, u32[]{:S(2)}, u32[]{:S(2)}) collective-permute-start(f32[144,384]{1,0:T(8,128)S(1)} %chip_merge.1.refs_3_.chip_ref), channel_id=1, source_target_pairs={{0,16},{8,24},{16,0},{24,8},{32,48},{40,56},{48,32},{56,40},{64,80... | collective-permute-start | bytes 663560 | tf_op jit(solution)/shard_map/ppermute | solution.py:766
  23.8 4.3 %local_filter.5._.z0_ref = f32[16,48,384]{2,1,0:T(8,128)S(1)} custom-call(f32[48,128]{1,0:T(8,128)S(1)} %get-tuple-element.21.refs_0_.table_ref, f32[48,512]{1,0:T(8,128)S(1)} %get-tuple-element.30.refs_1_, f32[48,48,384]{2,1,0:T(8,128)S(1)} %get-tuple-element.24.refs_1_.x_ref.refs_2_, f32[144,384]{1,0:T(8,128)S(1)} %chip_merge.1.refs_3_.chip_ref), custom_call_target="tpu_custom_call" | custom-call | flops 480000000 | bytes 2400000 | tf_op jit(solution)/shard_map/local_filter/pallas_call | solution.py:663
  28.1 2.1 %collective-permute-done.5.pair_ref = f32[144,384]{1,0:T(8,128)S(1)} collective-permute-done((f32[144,384]{1,0:T(8,128)S(1)}, f32[144,384]{1,0:T(8,128)S(1)}, u32[]{:S(2)}, u32[]{:S(2)}) %collective-permute-start.5) | collective-permute-done | bytes 221216 | tf_op jit(solution)/shard_map/ppermute | solution.py:766
  30.1 0.1 quad_merge.1
  30.2 3.7 %collective-permute-start.6 = (f32[72,384]{1,0:T(8,128)S(1)}, f32[72,384]{1,0:T(8,128)S(1)}, u32[]{:S(2)}, u32[]{:S(2)}) collective-permute-start(f32[72,384]{1,0:T(8,128)S(1)} %get-tuple-element.32), channel_id=1, source_target_pairs={{0,64},{8,72},{16,80},{24,88},{32,96},{40,104},{48,112},{56,120},{... | collective-permute-start | bytes 331784 | tf_op jit(solution)/shard_map/ppermute | solution.py:769
  33.9 0.7 %collective-permute-start.7 = (f32[72,384]{1,0:T(8,128)S(1)}, f32[72,384]{1,0:T(8,128)S(1)}, u32[]{:S(2)}, u32[]{:S(2)}) collective-permute-start(f32[72,384]{1,0:T(8,128)S(1)} %get-tuple-element.33), channel_id=1, source_target_pairs={{0,32},{8,40},{16,48},{24,56},{32,0},{40,8},{48,16},{56,24},{64,96... | collective-permute-start | bytes 331784 | tf_op jit(solution)/shard_map/ppermute | solution.py:769
  34.6 0.0 collective-permute-start.8
  34.6 2.8 %local_filter.6.refs_3_.z1_ref = f32[16,48,384]{2,1,0:T(8,128)S(1)} custom-call(f32[48,128]{1,0:T(8,128)S(1)} %get-tuple-element.21.refs_0_.table_ref, f32[48,512]{1,0:T(8,128)S(1)} %get-tuple-element.30.refs_1_, f32[48,48,384]{2,1,0:T(8,128)S(1)} %get-tuple-element.24.refs_1_.x_ref.refs_2_, f32[72,384]{1,0:T(8,128)S(1)} %get-tuple-element.31.refs_3_.left_ref), custom_call_target="tpu_custom_call" | custom-call | flops 480000000 | bytes 2400000 | tf_op jit(solution)/shard_map/local_filter/pallas_call | solution.py:663
  37.5 1.3 %local_filter.7._.z2_ref = f32[16,48,384]{2,1,0:T(8,128)S(1)} custom-call(f32[48,128]{1,0:T(8,128)S(1)} %get-tuple-element.21.refs_0_.table_ref, f32[48,512]{1,0:T(8,128)S(1)} %get-tuple-element.30.refs_1_, f32[16,48,384]{2,1,0:T(8,128)S(1)} %local_filter.4._.refs_2_, f32[16,48,384]{2,1,0:T(8,128)S(1)} %local_filter.6.refs_3_.z1_ref), custom_call_target="tpu_custom_call" | custom-call | flops 480000000 | bytes 2400000 | tf_op jit(solution)/shard_map/local_filter/pallas_call | solution.py:663
  38.8 0.0 collective-permute-done.6.g2_ref
  38.8 0.0 collective-permute-done.7.g1_ref
  38.8 0.7 %collective-permute-done.8.g3_ref = f32[72,384]{1,0:T(8,128)S(1)} collective-permute-done((f32[72,384]{1,0:T(8,128)S(1)}, f32[72,384]{1,0:T(8,128)S(1)}, u32[]{:S(2)}, u32[]{:S(2)}) %collective-permute-start.8) | collective-permute-done | bytes 110624 | tf_op jit(solution)/shard_map/ppermute | solution.py:769
  39.5 0.2 lat_carry.1
  39.7 2.9 %collective-permute-start.9 = (f32[144,384]{1,0:T(8,128)S(1)}, f32[144,384]{1,0:T(8,128)S(1)}, u32[]{:S(2)}, u32[]{:S(2)}) collective-permute-start(f32[144,384]{1,0:T(8,128)S(1)} %get-tuple-element.35), channel_id=1, source_target_pairs={{0,8},{8,0},{16,24},{24,16},{32,40},{40,32},{48,56},{56,48},{64,72... | collective-permute-start | bytes 663560 | tf_op jit(solution)/shard_map/ppermute | solution.py:773
  42.6 1.1 %finish_own.1.own_ref = f32[24,48,384]{2,1,0:T(8,128)S(1)} custom-call(f32[48,128]{1,0:T(8,128)S(1)} %get-tuple-element.21.refs_0_.table_ref, f32[2,3,3,8,384]{4,3,2,1,0:T(8,128)S(1)} %bitcast.6, f32[16,48,384]{2,1,0:T(8,128)S(1)} %local_filter.5._.z0_ref, f32[16,48,384]{2,1,0:T(8,128)S(1)} %local_filter.6.refs_3_.z1_ref, ...), custom_call_target="tpu_custom_call" | custom-call | flops 1000000000 | bytes 2000000 | tf_op jit(solution)/shard_map/finish_own/pallas_call | solution.py:710
  43.8 0.0 collective-permute-done.9
  43.8 2.4 %finish.1 = f32[48,48,384]{2,1,0:T(8,128)} custom-call(f32[48,128]{1,0:T(8,128)S(1)} %get-tuple-element.21.refs_0_.table_ref, f32[2,3,3,8,384]{4,3,2,1,0:T(8,128)S(1)} %bitcast.7, f32[16,48,384]{2,1,0:T(8,128)S(1)} %local_filter.5._.z0_ref, f32[16,48,384]{2,1,0:T(8,128)S(1)} %local_filter.6.refs_3_.z1_ref, f32[16,48,384]{2,1,0:T(8,128)S(1)} %local_filter.7._.z2_ref, ...), custom_call_target="tpu_custom_call" | custom-call | tf_op jit(solution)/shard_map/finish/pallas_call | solution.py:739
  (1 shorter events, 0.0 us)
Async XLA Ops:
  4.0 7.3 %collective-permute-start.2 = (f32[48,512]{1,0:T(8,128)S(1)}, f32[48,512]{1,0:T(8,128)S(1)}, u32[]{:S(2)}, u32[]{:S(2)}) collective-permute-start(f32[48,512]{1,0:T(8,128)S(1)} %get-tuple-element.23.refs_2_.own_ref), channel_id=1, source_target_pairs={{0,2},{1,3},{2,0},{3,1},{4,6},{5,7},{6,4},{7,5},{8,10},{9,11},{10,... | collective-permute-start | bytes 294920 | tf_op jit(solution)/shard_map/ppermute | solution.py:757
  7.9 4.7 %collective-permute-start.1 = (f32[48,512]{1,0:T(8,128)S(1)}, f32[48,512]{1,0:T(8,128)S(1)}, u32[]{:S(2)}, u32[]{:S(2)}) collective-permute-start(f32[48,512]{1,0:T(8,128)S(1)} %get-tuple-element.23.refs_2_.own_ref), channel_id=1, source_target_pairs={{0,3},{1,2},{2,1},{3,0},{4,7},{5,6},{6,5},{7,4},{8,11},{9,10},{10,... | collective-permute-start | bytes 294920 | tf_op jit(solution)/shard_map/ppermute | solution.py:757
  8.7 3.9 %collective-permute-start = (f32[48,512]{1,0:T(8,128)S(1)}, f32[48,512]{1,0:T(8,128)S(1)}, u32[]{:S(2)}, u32[]{:S(2)}) collective-permute-start(f32[48,512]{1,0:T(8,128)S(1)} %get-tuple-element.23.refs_2_.own_ref), channel_id=1, source_target_pairs={{0,1},{1,0},{2,3},{3,2},{4,5},{5,4},{6,7},{7,6},{8,9},{9,8},{10,11... | collective-permute-start | bytes 294920 | tf_op jit(solution)/shard_map/ppermute | solution.py:757
  12.6 6.5 %collective-permute-start.3 = (f32[48,256]{1,0:T(8,128)S(1)}, f32[48,256]{1,0:T(8,128)S(1)}, u32[]{:S(2)}, u32[]{:S(2)}) collective-permute-start(f32[48,256]{1,0:T(8,128)S(1)} %get-tuple-element.26), channel_id=1, source_target_pairs={{0,4},{1,5},{2,6},{3,7},{4,0},{5,1},{6,2},{7,3},{8,12},{9,13},{10,... | collective-permute-start | bytes 147464 | tf_op jit(solution)/shard_map/ppermute | solution.py:760
  19.6 3.6 %collective-permute-start.4 = (f32[144,384]{1,0:T(8,128)S(1)}, f32[144,384]{1,0:T(8,128)S(1)}, u32[]{:S(2)}, u32[]{:S(2)}) collective-permute-start(f32[144,384]{1,0:T(8,128)S(1)} %get-tuple-element.29), channel_id=1, source_target_pairs={{0,8},{8,0},{16,24},{24,16},{32,40},{40,32},{48,56},{56,48},{64,72... | collective-permute-start | bytes 663560 | tf_op jit(solution)/shard_map/ppermute | solution.py:764
  23.2 6.9 %collective-permute-start.5 = (f32[144,384]{1,0:T(8,128)S(1)}, f32[144,384]{1,0:T(8,128)S(1)}, u32[]{:S(2)}, u32[]{:S(2)}) collective-permute-start(f32[144,384]{1,0:T(8,128)S(1)} %chip_merge.1.refs_3_.chip_ref), channel_id=1, source_target_pairs={{0,16},{8,24},{16,0},{24,8},{32,48},{40,56},{48,32},{56,40},{64,80... | collective-permute-start | bytes 663560 | tf_op jit(solution)/shard_map/ppermute | solution.py:766
  30.2 8.6 %collective-permute-start.6 = (f32[72,384]{1,0:T(8,128)S(1)}, f32[72,384]{1,0:T(8,128)S(1)}, u32[]{:S(2)}, u32[]{:S(2)}) collective-permute-start(f32[72,384]{1,0:T(8,128)S(1)} %get-tuple-element.32), channel_id=1, source_target_pairs={{0,64},{8,72},{16,80},{24,88},{32,96},{40,104},{48,112},{56,120},{... | collective-permute-start | bytes 331784 | tf_op jit(solution)/shard_map/ppermute | solution.py:769
  33.9 4.9 %collective-permute-start.7 = (f32[72,384]{1,0:T(8,128)S(1)}, f32[72,384]{1,0:T(8,128)S(1)}, u32[]{:S(2)}, u32[]{:S(2)}) collective-permute-start(f32[72,384]{1,0:T(8,128)S(1)} %get-tuple-element.33), channel_id=1, source_target_pairs={{0,32},{8,40},{16,48},{24,56},{32,0},{40,8},{48,16},{56,24},{64,96... | collective-permute-start | bytes 331784 | tf_op jit(solution)/shard_map/ppermute | solution.py:769
  34.6 4.9 %collective-permute-start.8 = (f32[72,384]{1,0:T(8,128)S(1)}, f32[72,384]{1,0:T(8,128)S(1)}, u32[]{:S(2)}, u32[]{:S(2)}) collective-permute-start(f32[72,384]{1,0:T(8,128)S(1)} %get-tuple-element.34), channel_id=1, source_target_pairs={{0,96},{8,104},{16,112},{24,120},{32,64},{40,72},{48,80},{56,88},{... | collective-permute-start | bytes 331784 | tf_op jit(solution)/shard_map/ppermute | solution.py:769
  39.7 4.1 %collective-permute-start.9 = (f32[144,384]{1,0:T(8,128)S(1)}, f32[144,384]{1,0:T(8,128)S(1)}, u32[]{:S(2)}, u32[]{:S(2)}) collective-permute-start(f32[144,384]{1,0:T(8,128)S(1)} %get-tuple-element.35), channel_id=1, source_target_pairs={{0,8},{8,0},{16,24},{24,16},{32,40},{40,32},{48,56},{56,48},{64,72... | collective-permute-start | bytes 663560 | tf_op jit(solution)/shard_map/ppermute | solution.py:773

commit v8 on v7

--- a/solution.py
+++ b/solution.py
@@ -179,7 +179,7 @@
     return 0.5 * (ahead - behind)
 
 
-def local_sums_kernel(table_ref, x_ref, _, out_ref):
+def column_piece_sums(table_ref, x_ref, groups):
     top = lat_index() == 0
     count = 2 * SCALES * GROUP
     shape = (count, LANES)
@@ -217,9 +217,36 @@
                 acc += weighted(plain, x_ref[group * GROUP + i], i)
         return acc, row_rate
 
-    made = [group_sums(group, group < 2) for group in range(GROUPS)]
-    acc = jnp.concatenate([m[0] for m in made], axis=0)
-    factor = jnp.concatenate([jnp.broadcast_to(jnp.exp(-m[1]), (count, LANES)) for m in made], axis=0)
+    return [group_sums(group, group < 2) for group in groups]
+
+
+def wind_sums_kernel(table_ref, x_ref, _, out_ref):
+    made = column_piece_sums(table_ref, x_ref, (0, 1))
+    out_ref[...] = jnp.concatenate([m[0] for m in made], axis=0)
+
+
+def wind_sums(table, x, before):
+    return pl.pallas_call(
+        wind_sums_kernel,
+        in_specs=[VMEM, VMEM, ANY],
+        out_specs=VMEM,
+        out_shape=jax.ShapeDtypeStruct((4 * SCALES * GROUP, COLS), F32),
+        compiler_params=params(),
+        cost_estimate=pl.CostEstimate(flops=300_000_000, bytes_accessed=1_000_000, transcendentals=0),
+        name="wind_sums",
+    )(table, x, before)
+
+
+def local_sums_kernel(table_ref, x_ref, winds_ref, _, out_ref):
+    count = 2 * SCALES * GROUP
+    made = column_piece_sums(table_ref, x_ref, range(2, GROUPS))
+    acc = jnp.concatenate([winds_ref[...]] + [m[0] for m in made], axis=0)
+    factors = []
+    for group in range(GROUPS):
+        rate = table_ref[group * GROUP:(group + 1) * GROUP, :]
+        row_rate = jnp.concatenate([rate[:, s:s + 1] for _ in range(2) for s in range(SCALES)], axis=0)
+        factors.append(jnp.broadcast_to(jnp.exp(-row_rate), (count, LANES)))
+    factor = jnp.concatenate(factors, axis=0)
     factor = jnp.concatenate([factor] * PARTS, axis=1)
     column = iota(acc.shape, 1)
     forward, backward = acc, acc
@@ -237,16 +264,16 @@
                 out_ref[group // 3, side, s, group % 3] = acc[k:k + GROUP]
 
 
-def local_sums(table, x, before):
+def local_sums(table, x, winds, before):
     out = pl.pallas_call(
         local_sums_kernel,
-        in_specs=[VMEM, VMEM, ANY],
+        in_specs=[VMEM, VMEM, VMEM, ANY],
         out_specs=VMEM,
         out_shape=jax.ShapeDtypeStruct((2, 2, SCALES, 3, GROUP, COLS), F32),
         compiler_params=params(),
         cost_estimate=pl.CostEstimate(flops=600000000, bytes_accessed=4_000_000, transcendentals=0),
         name="local_sums",
-    )(table, x, before)
+    )(table, x, winds, before)
     return out.reshape(2, 2 * HALF_ROWS, COLS)
 
 
@@ -756,20 +783,21 @@
     sums, edge, table, lanes, held = row_sums(facts, x)
     got = [partner("lon", NLON, d)(sums) for d in (1, 2, 3)]
     early = local_filter(table, None, held, 32, 16, sums)
-    part, half = lon_merge(lanes, sums, got, early)
+    winds = wind_sums(table, held, early)
+    part, half = lon_merge(lanes, sums, got, winds)
     theirs = partner("lon", NLON, 4)(half)
-    local = local_sums(table, held, part)
+    local = local_sums(table, held, winds, part)
     steps = lat_steps(table, part)
     carry, keep, send = column_sums(table, lanes, part, theirs, edge, local)
     got_core = partner("lat", NLAT, 1)(send)
     chip = chip_merge(steps, keep, got_core)
     pair = partner("lat", NLAT, 2)(chip)
-    z0 = local_filter(table, carry, held, 0, 16, chip)
+    z2 = local_filter(table, carry, held, 32, 16, chip, early)
+    z0 = local_filter(table, carry, held, 0, 16, z2)
     left, *sends = quad_merge(steps, chip, pair, z0)
     gs = [partner("lat", NLAT, 4 * d)(t) for d, t in zip((1, 2, 3), sends)]
     z1 = local_filter(table, carry, held, 16, 16, left)
-    z2 = local_filter(table, carry, held, 32, 16, z1, early)
-    own, other = lat_carry(steps, keep, got_core, pair, left, gs, z2)
+    own, other = lat_carry(steps, keep, got_core, pair, left, gs, z1)
     got_carry = partner("lat", NLAT, 1)(other)
     done = finish_own(table, own, (z0, z1, z2))
     return finish(table, got_carry, (z0, z1, z2), done)

time: 46.4 us -> 45.4 us (0.978)
  waiting for transfers between devices: 4.87 us -> 2.89 us
  starting transfers between devices: 17.8 us -> 18.5 us
    ppermute x1, waiting for transfers between devices: 2.07 us -> 0.01 us  [shards(): pair = partner('lat', NLAT, 2)(chip)]
    ppermute x3, waiting for transfers between devices: 0.71 us -> 1.95 us  [shards(): gs = [partner('lat', NLAT, 4 * d)(t) for d, t in zip((1, 2, 3), sends)]]
    ppermute x3, waiting for transfers between devices: 1.17 us -> 0.01 us  [shards(): got = [partner('lon', NLON, d)(sums) for d in (1, 2, 3)]]
    ppermute x1, starting transfers between devices: 0.57 us -> 1.47 us  [shards(): pair = partner('lat', NLAT, 2)(chip)]
    pallas_call x1 -> x2, Pallas kernels: 3.67 us -> 3.71 us  [the longest x1 2.4 us: local_sums(): pl.pallas_call(local_sums_kernel, in_specs=[VMEM, VMEM, VMEM, ANY], out_s...]
  transfers between devices with their start and end apart: 10 -> 10, of which waited for: 4 -> 3; matrix products, arithmetic and copies ran while one was open for 0% -> 0% of each run, Pallas kernels for 35% -> 36%
where the time goes in v8:
time: 45.4 us; the launch traced here: 45.3 us
  Pallas kernels  22.8 us (50%)
  starting transfers between devices  18.5 us (41%)
  waiting for transfers between devices  2.89 us (6%)
  other arithmetic  0.71 us (2%)
    pallas_call x4, Pallas kernels, local_filter(): pl.pallas_call(body, in_specs=[specs.get(n, VMEM) for n in names], out_sp...  11.2 us
    ppermute x3, starting transfers between devices, shards(): got = [partner('lon', NLON, d)(sums) for d in (1, 2, 3)]  4.6 us
    ppermute x3, starting transfers between devices, shards(): gs = [partner('lat', NLAT, 4 * d)(t) for d, t in zip((1, 2, 3), sends)]  4.41 us
    pallas_call x1, Pallas kernels, row_sums(): pl.pallas_call(row_sums_kernel, in_specs=[VMEM, HBM], out_specs=[VMEM] *...  3.4 us
    ppermute x1, starting transfers between devices, shards(): theirs = partner('lon', NLON, 4)(half)  2.83 us
    ppermute x1, starting transfers between devices, shards(): got_carry = partner('lat', NLAT, 1)(other)  2.82 us
    ppermute x1, starting transfers between devices, shards(): got_core = partner('lat', NLAT, 1)(send)  2.41 us
    pallas_call x1, Pallas kernels, local_sums(): pl.pallas_call(local_sums_kernel, in_specs=[VMEM, VMEM, VMEM, ANY], out_s...  2.4 us
  transfers between devices with their start and end apart: 10, of which 3 were waited for; matrix products, arithmetic and copies ran while one was open for 0% of the time, Pallas kernels for 36%

profile of v8, /device:TPU:1, one launch (start us, length us, event | category | flops | bytes accessed | tf_op | source)
XLA Modules:
  0.0 45.3 jit_solution(15413518682419751161)
XLA Ops:
  0.0 0.7 %pad_maximum_fusion.len_ref = f32[6,48]{1,0:T(8,128)S(1)} fusion(f32[3,48]{1,0:T(4,128)} %bitcast.8, f32[3,48]{1,0:T(4,128)} %bitcast.9), kind=kLoop, calls=%fused_computation | loop fusion | flops 288 | bytes 2304 | tf_op jit(solution)/shard_map/concatenate | solution.py:782
  0.7 3.4 %row_sums.1 = (f32[48,512]{1,0:T(8,128)S(1)}, f32[48,256]{1,0:T(8,128)S(1)}, f32[48,128]{1,0:T(8,128)S(1)}, f32[8,128]{1,0:T(8,128)S(1)}, f32[48,48,384]{2,1,0:T(8,128)S(1)}) custom-call(f32[6,48]{1,0:T(8,128)S(1)} %pad_maximum_fusion.len_ref, f32[48,48,384]{2,1,0:T(8,128)} %x_ref.1), custom_call_target="tpu_custom_call" | custom-call | tf_op jit(solution)/shard_map/row_sums/pallas_call | solution.py:160
  4.1 3.8 %collective-permute-start.2 = (f32[48,512]{1,0:T(8,128)S(1)}, f32[48,512]{1,0:T(8,128)S(1)}, u32[]{:S(2)}, u32[]{:S(2)}) collective-permute-start(f32[48,512]{1,0:T(8,128)S(1)} %get-tuple-element.23.refs_2_.own_ref), channel_id=1, source_target_pairs={{0,2},{1,3},{2,0},{3,1},{4,6},{5,7},{6,4},{7,5},{8,10},{9,11},{10,... | collective-permute-start | bytes 294920 | tf_op jit(solution)/shard_map/ppermute | solution.py:784
  7.9 0.8 %collective-permute-start.1 = (f32[48,512]{1,0:T(8,128)S(1)}, f32[48,512]{1,0:T(8,128)S(1)}, u32[]{:S(2)}, u32[]{:S(2)}) collective-permute-start(f32[48,512]{1,0:T(8,128)S(1)} %get-tuple-element.23.refs_2_.own_ref), channel_id=1, source_target_pairs={{0,3},{1,2},{2,1},{3,0},{4,7},{5,6},{6,5},{7,4},{8,11},{9,10},{10,... | collective-permute-start | bytes 294920 | tf_op jit(solution)/shard_map/ppermute | solution.py:784
  8.7 0.0 collective-permute-start
  8.7 2.7 %local_filter.4._.refs_2_ = f32[16,48,384]{2,1,0:T(8,128)S(1)} custom-call(f32[48,128]{1,0:T(8,128)S(1)} %get-tuple-element.21.refs_0_.table_ref, f32[48,48,384]{2,1,0:T(8,128)S(1)} %get-tuple-element.24.refs_1_.x_ref.refs_2_, f32[48,512]{1,0:T(8,128)S(1)} %get-tuple-element.23.refs_2_.own_ref), custom_call_target="tpu_custom_call" | custom-call | flops 480000000 | bytes 2400000 | tf_op jit(solution)/shard_map/local_filter/pallas_call | solution.py:690
  11.5 1.3 %wind_sums.1._.winds_ref = f32[96,384]{1,0:T(8,128)S(1)} custom-call(f32[48,128]{1,0:T(8,128)S(1)} %get-tuple-element.21.refs_0_.table_ref, f32[48,48,384]{2,1,0:T(8,128)S(1)} %get-tuple-element.24.refs_1_.x_ref.refs_2_, f32[16,48,384]{2,1,0:T(8,128)S(1)} %local_filter.4._.refs_2_), custom_call_target="tpu_custom_call" | custom-call | flops 300000000 | bytes 1000000 | tf_op jit(solution)/shard_map/wind_sums/pallas_call | solution.py:229
  12.8 0.0 collective-permute-done.2.g2_ref
  12.8 0.0 collective-permute-done.1.g3_ref
  12.8 0.0 collective-permute-done.g1_ref
  12.8 0.1 lon_merge.1
  12.9 2.8 %collective-permute-start.3 = (f32[48,256]{1,0:T(8,128)S(1)}, f32[48,256]{1,0:T(8,128)S(1)}, u32[]{:S(2)}, u32[]{:S(2)}) collective-permute-start(f32[48,256]{1,0:T(8,128)S(1)} %get-tuple-element.26), channel_id=1, source_target_pairs={{0,4},{1,5},{2,6},{3,7},{4,0},{5,1},{6,2},{7,3},{8,12},{9,13},{10,... | collective-permute-start | bytes 147464 | tf_op jit(solution)/shard_map/ppermute | solution.py:788
  15.7 2.4 %local_sums.1 = f32[2,2,3,3,8,384]{5,4,3,2,1,0:T(8,128)S(1)} custom-call(f32[48,128]{1,0:T(8,128)S(1)} %get-tuple-element.21.refs_0_.table_ref, f32[48,48,384]{2,1,0:T(8,128)S(1)} %get-tuple-element.24.refs_1_.x_ref.refs_2_, f32[96,384]{1,0:T(8,128)S(1)} %wind_sums.1._.winds_ref, f32[48,768]{1,0:T(8,128)S(1)} %get-tuple-element.25._.part_ref), custom_call_target="tpu_custom_call" | custom-call | flops 600000000 | bytes 4000000 | tf_op jit(solution)/shard_map/local_sums/pallas_call | solution.py:268
  18.1 0.0 collective-permute-done.3.theirs_ref
  18.1 0.5 %column_sums.1 = (f32[48,512]{1,0:T(8,128)S(1)}, f32[144,384]{1,0:T(8,128)S(1)}, f32[144,384]{1,0:T(8,128)S(1)}) custom-call(f32[48,128]{1,0:T(8,128)S(1)} %get-tuple-element.21.refs_0_.table_ref, f32[8,128]{1,0:T(8,128)S(1)} %get-tuple-element.22.lanes_ref, f32[48,768]{1,0:T(8,128)S(1)} %get-tuple-element.25._.part_ref, ...), custom_call_target="tpu_custom_call" | custom-call | tf_op jit(solution)/shard_map/column_sums/pallas_call | solution.py:407
  18.6 2.4 %collective-permute-start.4 = (f32[144,384]{1,0:T(8,128)S(1)}, f32[144,384]{1,0:T(8,128)S(1)}, u32[]{:S(2)}, u32[]{:S(2)}) collective-permute-start(f32[144,384]{1,0:T(8,128)S(1)} %get-tuple-element.29), channel_id=1, source_target_pairs={{0,8},{8,0},{16,24},{24,16},{32,40},{40,32},{48,56},{56,48},{64,72... | collective-permute-start | bytes 663560 | tf_op jit(solution)/shard_map/ppermute | solution.py:792
  21.1 0.2 lat_steps.1.steps_ref
  21.2 0.9 %collective-permute-done.4.got_ref = f32[144,384]{1,0:T(8,128)S(1)} collective-permute-done((f32[144,384]{1,0:T(8,128)S(1)}, f32[144,384]{1,0:T(8,128)S(1)}, u32[]{:S(2)}, u32[]{:S(2)}) %collective-permute-start.4) | collective-permute-done | bytes 221216 | tf_op jit(solution)/shard_map/ppermute | solution.py:792
  22.2 1.5 %collective-permute-start.5 = (f32[144,384]{1,0:T(8,128)S(1)}, f32[144,384]{1,0:T(8,128)S(1)}, u32[]{:S(2)}, u32[]{:S(2)}) collective-permute-start(f32[144,384]{1,0:T(8,128)S(1)} %chip_merge.1.refs_3_.chip_ref), channel_id=1, source_target_pairs={{0,16},{8,24},{16,0},{24,8},{32,48},{40,56},{48,32},{56,40},{64,80... | collective-permute-start | bytes 663560 | tf_op jit(solution)/shard_map/ppermute | solution.py:794
  23.7 1.3 %local_filter.5.refs_3_.z2_ref = f32[16,48,384]{2,1,0:T(8,128)S(1)} custom-call(f32[48,128]{1,0:T(8,128)S(1)} %get-tuple-element.21.refs_0_.table_ref, f32[48,512]{1,0:T(8,128)S(1)} %get-tuple-element.30.refs_1_, f32[16,48,384]{2,1,0:T(8,128)S(1)} %local_filter.4._.refs_2_, f32[144,384]{1,0:T(8,128)S(1)} %chip_merge.1.refs_3_.chip_ref), custom_call_target="tpu_custom_call" | custom-call | flops 480000000 | bytes 2400000 | tf_op jit(solution)/shard_map/local_filter/pallas_call | solution.py:690
  24.9 4.3 %local_filter.6._.z0_ref = f32[16,48,384]{2,1,0:T(8,128)S(1)} custom-call(f32[48,128]{1,0:T(8,128)S(1)} %get-tuple-element.21.refs_0_.table_ref, f32[48,512]{1,0:T(8,128)S(1)} %get-tuple-element.30.refs_1_, f32[48,48,384]{2,1,0:T(8,128)S(1)} %get-tuple-element.24.refs_1_.x_ref.refs_2_, f32[16,48,384]{2,1,0:T(8,128)S(1)} %local_filter.5.refs_3_.z2_ref), custom_call_target="tpu_custom_call" | custom-call | flops 480000000 | bytes 2400000 | tf_op jit(solution)/shard_map/local_filter/pallas_call | solution.py:690
  29.3 0.0 collective-permute-done.5.pair_ref
  29.3 0.1 quad_merge.1
  29.3 3.7 %collective-permute-start.6 = (f32[72,384]{1,0:T(8,128)S(1)}, f32[72,384]{1,0:T(8,128)S(1)}, u32[]{:S(2)}, u32[]{:S(2)}) collective-permute-start(f32[72,384]{1,0:T(8,128)S(1)} %get-tuple-element.32), channel_id=1, source_target_pairs={{0,64},{8,72},{16,80},{24,88},{32,96},{40,104},{48,112},{56,120},{... | collective-permute-start | bytes 331784 | tf_op jit(solution)/shard_map/ppermute | solution.py:798
  33.0 0.7 %collective-permute-start.7 = (f32[72,384]{1,0:T(8,128)S(1)}, f32[72,384]{1,0:T(8,128)S(1)}, u32[]{:S(2)}, u32[]{:S(2)}) collective-permute-start(f32[72,384]{1,0:T(8,128)S(1)} %get-tuple-element.33), channel_id=1, source_target_pairs={{0,32},{8,40},{16,48},{24,56},{32,0},{40,8},{48,16},{56,24},{64,96... | collective-permute-start | bytes 331784 | tf_op jit(solution)/shard_map/ppermute | solution.py:798
  33.7 0.0 collective-permute-start.8
  33.7 2.8 %local_filter.7._.z1_ref = f32[16,48,384]{2,1,0:T(8,128)S(1)} custom-call(f32[48,128]{1,0:T(8,128)S(1)} %get-tuple-element.21.refs_0_.table_ref, f32[48,512]{1,0:T(8,128)S(1)} %get-tuple-element.30.refs_1_, f32[48,48,384]{2,1,0:T(8,128)S(1)} %get-tuple-element.24.refs_1_.x_ref.refs_2_, f32[72,384]{1,0:T(8,128)S(1)} %get-tuple-element.31.refs_3_.left_ref), custom_call_target="tpu_custom_call" | custom-call | flops 480000000 | bytes 2400000 | tf_op jit(solution)/shard_map/local_filter/pallas_call | solution.py:690
  36.6 0.0 collective-permute-done.6.g2_ref
  36.6 1.3 %collective-permute-done.7.g1_ref = f32[72,384]{1,0:T(8,128)S(1)} collective-permute-done((f32[72,384]{1,0:T(8,128)S(1)}, f32[72,384]{1,0:T(8,128)S(1)}, u32[]{:S(2)}, u32[]{:S(2)}) %collective-permute-start.7) | collective-permute-done | bytes 110624 | tf_op jit(solution)/shard_map/ppermute | solution.py:798
  37.9 0.7 %collective-permute-done.8.g3_ref = f32[72,384]{1,0:T(8,128)S(1)} collective-permute-done((f32[72,384]{1,0:T(8,128)S(1)}, f32[72,384]{1,0:T(8,128)S(1)}, u32[]{:S(2)}, u32[]{:S(2)}) %collective-permute-start.8) | collective-permute-done | bytes 110624 | tf_op jit(solution)/shard_map/ppermute | solution.py:798
  38.6 0.2 lat_carry.1
  38.8 2.8 %collective-permute-start.9 = (f32[144,384]{1,0:T(8,128)S(1)}, f32[144,384]{1,0:T(8,128)S(1)}, u32[]{:S(2)}, u32[]{:S(2)}) collective-permute-start(f32[144,384]{1,0:T(8,128)S(1)} %get-tuple-element.35), channel_id=1, source_target_pairs={{0,8},{8,0},{16,24},{24,16},{32,40},{40,32},{48,56},{56,48},{64,72... | collective-permute-start | bytes 663560 | tf_op jit(solution)/shard_map/ppermute | solution.py:801
  41.6 1.1 %finish_own.1.own_ref = f32[24,48,384]{2,1,0:T(8,128)S(1)} custom-call(f32[48,128]{1,0:T(8,128)S(1)} %get-tuple-element.21.refs_0_.table_ref, f32[2,3,3,8,384]{4,3,2,1,0:T(8,128)S(1)} %bitcast.6, f32[16,48,384]{2,1,0:T(8,128)S(1)} %local_filter.6._.z0_ref, f32[16,48,384]{2,1,0:T(8,128)S(1)} %local_filter.7._.z1_ref, ...), custom_call_target="tpu_custom_call" | custom-call | flops 1000000000 | bytes 2000000 | tf_op jit(solution)/shard_map/finish_own/pallas_call | solution.py:737
  42.7 0.0 collective-permute-done.9
  42.7 2.4 %finish.1 = f32[48,48,384]{2,1,0:T(8,128)} custom-call(f32[48,128]{1,0:T(8,128)S(1)} %get-tuple-element.21.refs_0_.table_ref, f32[2,3,3,8,384]{4,3,2,1,0:T(8,128)S(1)} %bitcast.7, f32[16,48,384]{2,1,0:T(8,128)S(1)} %local_filter.6._.z0_ref, f32[16,48,384]{2,1,0:T(8,128)S(1)} %local_filter.7._.z1_ref, f32[16,48,384]{2,1,0:T(8,128)S(1)} %local_filter.5.refs_3_.z2_ref, ...), custom_call_target="tpu_custom_call" | custom-call | tf_op jit(solution)/shard_map/finish/pallas_call | solution.py:766
  (1 shorter events, 0.0 us)
Async XLA Ops:
  4.1 8.7 %collective-permute-start.2 = (f32[48,512]{1,0:T(8,128)S(1)}, f32[48,512]{1,0:T(8,128)S(1)}, u32[]{:S(2)}, u32[]{:S(2)}) collective-permute-start(f32[48,512]{1,0:T(8,128)S(1)} %get-tuple-element.23.refs_2_.own_ref), channel_id=1, source_target_pairs={{0,2},{1,3},{2,0},{3,1},{4,6},{5,7},{6,4},{7,5},{8,10},{9,11},{10,... | collective-permute-start | bytes 294920 | tf_op jit(solution)/shard_map/ppermute | solution.py:784
  7.9 4.8 %collective-permute-start.1 = (f32[48,512]{1,0:T(8,128)S(1)}, f32[48,512]{1,0:T(8,128)S(1)}, u32[]{:S(2)}, u32[]{:S(2)}) collective-permute-start(f32[48,512]{1,0:T(8,128)S(1)} %get-tuple-element.23.refs_2_.own_ref), channel_id=1, source_target_pairs={{0,3},{1,2},{2,1},{3,0},{4,7},{5,6},{6,5},{7,4},{8,11},{9,10},{10,... | collective-permute-start | bytes 294920 | tf_op jit(solution)/shard_map/ppermute | solution.py:784
  8.7 4.1 %collective-permute-start = (f32[48,512]{1,0:T(8,128)S(1)}, f32[48,512]{1,0:T(8,128)S(1)}, u32[]{:S(2)}, u32[]{:S(2)}) collective-permute-start(f32[48,512]{1,0:T(8,128)S(1)} %get-tuple-element.23.refs_2_.own_ref), channel_id=1, source_target_pairs={{0,1},{1,0},{2,3},{3,2},{4,5},{5,4},{6,7},{7,6},{8,9},{9,8},{10,11... | collective-permute-start | bytes 294920 | tf_op jit(solution)/shard_map/ppermute | solution.py:784
  12.9 5.2 %collective-permute-start.3 = (f32[48,256]{1,0:T(8,128)S(1)}, f32[48,256]{1,0:T(8,128)S(1)}, u32[]{:S(2)}, u32[]{:S(2)}) collective-permute-start(f32[48,256]{1,0:T(8,128)S(1)} %get-tuple-element.26), channel_id=1, source_target_pairs={{0,4},{1,5},{2,6},{3,7},{4,0},{5,1},{6,2},{7,3},{8,12},{9,13},{10,... | collective-permute-start | bytes 147464 | tf_op jit(solution)/shard_map/ppermute | solution.py:788
  18.6 3.5 %collective-permute-start.4 = (f32[144,384]{1,0:T(8,128)S(1)}, f32[144,384]{1,0:T(8,128)S(1)}, u32[]{:S(2)}, u32[]{:S(2)}) collective-permute-start(f32[144,384]{1,0:T(8,128)S(1)} %get-tuple-element.29), channel_id=1, source_target_pairs={{0,8},{8,0},{16,24},{24,16},{32,40},{40,32},{48,56},{56,48},{64,72... | collective-permute-start | bytes 663560 | tf_op jit(solution)/shard_map/ppermute | solution.py:792
  22.2 7.1 %collective-permute-start.5 = (f32[144,384]{1,0:T(8,128)S(1)}, f32[144,384]{1,0:T(8,128)S(1)}, u32[]{:S(2)}, u32[]{:S(2)}) collective-permute-start(f32[144,384]{1,0:T(8,128)S(1)} %chip_merge.1.refs_3_.chip_ref), channel_id=1, source_target_pairs={{0,16},{8,24},{16,0},{24,8},{32,48},{40,56},{48,32},{56,40},{64,80... | collective-permute-start | bytes 663560 | tf_op jit(solution)/shard_map/ppermute | solution.py:794
  29.3 7.3 %collective-permute-start.6 = (f32[72,384]{1,0:T(8,128)S(1)}, f32[72,384]{1,0:T(8,128)S(1)}, u32[]{:S(2)}, u32[]{:S(2)}) collective-permute-start(f32[72,384]{1,0:T(8,128)S(1)} %get-tuple-element.32), channel_id=1, source_target_pairs={{0,64},{8,72},{16,80},{24,88},{32,96},{40,104},{48,112},{56,120},{... | collective-permute-start | bytes 331784 | tf_op jit(solution)/shard_map/ppermute | solution.py:798
  33.0 4.9 %collective-permute-start.7 = (f32[72,384]{1,0:T(8,128)S(1)}, f32[72,384]{1,0:T(8,128)S(1)}, u32[]{:S(2)}, u32[]{:S(2)}) collective-permute-start(f32[72,384]{1,0:T(8,128)S(1)} %get-tuple-element.33), channel_id=1, source_target_pairs={{0,32},{8,40},{16,48},{24,56},{32,0},{40,8},{48,16},{56,24},{64,96... | collective-permute-start | bytes 331784 | tf_op jit(solution)/shard_map/ppermute | solution.py:798
  33.7 4.8 %collective-permute-start.8 = (f32[72,384]{1,0:T(8,128)S(1)}, f32[72,384]{1,0:T(8,128)S(1)}, u32[]{:S(2)}, u32[]{:S(2)}) collective-permute-start(f32[72,384]{1,0:T(8,128)S(1)} %get-tuple-element.34), channel_id=1, source_target_pairs={{0,96},{8,104},{16,112},{24,120},{32,64},{40,72},{48,80},{56,88},{... | collective-permute-start | bytes 331784 | tf_op jit(solution)/shard_map/ppermute | solution.py:798
  38.8 4.0 %collective-permute-start.9 = (f32[144,384]{1,0:T(8,128)S(1)}, f32[144,384]{1,0:T(8,128)S(1)}, u32[]{:S(2)}, u32[]{:S(2)}) collective-permute-start(f32[144,384]{1,0:T(8,128)S(1)} %get-tuple-element.35), channel_id=1, source_target_pairs={{0,8},{8,0},{16,24},{24,16},{32,40},{40,32},{48,56},{56,48},{64,72... | collective-permute-start | bytes 663560 | tf_op jit(solution)/shard_map/ppermute | solution.py:801

commit v9 on v8

--- a/solution.py
+++ b/solution.py
@@ -725,29 +725,41 @@
             store(i, lanes, total)
 
 
-def finish_own_kernel(table_ref, carry_ref, z0_ref, z1_ref, z2_ref, out_ref):
-    for part in range(3):
+def finish_own_kernel(table_ref, carry_ref, z0_ref, z1_ref, z2_ref, out_ref, own_ref, buf_ref, sem):
+    half = lat_index() & 1
+    z_refs = (z0_ref, z1_ref, z2_ref)
+
+    def store_first(i, lanes, value):
+        buf_ref[i, :, lanes] = value
+
+    add_carries(half, table_ref, carry_ref, z_refs, 0, store_first)
+    copy = pltpu.make_async_copy(buf_ref, out_ref.at[pl.ds(half * HALF, GROUP)], sem)
+    copy.start()
+    for part in (1, 2):
         def store(i, lanes, value):
-            out_ref[part * GROUP + i, :, lanes] = value
-
-        add_carries(lat_index() & 1, table_ref, carry_ref, (z0_ref, z1_ref, z2_ref), part, store)
+            own_ref[(part - 1) * GROUP + i, :, lanes] = value
+
+        add_carries(half, table_ref, carry_ref, z_refs, part, store)
+    copy.wait()
 
 
 def finish_own(table, carry, parts):
     return pl.pallas_call(
         finish_own_kernel,
         in_specs=[VMEM] * 5,
-        out_specs=VMEM,
-        out_shape=jax.ShapeDtypeStruct((HALF, ROWS, COLS), F32),
+        out_specs=[HBM, VMEM],
+        out_shape=[jax.ShapeDtypeStruct((FIELDS, ROWS, COLS), F32), jax.ShapeDtypeStruct((2 * GROUP, ROWS, COLS), F32)],
+        scratch_shapes=[pltpu.VMEM((GROUP, ROWS, COLS), F32), pltpu.SemaphoreType.DMA],
         compiler_params=params(),
         cost_estimate=pl.CostEstimate(flops=1_000_000_000, bytes_accessed=2_000_000, transcendentals=0),
         name="finish_own",
     )(table, carry.reshape(2, SCALES, 3, GROUP, COLS), *parts)
 
 
-def finish_kernel(table_ref, carry_ref, z0_ref, z1_ref, z2_ref, own_ref, out_ref, buf_ref, sem):
+def finish_kernel(table_ref, carry_ref, z0_ref, z1_ref, z2_ref, own_ref, _, out_ref, buf_ref, sem):
     half = 1 - (lat_index() & 1)
-    ready = pltpu.make_async_copy(own_ref, out_ref.at[pl.ds((1 - half) * HALF, HALF)], sem.at[3])
+    mine = (1 - half) * HALF + GROUP
+    ready = pltpu.make_async_copy(own_ref, out_ref.at[pl.ds(mine, 2 * GROUP)], sem.at[3])
     ready.start()
     copies = [ready]
     for part in range(3):
@@ -762,16 +774,17 @@
         copy.wait()
 
 
-def finish(table, carry, parts, own):
+def finish(table, carry, parts, own, out):
     return pl.pallas_call(
         finish_kernel,
-        in_specs=[VMEM] * 6,
+        in_specs=[VMEM] * 6 + [HBM],
         out_specs=HBM,
         out_shape=jax.ShapeDtypeStruct((FIELDS, ROWS, COLS), F32),
         scratch_shapes=[pltpu.VMEM((3, GROUP, ROWS, COLS), F32), pltpu.SemaphoreType.DMA((4,))],
+        input_output_aliases={6: 0},
         compiler_params=params(),
         name="finish",
-    )(table, carry.reshape(2, SCALES, 3, GROUP, COLS), *parts, own)
+    )(table, carry.reshape(2, SCALES, 3, GROUP, COLS), *parts, own, out)
 
 
 def partner(axis, count, bit):
@@ -799,8 +812,8 @@
     z1 = local_filter(table, carry, held, 16, 16, left)
     own, other = lat_carry(steps, keep, got_core, pair, left, gs, z1)
     got_carry = partner("lat", NLAT, 1)(other)
-    done = finish_own(table, own, (z0, z1, z2))
-    return finish(table, got_carry, (z0, z1, z2), done)
+    out, done = finish_own(table, own, (z0, z1, z2))
+    return finish(table, got_carry, (z0, z1, z2), done, out)
 
 
 def solution(mesh):

time: 45.4 us -> 45.8 us (level)
  transfers between devices with their start and end apart: 10 -> 10, of which waited for: 3 -> 3; matrix products, arithmetic and copies ran while one was open for 0% -> 0% of each run, Pallas kernels for 36% -> 37%
where the time goes in v9:
time: 45.8 us; the launch traced here: 45.7 us
  Pallas kernels  23.2 us (51%)
  starting transfers between devices  18.5 us (40%)
  waiting for transfers between devices  2.89 us (6%)
  other arithmetic  0.71 us (2%)
    pallas_call x4, Pallas kernels, local_filter(): pl.pallas_call(body, in_specs=[specs.get(n, VMEM) for n in names], out_sp...  11.2 us
    ppermute x3, starting transfers between devices, shards(): got = [partner('lon', NLON, d)(sums) for d in (1, 2, 3)]  4.6 us
    ppermute x3, starting transfers between devices, shards(): gs = [partner('lat', NLAT, 4 * d)(t) for d, t in zip((1, 2, 3), sends)]  4.41 us
    pallas_call x1, Pallas kernels, row_sums(): pl.pallas_call(row_sums_kernel, in_specs=[VMEM, HBM], out_specs=[VMEM] *...  3.4 us
    ppermute x1, starting transfers between devices, shards(): theirs = partner('lon', NLON, 4)(half)  2.83 us
    ppermute x1, starting transfers between devices, shards(): got_carry = partner('lat', NLAT, 1)(other)  2.82 us
    ppermute x1, starting transfers between devices, shards(): got_core = partner('lat', NLAT, 1)(send)  2.41 us
    pallas_call x1, Pallas kernels, local_sums(): pl.pallas_call(local_sums_kernel, in_specs=[VMEM, VMEM, VMEM, ANY], out_s...  2.4 us
  transfers between devices with their start and end apart: 10, of which 3 were waited for; matrix products, arithmetic and copies ran while one was open for 0% of the time, Pallas kernels for 37%

profile of v9, /device:TPU:1, one launch (start us, length us, event | category | flops | bytes accessed | tf_op | source)
XLA Modules:
  0.0 45.7 jit_solution(4601677946585037537)
XLA Ops:
  0.0 0.7 %pad_maximum_fusion.len_ref = f32[6,48]{1,0:T(8,128)S(1)} fusion(f32[3,48]{1,0:T(4,128)} %bitcast.8, f32[3,48]{1,0:T(4,128)} %bitcast.9), kind=kLoop, calls=%fused_computation | loop fusion | flops 288 | bytes 2304 | tf_op jit(solution)/shard_map/concatenate | solution.py:795
  0.7 3.4 %row_sums.1 = (f32[48,512]{1,0:T(8,128)S(1)}, f32[48,256]{1,0:T(8,128)S(1)}, f32[48,128]{1,0:T(8,128)S(1)}, f32[8,128]{1,0:T(8,128)S(1)}, f32[48,48,384]{2,1,0:T(8,128)S(1)}) custom-call(f32[6,48]{1,0:T(8,128)S(1)} %pad_maximum_fusion.len_ref, f32[48,48,384]{2,1,0:T(8,128)} %x_ref.1), custom_call_target="tpu_custom_call" | custom-call | tf_op jit(solution)/shard_map/row_sums/pallas_call | solution.py:160
  4.1 3.8 %collective-permute-start.2 = (f32[48,512]{1,0:T(8,128)S(1)}, f32[48,512]{1,0:T(8,128)S(1)}, u32[]{:S(2)}, u32[]{:S(2)}) collective-permute-start(f32[48,512]{1,0:T(8,128)S(1)} %get-tuple-element.25.refs_2_.own_ref), channel_id=1, source_target_pairs={{0,2},{1,3},{2,0},{3,1},{4,6},{5,7},{6,4},{7,5},{8,10},{9,11},{10,... | collective-permute-start | bytes 294920 | tf_op jit(solution)/shard_map/ppermute | solution.py:797
  7.9 0.8 %collective-permute-start.1 = (f32[48,512]{1,0:T(8,128)S(1)}, f32[48,512]{1,0:T(8,128)S(1)}, u32[]{:S(2)}, u32[]{:S(2)}) collective-permute-start(f32[48,512]{1,0:T(8,128)S(1)} %get-tuple-element.25.refs_2_.own_ref), channel_id=1, source_target_pairs={{0,3},{1,2},{2,1},{3,0},{4,7},{5,6},{6,5},{7,4},{8,11},{9,10},{10,... | collective-permute-start | bytes 294920 | tf_op jit(solution)/shard_map/ppermute | solution.py:797
  8.7 0.0 collective-permute-start
  8.7 2.7 %local_filter.4._.refs_2_ = f32[16,48,384]{2,1,0:T(8,128)S(1)} custom-call(f32[48,128]{1,0:T(8,128)S(1)} %get-tuple-element.23.refs_0_.table_ref, f32[48,48,384]{2,1,0:T(8,128)S(1)} %get-tuple-element.26.refs_1_.x_ref.refs_2_, f32[48,512]{1,0:T(8,128)S(1)} %get-tuple-element.25.refs_2_.own_ref), custom_call_target="tpu_custom_call" | custom-call | flops 480000000 | bytes 2400000 | tf_op jit(solution)/shard_map/local_filter/pallas_call | solution.py:690
  11.5 1.3 %wind_sums.1._.winds_ref = f32[96,384]{1,0:T(8,128)S(1)} custom-call(f32[48,128]{1,0:T(8,128)S(1)} %get-tuple-element.23.refs_0_.table_ref, f32[48,48,384]{2,1,0:T(8,128)S(1)} %get-tuple-element.26.refs_1_.x_ref.refs_2_, f32[16,48,384]{2,1,0:T(8,128)S(1)} %local_filter.4._.refs_2_), custom_call_target="tpu_custom_call" | custom-call | flops 300000000 | bytes 1000000 | tf_op jit(solution)/shard_map/wind_sums/pallas_call | solution.py:229
  12.8 0.0 collective-permute-done.2.g2_ref
  12.8 0.0 collective-permute-done.1.g3_ref
  12.8 0.0 collective-permute-done.g1_ref
  12.8 0.1 lon_merge.1
  12.9 2.8 %collective-permute-start.3 = (f32[48,256]{1,0:T(8,128)S(1)}, f32[48,256]{1,0:T(8,128)S(1)}, u32[]{:S(2)}, u32[]{:S(2)}) collective-permute-start(f32[48,256]{1,0:T(8,128)S(1)} %get-tuple-element.28), channel_id=1, source_target_pairs={{0,4},{1,5},{2,6},{3,7},{4,0},{5,1},{6,2},{7,3},{8,12},{9,13},{10,... | collective-permute-start | bytes 147464 | tf_op jit(solution)/shard_map/ppermute | solution.py:801
  15.7 2.4 %local_sums.1 = f32[2,2,3,3,8,384]{5,4,3,2,1,0:T(8,128)S(1)} custom-call(f32[48,128]{1,0:T(8,128)S(1)} %get-tuple-element.23.refs_0_.table_ref, f32[48,48,384]{2,1,0:T(8,128)S(1)} %get-tuple-element.26.refs_1_.x_ref.refs_2_, f32[96,384]{1,0:T(8,128)S(1)} %wind_sums.1._.winds_ref, f32[48,768]{1,0:T(8,128)S(1)} %get-tuple-element.27._.part_ref), custom_call_target="tpu_custom_call" | custom-call | flops 600000000 | bytes 4000000 | tf_op jit(solution)/shard_map/local_sums/pallas_call | solution.py:268
  18.1 0.0 collective-permute-done.3.theirs_ref
  18.1 0.5 %column_sums.1 = (f32[48,512]{1,0:T(8,128)S(1)}, f32[144,384]{1,0:T(8,128)S(1)}, f32[144,384]{1,0:T(8,128)S(1)}) custom-call(f32[48,128]{1,0:T(8,128)S(1)} %get-tuple-element.23.refs_0_.table_ref, f32[8,128]{1,0:T(8,128)S(1)} %get-tuple-element.24.lanes_ref, f32[48,768]{1,0:T(8,128)S(1)} %get-tuple-element.27._.part_ref, ...), custom_call_target="tpu_custom_call" | custom-call | tf_op jit(solution)/shard_map/column_sums/pallas_call | solution.py:407
  18.6 2.4 %collective-permute-start.4 = (f32[144,384]{1,0:T(8,128)S(1)}, f32[144,384]{1,0:T(8,128)S(1)}, u32[]{:S(2)}, u32[]{:S(2)}) collective-permute-start(f32[144,384]{1,0:T(8,128)S(1)} %get-tuple-element.31), channel_id=1, source_target_pairs={{0,8},{8,0},{16,24},{24,16},{32,40},{40,32},{48,56},{56,48},{64,72... | collective-permute-start | bytes 663560 | tf_op jit(solution)/shard_map/ppermute | solution.py:805
  21.1 0.2 lat_steps.1.steps_ref
  21.2 0.9 %collective-permute-done.4.got_ref = f32[144,384]{1,0:T(8,128)S(1)} collective-permute-done((f32[144,384]{1,0:T(8,128)S(1)}, f32[144,384]{1,0:T(8,128)S(1)}, u32[]{:S(2)}, u32[]{:S(2)}) %collective-permute-start.4) | collective-permute-done | bytes 221216 | tf_op jit(solution)/shard_map/ppermute | solution.py:805
  22.2 1.5 %collective-permute-start.5 = (f32[144,384]{1,0:T(8,128)S(1)}, f32[144,384]{1,0:T(8,128)S(1)}, u32[]{:S(2)}, u32[]{:S(2)}) collective-permute-start(f32[144,384]{1,0:T(8,128)S(1)} %chip_merge.1.refs_3_.chip_ref), channel_id=1, source_target_pairs={{0,16},{8,24},{16,0},{24,8},{32,48},{40,56},{48,32},{56,40},{64,80... | collective-permute-start | bytes 663560 | tf_op jit(solution)/shard_map/ppermute | solution.py:807
  23.7 1.3 %local_filter.5.refs_3_.z2_ref = f32[16,48,384]{2,1,0:T(8,128)S(1)} custom-call(f32[48,128]{1,0:T(8,128)S(1)} %get-tuple-element.23.refs_0_.table_ref, f32[48,512]{1,0:T(8,128)S(1)} %get-tuple-element.32.refs_1_, f32[16,48,384]{2,1,0:T(8,128)S(1)} %local_filter.4._.refs_2_, f32[144,384]{1,0:T(8,128)S(1)} %chip_merge.1.refs_3_.chip_ref), custom_call_target="tpu_custom_call" | custom-call | flops 480000000 | bytes 2400000 | tf_op jit(solution)/shard_map/local_filter/pallas_call | solution.py:690
  24.9 4.3 %local_filter.6._.z0_ref = f32[16,48,384]{2,1,0:T(8,128)S(1)} custom-call(f32[48,128]{1,0:T(8,128)S(1)} %get-tuple-element.23.refs_0_.table_ref, f32[48,512]{1,0:T(8,128)S(1)} %get-tuple-element.32.refs_1_, f32[48,48,384]{2,1,0:T(8,128)S(1)} %get-tuple-element.26.refs_1_.x_ref.refs_2_, f32[16,48,384]{2,1,0:T(8,128)S(1)} %local_filter.5.refs_3_.z2_ref), custom_call_target="tpu_custom_call" | custom-call | flops 480000000 | bytes 2400000 | tf_op jit(solution)/shard_map/local_filter/pallas_call | solution.py:690
  29.3 0.0 collective-permute-done.5.pair_ref
  29.3 0.1 quad_merge.1
  29.3 3.7 %collective-permute-start.6 = (f32[72,384]{1,0:T(8,128)S(1)}, f32[72,384]{1,0:T(8,128)S(1)}, u32[]{:S(2)}, u32[]{:S(2)}) collective-permute-start(f32[72,384]{1,0:T(8,128)S(1)} %get-tuple-element.34), channel_id=1, source_target_pairs={{0,64},{8,72},{16,80},{24,88},{32,96},{40,104},{48,112},{56,120},{... | collective-permute-start | bytes 331784 | tf_op jit(solution)/shard_map/ppermute | solution.py:811
  33.0 0.7 %collective-permute-start.7 = (f32[72,384]{1,0:T(8,128)S(1)}, f32[72,384]{1,0:T(8,128)S(1)}, u32[]{:S(2)}, u32[]{:S(2)}) collective-permute-start(f32[72,384]{1,0:T(8,128)S(1)} %get-tuple-element.35), channel_id=1, source_target_pairs={{0,32},{8,40},{16,48},{24,56},{32,0},{40,8},{48,16},{56,24},{64,96... | collective-permute-start | bytes 331784 | tf_op jit(solution)/shard_map/ppermute | solution.py:811
  33.7 0.0 collective-permute-start.8
  33.7 2.8 %local_filter.7._.z1_ref = f32[16,48,384]{2,1,0:T(8,128)S(1)} custom-call(f32[48,128]{1,0:T(8,128)S(1)} %get-tuple-element.23.refs_0_.table_ref, f32[48,512]{1,0:T(8,128)S(1)} %get-tuple-element.32.refs_1_, f32[48,48,384]{2,1,0:T(8,128)S(1)} %get-tuple-element.26.refs_1_.x_ref.refs_2_, f32[72,384]{1,0:T(8,128)S(1)} %get-tuple-element.33.refs_3_.left_ref), custom_call_target="tpu_custom_call" | custom-call | flops 480000000 | bytes 2400000 | tf_op jit(solution)/shard_map/local_filter/pallas_call | solution.py:690
  36.6 0.0 collective-permute-done.6.g2_ref
  36.6 1.3 %collective-permute-done.7.g1_ref = f32[72,384]{1,0:T(8,128)S(1)} collective-permute-done((f32[72,384]{1,0:T(8,128)S(1)}, f32[72,384]{1,0:T(8,128)S(1)}, u32[]{:S(2)}, u32[]{:S(2)}) %collective-permute-start.7) | collective-permute-done | bytes 110624 | tf_op jit(solution)/shard_map/ppermute | solution.py:811
  37.9 0.7 %collective-permute-done.8.g3_ref = f32[72,384]{1,0:T(8,128)S(1)} collective-permute-done((f32[72,384]{1,0:T(8,128)S(1)}, f32[72,384]{1,0:T(8,128)S(1)}, u32[]{:S(2)}, u32[]{:S(2)}) %collective-permute-start.8) | collective-permute-done | bytes 110624 | tf_op jit(solution)/shard_map/ppermute | solution.py:811
  38.6 0.2 lat_carry.1
  38.8 2.8 %collective-permute-start.9 = (f32[144,384]{1,0:T(8,128)S(1)}, f32[144,384]{1,0:T(8,128)S(1)}, u32[]{:S(2)}, u32[]{:S(2)}) collective-permute-start(f32[144,384]{1,0:T(8,128)S(1)} %get-tuple-element.37), channel_id=1, source_target_pairs={{0,8},{8,0},{16,24},{24,16},{32,40},{40,32},{48,56},{56,48},{64,72... | collective-permute-start | bytes 663560 | tf_op jit(solution)/shard_map/ppermute | solution.py:814
  41.6 1.7 %finish_own.1 = (f32[48,48,384]{2,1,0:T(8,128)}, f32[16,48,384]{2,1,0:T(8,128)S(1)}) custom-call(f32[48,128]{1,0:T(8,128)S(1)} %get-tuple-element.23.refs_0_.table_ref, f32[2,3,3,8,384]{4,3,2,1,0:T(8,128)S(1)} %bitcast.7, f32[16,48,384]{2,1,0:T(8,128)S(1)} %local_filter.6._.z0_ref, f32[16,48,384]{2,1,0:T(8,128)S(1)} %local_filter.7._.z1_ref, ...), custom_call_target="tpu_custom_call" | custom-call | flops 1000000000 | bytes 2000000 | tf_op jit(solution)/shard_map/finish_own/pallas_call | solution.py:747
  43.3 0.0 collective-permute-done.9
  43.3 2.2 %finish.1 = f32[48,48,384]{2,1,0:T(8,128)} custom-call(f32[48,128]{1,0:T(8,128)S(1)} %get-tuple-element.23.refs_0_.table_ref, f32[2,3,3,8,384]{4,3,2,1,0:T(8,128)S(1)} %bitcast.6, f32[16,48,384]{2,1,0:T(8,128)S(1)} %local_filter.6._.z0_ref, f32[16,48,384]{2,1,0:T(8,128)S(1)} %local_filter.7._.z1_ref, ...), custom_call_target="tpu_custom_call", output_to_operand_aliasing={{}: (6, {})} | custom-call | tf_op jit(solution)/shard_map/finish/pallas_call | solution.py:778
  (1 shorter events, 0.0 us)
Async XLA Ops:
  4.1 8.7 %collective-permute-start.2 = (f32[48,512]{1,0:T(8,128)S(1)}, f32[48,512]{1,0:T(8,128)S(1)}, u32[]{:S(2)}, u32[]{:S(2)}) collective-permute-start(f32[48,512]{1,0:T(8,128)S(1)} %get-tuple-element.25.refs_2_.own_ref), channel_id=1, source_target_pairs={{0,2},{1,3},{2,0},{3,1},{4,6},{5,7},{6,4},{7,5},{8,10},{9,11},{10,... | collective-permute-start | bytes 294920 | tf_op jit(solution)/shard_map/ppermute | solution.py:797
  7.9 4.8 %collective-permute-start.1 = (f32[48,512]{1,0:T(8,128)S(1)}, f32[48,512]{1,0:T(8,128)S(1)}, u32[]{:S(2)}, u32[]{:S(2)}) collective-permute-start(f32[48,512]{1,0:T(8,128)S(1)} %get-tuple-element.25.refs_2_.own_ref), channel_id=1, source_target_pairs={{0,3},{1,2},{2,1},{3,0},{4,7},{5,6},{6,5},{7,4},{8,11},{9,10},{10,... | collective-permute-start | bytes 294920 | tf_op jit(solution)/shard_map/ppermute | solution.py:797
  8.7 4.1 %collective-permute-start = (f32[48,512]{1,0:T(8,128)S(1)}, f32[48,512]{1,0:T(8,128)S(1)}, u32[]{:S(2)}, u32[]{:S(2)}) collective-permute-start(f32[48,512]{1,0:T(8,128)S(1)} %get-tuple-element.25.refs_2_.own_ref), channel_id=1, source_target_pairs={{0,1},{1,0},{2,3},{3,2},{4,5},{5,4},{6,7},{7,6},{8,9},{9,8},{10,11... | collective-permute-start | bytes 294920 | tf_op jit(solution)/shard_map/ppermute | solution.py:797
  12.9 5.2 %collective-permute-start.3 = (f32[48,256]{1,0:T(8,128)S(1)}, f32[48,256]{1,0:T(8,128)S(1)}, u32[]{:S(2)}, u32[]{:S(2)}) collective-permute-start(f32[48,256]{1,0:T(8,128)S(1)} %get-tuple-element.28), channel_id=1, source_target_pairs={{0,4},{1,5},{2,6},{3,7},{4,0},{5,1},{6,2},{7,3},{8,12},{9,13},{10,... | collective-permute-start | bytes 147464 | tf_op jit(solution)/shard_map/ppermute | solution.py:801
  18.6 3.5 %collective-permute-start.4 = (f32[144,384]{1,0:T(8,128)S(1)}, f32[144,384]{1,0:T(8,128)S(1)}, u32[]{:S(2)}, u32[]{:S(2)}) collective-permute-start(f32[144,384]{1,0:T(8,128)S(1)} %get-tuple-element.31), channel_id=1, source_target_pairs={{0,8},{8,0},{16,24},{24,16},{32,40},{40,32},{48,56},{56,48},{64,72... | collective-permute-start | bytes 663560 | tf_op jit(solution)/shard_map/ppermute | solution.py:805
  22.2 7.1 %collective-permute-start.5 = (f32[144,384]{1,0:T(8,128)S(1)}, f32[144,384]{1,0:T(8,128)S(1)}, u32[]{:S(2)}, u32[]{:S(2)}) collective-permute-start(f32[144,384]{1,0:T(8,128)S(1)} %chip_merge.1.refs_3_.chip_ref), channel_id=1, source_target_pairs={{0,16},{8,24},{16,0},{24,8},{32,48},{40,56},{48,32},{56,40},{64,80... | collective-permute-start | bytes 663560 | tf_op jit(solution)/shard_map/ppermute | solution.py:807
  29.3 7.3 %collective-permute-start.6 = (f32[72,384]{1,0:T(8,128)S(1)}, f32[72,384]{1,0:T(8,128)S(1)}, u32[]{:S(2)}, u32[]{:S(2)}) collective-permute-start(f32[72,384]{1,0:T(8,128)S(1)} %get-tuple-element.34), channel_id=1, source_target_pairs={{0,64},{8,72},{16,80},{24,88},{32,96},{40,104},{48,112},{56,120},{... | collective-permute-start | bytes 331784 | tf_op jit(solution)/shard_map/ppermute | solution.py:811
  33.0 4.9 %collective-permute-start.7 = (f32[72,384]{1,0:T(8,128)S(1)}, f32[72,384]{1,0:T(8,128)S(1)}, u32[]{:S(2)}, u32[]{:S(2)}) collective-permute-start(f32[72,384]{1,0:T(8,128)S(1)} %get-tuple-element.35), channel_id=1, source_target_pairs={{0,32},{8,40},{16,48},{24,56},{32,0},{40,8},{48,16},{56,24},{64,96... | collective-permute-start | bytes 331784 | tf_op jit(solution)/shard_map/ppermute | solution.py:811
  33.7 4.8 %collective-permute-start.8 = (f32[72,384]{1,0:T(8,128)S(1)}, f32[72,384]{1,0:T(8,128)S(1)}, u32[]{:S(2)}, u32[]{:S(2)}) collective-permute-start(f32[72,384]{1,0:T(8,128)S(1)} %get-tuple-element.36), channel_id=1, source_target_pairs={{0,96},{8,104},{16,112},{24,120},{32,64},{40,72},{48,80},{56,88},{... | collective-permute-start | bytes 331784 | tf_op jit(solution)/shard_map/ppermute | solution.py:811
  38.8 4.5 %collective-permute-start.9 = (f32[144,384]{1,0:T(8,128)S(1)}, f32[144,384]{1,0:T(8,128)S(1)}, u32[]{:S(2)}, u32[]{:S(2)}) collective-permute-start(f32[144,384]{1,0:T(8,128)S(1)} %get-tuple-element.37), channel_id=1, source_target_pairs={{0,8},{8,0},{16,24},{24,16},{32,40},{40,32},{48,56},{56,48},{64,72... | collective-permute-start | bytes 663560 | tf_op jit(solution)/shard_map/ppermute | solution.py:814

commit v10 on v8

--- a/solution.py
+++ b/solution.py
@@ -698,6 +698,9 @@
     )(*[arrays[n] for n in names])
 
 
+PLACE = ((0, 0), (0, 1), (1, 0), (1, 1), (1, 2), (2, 0))
+
+
 def add_carries(half, table_ref, carry_ref, z_refs, part, store):
     row = fiota((8, LANES), 0)
     up_steps, down_steps = row + 1.0, 8.0 - row
@@ -718,8 +721,8 @@
             ups.append((jnp.concatenate(up, axis=0), jnp.concatenate(down, axis=0)))
         for b in range(PARTS):
             lanes = slice(b * LANES, (b + 1) * LANES)
-            total = jnp.where(half == 0, z_refs[part // 2][part % 2 * GROUP + i, :, lanes],
-                              z_refs[(3 + part) // 2][(3 + part) % 2 * GROUP + i, :, lanes])
+            total = jnp.where(half == 0, z_refs[PLACE[part][0]][PLACE[part][1] * GROUP + i, :, lanes],
+                              z_refs[PLACE[3 + part][0]][PLACE[3 + part][1] * GROUP + i, :, lanes])
             for s in range(SCALES):
                 total = total + ups[s][0] * tables[s][i:i + 1, lanes] + ups[s][1] * tables[SCALES + s][i:i + 1, lanes]
             store(i, lanes, total)
@@ -782,7 +785,7 @@
     facts = jnp.concatenate([lengths.T, weights.T], axis=0)
     sums, edge, table, lanes, held = row_sums(facts, x)
     got = [partner("lon", NLON, d)(sums) for d in (1, 2, 3)]
-    early = local_filter(table, None, held, 32, 16, sums)
+    early = local_filter(table, None, held, 40, 8, sums)
     winds = wind_sums(table, held, early)
     part, half = lon_merge(lanes, sums, got, winds)
     theirs = partner("lon", NLON, 4)(half)
@@ -792,11 +795,11 @@
     got_core = partner("lat", NLAT, 1)(send)
     chip = chip_merge(steps, keep, got_core)
     pair = partner("lat", NLAT, 2)(chip)
-    z2 = local_filter(table, carry, held, 32, 16, chip, early)
+    z2 = local_filter(table, carry, held, 40, 8, chip, early)
     z0 = local_filter(table, carry, held, 0, 16, z2)
     left, *sends = quad_merge(steps, chip, pair, z0)
     gs = [partner("lat", NLAT, 4 * d)(t) for d, t in zip((1, 2, 3), sends)]
-    z1 = local_filter(table, carry, held, 16, 16, left)
+    z1 = local_filter(table, carry, held, 16, 24, left)
     own, other = lat_carry(steps, keep, got_core, pair, left, gs, z1)
     got_carry = partner("lat", NLAT, 1)(other)
     done = finish_own(table, own, (z0, z1, z2))

time: 45.4 us -> 45.4 us (level)
  Pallas kernels: 22.8 us -> 22.3 us
    ppermute x3, waiting for transfers between devices: 1.95 us -> 0.75 us  [shards(): gs = [partner('lat', NLAT, 4 * d)(t) for d, t in zip((1, 2, 3), sends)]]
    ppermute x3, waiting for transfers between devices: 0.01 us -> 1.06 us  [shards(): got = [partner('lon', NLON, d)(sums) for d in (1, 2, 3)]]
    pallas_call x4, Pallas kernels: 11.2 us -> 10.6 us  [local_filter(): pl.pallas_call(body, in_specs=[specs.get(n, VMEM) for n in names], out_sp...]
  transfers between devices with their start and end apart: 10 -> 10, of which waited for: 3 -> 4; matrix products, arithmetic and copies ran while one was open for 0% -> 0% of each run, Pallas kernels for 36% -> 35%
where the time goes in v10:
time: 45.4 us; the launch traced here: 45.3 us
  Pallas kernels  22.3 us (49%)
  starting transfers between devices  18.9 us (42%)
  waiting for transfers between devices  3.13 us (7%)
  other arithmetic  0.71 us (2%)
    pallas_call x4, Pallas kernels, local_filter(): pl.pallas_call(body, in_specs=[specs.get(n, VMEM) for n in names], out_sp...  10.6 us
    ppermute x3, starting transfers between devices, shards(): got = [partner('lon', NLON, d)(sums) for d in (1, 2, 3)]  4.6 us
    ppermute x3, starting transfers between devices, shards(): gs = [partner('lat', NLAT, 4 * d)(t) for d, t in zip((1, 2, 3), sends)]  4.42 us
    pallas_call x1, Pallas kernels, row_sums(): pl.pallas_call(row_sums_kernel, in_specs=[VMEM, HBM], out_specs=[VMEM] *...  3.38 us
    ppermute x1, starting transfers between devices, shards(): got_carry = partner('lat', NLAT, 1)(other)  2.93 us
    ppermute x1, starting transfers between devices, shards(): theirs = partner('lon', NLON, 4)(half)  2.82 us
    ppermute x1, starting transfers between devices, shards(): got_core = partner('lat', NLAT, 1)(send)  2.63 us
    pallas_call x1, Pallas kernels, local_sums(): pl.pallas_call(local_sums_kernel, in_specs=[VMEM, VMEM, VMEM, ANY], out_s...  2.38 us
  transfers between devices with their start and end apart: 10, of which 4 were waited for; matrix products, arithmetic and copies ran while one was open for 0% of the time, Pallas kernels for 35%

profile of v10, /device:TPU:1, one launch (start us, length us, event | category | flops | bytes accessed | tf_op | source)
XLA Modules:
  0.0 45.3 jit_solution(13360616166931853849)
XLA Ops:
  0.0 0.7 %pad_maximum_fusion.len_ref = f32[6,48]{1,0:T(8,128)S(1)} fusion(f32[3,48]{1,0:T(4,128)} %bitcast.8, f32[3,48]{1,0:T(4,128)} %bitcast.9), kind=kLoop, calls=%fused_computation | loop fusion | flops 288 | bytes 2304 | tf_op jit(solution)/shard_map/concatenate | solution.py:785
  0.7 3.4 %row_sums.1 = (f32[48,512]{1,0:T(8,128)S(1)}, f32[48,256]{1,0:T(8,128)S(1)}, f32[48,128]{1,0:T(8,128)S(1)}, f32[8,128]{1,0:T(8,128)S(1)}, f32[48,48,384]{2,1,0:T(8,128)S(1)}) custom-call(f32[6,48]{1,0:T(8,128)S(1)} %pad_maximum_fusion.len_ref, f32[48,48,384]{2,1,0:T(8,128)} %x_ref.1), custom_call_target="tpu_custom_call" | custom-call | tf_op jit(solution)/shard_map/row_sums/pallas_call | solution.py:160
  4.1 3.8 %collective-permute-start.2 = (f32[48,512]{1,0:T(8,128)S(1)}, f32[48,512]{1,0:T(8,128)S(1)}, u32[]{:S(2)}, u32[]{:S(2)}) collective-permute-start(f32[48,512]{1,0:T(8,128)S(1)} %get-tuple-element.23.refs_2_.own_ref), channel_id=1, source_target_pairs={{0,2},{1,3},{2,0},{3,1},{4,6},{5,7},{6,4},{7,5},{8,10},{9,11},{10,... | collective-permute-start | bytes 294920 | tf_op jit(solution)/shard_map/ppermute | solution.py:787
  7.9 0.8 %collective-permute-start.1 = (f32[48,512]{1,0:T(8,128)S(1)}, f32[48,512]{1,0:T(8,128)S(1)}, u32[]{:S(2)}, u32[]{:S(2)}) collective-permute-start(f32[48,512]{1,0:T(8,128)S(1)} %get-tuple-element.23.refs_2_.own_ref), channel_id=1, source_target_pairs={{0,3},{1,2},{2,1},{3,0},{4,7},{5,6},{6,5},{7,4},{8,11},{9,10},{10,... | collective-permute-start | bytes 294920 | tf_op jit(solution)/shard_map/ppermute | solution.py:787
  8.7 0.0 collective-permute-start
  8.7 1.5 %local_filter.4._.refs_2_ = f32[8,48,384]{2,1,0:T(8,128)S(1)} custom-call(f32[48,128]{1,0:T(8,128)S(1)} %get-tuple-element.21.refs_0_.table_ref, f32[48,48,384]{2,1,0:T(8,128)S(1)} %get-tuple-element.24.refs_1_.x_ref.refs_2_, f32[48,512]{1,0:T(8,128)S(1)} %get-tuple-element.23.refs_2_.own_ref), custom_call_target="tpu_custom_call" | custom-call | flops 240000000 | bytes 1200000 | tf_op jit(solution)/shard_map/local_filter/pallas_call | solution.py:690
  10.2 1.3 %wind_sums.1._.winds_ref = f32[96,384]{1,0:T(8,128)S(1)} custom-call(f32[48,128]{1,0:T(8,128)S(1)} %get-tuple-element.21.refs_0_.table_ref, f32[48,48,384]{2,1,0:T(8,128)S(1)} %get-tuple-element.24.refs_1_.x_ref.refs_2_, f32[8,48,384]{2,1,0:T(8,128)S(1)} %local_filter.4._.refs_2_), custom_call_target="tpu_custom_call" | custom-call | flops 300000000 | bytes 1000000 | tf_op jit(solution)/shard_map/wind_sums/pallas_call | solution.py:229
  11.5 0.0 collective-permute-done.2.g2_ref
  11.5 1.1 %collective-permute-done.1.g3_ref = f32[48,512]{1,0:T(8,128)S(1)} collective-permute-done((f32[48,512]{1,0:T(8,128)S(1)}, f32[48,512]{1,0:T(8,128)S(1)}, u32[]{:S(2)}, u32[]{:S(2)}) %collective-permute-start.1) | collective-permute-done | bytes 98336 | tf_op jit(solution)/shard_map/ppermute | solution.py:787
  12.6 0.0 collective-permute-done.g1_ref
  12.6 0.1 lon_merge.1
  12.7 2.8 %collective-permute-start.3 = (f32[48,256]{1,0:T(8,128)S(1)}, f32[48,256]{1,0:T(8,128)S(1)}, u32[]{:S(2)}, u32[]{:S(2)}) collective-permute-start(f32[48,256]{1,0:T(8,128)S(1)} %get-tuple-element.26), channel_id=1, source_target_pairs={{0,4},{1,5},{2,6},{3,7},{4,0},{5,1},{6,2},{7,3},{8,12},{9,13},{10,... | collective-permute-start | bytes 147464 | tf_op jit(solution)/shard_map/ppermute | solution.py:791
  15.5 2.4 %local_sums.1 = f32[2,2,3,3,8,384]{5,4,3,2,1,0:T(8,128)S(1)} custom-call(f32[48,128]{1,0:T(8,128)S(1)} %get-tuple-element.21.refs_0_.table_ref, f32[48,48,384]{2,1,0:T(8,128)S(1)} %get-tuple-element.24.refs_1_.x_ref.refs_2_, f32[96,384]{1,0:T(8,128)S(1)} %wind_sums.1._.winds_ref, f32[48,768]{1,0:T(8,128)S(1)} %get-tuple-element.25._.part_ref), custom_call_target="tpu_custom_call" | custom-call | flops 600000000 | bytes 4000000 | tf_op jit(solution)/shard_map/local_sums/pallas_call | solution.py:268
  17.9 0.0 collective-permute-done.3.theirs_ref
  17.9 0.5 %column_sums.1 = (f32[48,512]{1,0:T(8,128)S(1)}, f32[144,384]{1,0:T(8,128)S(1)}, f32[144,384]{1,0:T(8,128)S(1)}) custom-call(f32[48,128]{1,0:T(8,128)S(1)} %get-tuple-element.21.refs_0_.table_ref, f32[8,128]{1,0:T(8,128)S(1)} %get-tuple-element.22.lanes_ref, f32[48,768]{1,0:T(8,128)S(1)} %get-tuple-element.25._.part_ref, ...), custom_call_target="tpu_custom_call" | custom-call | tf_op jit(solution)/shard_map/column_sums/pallas_call | solution.py:407
  18.4 2.6 %collective-permute-start.4 = (f32[144,384]{1,0:T(8,128)S(1)}, f32[144,384]{1,0:T(8,128)S(1)}, u32[]{:S(2)}, u32[]{:S(2)}) collective-permute-start(f32[144,384]{1,0:T(8,128)S(1)} %get-tuple-element.29), channel_id=1, source_target_pairs={{0,8},{8,0},{16,24},{24,16},{32,40},{40,32},{48,56},{56,48},{64,72... | collective-permute-start | bytes 663560 | tf_op jit(solution)/shard_map/ppermute | solution.py:795
  21.0 0.2 lat_steps.1.steps_ref
  21.2 0.9 %collective-permute-done.4.got_ref = f32[144,384]{1,0:T(8,128)S(1)} collective-permute-done((f32[144,384]{1,0:T(8,128)S(1)}, f32[144,384]{1,0:T(8,128)S(1)}, u32[]{:S(2)}, u32[]{:S(2)}) %collective-permute-start.4) | collective-permute-done | bytes 221216 | tf_op jit(solution)/shard_map/ppermute | solution.py:795
  22.2 1.5 %collective-permute-start.5 = (f32[144,384]{1,0:T(8,128)S(1)}, f32[144,384]{1,0:T(8,128)S(1)}, u32[]{:S(2)}, u32[]{:S(2)}) collective-permute-start(f32[144,384]{1,0:T(8,128)S(1)} %chip_merge.1.refs_3_.chip_ref), channel_id=1, source_target_pairs={{0,16},{8,24},{16,0},{24,8},{32,48},{40,56},{48,32},{56,40},{64,80... | collective-permute-start | bytes 663560 | tf_op jit(solution)/shard_map/ppermute | solution.py:797
  23.7 0.8 %local_filter.5.refs_3_.z2_ref = f32[8,48,384]{2,1,0:T(8,128)S(1)} custom-call(f32[48,128]{1,0:T(8,128)S(1)} %get-tuple-element.21.refs_0_.table_ref, f32[48,512]{1,0:T(8,128)S(1)} %get-tuple-element.30.refs_1_, f32[8,48,384]{2,1,0:T(8,128)S(1)} %local_filter.4._.refs_2_, f32[144,384]{1,0:T(8,128)S(1)} %chip_merge.1.refs_3_.chip_ref), custom_call_target="tpu_custom_call" | custom-call | flops 240000000 | bytes 1200000 | tf_op jit(solution)/shard_map/local_filter/pallas_call | solution.py:690
  24.4 4.3 %local_filter.6._.z0_ref = f32[16,48,384]{2,1,0:T(8,128)S(1)} custom-call(f32[48,128]{1,0:T(8,128)S(1)} %get-tuple-element.21.refs_0_.table_ref, f32[48,512]{1,0:T(8,128)S(1)} %get-tuple-element.30.refs_1_, f32[48,48,384]{2,1,0:T(8,128)S(1)} %get-tuple-element.24.refs_1_.x_ref.refs_2_, f32[8,48,384]{2,1,0:T(8,128)S(1)} %local_filter.5.refs_3_.z2_ref), custom_call_target="tpu_custom_call" | custom-call | flops 480000000 | bytes 2400000 | tf_op jit(solution)/shard_map/local_filter/pallas_call | solution.py:690
  28.7 0.4 collective-permute-done.5.pair_ref
  29.1 0.1 quad_merge.1
  29.1 3.7 %collective-permute-start.6 = (f32[72,384]{1,0:T(8,128)S(1)}, f32[72,384]{1,0:T(8,128)S(1)}, u32[]{:S(2)}, u32[]{:S(2)}) collective-permute-start(f32[72,384]{1,0:T(8,128)S(1)} %get-tuple-element.32), channel_id=1, source_target_pairs={{0,64},{8,72},{16,80},{24,88},{32,96},{40,104},{48,112},{56,120},{... | collective-permute-start | bytes 331784 | tf_op jit(solution)/shard_map/ppermute | solution.py:801
  32.8 0.7 %collective-permute-start.7 = (f32[72,384]{1,0:T(8,128)S(1)}, f32[72,384]{1,0:T(8,128)S(1)}, u32[]{:S(2)}, u32[]{:S(2)}) collective-permute-start(f32[72,384]{1,0:T(8,128)S(1)} %get-tuple-element.33), channel_id=1, source_target_pairs={{0,32},{8,40},{16,48},{24,56},{32,0},{40,8},{48,16},{56,24},{64,96... | collective-permute-start | bytes 331784 | tf_op jit(solution)/shard_map/ppermute | solution.py:801
  33.6 0.0 collective-permute-start.8
  33.6 4.1 %local_filter.7._.z1_ref = f32[24,48,384]{2,1,0:T(8,128)S(1)} custom-call(f32[48,128]{1,0:T(8,128)S(1)} %get-tuple-element.21.refs_0_.table_ref, f32[48,512]{1,0:T(8,128)S(1)} %get-tuple-element.30.refs_1_, f32[48,48,384]{2,1,0:T(8,128)S(1)} %get-tuple-element.24.refs_1_.x_ref.refs_2_, f32[72,384]{1,0:T(8,128)S(1)} %get-tuple-element.31.refs_3_.left_ref), custom_call_target="tpu_custom_call" | custom-call | flops 720000000 | bytes 3600000 | tf_op jit(solution)/shard_map/local_filter/pallas_call | solution.py:690
  37.7 0.0 collective-permute-done.6.g2_ref
  37.7 0.0 collective-permute-done.7.g1_ref
  37.7 0.7 %collective-permute-done.8.g3_ref = f32[72,384]{1,0:T(8,128)S(1)} collective-permute-done((f32[72,384]{1,0:T(8,128)S(1)}, f32[72,384]{1,0:T(8,128)S(1)}, u32[]{:S(2)}, u32[]{:S(2)}) %collective-permute-start.8) | collective-permute-done | bytes 110624 | tf_op jit(solution)/shard_map/ppermute | solution.py:801
  38.4 0.2 lat_carry.1
  38.6 2.9 %collective-permute-start.9 = (f32[144,384]{1,0:T(8,128)S(1)}, f32[144,384]{1,0:T(8,128)S(1)}, u32[]{:S(2)}, u32[]{:S(2)}) collective-permute-start(f32[144,384]{1,0:T(8,128)S(1)} %get-tuple-element.35), channel_id=1, source_target_pairs={{0,8},{8,0},{16,24},{24,16},{32,40},{40,32},{48,56},{56,48},{64,72... | collective-permute-start | bytes 663560 | tf_op jit(solution)/shard_map/ppermute | solution.py:804
  41.6 1.1 %finish_own.1.own_ref = f32[24,48,384]{2,1,0:T(8,128)S(1)} custom-call(f32[48,128]{1,0:T(8,128)S(1)} %get-tuple-element.21.refs_0_.table_ref, f32[2,3,3,8,384]{4,3,2,1,0:T(8,128)S(1)} %bitcast.6, f32[16,48,384]{2,1,0:T(8,128)S(1)} %local_filter.6._.z0_ref, f32[24,48,384]{2,1,0:T(8,128)S(1)} %local_filter.7._.z1_ref, f32[8,48,384]{2,1,0:T(8,128)S(1)} %local_filter.5.refs_3_.z2_ref), custom_call_target="tpu_custom_call" | custom-call | flops 1000000000 | bytes 2000000 | tf_op jit(solution)/shard_map/finish_own/pallas_call | solution.py:740
  42.7 0.0 collective-permute-done.9
  42.7 2.4 %finish.1 = f32[48,48,384]{2,1,0:T(8,128)} custom-call(f32[48,128]{1,0:T(8,128)S(1)} %get-tuple-element.21.refs_0_.table_ref, f32[2,3,3,8,384]{4,3,2,1,0:T(8,128)S(1)} %bitcast.7, f32[16,48,384]{2,1,0:T(8,128)S(1)} %local_filter.6._.z0_ref, f32[24,48,384]{2,1,0:T(8,128)S(1)} %local_filter.7._.z1_ref, f32[8,48,384]{2,1,0:T(8,128)S(1)} %local_filter.5.refs_3_.z2_ref, ...), custom_call_target="tpu_custom_call" | custom-call | tf_op jit(solution)/shard_map/finish/pallas_call | solution.py:769
  (1 shorter events, 0.0 us)
Async XLA Ops:
  4.1 7.4 %collective-permute-start.2 = (f32[48,512]{1,0:T(8,128)S(1)}, f32[48,512]{1,0:T(8,128)S(1)}, u32[]{:S(2)}, u32[]{:S(2)}) collective-permute-start(f32[48,512]{1,0:T(8,128)S(1)} %get-tuple-element.23.refs_2_.own_ref), channel_id=1, source_target_pairs={{0,2},{1,3},{2,0},{3,1},{4,6},{5,7},{6,4},{7,5},{8,10},{9,11},{10,... | collective-permute-start | bytes 294920 | tf_op jit(solution)/shard_map/ppermute | solution.py:787
  7.9 4.7 %collective-permute-start.1 = (f32[48,512]{1,0:T(8,128)S(1)}, f32[48,512]{1,0:T(8,128)S(1)}, u32[]{:S(2)}, u32[]{:S(2)}) collective-permute-start(f32[48,512]{1,0:T(8,128)S(1)} %get-tuple-element.23.refs_2_.own_ref), channel_id=1, source_target_pairs={{0,3},{1,2},{2,1},{3,0},{4,7},{5,6},{6,5},{7,4},{8,11},{9,10},{10,... | collective-permute-start | bytes 294920 | tf_op jit(solution)/shard_map/ppermute | solution.py:787
  8.7 3.9 %collective-permute-start = (f32[48,512]{1,0:T(8,128)S(1)}, f32[48,512]{1,0:T(8,128)S(1)}, u32[]{:S(2)}, u32[]{:S(2)}) collective-permute-start(f32[48,512]{1,0:T(8,128)S(1)} %get-tuple-element.23.refs_2_.own_ref), channel_id=1, source_target_pairs={{0,1},{1,0},{2,3},{3,2},{4,5},{5,4},{6,7},{7,6},{8,9},{9,8},{10,11... | collective-permute-start | bytes 294920 | tf_op jit(solution)/shard_map/ppermute | solution.py:787
  12.7 5.2 %collective-permute-start.3 = (f32[48,256]{1,0:T(8,128)S(1)}, f32[48,256]{1,0:T(8,128)S(1)}, u32[]{:S(2)}, u32[]{:S(2)}) collective-permute-start(f32[48,256]{1,0:T(8,128)S(1)} %get-tuple-element.26), channel_id=1, source_target_pairs={{0,4},{1,5},{2,6},{3,7},{4,0},{5,1},{6,2},{7,3},{8,12},{9,13},{10,... | collective-permute-start | bytes 147464 | tf_op jit(solution)/shard_map/ppermute | solution.py:791
  18.4 3.7 %collective-permute-start.4 = (f32[144,384]{1,0:T(8,128)S(1)}, f32[144,384]{1,0:T(8,128)S(1)}, u32[]{:S(2)}, u32[]{:S(2)}) collective-permute-start(f32[144,384]{1,0:T(8,128)S(1)} %get-tuple-element.29), channel_id=1, source_target_pairs={{0,8},{8,0},{16,24},{24,16},{32,40},{40,32},{48,56},{56,48},{64,72... | collective-permute-start | bytes 663560 | tf_op jit(solution)/shard_map/ppermute | solution.py:795
  22.2 6.9 %collective-permute-start.5 = (f32[144,384]{1,0:T(8,128)S(1)}, f32[144,384]{1,0:T(8,128)S(1)}, u32[]{:S(2)}, u32[]{:S(2)}) collective-permute-start(f32[144,384]{1,0:T(8,128)S(1)} %chip_merge.1.refs_3_.chip_ref), channel_id=1, source_target_pairs={{0,16},{8,24},{16,0},{24,8},{32,48},{40,56},{48,32},{56,40},{64,80... | collective-permute-start | bytes 663560 | tf_op jit(solution)/shard_map/ppermute | solution.py:797
  29.1 8.5 %collective-permute-start.6 = (f32[72,384]{1,0:T(8,128)S(1)}, f32[72,384]{1,0:T(8,128)S(1)}, u32[]{:S(2)}, u32[]{:S(2)}) collective-permute-start(f32[72,384]{1,0:T(8,128)S(1)} %get-tuple-element.32), channel_id=1, source_target_pairs={{0,64},{8,72},{16,80},{24,88},{32,96},{40,104},{48,112},{56,120},{... | collective-permute-start | bytes 331784 | tf_op jit(solution)/shard_map/ppermute | solution.py:801
  32.8 4.8 %collective-permute-start.7 = (f32[72,384]{1,0:T(8,128)S(1)}, f32[72,384]{1,0:T(8,128)S(1)}, u32[]{:S(2)}, u32[]{:S(2)}) collective-permute-start(f32[72,384]{1,0:T(8,128)S(1)} %get-tuple-element.33), channel_id=1, source_target_pairs={{0,32},{8,40},{16,48},{24,56},{32,0},{40,8},{48,16},{56,24},{64,96... | collective-permute-start | bytes 331784 | tf_op jit(solution)/shard_map/ppermute | solution.py:801
  33.6 4.9 %collective-permute-start.8 = (f32[72,384]{1,0:T(8,128)S(1)}, f32[72,384]{1,0:T(8,128)S(1)}, u32[]{:S(2)}, u32[]{:S(2)}) collective-permute-start(f32[72,384]{1,0:T(8,128)S(1)} %get-tuple-element.34), channel_id=1, source_target_pairs={{0,96},{8,104},{16,112},{24,120},{32,64},{40,72},{48,80},{56,88},{... | collective-permute-start | bytes 331784 | tf_op jit(solution)/shard_map/ppermute | solution.py:801
  38.6 4.1 %collective-permute-start.9 = (f32[144,384]{1,0:T(8,128)S(1)}, f32[144,384]{1,0:T(8,128)S(1)}, u32[]{:S(2)}, u32[]{:S(2)}) collective-permute-start(f32[144,384]{1,0:T(8,128)S(1)} %get-tuple-element.35), channel_id=1, source_target_pairs={{0,8},{8,0},{16,24},{24,16},{32,40},{40,32},{48,56},{56,48},{64,72... | collective-permute-start | bytes 663560 | tf_op jit(solution)/shard_map/ppermute | solution.py:804
